TPU v7x, 128 devices: a whole 4x4x4 slice. The times are simulated.
128 devices in a mesh: expert: 32 (over z, y, x_lo), dp: 4 (over x_hi, core).
Axes of the slice: x: 4 (x_hi: 2, x_lo: 2; x = x_hi * 2 + x_lo), y: 4, z: 4, core: 2. Of those that a mesh axis runs over, the one named last changes fastest.
Arguments:
- tokens: bfloat16 [2048, 4096], P(('expert', 'dp')), may hold values from -6 to 6
- expert_ids: int32 [2048, 8], P(('expert', 'dp')), may hold values from 0 to 63, all different within a row; in each aligned block of 16 rows (0 to 15, 16 to 31, ...) at most 4 rows name the same one
- gate_weights: float32 [2048, 8], P(('expert', 'dp')), may hold values from 0.1 to 0.5
- placement: int32 [64], replicated, may hold values from 0 to 63, as said below
- w_gate: bfloat16 [64, 4096, 1536], P('expert', None, 'dp'), may hold values from -0.09375 to 0.09375
- w_up: bfloat16 [64, 4096, 1536], P('expert', None, 'dp'), may hold values from -0.09375 to 0.09375
- w_down: bfloat16 [64, 1536, 4096], P('expert', 'dp'), may hold values from -0.15625 to 0.15625
Outputs:
- mixed: bfloat16 [2048, 4096], P(('expert', 'dp'))
Inputs may be any that keep to these rules, and one draw needn't show every extreme that they name: `expert_ids`: each token names 8 different experts; among the 16 tokens of one device no expert is named more than 4 times. `placement`: A permutation of the 64 slots; slot s lies on index s // 2 of the expert axis. The indices of the expert axis are matched in pairs and each pair exchanges one expert; every other expert e sits in slot e.
All inputs are finite; a program needn't handle non-finite values.
Results may differ from a plain program's by a relative error of at most 0.014.
Values may be sent and summed in bfloat16 or wider, within the bound.
No kernel may reach another device: no remote copies, remote signals or barrier semaphores. Data moves between devices by JAX's collectives and lax.ppermute only.
A program may use at most 128 MiB of HBM per device.

v0:
```python
import jax
import jax.numpy as jnp
from jax import lax
from jax.sharding import PartitionSpec as P


def shards(tokens, expert_ids, gate_weights, placement, w_gate, w_up, w_down):
    n_expert = lax.axis_size("expert")
    n_quarter = lax.axis_size("dp")
    per_device = w_gate.shape[0]
    tok_count = expert_ids.shape[0]
    top_count = expert_ids.shape[1]
    width = tokens.shape[1]
    slots = per_device * n_expert
    capacity = max(4, 2 * tok_count * top_count // slots)
    flat_ids = expert_ids.reshape(-1)
    slot_range = jnp.arange(slots, dtype=jnp.int32)
    lookup = (flat_ids[:, None] == slot_range[None, :]).astype(jnp.int32)
    slot_of = jnp.sum(lookup * placement[None, :], axis=1)
    onehot = (slot_of[:, None] == slot_range[None, :]).astype(jnp.int32)
    earlier = jnp.cumsum(onehot, axis=0) - onehot
    order_in = jnp.sum(earlier * onehot, axis=1)
    target = slot_of * capacity + order_in
    source_rows = jnp.repeat(tokens, top_count, axis=0)
    outgoing = jnp.zeros((slots * capacity, width), tokens.dtype).at[target].set(source_rows)
    outgoing = outgoing.reshape(n_expert, per_device, capacity, width)
    arrived = lax.all_to_all(outgoing, "expert", split_axis=0, concat_axis=0, tiled=True)
    rows_in = lax.all_gather(arrived[:, None], "dp", axis=1, tiled=True)
    gate = jnp.einsum("sqlcd,ldf->sqlcf", rows_in, w_gate, preferred_element_type=jnp.float32)
    up = jnp.einsum("sqlcd,ldf->sqlcf", rows_in, w_up, preferred_element_type=jnp.float32)
    hidden = (jax.nn.silu(gate) * up).astype(jnp.bfloat16)
    partial_value = jnp.einsum(
        "sqlcf,lfd->sqlcd", hidden, w_down, preferred_element_type=jnp.float32
    ).astype(jnp.bfloat16)
    sending = partial_value.reshape(n_expert * n_quarter, per_device, capacity, width)
    came_back = lax.all_to_all(sending, ("expert", "dp"), split_axis=0, concat_axis=0, tiled=True)
    came_back = came_back.reshape(n_expert, n_quarter, per_device, capacity, width)
    returned = jnp.sum(came_back.astype(jnp.float32), axis=1).astype(jnp.bfloat16)
    picked = returned.reshape(slots * capacity, width)[target].reshape(tok_count, top_count, width)
    mixed = jnp.einsum("tk,tkd->td", gate_weights, picked.astype(jnp.float32))
    return mixed.astype(jnp.bfloat16)


def solution(mesh):
    in_specs = (
        P(("expert", "dp"), None),
        P(("expert", "dp"), None),
        P(("expert", "dp"), None),
        P(),
        P("expert", None, "dp"),
        P("expert", None, "dp"),
        P("expert", "dp", None),
    )
    out_specs = P(("expert", "dp"), None)
    return jax.shard_map(shards, mesh=mesh, in_specs=in_specs, out_specs=out_specs, check_vma=False)
```

profile of v0, /device:TPU:0, one launch (start us, length us, event | category | flops | bytes accessed | tf_op | source)
XLA Modules:
  0.0 288.4 jit_solution(4663890106599051941)
XLA Ops:
  6.5 0.0 copy-start
  6.5 0.0 all-gather.3.cloned.1.call-start
  6.5 0.8 copy.12
  7.3 0.1 eq.28
  7.4 0.8 select_reduce_fusion.1
  8.3 0.1 fusion.26
  8.4 0.2 reduce_window_sum.11
  8.5 0.2 select_reduce_fusion
  8.7 0.0 copy-done
  8.7 2.7 scatter_custom_fusion
  11.5 2.2 reshape.48
  13.7 38.6 %all_to_all.10 = bf16[32,2,4,4096]{3,2,1,0:T(4,128)(2,1)} all-to-all(bf16[32,2,4,4096]{3,2,1,0:T(4,128)(2,1)} %reshape.48), channel_id=1, replica_groups=mesh['expert'=32,'dp'=4] {'expert'}, dimensions={0} | all-to-all | bytes 4194304 | tf_op jit(solution)/shard_map/all_to_all | solution.py:27
  52.3 0.0 all-gather.3.cloned.1.call-update
  52.3 59.6 %all-gather.3.cloned.1.call-done = bf16[32,8,4,4096]{3,2,1,0:T(4,128)(2,1)} async-done(((bf16[32,2,4,4096]{3,2,1,0:T(4,128)(2,1)}), bf16[32,8,4,4096]{3,2,1,0:T(4,128)(2,1)}) %all-gather.3.cloned.1.call-update) | async-done | bytes 8388624 | tf_op jit(solution)/shard_map/all_gather | solution.py:28
  111.9 11.5 %copy.13 = bf16[32,8,4,4096]{3,0,2,1:T(8,128)(2,1)} copy(bf16[32,8,4,4096]{3,2,1,0:T(4,128)(2,1)} %all-gather.3.cloned.1.call-done) | data formatting | bytes 16777216 | tf_op jit(solution)/shard_map/all_gather | solution.py:28
  123.3 9.1 %fusion.2 = f32[2,32,4,4,384]{4,1,3,2,0:T(8,128)S(1)} fusion(bf16[32,4,2,4,4096]{4,0,3,2,1:T(8,128)(2,1)} %bitcast.62, bf16[2,4096,384]{2,1,0:T(8,128)(2,1)} %param.11), kind=kOutput, calls=%fused_computation.6 | convolution fusion | flops 3221225472 | bytes 16252928 | tf_op jit(solution)/shard_map/sqlcd,ldf->sqlcf/dot_general | solution.py:29
  132.5 15.1 %convert_bitcast_fusion = bf16[32,4,2,4,4096]{4,0,3,1,2:T(8,128)(2,1)} fusion(bf16[2,384,4096]{2,1,0:T(8,128)(2,1)} %param.13, f32[2,32,4,4,384]{4,1,3,2,0:T(8,128)S(1)} %fusion.2, bf16[2,4096,384]{2,1,0:T(8,128)(2,1)} %param.12, bf16[32,4,2,4,4096]{4,0,3,2,1:T(8,128)(2,1)} %bitcast.63), kind=kOutput, calls=%fused_computation.3 | convolution fusion | flops 6449004544 | bytes 30932992 | tf_op jit(solution)/shard_map/sqlcf,lfd->sqlcd/dot_general | solution.py:32
  147.6 12.2 %copy.16 = bf16[32,4,2,4,4096]{4,3,2,1,0:T(4,128)(2,1)} copy(bf16[32,4,2,4,4096]{4,0,3,1,2:T(8,128)(2,1)} %convert_bitcast_fusion) | data formatting | bytes 16777216 | tf_op jit(solution)/shard_map/convert_element_type | solution.py:34
  159.7 0.0 copy-start.2
  159.7 8.7 %all-to-all-start.1 = ((bf16[128,2,4,4096]{3,2,1,0:T(4,128)(2,1)}), bf16[128,2,4,4096]{3,2,1,0:T(4,128)(2,1)}, u32[]{:S(2)}, u32[]{:S(2)}) async-start(bf16[128,2,4,4096]{3,2,1,0:T(4,128)(2,1)} %bitcast.61), calls=%async_computation.1 | async-start | bytes 16777216 | tf_op jit(solution)/shard_map/all_to_all | solution.py:36
  168.4 0.0 copy-done.2
  168.4 0.1 copy.20
  168.5 97.9 %all-to-all-done.1 = bf16[128,2,4,4096]{3,2,1,0:T(4,128)(2,1)} async-done(((bf16[128,2,4,4096]{3,2,1,0:T(4,128)(2,1)}), bf16[128,2,4,4096]{3,2,1,0:T(4,128)(2,1)}, u32[]{:S(2)}, u32[]{:S(2)}) %all-to-all-start.1) | async-done | bytes 8388640 | tf_op jit(solution)/shard_map/all_to_all | solution.py:36
  266.4 10.2 %bitcast_reduce_fusion = bf16[32,2,4,4096]{3,2,1,0:T(4,128)(2,1)} fusion(bf16[128,2,4,4096]{3,2,1,0:T(4,128)(2,1)} %all-to-all-done.1), kind=kLoop, calls=%fused_computation.2 | loop fusion | flops 3145728 | bytes 10485760 | tf_op jit(solution)/shard_map/reduce_sum | solution.py:38
  276.6 0.0 copy-start.1
  276.6 2.6 reshape.51
  279.2 1.2 gather_fusion
  280.4 0.4 fusion.19
  280.8 0.8 copy.31
  281.6 0.0 copy-done.1
  (2 shorter events, 0.0 us)
Async XLA Ops:
  6.5 2.2 copy-start
  6.5 105.4 %all-gather.3.cloned.1.call-start = ((), (), s32[]{:S(2)}) async-start(), calls=%async_computation.2 | async-start | bytes 10485760 | tf_op jit(solution)/shard_map/all_gather | solution.py:28
  159.7 8.7 %copy-start.2 = (f32[16,8]{0,1:T(8,128)S(1)}, f32[16,8]{0,1:T(8,128)}, u32[]{:S(2)}) copy-start(f32[16,8]{0,1:T(8,128)} %param.9) | copy-start | bytes 1540
  159.7 106.6 %all-to-all-start.1 = ((bf16[128,2,4,4096]{3,2,1,0:T(4,128)(2,1)}), bf16[128,2,4,4096]{3,2,1,0:T(4,128)(2,1)}, u32[]{:S(2)}, u32[]{:S(2)}) async-start(bf16[128,2,4,4096]{3,2,1,0:T(4,128)(2,1)} %bitcast.61), calls=%async_computation.1 | async-start | bytes 16777216 | tf_op jit(solution)/shard_map/all_to_all | solution.py:36
  276.6 5.0 %copy-start.1 = (bf16[16,4096]{1,0:T(8,128)(2,1)S(1)}, bf16[16,4096]{1,0:T(8,128)(2,1)}, u32[]{:S(2)}) copy-start(bf16[16,4096]{1,0:T(8,128)(2,1)} %param.7) | copy-start | bytes 393220
Sparse Core Ops, SparseCore 0:
  52.4 59.4 all-gather.2
where the time goes:
time: 290 us; the launch traced here: 288 us
  waiting for transfers between devices  157 us (54%)
  blocking collectives  38.6 us (13%)
  local copies, waits for them, and re-layouts  34.1 us (12%)
  matrix products  24.6 us (8%)
  between operations  13.5 us (5%)
  other arithmetic  11.5 us (4%)
  starting transfers between devices  8.67 us (3%)
    all_to_all x1, waiting for transfers between devices, shards(): lax.all_to_all(sending, ('expert', 'dp'), split_axis=0, concat_axis=0, ti...  97.9 us
    all_gather x1, waiting for transfers between devices, shards(): rows_in = lax.all_gather(arrived[:, None], 'dp', axis=1, tiled=True)  59.6 us
    all_to_all x1, blocking collectives, shards(): lax.all_to_all(outgoing, 'expert', split_axis=0, concat_axis=0, tiled=True)  38.6 us
    dot_general x1, matrix products, shards(): jnp.einsum('sqlcf,lfd->sqlcd', hidden, w_down, preferred_element_type=jnp...  15.1 us
    convert_element_type x1, local copies, waits for them, and re-layouts, shards(): partial_value = jnp.einsum('sqlcf,lfd->sqlcd', hidden, w_down, preferred_...  12.2 us
    all_gather x1, local copies, waits for them, and re-layouts, shards(): rows_in = lax.all_gather(arrived[:, None], 'dp', axis=1, tiled=True)  11.5 us
    reduce_sum x1, other arithmetic, shards(): jnp.sum(came_back.astype(jnp.float32), axis=1).astype(jnp.bfloat16)  10.2 us
    dot_general x1, matrix products, shards(): jnp.einsum('sqlcd,ldf->sqlcf', rows_in, w_gate, preferred_element_type=jn...  9.1 us
  transfers between devices with their start and end apart: 2, of which 2 were waited for; matrix products, arithmetic and copies ran while one was open for 0% of the time, Pallas kernels for 0%

commit v1 on v0

v1 whole, which is shorter than its diff:
```python
import jax
import jax.numpy as jnp
from jax import lax
from jax.sharding import PartitionSpec as P

AXES = ("expert", "dp")
SIDE = 4
META = 128
FIRST, SECOND = (1, 3), (3, 1)


def partners(axis, masks):
    pairs = []
    for z in range(SIDE):
        for y in range(SIDE):
            for x in range(SIDE):
                for core in range(2):
                    other, to_core = [z, y, x], core
                    if axis == "core":
                        to_core = 1 - core
                    else:
                        other["zyx".index(axis)] ^= masks[core]
                    pairs.append((place(z, y, x, core), place(*other, to_core)))
    return pairs


def place(z, y, x, core):
    return ((z * SIDE + y) * 2 + x % 2) * 4 + (x // 2) * 2 + core


def swap(value, axis, masks=None):
    return lax.ppermute(value, AXES, partners(axis, masks))


def gather_line(value, axis):
    pair = jnp.stack([value, swap(value, axis, FIRST)])
    return jnp.concatenate([pair, swap(pair, axis, SECOND)])


def sum_line(value, axis):
    here = value[:2] + swap(value[2:].astype(jnp.bfloat16), axis, SECOND).astype(jnp.float32)
    return here[0] + swap(here[1].astype(jnp.bfloat16), axis, FIRST).astype(jnp.float32)


def chooser(rows, slots, half, tok_count, cap):
    count = rows.shape[0]
    named_slots = rows[:, half : half + 8].astype(jnp.float32).astype(jnp.int32)
    named = jnp.any(named_slots[None] == slots[:, None, None], axis=2)
    grouped = named.reshape(slots.shape[0], -1, tok_count)
    earlier = jnp.arange(tok_count)[:, None] > jnp.arange(tok_count)[None, :]
    rank = jnp.sum((grouped[:, :, None, :] & earlier[None, None]).astype(jnp.int32), axis=3)
    rank = jnp.where(grouped, rank, -1).reshape(slots.shape[0], count)
    lines = (count // tok_count) * cap
    line = jnp.arange(lines, dtype=jnp.int32)
    block = jnp.arange(count, dtype=jnp.int32) // tok_count
    hit = (rank[:, None, :] == (line % cap)[None, :, None]) & (block[None, :] == (line // cap)[:, None])[None]
    return hit.reshape(slots.shape[0] * lines, count).astype(jnp.bfloat16)


def shards(tokens, expert_ids, gate_weights, placement, w_gate, w_up, w_down):
    tok_count, width = tokens.shape
    top_count = expert_ids.shape[1]
    per_device = w_gate.shape[0]
    half = width // 2
    cap = 4
    core = lax.axis_index("dp") % 2
    own_slot = lax.axis_index("expert") * per_device
    mask_1 = jnp.where(core == 0, FIRST[0], FIRST[1])
    mask_2 = jnp.where(core == 0, SECOND[0], SECOND[1])

    slot_range = jnp.arange(placement.shape[0], dtype=jnp.int32)
    slot_of = jnp.sum((expert_ids[:, :, None] == slot_range) * placement, axis=2)
    high = lax.reduce_precision(gate_weights, 8, 7)
    middle = lax.reduce_precision(gate_weights - high, 8, 7)
    low = gate_weights - high - middle
    meta = jnp.concatenate([slot_of.astype(jnp.float32), high, middle, low], axis=1)
    meta = jnp.pad(meta, ((0, 0), (0, META - 4 * top_count))).astype(jnp.bfloat16)
    extended = jnp.concatenate([tokens[:, :half], meta, tokens[:, half:]], axis=1)

    near = gather_line(extended, "z").reshape(SIDE * tok_count, width + META)
    plane_a = gather_line(near[:, : half + META], "y").reshape(-1, half + META)
    plane_b = gather_line(
        jnp.concatenate([near[:, half + META :], near[:, half : half + META]], axis=1), "x"
    ).reshape(-1, half + META)

    local = jnp.arange(per_device, dtype=jnp.int32)
    arrived, choosers = [], []
    for plane, axis, bit in ((plane_a, "x", 2), (plane_b, "y", 4)):
        masks = jnp.stack([mask_1, jnp.int32(2), mask_2, jnp.int32(0)])
        moved = (masks & 1) * 2 if axis == "x" else masks * 4
        slots = ((own_slot ^ moved)[:, None] + local[None, :]).reshape(-1)
        choose = chooser(plane, slots, half, tok_count, cap)
        packed = jnp.dot(choose, plane, preferred_element_type=jnp.bfloat16)
        quarter = packed.shape[0] // 4
        got_1 = swap(packed[: 2 * quarter], axis, FIRST)
        send_2 = jnp.concatenate([packed[2 * quarter : 3 * quarter], got_1[quarter:]])
        got_2 = swap(send_2, axis, SECOND)
        mine = jnp.concatenate([packed[3 * quarter :], got_1[:quarter], got_2])
        arrived.append(mine.reshape(SIDE, per_device, SIDE, -1, half + META))
        choosers.append(choose)
    own_a = arrived[0].transpose(1, 0, 2, 3, 4)
    own_b = arrived[1].transpose(1, 2, 0, 3, 4)
    granule = own_a.shape[3]
    own_a = own_a.reshape(per_device, -1, half + META)
    own_b = own_b.reshape(per_device, -1, half + META)[:, :, :half]
    sets = ((own_a, own_b), (swap(own_a, "core"), swap(own_b, "core")))

    scaled = []
    for rows_a, rows_b in sets:
        info = rows_a[:, :, half:].astype(jnp.float32)
        named = info[:, :, :top_count].astype(jnp.int32) == (own_slot + local)[:, None, None]
        parts = [info[:, :, k * top_count : (k + 1) * top_count] for k in (1, 2, 3)]
        weight = jnp.sum(jnp.where(named, parts[0] + parts[1] + parts[2], 0.0), axis=2)

        def project(w):
            return jnp.einsum(
                "ltd,ldf->ltf", rows_a[:, :, :half], w[:, :half], preferred_element_type=jnp.float32
            ) + jnp.einsum("ltd,ldf->ltf", rows_b, w[:, half:], preferred_element_type=jnp.float32)

        hidden = (jax.nn.silu(project(w_gate)) * project(w_up)).astype(jnp.bfloat16)
        scaled.append((hidden, weight[:, :, None]))

    def down(which, columns):
        hidden, weight = scaled[which]
        return weight * jnp.einsum(
            "ltf,lfd->ltd", hidden, w_down[:, :, columns], preferred_element_type=jnp.float32
        )

    sums = []
    for index, axis, line, columns in ((0, "x", "y", slice(0, half)), (1, "y", "x", slice(half, None))):
        other = swap(down(1, columns).astype(jnp.bfloat16), "core")
        both = (down(0, columns) + other.astype(jnp.float32)).astype(jnp.bfloat16)
        both = both.reshape(per_device, SIDE, SIDE, granule, half)
        both = both.transpose((1, 0, 2, 3, 4) if axis == "x" else (2, 0, 1, 3, 4))
        both = both.reshape(SIDE, -1, half)
        quarter = both.shape[1]
        back_2 = swap(both[2:].reshape(-1, half), axis, SECOND)
        back_1 = swap(jnp.concatenate([both[1], back_2[quarter:]]), axis, FIRST)
        values = jnp.concatenate([back_1, back_2[:quarter], both[0]])
        dense = lax.dot_general(
            choosers[index], values, (((0,), (0,)), ((), ())), preferred_element_type=jnp.float32
        )
        sums.append(sum_line(dense.reshape(SIDE, -1, half), line))
    total = jnp.concatenate(sums, axis=1).reshape(SIDE, tok_count, width)
    return sum_line(total, "z").astype(jnp.bfloat16)


def solution(mesh):
    in_specs = (
        P(AXES, None),
        P(AXES, None),
        P(AXES, None),
        P(),
        P("expert", None, "dp"),
        P("expert", None, "dp"),
        P("expert", "dp", None),
    )
    return jax.shard_map(shards, mesh=mesh, in_specs=in_specs, out_specs=P(AXES, None), check_vma=False)
```

time: 290 us -> 175 us (0.60)
  waiting for transfers between devices: 157 us -> 101 us
  blocking collectives: 38.6 us -> 0 us
  local copies, waits for them, and re-layouts: 34.1 us -> 7.15 us
  starting transfers between devices: 8.67 us -> 33.4 us
  between operations: 13.5 us -> 0.7 us
  matrix products: 24.6 us -> 21.2 us
    ppermute x0 -> x24, waiting for transfers between devices: none -> 101 us  [swap(): return lax.ppermute(value, AXES, partners(axis, masks))]
    all_to_all x1 -> x0, waiting for transfers between devices: 97.9 us -> none  [shards(): lax.all_to_all(sending, ('expert', 'dp'), split_axis=0, concat_axis=0, ti...]
    all_gather x1 -> x0, waiting for transfers between devices: 59.6 us -> none  [shards(): rows_in = lax.all_gather(arrived[:, None], 'dp', axis=1, tiled=True)]
    all_to_all x1 -> x0, blocking collectives: 38.6 us -> none  [shards(): lax.all_to_all(outgoing, 'expert', split_axis=0, concat_axis=0, tiled=True)]
    ppermute x0 -> x24, starting transfers between devices: none -> 33.4 us  [swap(): return lax.ppermute(value, AXES, partners(axis, masks))]
    convert_element_type x1 -> x3, local copies, waits for them, and re-layouts: 12.2 us -> 0.08 us  [sum_line(): here[1].astype(jnp.bfloat16)]
    all_gather x1 -> x0, local copies, waits for them, and re-layouts: 11.5 us -> none  [shards(): rows_in = lax.all_gather(arrived[:, None], 'dp', axis=1, tiled=True)]
    all_to_all x1 -> x0, starting transfers between devices: 8.66 us -> none  [shards(): lax.all_to_all(sending, ('expert', 'dp'), split_axis=0, concat_axis=0, ti...]
  transfers between devices with their start and end apart: 2 -> 24, of which waited for: 2 -> 18; matrix products, arithmetic and copies ran while one was open for 0% -> 13% of each run, Pallas kernels for 0% -> 0%
where the time goes in v1:
time: 175 us
  waiting for transfers between devices  101 us (58%)
  starting transfers between devices  33.4 us (19%)
  matrix products  21.2 us (12%)
  other arithmetic  11 us (6%)
  local copies, waits for them, and re-layouts  7.15 us (4%)
    ppermute x24, waiting for transfers between devices, swap(): return lax.ppermute(value, AXES, partners(axis, masks))  101 us
    ppermute x24, starting transfers between devices, swap(): return lax.ppermute(value, AXES, partners(axis, masks))  33.4 us
    dot_general x4, matrix products, down(): jnp.einsum('ltf,lfd->ltd', hidden, w_down[:, :, columns], preferred_eleme...  5.23 us
    dot_general x4, matrix products, project(): jnp.einsum('ltd,ldf->ltf', rows_a[:, :, :half], w[:, :half], preferred_el...  5.19 us
    dot_general x4, matrix products, project(): jnp.einsum('ltd,ldf->ltf', rows_b, w[:, half:], preferred_element_type=jn...  5.08 us
    reduce_sum x1, other arithmetic, chooser(): jnp.sum((grouped[:, :, None, :] & earlier[None, None]).astype(jnp.int32),...  4.39 us
    dot_general x2, matrix products, shards(): lax.dot_general(choosers[index], values, (((0,), (0,)), ((), ())), prefer...  4.12 us
  transfers between devices with their start and end apart: 24, of which 18 were waited for; matrix products, arithmetic and copies ran while one was open for 13% of the time, Pallas kernels for 0%

profile of v1, /device:TPU:0, one launch (start us, length us, event | category | flops | bytes accessed | tf_op | source)
XLA Modules:
  0.0 174.7 jit_solution(8600516918614552065)
XLA Ops:
  1.5 1.1 select_reduce_fusion
  2.7 0.9 fusion.99
  3.6 2.1 %collective-permute-start = (bf16[16,4224]{1,0:T(8,128)(2,1)S(1)}, bf16[16,4224]{1,0:T(8,128)(2,1)S(1)}, u32[]{:S(2)}, u32[]{:S(2)}) collective-permute-start(bf16[16,4224]{1,0:T(8,128)(2,1)S(1)} %fusion.83), channel_id=1, source_target_pairs={{0,32},{1,97},{4,36},{5,101},{2,34},{3,99},{6,38},{7,103},{8,40},{... | collective-permute-start | bytes 405512 | tf_op jit(solution)/shard_map/ppermute | solution.py:32
  6.0 2.8 %collective-permute-done = bf16[16,4224]{1,0:T(8,128)(2,1)S(1)} collective-permute-done((bf16[16,4224]{1,0:T(8,128)(2,1)S(1)}, bf16[16,4224]{1,0:T(8,128)(2,1)S(1)}, u32[]{:S(2)}, u32[]{:S(2)}) %collective-permute-start) | collective-permute-done | bytes 135200 | tf_op jit(solution)/shard_map/ppermute | solution.py:32
  8.7 4.2 %collective-permute-start.1 = (bf16[2,16,4224]{2,1,0:T(8,128)(2,1)S(1)}, bf16[2,16,4224]{2,1,0:T(8,128)(2,1)S(1)}, u32[]{:S(2)}, u32[]{:S(2)}) collective-permute-start(bf16[2,16,4224]{2,1,0:T(8,128)(2,1)S(1)} %pad_maximum_fusion.13), channel_id=1, source_target_pairs={{0,96},{1,33},{4,100},{5,37},{2,98},{3,35},{6,102},{7,39},{8,104},... | collective-permute-start | bytes 811016 | tf_op jit(solution)/shard_map/ppermute | solution.py:32
  13.1 4.3 %collective-permute-done.1 = bf16[2,16,4224]{2,1,0:T(8,128)(2,1)S(1)} collective-permute-done((bf16[2,16,4224]{2,1,0:T(8,128)(2,1)S(1)}, bf16[2,16,4224]{2,1,0:T(8,128)(2,1)S(1)}, u32[]{:S(2)}, u32[]{:S(2)}) %collective-permute-start.1) | collective-permute-done | bytes 270368 | tf_op jit(solution)/shard_map/ppermute | solution.py:32
  17.5 1.6 collective-permute-start.6
  19.1 1.7 collective-permute-start.2
  20.8 3.4 %collective-permute-done.6 = bf16[64,2176]{1,0:T(8,128)(2,1)S(1)} collective-permute-done((bf16[64,2176]{1,0:T(8,128)(2,1)S(1)}, bf16[64,2176]{1,0:T(8,128)(2,1)S(1)}, u32[]{:S(2)}, u32[]{:S(2)}) %collective-permute-start.6) | collective-permute-done | bytes 278560 | tf_op jit(solution)/shard_map/ppermute | solution.py:32
  24.2 2.8 %collective-permute-start.7 = (bf16[2,64,2176]{2,1,0:T(8,128)(2,1)S(1)}, bf16[2,64,2176]{2,1,0:T(8,128)(2,1)S(1)}, u32[]{:S(2)}, u32[]{:S(2)}) collective-permute-start(bf16[2,64,2176]{2,1,0:T(8,128)(2,1)S(1)} %pad_maximum_fusion.9), channel_id=1, source_target_pairs={{0,6},{1,5},{4,2},{5,1},{2,4},{3,7},{6,0},{7,3},{8,14},{9,13},{12,... | collective-permute-start | bytes 1671176 | tf_op jit(solution)/shard_map/ppermute | solution.py:32
  28.0 3.0 %collective-permute-start.3 = (bf16[2,64,2176]{2,1,0:T(8,128)(2,1)}, bf16[2,64,2176]{2,1,0:T(8,128)(2,1)S(1)}, u32[]{:S(2)}, u32[]{:S(2)}) collective-permute-start(bf16[2,64,2176]{2,1,0:T(8,128)(2,1)} %pad_maximum_fusion.8), channel_id=1, source_target_pairs={{0,24},{1,9},{4,28},{5,13},{2,26},{3,11},{6,30},{7,15},{8,16},{9,1... | collective-permute-start | bytes 1671176 | tf_op jit(solution)/shard_map/ppermute | solution.py:32
  31.0 4.0 %collective-permute-done.7 = bf16[2,64,2176]{2,1,0:T(8,128)(2,1)S(1)} collective-permute-done((bf16[2,64,2176]{2,1,0:T(8,128)(2,1)S(1)}, bf16[2,64,2176]{2,1,0:T(8,128)(2,1)S(1)}, u32[]{:S(2)}, u32[]{:S(2)}) %collective-permute-start.7) | collective-permute-done | bytes 557088 | tf_op jit(solution)/shard_map/ppermute | solution.py:32
  35.5 3.5 %collective-permute-done.3 = bf16[2,64,2176]{2,1,0:T(8,128)(2,1)S(1)} collective-permute-done((bf16[2,64,2176]{2,1,0:T(8,128)(2,1)}, bf16[2,64,2176]{2,1,0:T(8,128)(2,1)S(1)}, u32[]{:S(2)}, u32[]{:S(2)}) %collective-permute-start.3) | collective-permute-done | bytes 557088 | tf_op jit(solution)/shard_map/ppermute | solution.py:32
  39.4 4.4 %convert_reduce_fusion = (s32[8,16,16]{2,1,0:T(8,128)S(1)}, s32[8,16,16]{2,1,0:T(8,128)S(1)}) fusion(pred[8,16,16]{2,1,0:T(8,128)(4,1)S(1)} %and.165, pred[16,16]{1,0:T(8,128)(4,1)S(1)} %iota_compare_fusion.3, pred[8,16,16]{2,1,0:T(8,128)(4,1)S(1)} %and.153), kind=kLoop, calls=%fused_computation.62 | loop fusion | flops 192512 | bytes 20736 | tf_op jit(solution)/shard_map/reduce_sum | solution.py:51
  46.9 16.0 %collective-permute-done.8 = bf16[256,2176]{1,0:T(8,128)(2,1)S(1)} collective-permute-done((bf16[256,2176]{1,0:T(8,128)(2,1)S(1)}, bf16[256,2176]{1,0:T(8,128)(2,1)S(1)}, u32[]{:S(2)}, u32[]{:S(2)}) %collective-permute-start.8) | collective-permute-done | bytes 1114144 | tf_op jit(solution)/shard_map/ppermute | solution.py:32
  63.0 3.2 %collective-permute-start.9 = (bf16[256,2176]{1,0:T(8,128)(2,1)S(1)}, bf16[256,2176]{1,0:T(8,128)(2,1)S(1)}, u32[]{:S(2)}, u32[]{:S(2)}) collective-permute-start(bf16[256,2176]{1,0:T(8,128)(2,1)S(1)} %pad_maximum_fusion.5), channel_id=1, source_target_pairs={{0,24},{1,9},{4,28},{5,13},{2,26},{3,11},{6,30},{7,15},{8,16},{9,1... | collective-permute-start | bytes 3342344 | tf_op jit(solution)/shard_map/ppermute | solution.py:32
  66.4 1.0 collective-permute-start.5
  67.4 12.4 %collective-permute-done.9 = bf16[256,2176]{1,0:T(8,128)(2,1)S(1)} collective-permute-done((bf16[256,2176]{1,0:T(8,128)(2,1)S(1)}, bf16[256,2176]{1,0:T(8,128)(2,1)S(1)}, u32[]{:S(2)}, u32[]{:S(2)}) %collective-permute-start.9) | collective-permute-done | bytes 1114144 | tf_op jit(solution)/shard_map/ppermute | solution.py:32
  80.5 2.6 %collective-permute-done.5 = bf16[256,2176]{1,0:T(8,128)(2,1)S(1)} collective-permute-done((bf16[256,2176]{1,0:T(8,128)(2,1)S(1)}, bf16[256,2176]{1,0:T(8,128)(2,1)S(1)}, u32[]{:S(2)}, u32[]{:S(2)}) %collective-permute-start.5) | collective-permute-done | bytes 1114144 | tf_op jit(solution)/shard_map/ppermute | solution.py:32
  84.7 1.3 fusion.4
  86.1 1.3 fusion.12
  88.8 1.3 fusion.41
  90.1 1.3 multiply_convert_fusion.2
  91.9 1.3 multiply_convert_fusion.1
  93.4 1.3 multiply_convert_fusion
  95.4 1.3 fusion.14
  96.7 1.3 fusion.6
  97.9 1.3 fusion.36
  99.2 1.3 fusion.61
  100.5 1.4 add_convert_fusion.1
  102.2 1.0 collective-permute-start.13
  103.3 1.3 add_convert_fusion
  105.0 2.9 %collective-permute-start.18 = (bf16[256,2048]{1,0:T(8,128)(2,1)S(1)}, bf16[256,2048]{1,0:T(8,128)(2,1)S(1)}, u32[]{:S(2)}, u32[]{:S(2)}) collective-permute-start(bf16[256,2048]{1,0:T(8,128)(2,1)S(1)} %bitcast.119), channel_id=1, source_target_pairs={{0,24},{1,9},{4,28},{5,13},{2,26},{3,11},{6,30},{7,15},{8,16},{9,1... | collective-permute-start | bytes 3145736 | tf_op jit(solution)/shard_map/ppermute | solution.py:32
  108.0 10.3 %collective-permute-done.13 = bf16[256,2048]{1,0:T(8,128)(2,1)S(1)} collective-permute-done((bf16[256,2048]{1,0:T(8,128)(2,1)S(1)}, bf16[256,2048]{1,0:T(8,128)(2,1)S(1)}, u32[]{:S(2)}, u32[]{:S(2)}) %collective-permute-start.13) | collective-permute-done | bytes 1048608 | tf_op jit(solution)/shard_map/ppermute | solution.py:32
  118.3 0.9 fusion.98
  119.4 1.7 collective-permute-done.18
  121.1 0.9 fusion.97
  122.4 11.8 %collective-permute-done.14 = bf16[256,2048]{1,0:T(8,128)(2,1)} collective-permute-done((bf16[256,2048]{1,0:T(8,128)(2,1)S(1)}, bf16[256,2048]{1,0:T(8,128)(2,1)}, u32[]{:S(2)}, u32[]{:S(2)}) %collective-permute-start.14) | collective-permute-done | bytes 1048608 | tf_op jit(solution)/shard_map/ppermute | solution.py:32
  134.3 2.1 %fusion.20 = f32[256,2048]{1,0:T(8,128)S(1)} fusion(pred[512,256]{1,0:T(32,128)(4,1)S(1)} %get-tuple-element.34, bf16[128,2048]{1,0:T(8,128)(2,1)S(1)} %bitcast.125, bf16[128,2048]{1,0:T(8,128)(2,1)} %get-tuple-element.26, bf16[256,2048]{1,0:T(8,128)(2,1)} %collective-permute-done.14), kind=kOutput, calls=%fused_computation.26 | convolution fusion | flops 543162368 | bytes 4325376 | tf_op jit(solution)/shard_map/dot_general | solution.py:140
  136.5 2.9 %collective-permute-start.15 = (bf16[2,64,2048]{2,1,0:T(8,128)(2,1)S(1)}, bf16[2,64,2048]{2,1,0:T(8,128)(2,1)S(1)}, u32[]{:S(2)}, u32[]{:S(2)}) collective-permute-start(bf16[2,64,2048]{2,1,0:T(8,128)(2,1)S(1)} %bitcast.122), channel_id=1, source_target_pairs={{0,24},{1,9},{4,28},{5,13},{2,26},{3,11},{6,30},{7,15},{8,16},{9,1... | collective-permute-start | bytes 1572872 | tf_op jit(solution)/shard_map/ppermute | solution.py:32
  139.4 2.0 %fusion.26 = f32[256,2048]{1,0:T(8,128)S(1)} fusion(pred[512,256]{1,0:T(32,128)(4,1)S(1)} %get-tuple-element.33, bf16[128,2048]{1,0:T(8,128)(2,1)S(1)} %bitcast.124, bf16[128,2048]{1,0:T(8,128)(2,1)S(1)} %copy-done.1, bf16[256,2048]{1,0:T(8,128)(2,1)} %collective-permute-done.19), kind=kOutput, calls=%fused_computation.32 | convolution fusion | flops 543162368 | bytes 4325376 | tf_op jit(solution)/shard_map/dot_general | solution.py:140
  141.6 1.0 collective-permute-start.20
  142.6 4.4 %collective-permute-done.15 = bf16[2,64,2048]{2,1,0:T(8,128)(2,1)S(1)} collective-permute-done((bf16[2,64,2048]{2,1,0:T(8,128)(2,1)S(1)}, bf16[2,64,2048]{2,1,0:T(8,128)(2,1)S(1)}, u32[]{:S(2)}, u32[]{:S(2)}) %collective-permute-start.15) | collective-permute-done | bytes 524320 | tf_op jit(solution)/shard_map/ppermute | solution.py:32
  147.3 6.2 %collective-permute-done.20 = bf16[2,64,2048]{2,1,0:T(8,128)(2,1)S(1)} collective-permute-done((bf16[2,64,2048]{2,1,0:T(8,128)(2,1)S(1)}, bf16[2,64,2048]{2,1,0:T(8,128)(2,1)S(1)}, u32[]{:S(2)}, u32[]{:S(2)}) %collective-permute-start.20) | collective-permute-done | bytes 524320 | tf_op jit(solution)/shard_map/ppermute | solution.py:32
  153.8 6.3 %collective-permute-done.21 = bf16[64,2048]{1,0:T(8,128)(2,1)S(1)} collective-permute-done((bf16[64,2048]{1,0:T(8,128)(2,1)S(1)}, bf16[64,2048]{1,0:T(8,128)(2,1)S(1)}, u32[]{:S(2)}, u32[]{:S(2)}) %collective-permute-start.21) | collective-permute-done | bytes 262176 | tf_op jit(solution)/shard_map/ppermute | solution.py:32
  160.2 3.6 %collective-permute-start.22 = (bf16[2,16,4096]{2,1,0:T(8,128)(2,1)S(1)}, bf16[2,16,4096]{2,1,0:T(8,128)(2,1)S(1)}, u32[]{:S(2)}, u32[]{:S(2)}) collective-permute-start(bf16[2,16,4096]{2,1,0:T(8,128)(2,1)S(1)} %bitcast.128), channel_id=1, source_target_pairs={{0,96},{1,33},{4,100},{5,37},{2,98},{3,35},{6,102},{7,39},{8,104},... | collective-permute-start | bytes 786440 | tf_op jit(solution)/shard_map/ppermute | solution.py:32
  163.8 5.1 %collective-permute-done.22 = bf16[2,16,4096]{2,1,0:T(8,128)(2,1)S(1)} collective-permute-done((bf16[2,16,4096]{2,1,0:T(8,128)(2,1)S(1)}, bf16[2,16,4096]{2,1,0:T(8,128)(2,1)S(1)}, u32[]{:S(2)}, u32[]{:S(2)}) %collective-permute-start.22) | collective-permute-done | bytes 262176 | tf_op jit(solution)/shard_map/ppermute | solution.py:32
  169.1 5.0 %collective-permute-done.23 = bf16[16,4096]{1,0:T(8,128)(2,1)S(1)} collective-permute-done((bf16[16,4096]{1,0:T(8,128)(2,1)S(1)}, bf16[16,4096]{1,0:T(8,128)(2,1)S(1)}, u32[]{:S(2)}, u32[]{:S(2)}) %collective-permute-start.23) | collective-permute-done | bytes 131104 | tf_op jit(solution)/shard_map/ppermute | solution.py:32
  (127 shorter events, 15.6 us)
Async XLA Ops:
  3.6 5.1 %collective-permute-start = (bf16[16,4224]{1,0:T(8,128)(2,1)S(1)}, bf16[16,4224]{1,0:T(8,128)(2,1)S(1)}, u32[]{:S(2)}, u32[]{:S(2)}) collective-permute-start(bf16[16,4224]{1,0:T(8,128)(2,1)S(1)} %fusion.83), channel_id=1, source_target_pairs={{0,32},{1,97},{4,36},{5,101},{2,34},{3,99},{6,38},{7,103},{8,40},{... | collective-permute-start | bytes 405512 | tf_op jit(solution)/shard_map/ppermute | solution.py:32
  8.7 8.6 %collective-permute-start.1 = (bf16[2,16,4224]{2,1,0:T(8,128)(2,1)S(1)}, bf16[2,16,4224]{2,1,0:T(8,128)(2,1)S(1)}, u32[]{:S(2)}, u32[]{:S(2)}) collective-permute-start(bf16[2,16,4224]{2,1,0:T(8,128)(2,1)S(1)} %pad_maximum_fusion.13), channel_id=1, source_target_pairs={{0,96},{1,33},{4,100},{5,37},{2,98},{3,35},{6,102},{7,39},{8,104},... | collective-permute-start | bytes 811016 | tf_op jit(solution)/shard_map/ppermute | solution.py:32
  17.5 6.6 %collective-permute-start.6 = (bf16[64,2176]{1,0:T(8,128)(2,1)S(1)}, bf16[64,2176]{1,0:T(8,128)(2,1)S(1)}, u32[]{:S(2)}, u32[]{:S(2)}) collective-permute-start(bf16[64,2176]{1,0:T(8,128)(2,1)S(1)} %get-tuple-element.30), channel_id=1, source_target_pairs={{0,4},{1,7},{4,0},{5,3},{2,6},{3,5},{6,2},{7,1},{8,12},{9,15},{12,... | collective-permute-start | bytes 835592 | tf_op jit(solution)/shard_map/ppermute | solution.py:32
  19.1 8.0 %collective-permute-start.2 = (bf16[64,2176]{1,0:T(8,128)(2,1)S(1)}, bf16[64,2176]{1,0:T(8,128)(2,1)S(1)}, u32[]{:S(2)}, u32[]{:S(2)}) collective-permute-start(bf16[64,2176]{1,0:T(8,128)(2,1)S(1)} %get-tuple-element.28), channel_id=1, source_target_pairs={{0,8},{1,25},{4,12},{5,29},{2,10},{3,27},{6,14},{7,31},{8,0},{9,17... | collective-permute-start | bytes 835592 | tf_op jit(solution)/shard_map/ppermute | solution.py:32
  24.2 10.8 %collective-permute-start.7 = (bf16[2,64,2176]{2,1,0:T(8,128)(2,1)S(1)}, bf16[2,64,2176]{2,1,0:T(8,128)(2,1)S(1)}, u32[]{:S(2)}, u32[]{:S(2)}) collective-permute-start(bf16[2,64,2176]{2,1,0:T(8,128)(2,1)S(1)} %pad_maximum_fusion.9), channel_id=1, source_target_pairs={{0,6},{1,5},{4,2},{5,1},{2,4},{3,7},{6,0},{7,3},{8,14},{9,13},{12,... | collective-permute-start | bytes 1671176 | tf_op jit(solution)/shard_map/ppermute | solution.py:32
  28.0 11.0 %collective-permute-start.3 = (bf16[2,64,2176]{2,1,0:T(8,128)(2,1)}, bf16[2,64,2176]{2,1,0:T(8,128)(2,1)S(1)}, u32[]{:S(2)}, u32[]{:S(2)}) collective-permute-start(bf16[2,64,2176]{2,1,0:T(8,128)(2,1)} %pad_maximum_fusion.8), channel_id=1, source_target_pairs={{0,24},{1,9},{4,28},{5,13},{2,26},{3,11},{6,30},{7,15},{8,16},{9,1... | collective-permute-start | bytes 1671176 | tf_op jit(solution)/shard_map/ppermute | solution.py:32
  46.0 16.8 %collective-permute-start.8 = (bf16[256,2176]{1,0:T(8,128)(2,1)S(1)}, bf16[256,2176]{1,0:T(8,128)(2,1)S(1)}, u32[]{:S(2)}, u32[]{:S(2)}) collective-permute-start(bf16[256,2176]{1,0:T(8,128)(2,1)S(1)} %slice.284), channel_id=1, source_target_pairs={{0,8},{1,25},{4,12},{5,29},{2,10},{3,27},{6,14},{7,31},{8,0},{9,17... | collective-permute-start | bytes 3342344 | tf_op jit(solution)/shard_map/ppermute | solution.py:32
  46.5 19.7 %collective-permute-start.4 = (bf16[256,2176]{1,0:T(8,128)(2,1)S(1)}, bf16[256,2176]{1,0:T(8,128)(2,1)S(1)}, u32[]{:S(2)}, u32[]{:S(2)}) collective-permute-start(bf16[256,2176]{1,0:T(8,128)(2,1)S(1)} %slice.270), channel_id=1, source_target_pairs={{0,4},{1,7},{4,0},{5,3},{2,6},{3,5},{6,2},{7,1},{8,12},{9,15},{12,... | collective-permute-start | bytes 3342344 | tf_op jit(solution)/shard_map/ppermute | solution.py:32
  63.0 16.8 %collective-permute-start.9 = (bf16[256,2176]{1,0:T(8,128)(2,1)S(1)}, bf16[256,2176]{1,0:T(8,128)(2,1)S(1)}, u32[]{:S(2)}, u32[]{:S(2)}) collective-permute-start(bf16[256,2176]{1,0:T(8,128)(2,1)S(1)} %pad_maximum_fusion.5), channel_id=1, source_target_pairs={{0,24},{1,9},{4,28},{5,13},{2,26},{3,11},{6,30},{7,15},{8,16},{9,1... | collective-permute-start | bytes 3342344 | tf_op jit(solution)/shard_map/ppermute | solution.py:32
  66.4 16.8 %collective-permute-start.5 = (bf16[256,2176]{1,0:T(8,128)(2,1)S(1)}, bf16[256,2176]{1,0:T(8,128)(2,1)S(1)}, u32[]{:S(2)}, u32[]{:S(2)}) collective-permute-start(bf16[256,2176]{1,0:T(8,128)(2,1)S(1)} %pad_maximum_fusion.3), channel_id=1, source_target_pairs={{0,6},{1,5},{4,2},{5,1},{2,4},{3,7},{6,0},{7,3},{8,14},{9,13},{12,... | collective-permute-start | bytes 3342344 | tf_op jit(solution)/shard_map/ppermute | solution.py:32
  79.8 4.9 %slice-start.3 = ((s8[6291456]{0:T(1024)(128)(4,1)}), s8[4194304]{0:T(1024)(128)(4,1)S(1)}, s32[]{:S(2)}) async-start(s8[6291456]{0:T(1024)(128)(4,1)} %bitcast.131), calls=%async_computation.3 | async-start | bytes 8388608
  80.2 4.5 %slice-start.4 = ((s8[6291456]{0:T(1024)(128)(4,1)}), s8[2097152]{0:T(1024)(128)(4,1)S(1)}, s32[]{:S(2)}) async-start(s8[6291456]{0:T(1024)(128)(4,1)} %bitcast.131), calls=%async_computation.4 | async-start | bytes 4194304
  80.5 4.2 %collective-permute-start.11 = (bf16[2,256,2048]{2,1,0:T(8,128)(2,1)S(1)}, bf16[2,256,2048]{2,1,0:T(8,128)(2,1)S(1)}, u32[]{:S(2)}, u32[]{:S(2)}) collective-permute-start(bf16[2,256,2048]{2,1,0:T(8,128)(2,1)S(1)} %slice.288), channel_id=1, source_target_pairs={{0,1},{1,0},{4,5},{5,4},{2,3},{3,2},{6,7},{7,6},{8,9},{9,8},{12,13... | collective-permute-start | bytes 6291464 | tf_op jit(solution)/shard_map/ppermute | solution.py:32
  83.2 2.8 %slice-start.1 = ((s8[6291456]{0:T(1024)(128)(4,1)}), s8[4194304]{0:T(1024)(128)(4,1)S(1)}, s32[]{:S(2)}) async-start(s8[6291456]{0:T(1024)(128)(4,1)} %bitcast.129), calls=%async_computation.1 | async-start | bytes 8388608
  83.3 2.7 %slice-start.2 = ((s8[6291456]{0:T(1024)(128)(4,1)}), s8[2097152]{0:T(1024)(128)(4,1)S(1)}, s32[]{:S(2)}) async-start(s8[6291456]{0:T(1024)(128)(4,1)} %bitcast.129), calls=%async_computation.2 | async-start | bytes 4194304
  83.5 4.6 %collective-permute-start.10 = (bf16[2,256,2176]{2,1,0:T(8,128)(2,1)S(1)}, bf16[2,256,2176]{2,1,0:T(8,128)(2,1)S(1)}, u32[]{:S(2)}, u32[]{:S(2)}) collective-permute-start(bf16[2,256,2176]{2,1,0:T(8,128)(2,1)S(1)} %bitcast.102), channel_id=1, source_target_pairs={{0,1},{1,0},{4,5},{5,4},{2,3},{3,2},{6,7},{7,6},{8,9},{9,8},{12,13... | collective-permute-start | bytes 6684680 | tf_op jit(solution)/shard_map/ppermute | solution.py:32
  88.8 2.6 %slice-start.5 = ((s8[6291456]{0:T(1024)(128)(4,1)}), s8[4194304]{0:T(1024)(128)(4,1)S(1)}, s32[]{:S(2)}) async-start(s8[6291456]{0:T(1024)(128)(4,1)} %bitcast.133), calls=%async_computation.5 | async-start | bytes 8388608
  90.1 1.8 %slice-start.6 = ((s8[6291456]{0:T(1024)(128)(4,1)}), s8[2097152]{0:T(1024)(128)(4,1)S(1)}, s32[]{:S(2)}) async-start(s8[6291456]{0:T(1024)(128)(4,1)} %bitcast.133), calls=%async_computation.6 | async-start | bytes 4194304
  93.2 7.3 %collective-permute-start.12 = (bf16[2,256,2048]{2,1,0:T(8,128)(2,1)S(1)}, bf16[2,256,2048]{2,1,0:T(8,128)(2,1)S(1)}, u32[]{:S(2)}, u32[]{:S(2)}) collective-permute-start(bf16[2,256,2048]{2,1,0:T(8,128)(2,1)S(1)} %multiply_convert_fusion.1), channel_id=1, source_target_pairs={{0,1},{1,0},{4,5},{5,4},{2,3},{3,2},{6,7},{7,6},{8,9},{9,8},{12,13... | collective-permute-start | bytes 6291464 | tf_op jit(solution)/shard_map/ppermute | solution.py:32
  94.7 8.6 %collective-permute-start.17 = (bf16[2,256,2048]{2,1,0:T(8,128)(2,1)S(1)}, bf16[2,256,2048]{2,1,0:T(8,128)(2,1)S(1)}, u32[]{:S(2)}, u32[]{:S(2)}) collective-permute-start(bf16[2,256,2048]{2,1,0:T(8,128)(2,1)S(1)} %multiply_convert_fusion), channel_id=1, source_target_pairs={{0,1},{1,0},{4,5},{5,4},{2,3},{3,2},{6,7},{7,6},{8,9},{9,8},{12,13... | collective-permute-start | bytes 6291464 | tf_op jit(solution)/shard_map/ppermute | solution.py:32
  102.2 16.1 %collective-permute-start.13 = (bf16[256,2048]{1,0:T(8,128)(2,1)S(1)}, bf16[256,2048]{1,0:T(8,128)(2,1)S(1)}, u32[]{:S(2)}, u32[]{:S(2)}) collective-permute-start(bf16[256,2048]{1,0:T(8,128)(2,1)S(1)} %bitcast.118), channel_id=1, source_target_pairs={{0,6},{1,5},{4,2},{5,1},{2,4},{3,7},{6,0},{7,3},{8,14},{9,13},{12,... | collective-permute-start | bytes 3145736 | tf_op jit(solution)/shard_map/ppermute | solution.py:32
  105.0 16.1 %collective-permute-start.18 = (bf16[256,2048]{1,0:T(8,128)(2,1)S(1)}, bf16[256,2048]{1,0:T(8,128)(2,1)S(1)}, u32[]{:S(2)}, u32[]{:S(2)}) collective-permute-start(bf16[256,2048]{1,0:T(8,128)(2,1)S(1)} %bitcast.119), channel_id=1, source_target_pairs={{0,24},{1,9},{4,28},{5,13},{2,26},{3,11},{6,30},{7,15},{8,16},{9,1... | collective-permute-start | bytes 3145736 | tf_op jit(solution)/shard_map/ppermute | solution.py:32
  119.3 15.0 %collective-permute-start.14 = (bf16[256,2048]{1,0:T(8,128)(2,1)S(1)}, bf16[256,2048]{1,0:T(8,128)(2,1)}, u32[]{:S(2)}, u32[]{:S(2)}) collective-permute-start(bf16[256,2048]{1,0:T(8,128)(2,1)S(1)} %pad_maximum_fusion.6), channel_id=1, source_target_pairs={{0,4},{1,7},{4,0},{5,3},{2,6},{3,5},{6,2},{7,1},{8,12},{9,15},{12,... | collective-permute-start | bytes 3145736 | tf_op jit(solution)/shard_map/ppermute | solution.py:32
  122.0 17.4 %collective-permute-start.19 = (bf16[256,2048]{1,0:T(8,128)(2,1)S(1)}, bf16[256,2048]{1,0:T(8,128)(2,1)}, u32[]{:S(2)}, u32[]{:S(2)}) collective-permute-start(bf16[256,2048]{1,0:T(8,128)(2,1)S(1)} %pad_maximum_fusion.7), channel_id=1, source_target_pairs={{0,8},{1,25},{4,12},{5,29},{2,10},{3,27},{6,14},{7,31},{8,0},{9,17... | collective-permute-start | bytes 3145736 | tf_op jit(solution)/shard_map/ppermute | solution.py:32
  136.4 5.0 %copy-start = (f32[256,2048]{1,0:T(8,128)}, f32[256,2048]{1,0:T(8,128)S(1)}, u32[]{:S(2)}) copy-start(f32[256,2048]{1,0:T(8,128)S(1)} %fusion.20) | copy-start | bytes 6291460
  136.4 3.0 %copy-start.1 = (bf16[128,2048]{1,0:T(8,128)(2,1)S(1)}, bf16[128,2048]{1,0:T(8,128)(2,1)}, u32[]{:S(2)}) copy-start(bf16[128,2048]{1,0:T(8,128)(2,1)} %get-tuple-element.24) | copy-start | bytes 1572868
  136.5 10.5 %collective-permute-start.15 = (bf16[2,64,2048]{2,1,0:T(8,128)(2,1)S(1)}, bf16[2,64,2048]{2,1,0:T(8,128)(2,1)S(1)}, u32[]{:S(2)}, u32[]{:S(2)}) collective-permute-start(bf16[2,64,2048]{2,1,0:T(8,128)(2,1)S(1)} %bitcast.122), channel_id=1, source_target_pairs={{0,24},{1,9},{4,28},{5,13},{2,26},{3,11},{6,30},{7,15},{8,16},{9,1... | collective-permute-start | bytes 1572872 | tf_op jit(solution)/shard_map/ppermute | solution.py:32
  141.5 5.5 %slice-start = ((f32[256,2048]{1,0:T(8,128)}), f32[128,2048]{1,0:T(8,128)S(1)}, s32[]{:S(2)}) async-start(f32[256,2048]{1,0:T(8,128)} %copy-done), calls=%async_computation | async-start | bytes 2097152 | tf_op jit(solution)/shard_map/slice | solution.py:41
  141.6 11.9 %collective-permute-start.20 = (bf16[2,64,2048]{2,1,0:T(8,128)(2,1)S(1)}, bf16[2,64,2048]{2,1,0:T(8,128)(2,1)S(1)}, u32[]{:S(2)}, u32[]{:S(2)}) collective-permute-start(bf16[2,64,2048]{2,1,0:T(8,128)(2,1)S(1)} %bitcast.123), channel_id=1, source_target_pairs={{0,6},{1,5},{4,2},{5,1},{2,4},{3,7},{6,0},{7,3},{8,14},{9,13},{12,... | collective-permute-start | bytes 1572872 | tf_op jit(solution)/shard_map/ppermute | solution.py:32
  147.2 6.6 %collective-permute-start.16 = (bf16[64,2048]{1,0:T(8,128)(2,1)S(1)}, bf16[64,2048]{1,0:T(8,128)(2,1)S(1)}, u32[]{:S(2)}, u32[]{:S(2)}) collective-permute-start(bf16[64,2048]{1,0:T(8,128)(2,1)S(1)} %fusion.72), channel_id=1, source_target_pairs={{0,8},{1,25},{4,12},{5,29},{2,10},{3,27},{6,14},{7,31},{8,0},{9,17... | collective-permute-start | bytes 786440 | tf_op jit(solution)/shard_map/ppermute | solution.py:32
  153.6 6.5 %collective-permute-start.21 = (bf16[64,2048]{1,0:T(8,128)(2,1)S(1)}, bf16[64,2048]{1,0:T(8,128)(2,1)S(1)}, u32[]{:S(2)}, u32[]{:S(2)}) collective-permute-start(bf16[64,2048]{1,0:T(8,128)(2,1)S(1)} %fusion.73), channel_id=1, source_target_pairs={{0,4},{1,7},{4,0},{5,3},{2,6},{3,5},{6,2},{7,1},{8,12},{9,15},{12,... | collective-permute-start | bytes 786440 | tf_op jit(solution)/shard_map/ppermute | solution.py:32
  160.2 8.7 %collective-permute-start.22 = (bf16[2,16,4096]{2,1,0:T(8,128)(2,1)S(1)}, bf16[2,16,4096]{2,1,0:T(8,128)(2,1)S(1)}, u32[]{:S(2)}, u32[]{:S(2)}) collective-permute-start(bf16[2,16,4096]{2,1,0:T(8,128)(2,1)S(1)} %bitcast.128), channel_id=1, source_target_pairs={{0,96},{1,33},{4,100},{5,37},{2,98},{3,35},{6,102},{7,39},{8,104},... | collective-permute-start | bytes 786440 | tf_op jit(solution)/shard_map/ppermute | solution.py:32
  169.0 5.0 %collective-permute-start.23 = (bf16[16,4096]{1,0:T(8,128)(2,1)S(1)}, bf16[16,4096]{1,0:T(8,128)(2,1)S(1)}, u32[]{:S(2)}, u32[]{:S(2)}) collective-permute-start(bf16[16,4096]{1,0:T(8,128)(2,1)S(1)} %fusion.84), channel_id=1, source_target_pairs={{0,32},{1,97},{4,36},{5,101},{2,34},{3,99},{6,38},{7,103},{8,40},{... | collective-permute-start | bytes 393224 | tf_op jit(solution)/shard_map/ppermute | solution.py:32

commit v2 on v0

v2 whole, which is shorter than its diff:
```python
import functools

import jax
import jax.numpy as jnp
from jax import lax
from jax.experimental import pallas as pl
from jax.experimental.pallas import tpu as pltpu
from jax.sharding import PartitionSpec as P

AXES = ("expert", "dp")
SIDE = 4
META = 128
CAP = 4
PARTS = 2


def place(z, y, x, core):
    return ((z * SIDE + y) * 2 + x % 2) * 4 + (x // 2) * 2 + core


def partners(axes, mask):
    pairs = []
    for z in range(SIDE):
        for y in range(SIDE):
            for x in range(SIDE):
                for core in range(2):
                    other = [z, y, x]
                    other["zyx".index(axes[core])] ^= mask
                    pairs.append((place(z, y, x, core), place(*other, core)))
    return pairs


def exchange(value, axes):
    return [value[0]] + [lax.ppermute(value[j], AXES, partners(axes, j)) for j in (1, 2, 3)]


def gather_line(value, axes):
    return jnp.stack(exchange([value] * SIDE, axes))


def sum_line(value, axes):
    sent = value.astype(jnp.bfloat16)
    pieces = exchange([value[0], sent[1], sent[2], sent[3]], axes)
    return (pieces[0] + pieces[1].astype(jnp.float32)) + (pieces[2].astype(jnp.float32) + pieces[3].astype(jnp.float32))


def sibling(value):
    pairs = [(i, i ^ 1) for i in range(SIDE**3 * 2)]
    return lax.ppermute(value, AXES, pairs)


def pack_kernel(wanted_ref, *refs, top, tok_count, step):
    planes, outs, choice_ref = refs[:SIDE], refs[SIDE:-1], refs[-1]
    wanted = wanted_ref[...]
    tokens, lines = planes[0].shape[0], wanted.shape[1]
    blocks = tokens // tok_count
    token_block = lax.broadcasted_iota(jnp.int32, (tokens, lines), 0) // tok_count
    line_block = lax.broadcasted_iota(jnp.int32, (tokens, lines), 1) // CAP % blocks
    inside = token_block == line_block
    share = lines // SIDE
    for p in range(SIDE):
        codes = planes[p][:, PARTS * step :].astype(jnp.float32)
        found = codes[:, :1] == wanted
        for k in range(1, top):
            found = found | (codes[:, k : k + 1] == wanted)
        choice = jnp.where(found & inside, 1.0, 0.0)
        choice_ref[p] = choice.astype(jnp.bfloat16)
        take = choice.T.astype(jnp.bfloat16)
        for part in range(PARTS):
            end = (part + 1) * step if part < PARTS - 1 else planes[p].shape[1]
            rows = jnp.dot(take, planes[p][:, part * step : end], preferred_element_type=jnp.float32)
            rows = rows.astype(jnp.bfloat16)
            for j in range(SIDE):
                out = outs[part * SIDE + j]
                out[p] = rows[j * share : (j + 1) * share].reshape(out.shape[1:])


def gate_kernel(base_ref, *refs, sources, step, has_total, weigh, finish):
    refs = list(refs)
    slot_ref = refs.pop(0) if weigh else None
    pieces = [[refs.pop(0) for _ in range(SIDE)] for _ in sources]
    weights = [(refs.pop(0), refs.pop(0)) for _ in sources]
    total_in = refs.pop(0) if has_total else None
    total_ref = refs.pop(0)
    weight_ref = refs.pop(0) if weigh else None
    [rows_ref] = refs
    granule, columns = pieces[0][0].shape[2], weights[0][0].shape[2]
    gate = up = None
    for source, held, (gate_w, up_w) in zip(sources, pieces, weights):
        for last in range(SIDE):
            for plane in range(SIDE):
                piece = held[last][plane, 0] if source == "own" else held[plane][last, 0]
                line = (last * SIDE + plane) * granule
                rows_ref[line : line + granule] = piece[:, :step]
                if weigh:
                    info = piece[:, step:].astype(jnp.float32)
                    code = CAP * (slot_ref[0] + pl.program_id(0)).astype(jnp.float32)
                    named = (info >= code) & (info < code + CAP) & (lax.broadcasted_iota(jnp.int32, info.shape, 1) < META // 2)
                    value = pltpu.roll(info, META // 2, 1)
                    weight_ref[0, line : line + granule] = jnp.sum(jnp.where(named, value, 0.0), axis=1, keepdims=True)
        rows = rows_ref[...]
        one = jnp.dot(rows, gate_w[0], preferred_element_type=jnp.float32)
        two = jnp.dot(rows, up_w[0], preferred_element_type=jnp.float32)
        gate, up = (one, two) if gate is None else (gate + one, up + two)
    if has_total:
        gate, up = gate + total_in[0, :, :columns], up + total_in[0, :, columns:]
    if finish:
        total_ref[0] = (jax.nn.silu(gate) * up).astype(jnp.bfloat16)
    else:
        total_ref[0, :, :columns] = gate
        total_ref[0, :, columns:] = up


def down_kernel(base_ref, hidden_ref, weight_ref, w_ref, *refs, turned):
    outs, added = refs[-SIDE:], refs[:-SIDE]
    granule = outs[0].shape[2]
    value = weight_ref[0] * jnp.dot(hidden_ref[0], w_ref[0], preferred_element_type=jnp.float32)
    for last in range(SIDE):
        for plane in range(SIDE):
            line = (last * SIDE + plane) * granule
            rows = value[line : line + granule]
            if turned:
                outs[plane][last, 0] = rows.astype(jnp.bfloat16)
            else:
                outs[last][plane, 0] = (rows + added[last][plane, 0].astype(jnp.float32)).astype(jnp.bfloat16)


def unpack_kernel(choice_ref, *refs):
    pieces, outs = refs[:SIDE], refs[SIDE:]
    for p in range(SIDE):
        values = jnp.concatenate([piece[p].reshape(-1, piece.shape[3]) for piece in pieces])
        dense = jnp.dot(choice_ref[p], values, preferred_element_type=jnp.float32)
        outs[p][...] = dense.astype(outs[p].dtype)


def whole(count):
    return [pl.BlockSpec(memory_space=pltpu.VMEM)] * count


def params():
    return pltpu.CompilerParams(vmem_limit_bytes=48 * 2**20)


def cost(flops, read):
    return pl.CostEstimate(flops=int(flops), bytes_accessed=int(read), transcendentals=0)


def shards(tokens, expert_ids, gate_weights, placement, w_gate, w_up, w_down):
    tok_count, width = tokens.shape
    top = expert_ids.shape[1]
    per_device = w_gate.shape[0]
    half = width // 2
    core = lax.axis_index("dp") % 2
    first_core = core == 0
    own_slot = lax.axis_index("expert") * per_device
    local = jnp.arange(per_device, dtype=jnp.int32)

    slot_range = jnp.arange(placement.shape[0], dtype=jnp.int32)
    slot_of = jnp.sum((expert_ids[:, :, None] == slot_range) * placement, axis=2)
    same = jnp.any(slot_of[:, :, None, None] == slot_of[None, None], axis=3)
    earlier = jnp.arange(tok_count)[:, None] > jnp.arange(tok_count)[None, :]
    rank = jnp.sum((same & earlier[:, None, :]).astype(jnp.int32), axis=2)
    code = (slot_of * CAP + rank).astype(jnp.float32)
    high = lax.reduce_precision(gate_weights, 8, 7)
    middle = lax.reduce_precision(gate_weights - high, 8, 7)
    low = gate_weights - high - middle
    gap = jnp.full((tok_count, META // 2 - 3 * top), -1.0)
    meta = jnp.concatenate([code, code, code, gap, high, middle, low, gap], axis=1).astype(jnp.bfloat16)
    left, right = tokens[:, :half], tokens[:, half:]
    kept = jnp.concatenate([jnp.where(first_core, left, right), meta], axis=1)
    got = sibling(jnp.concatenate([jnp.where(first_core, right, left), meta], axis=1))
    both = jnp.concatenate([jnp.where(first_core, kept, got), jnp.where(first_core, got, kept)])

    near = gather_line(both, "zz").reshape(-1, META + half)
    planes = exchange([near] * SIDE, "yx")

    step = half // PARTS
    lines = near.shape[0] // tok_count * CAP * per_device * SIDE
    masks = jnp.arange(SIDE, dtype=jnp.int32)
    moved = jnp.where(first_core, (masks & 1) * 2, masks * 4)
    slots = ((own_slot ^ moved)[:, None] + local[None, :]).reshape(-1)
    wanted = slots[:, None, None] * CAP + jnp.zeros((1, near.shape[0] // tok_count, 1), jnp.int32) + jnp.arange(CAP, dtype=jnp.int32)
    wanted = wanted.astype(jnp.float32).reshape(1, lines)
    granule = near.shape[0] // tok_count * CAP
    rows_of = lambda columns: jax.ShapeDtypeStruct((SIDE, per_device, granule, columns), jnp.bfloat16)
    widths = [step] * (PARTS - 1) + [step + META]
    *packed, choice = pl.pallas_call(
        functools.partial(pack_kernel, top=top, tok_count=tok_count, step=step),
        out_shape=[rows_of(w) for w in widths for _ in range(SIDE)]
        + [jax.ShapeDtypeStruct((SIDE, near.shape[0], lines), jnp.bfloat16)],
        in_specs=whole(1 + SIDE),
        out_specs=whole(PARTS * SIDE + 1),
        compiler_params=params(),
    )(wanted, *planes)

    base = jnp.stack([core * PARTS, (1 - core) * PARTS]).astype(jnp.int32)
    rows_count, hidden_count = SIDE * SIDE * granule, w_gate.shape[2]

    def piece_spec(columns):
        return pl.BlockSpec((SIDE, 1, granule, columns), lambda slot, *_: (0, slot, 0, 0))

    def slot_spec(columns):
        return pl.BlockSpec((1, rows_count, columns), lambda slot, *_: (slot, 0, 0))

    def project(sources, part, total, weigh, finish):
        names = tuple(sources)
        in_specs = [piece_spec(widths[part])] * (SIDE * len(names))
        operands = [p for name in names for p in sources[name]]
        for name in names:
            which = 0 if name == "own" else 1
            spec = pl.BlockSpec((1, step, hidden_count), lambda slot, base, *_, which=which: (slot, base[which] + part, 0))
            in_specs += [spec, spec]
            operands += [w_gate, w_up]
        if total is not None:
            in_specs.append(slot_spec(2 * hidden_count))
            operands.append(total)
        if finish:
            out_shape = [jax.ShapeDtypeStruct((per_device, rows_count, hidden_count), jnp.bfloat16)]
            out_specs = [slot_spec(hidden_count)]
        else:
            out_shape = [jax.ShapeDtypeStruct((per_device, rows_count, 2 * hidden_count), jnp.float32)]
            out_specs = [slot_spec(2 * hidden_count)]
        if weigh:
            out_shape.append(jax.ShapeDtypeStruct((per_device, rows_count, 1), jnp.float32))
            out_specs.append(slot_spec(1))
        scalars = [base] + ([own_slot.reshape(1)] if weigh else [])
        return pl.pallas_call(
            functools.partial(gate_kernel, sources=names, step=step, has_total=total is not None, weigh=weigh, finish=finish),
            grid_spec=pltpu.PrefetchScalarGridSpec(
                num_scalar_prefetch=len(scalars),
                grid=(per_device,),
                in_specs=in_specs,
                out_specs=out_specs,
                scratch_shapes=[pltpu.VMEM((rows_count, step), jnp.bfloat16)],
            ),
            out_shape=out_shape,
            compiler_params=params(),
            cost_estimate=cost(len(names) * 4 * per_device * rows_count * step * hidden_count, 8e6),
        )(*scalars, *operands)

    arrived = []
    for part in range(PARTS):
        own = exchange(packed[part * SIDE : (part + 1) * SIDE], "xy")
        arrived.append((own, [sibling(piece) for piece in own]))
    [total] = project({"own": arrived[0][0], "sibling": arrived[0][1]}, 0, None, False, False)
    total, weight = project({"own": arrived[1][0]}, 1, total, True, False)
    [hidden] = project({"sibling": arrived[1][1]}, 1, total, False, True)

    def down(part, turned, added):
        spec = piece_spec(step)
        which = 1 if turned else 0
        return pl.pallas_call(
            functools.partial(down_kernel, turned=turned),
            grid_spec=pltpu.PrefetchScalarGridSpec(
                num_scalar_prefetch=1,
                grid=(per_device,),
                in_specs=[
                    slot_spec(hidden_count),
                    slot_spec(1),
                    pl.BlockSpec((1, hidden_count, step), lambda slot, base: (slot, 0, base[which] + part)),
                ]
                + [spec] * len(added),
                out_specs=[spec] * SIDE,
            ),
            out_shape=[rows_of(step)] * SIDE,
            compiler_params=params(),
            cost_estimate=cost(2 * per_device * rows_count * step * hidden_count, 5e6),
        )(base, hidden, weight, w_down, *added)

    sums = []
    for part in range(PARTS):
        added = [sibling(piece) for piece in down(part, True, [])]
        values = exchange(down(part, False, added), "xy")
        kinds = [jnp.float32] + [jnp.bfloat16] * (SIDE - 1)
        dense = pl.pallas_call(
            unpack_kernel,
            out_shape=[jax.ShapeDtypeStruct((near.shape[0], step), kind) for kind in kinds],
            in_specs=whole(1 + SIDE),
            out_specs=whole(SIDE),
            compiler_params=params(),
        )(choice, *values)
        sums.append(sum(piece.astype(jnp.float32) for piece in exchange(dense, "yx")))
    total = jnp.concatenate(sums, axis=1).reshape(SIDE, -1, half)
    total = sum_line(total, "zz").astype(jnp.bfloat16).reshape(2, tok_count, half)
    kept = jnp.where(first_core, total[0], total[1])
    got = sibling(jnp.where(first_core, total[1], total[0]))
    return jnp.concatenate([jnp.where(first_core, kept, got), jnp.where(first_core, got, kept)], axis=1)


def solution(mesh):
    in_specs = (
        P(AXES, None),
        P(AXES, None),
        P(AXES, None),
        P(),
        P("expert", None, "dp"),
        P("expert", None, "dp"),
        P("expert", "dp", None),
    )
    return jax.shard_map(shards, mesh=mesh, in_specs=in_specs, out_specs=P(AXES, None), check_vma=False)
```

time: 290 us -> 177 us (0.61)
  waiting for transfers between devices: 157 us -> 75 us
  blocking collectives: 38.6 us -> 0 us
  starting transfers between devices: 8.67 us -> 46.6 us
  Pallas kernels: 0 us -> 35.9 us
  matrix products: 24.6 us -> 0 us
  local copies, waits for them, and re-layouts: 34.1 us -> 12.9 us
  between operations: 13.5 us -> 0.32 us
  other arithmetic: 11.5 us -> 4.72 us
    all_to_all x1 -> x0, waiting for transfers between devices: 97.9 us -> none  [shards(): lax.all_to_all(sending, ('expert', 'dp'), split_axis=0, concat_axis=0, ti...]
    ppermute x0 -> x45, waiting for transfers between devices: none -> 75 us  [the longest x27 72.5 us: exchange(): lax.ppermute(value[j], AXES, partners(axes, j))]
    all_gather x1 -> x0, waiting for transfers between devices: 59.6 us -> none  [shards(): rows_in = lax.all_gather(arrived[:, None], 'dp', axis=1, tiled=True)]
    ppermute x0 -> x45, starting transfers between devices: none -> 46.6 us  [the longest x27 42.7 us: exchange(): lax.ppermute(value[j], AXES, partners(axes, j))]
    all_to_all x1 -> x0, blocking collectives: 38.6 us -> none  [shards(): lax.all_to_all(outgoing, 'expert', split_axis=0, concat_axis=0, tiled=True)]
    pallas_call x0 -> x10, Pallas kernels: none -> 35.9 us  [the longest x3 19.1 us: project(): pl.pallas_call(functools.partial(gate_kernel, sources=names, step=step, h...]
    dot_general x3 -> x0, matrix products: 24.6 us -> none  [the longest x1 15.1 us: shards(): jnp.einsum('sqlcf,lfd->sqlcd', hidden, w_down, preferred_element_type=jnp...]
    convert_element_type x1, local copies, waits for them, and re-layouts: 12.2 us -> 0.11 us  [shards(): wanted = wanted.astype(jnp.float32).reshape(1, lines)]
  transfers between devices with their start and end apart: 2 -> 45, of which waited for: 2 -> 23; matrix products, arithmetic and copies ran while one was open for 0% -> 0% of each run, Pallas kernels for 0% -> 14%
where the time goes in v2:
time: 177 us; the launch traced here: 175 us
  waiting for transfers between devices  75 us (42%)
  starting transfers between devices  46.6 us (26%)
  Pallas kernels  35.9 us (20%)
  local copies, waits for them, and re-layouts  12.9 us (7%)
  other arithmetic  4.72 us (3%)
    ppermute x27, waiting for transfers between devices, exchange(): lax.ppermute(value[j], AXES, partners(axes, j))  72.5 us
    ppermute x27, starting transfers between devices, exchange(): lax.ppermute(value[j], AXES, partners(axes, j))  42.7 us
    pallas_call x3, Pallas kernels, project(): pl.pallas_call(functools.partial(gate_kernel, sources=names, step=step, h...  19.1 us
    pallas_call x4, Pallas kernels, down(): pl.pallas_call(functools.partial(down_kernel, turned=turned), grid_spec=p...  13.3 us
    unnamed x24, local copies, waits for them, and re-layouts  12.3 us
    ppermute x18, starting transfers between devices, sibling(): return lax.ppermute(value, AXES, pairs)  3.89 us
  transfers between devices with their start and end apart: 45, of which 23 were waited for; matrix products, arithmetic and copies ran while one was open for 0% of the time, Pallas kernels for 14%

profile of v2, /device:TPU:0, one launch (start us, length us, event | category | flops | bytes accessed | tf_op | source)
XLA Modules:
  0.0 175.5 jit_solution(7153757026471929609)
XLA Ops:
  5.3 1.1 collective-permute-done
  6.5 2.1 %collective-permute-start.1 = (bf16[32,2176]{1,0:T(8,128)(2,1)S(1)}, bf16[32,2176]{1,0:T(8,128)(2,1)S(1)}, u32[]{:S(2)}, u32[]{:S(2)}) collective-permute-start(bf16[32,2176]{1,0:T(8,128)(2,1)S(1)} %get-tuple-element.81), channel_id=1, source_target_pairs={{0,32},{1,33},{4,36},{5,37},{2,34},{3,35},{6,38},{7,39},{8,40},{9,... | collective-permute-start | bytes 417800 | tf_op jit(solution)/shard_map/ppermute | solution.py:34
  8.5 3.6 %collective-permute-start.2 = (bf16[32,2176]{1,0:T(8,128)(2,1)S(1)}, bf16[32,2176]{1,0:T(8,128)(2,1)S(1)}, u32[]{:S(2)}, u32[]{:S(2)}) collective-permute-start(bf16[32,2176]{1,0:T(8,128)(2,1)S(1)} %get-tuple-element.81), channel_id=1, source_target_pairs={{0,64},{1,65},{4,68},{5,69},{2,66},{3,67},{6,70},{7,71},{8,72},{9,... | collective-permute-start | bytes 417800 | tf_op jit(solution)/shard_map/ppermute | solution.py:34
  12.6 6.3 %collective-permute-done.2 = bf16[32,2176]{1,0:T(8,128)(2,1)S(1)} collective-permute-done((bf16[32,2176]{1,0:T(8,128)(2,1)S(1)}, bf16[32,2176]{1,0:T(8,128)(2,1)S(1)}, u32[]{:S(2)}, u32[]{:S(2)}) %collective-permute-start.2) | collective-permute-done | bytes 139296 | tf_op jit(solution)/shard_map/ppermute | solution.py:34
  18.9 2.3 %collective-permute-done.3 = bf16[32,2176]{1,0:T(8,128)(2,1)S(1)} collective-permute-done((bf16[32,2176]{1,0:T(8,128)(2,1)S(1)}, bf16[32,2176]{1,0:T(8,128)(2,1)S(1)}, u32[]{:S(2)}, u32[]{:S(2)}) %collective-permute-start.3) | collective-permute-done | bytes 139296 | tf_op jit(solution)/shard_map/ppermute | solution.py:34
  21.3 1.7 collective-permute-start.4
  23.0 2.9 %collective-permute-start.5 = (bf16[128,2176]{1,0:T(8,128)(2,1)S(1)}, bf16[128,2176]{1,0:T(8,128)(2,1)S(1)}, u32[]{:S(2)}, u32[]{:S(2)}) collective-permute-start(bf16[128,2176]{1,0:T(8,128)(2,1)S(1)} %bitcast.10), channel_id=1, source_target_pairs={{0,16},{1,3},{4,20},{5,7},{2,18},{3,1},{6,22},{7,5},{8,24},{9,11},... | collective-permute-start | bytes 1671176 | tf_op jit(solution)/shard_map/ppermute | solution.py:34
  26.5 4.5 %collective-permute-done.4.refs_1_ = bf16[128,2176]{1,0:T(8,128)(2,1)S(1)} collective-permute-done((bf16[128,2176]{1,0:T(8,128)(2,1)S(1)}, bf16[128,2176]{1,0:T(8,128)(2,1)S(1)}, u32[]{:S(2)}, u32[]{:S(2)}) %collective-permute-start.4) | collective-permute-done | bytes 557088 | tf_op jit(solution)/shard_map/ppermute | solution.py:34
  31.0 8.5 %collective-permute-done.5.refs_2_ = bf16[128,2176]{1,0:T(8,128)(2,1)S(1)} collective-permute-done((bf16[128,2176]{1,0:T(8,128)(2,1)S(1)}, bf16[128,2176]{1,0:T(8,128)(2,1)S(1)}, u32[]{:S(2)}, u32[]{:S(2)}) %collective-permute-start.5) | collective-permute-done | bytes 557088 | tf_op jit(solution)/shard_map/ppermute | solution.py:34
  39.5 3.1 %collective-permute-done.6.refs_3_ = bf16[128,2176]{1,0:T(8,128)(2,1)S(1)} collective-permute-done((bf16[128,2176]{1,0:T(8,128)(2,1)S(1)}, bf16[128,2176]{1,0:T(8,128)(2,1)S(1)}, u32[]{:S(2)}, u32[]{:S(2)}) %collective-permute-start.6) | collective-permute-done | bytes 557088 | tf_op jit(solution)/shard_map/ppermute | solution.py:34
  42.6 2.7 %shard_map.73 = (bf16[4,2,32,1024]{3,2,1,0:T(8,128)(2,1)S(1)}, bf16[4,2,32,1024]{3,2,1,0:T(8,128)(2,1)S(1)}, bf16[4,2,32,1024]{3,2,1,0:T(8,128)(2,1)S(1)}, bf16[...) custom-call(f32[1,256]{1,0:T(1,128)S(1)} %convert_element_type.56.wa, ...), custom_call_target="tpu_custom_call" | custom-call | tf_op jit(solution)/shard_map/pallas_call | solution.py:187
  45.3 1.5 collective-permute-start.14
  46.8 2.7 %collective-permute-start.15 = (bf16[4,2,32,1024]{3,2,1,0:T(8,128)(2,1)S(1)}, bf16[4,2,32,1024]{3,2,1,0:T(8,128)(2,1)S(1)}, u32[]{:S(2)}, u32[]{:S(2)}) collective-permute-start(bf16[4,2,32,1024]{3,2,1,0:T(8,128)(2,1)S(1)} %get-tuple-element.47), channel_id=1, source_target_pairs={{0,2},{1,17},{4,6},{5,21},{2,0},{3,19},{6,4},{7,23},{8,10},{9,25},... | collective-permute-start | bytes 1572872 | tf_op jit(solution)/shard_map/ppermute | solution.py:34
  50.8 1.8 %collective-permute-start.10 = (bf16[4,2,32,1152]{3,2,1,0:T(8,128)(2,1)}, bf16[4,2,32,1152]{3,2,1,0:T(8,128)(2,1)S(1)}, u32[]{:S(2)}, u32[]{:S(2)}) collective-permute-start(bf16[4,2,32,1152]{3,2,1,0:T(8,128)(2,1)} %get-tuple-element.43), channel_id=1, source_target_pairs={{0,2},{1,17},{4,6},{5,21},{2,0},{3,19},{6,4},{7,23},{8,10},{9,25},... | collective-permute-start | bytes 1769480 | tf_op jit(solution)/shard_map/ppermute | solution.py:34
  52.6 1.9 %collective-permute-done.14.refs_1_ = bf16[4,2,32,1024]{3,2,1,0:T(8,128)(2,1)S(1)} collective-permute-done((bf16[4,2,32,1024]{3,2,1,0:T(8,128)(2,1)S(1)}, bf16[4,2,32,1024]{3,2,1,0:T(8,128)(2,1)S(1)}, u32[]{:S(2)}, u32[]{:S(2)}) %collective-permute-start.14) | collective-permute-done | bytes 524320 | tf_op jit(solution)/shard_map/ppermute | solution.py:34
  54.5 2.8 %collective-permute-start.12 = (bf16[4,2,32,1152]{3,2,1,0:T(8,128)(2,1)}, bf16[4,2,32,1152]{3,2,1,0:T(8,128)(2,1)S(1)}, u32[]{:S(2)}, u32[]{:S(2)}) collective-permute-start(bf16[4,2,32,1152]{3,2,1,0:T(8,128)(2,1)} %get-tuple-element.44), channel_id=1, source_target_pairs={{0,6},{1,25},{4,2},{5,29},{2,4},{3,27},{6,0},{7,31},{8,14},{9,17},... | collective-permute-start | bytes 1769480 | tf_op jit(solution)/shard_map/ppermute | solution.py:34
  57.2 5.2 %collective-permute-done.15.refs_2_ = bf16[4,2,32,1024]{3,2,1,0:T(8,128)(2,1)S(1)} collective-permute-done((bf16[4,2,32,1024]{3,2,1,0:T(8,128)(2,1)S(1)}, bf16[4,2,32,1024]{3,2,1,0:T(8,128)(2,1)S(1)}, u32[]{:S(2)}, u32[]{:S(2)}) %collective-permute-start.15) | collective-permute-done | bytes 524320 | tf_op jit(solution)/shard_map/ppermute | solution.py:34
  62.6 9.3 %collective-permute-done.16.refs_3_ = bf16[4,2,32,1024]{3,2,1,0:T(8,128)(2,1)} collective-permute-done((bf16[4,2,32,1024]{3,2,1,0:T(8,128)(2,1)S(1)}, bf16[4,2,32,1024]{3,2,1,0:T(8,128)(2,1)}, u32[]{:S(2)}, u32[]{:S(2)}) %collective-permute-start.16) | collective-permute-done | bytes 524320 | tf_op jit(solution)/shard_map/ppermute | solution.py:34
  74.1 4.1 %collective-permute-done.12.refs_4_ = bf16[4,2,32,1152]{3,2,1,0:T(8,128)(2,1)S(1)} collective-permute-done((bf16[4,2,32,1152]{3,2,1,0:T(8,128)(2,1)}, bf16[4,2,32,1152]{3,2,1,0:T(8,128)(2,1)S(1)}, u32[]{:S(2)}, u32[]{:S(2)}) %collective-permute-start.12) | collective-permute-done | bytes 589856 | tf_op jit(solution)/shard_map/ppermute | solution.py:34
  86.1 8.5 %shard_map.74.refs_7_ = f32[2,512,768]{2,1,0:T(8,128)} custom-call(s32[2]{0:T(128)S(1)} %pad_add_fusion.base_ref, bf16[4,2,32,1024]{3,2,1,0:T(8,128)(2,1)S(1)} %copy-done.2, bf16[4,2,32,1024]{3,2,1,0:T(8,128)(2,1)S(1)} %collective-permute-done.14.refs_1_, bf16[4,2,32,1024]{3,2,1,0:T(8,128)(2,1)S(1)} %copy-done.4, ...), custom_call_target="tpu_custom_call" | custom-call | flops 3221225472 | bytes 8000000 | tf_op jit(solution)/shard_map/pallas_call | solution.py:227
  94.6 5.1 %shard_map.75 = (f32[2,512,768]{2,1,0:T(8,128)S(1)}, f32[2,512,1]{2,1,0:T(8,128)S(1)}) custom-call(s32[2]{0:T(128)S(1)} %pad_add_fusion.base_ref, s32[1]{0:T(128)} %bitcast.7.refs_0_, bf16[4,2,32,1152]{3,2,1,0:T(8,128)(2,1)S(1)} %get-tuple-element.41.refs_1_, bf16[4,2,32,1152]{3,2,1,0:T(8,128)(2,1)S(1)} %collective-permute-done.8.refs_2_, ...), custom_call_target="tpu_custom_call" | custom-call | flops 1610612736 | bytes 8000000 | tf_op jit(solution)/shard_map/pallas_call | solution.py:227
  99.8 1.6 copy-done
  101.4 5.4 %shard_map.76.hidden_ref = bf16[2,512,384]{2,1,0:T(8,128)(2,1)S(1)} custom-call(s32[2]{0:T(128)S(1)} %pad_add_fusion.base_ref, bf16[4,2,32,1152]{3,2,1,0:T(8,128)(2,1)} %collective-permute-done.7.refs_0_, bf16[4,2,32,1152]{3,2,1,0:T(8,128)(2,1)} %collective-permute-done.9.refs_1_, bf16[4,2,32,1152]{3,2,1,0:T(8,128)(2,1)} %collective-permute-done.11.refs_2_, ...), custom_call_target="tpu_custom_call" | custom-call | flops 1610612736 | bytes 8000000 | tf_op jit(solution)/shard_map/pallas_call | solution.py:227
  106.8 3.3 %shard_map.80 = (bf16[4,2,32,1024]{3,2,1,0:T(8,128)(2,1)S(1)}, bf16[4,2,32,1024]{3,2,1,0:T(8,128)(2,1)S(1)}, bf16[4,2,32,1024]{3,2,1,0:T(8,128)(2,1)S(1)}, bf16[4,2,32,1024]{3,2,1,0:T(8,128)(2,1)S(1)}) custom-call(s32[2]{0:T(128)S(1)} %pad_add_fusion.base_ref, bf16[2,512,384]{2,1,0:T(8,128)(2,1)S(1)} %shard_map.76.hidden_ref, ...), custom_call_target="tpu_custom_call" | custom-call | flops 805306368 | bytes 5000000 | tf_op jit(solution)/shard_map/pallas_call | solution.py:252
  111.2 3.3 %shard_map.77 = (bf16[4,2,32,1024]{3,2,1,0:T(8,128)(2,1)S(1)}, bf16[4,2,32,1024]{3,2,1,0:T(8,128)(2,1)S(1)}, bf16[4,2,32,1024]{3,2,1,0:T(8,128)(2,1)S(1)}, bf16[4,2,32,1024]{3,2,1,0:T(8,128)(2,1)S(1)}) custom-call(s32[2]{0:T(128)S(1)} %pad_add_fusion.base_ref, bf16[2,512,384]{2,1,0:T(8,128)(2,1)S(1)} %shard_map.76.hidden_ref, ...), custom_call_target="tpu_custom_call" | custom-call | flops 805306368 | bytes 5000000 | tf_op jit(solution)/shard_map/pallas_call | solution.py:252
  115.7 3.3 %shard_map.81 = (bf16[4,2,32,1024]{3,2,1,0:T(8,128)(2,1)S(1)}, bf16[4,2,32,1024]{3,2,1,0:T(8,128)(2,1)S(1)}, bf16[4,2,32,1024]{3,2,1,0:T(8,128)(2,1)S(1)}, bf16[4,2,32,1024]{3,2,1,0:T(8,128)(2,1)S(1)}) custom-call(s32[2]{0:T(128)S(1)} %pad_add_fusion.base_ref, bf16[2,512,384]{2,1,0:T(8,128)(2,1)S(1)} %shard_map.76.hidden_ref, ...), custom_call_target="tpu_custom_call" | custom-call | flops 805306368 | bytes 5000000 | tf_op jit(solution)/shard_map/pallas_call | solution.py:252
  119.1 1.9 %collective-permute-start.36 = (bf16[4,2,32,1024]{3,2,1,0:T(8,128)(2,1)S(1)}, bf16[4,2,32,1024]{3,2,1,0:T(8,128)(2,1)S(1)}, u32[]{:S(2)}, u32[]{:S(2)}) collective-permute-start(bf16[4,2,32,1024]{3,2,1,0:T(8,128)(2,1)S(1)} %get-tuple-element.69), channel_id=1, source_target_pairs={{0,2},{1,17},{4,6},{5,21},{2,0},{3,19},{6,4},{7,23},{8,10},{9,25},... | collective-permute-start | bytes 1572872 | tf_op jit(solution)/shard_map/ppermute | solution.py:34
  121.0 2.8 %collective-permute-start.37 = (bf16[4,2,32,1024]{3,2,1,0:T(8,128)(2,1)S(1)}, bf16[4,2,32,1024]{3,2,1,0:T(8,128)(2,1)S(1)}, u32[]{:S(2)}, u32[]{:S(2)}) collective-permute-start(bf16[4,2,32,1024]{3,2,1,0:T(8,128)(2,1)S(1)} %get-tuple-element.70), channel_id=1, source_target_pairs={{0,6},{1,25},{4,2},{5,29},{2,4},{3,27},{6,0},{7,31},{8,14},{9,17},... | collective-permute-start | bytes 1572872 | tf_op jit(solution)/shard_map/ppermute | solution.py:34
  123.8 3.3 %shard_map.78 = (bf16[4,2,32,1024]{3,2,1,0:T(8,128)(2,1)S(1)}, bf16[4,2,32,1024]{3,2,1,0:T(8,128)(2,1)S(1)}, bf16[4,2,32,1024]{3,2,1,0:T(8,128)(2,1)S(1)}, bf16[4,2,32,1024]{3,2,1,0:T(8,128)(2,1)S(1)}) custom-call(s32[2]{0:T(128)S(1)} %pad_add_fusion.base_ref, bf16[2,512,384]{2,1,0:T(8,128)(2,1)S(1)} %shard_map.76.hidden_ref, ...), custom_call_target="tpu_custom_call" | custom-call | flops 805306368 | bytes 5000000 | tf_op jit(solution)/shard_map/pallas_call | solution.py:252
  127.2 1.9 %collective-permute-start.26 = (bf16[4,2,32,1024]{3,2,1,0:T(8,128)(2,1)S(1)}, bf16[4,2,32,1024]{3,2,1,0:T(8,128)(2,1)S(1)}, u32[]{:S(2)}, u32[]{:S(2)}) collective-permute-start(bf16[4,2,32,1024]{3,2,1,0:T(8,128)(2,1)S(1)} %get-tuple-element.57), channel_id=1, source_target_pairs={{0,2},{1,17},{4,6},{5,21},{2,0},{3,19},{6,4},{7,23},{8,10},{9,25},... | collective-permute-start | bytes 1572872 | tf_op jit(solution)/shard_map/ppermute | solution.py:34
  129.2 2.8 %collective-permute-start.27 = (bf16[4,2,32,1024]{3,2,1,0:T(8,128)(2,1)S(1)}, bf16[4,2,32,1024]{3,2,1,0:T(8,128)(2,1)S(1)}, u32[]{:S(2)}, u32[]{:S(2)}) collective-permute-start(bf16[4,2,32,1024]{3,2,1,0:T(8,128)(2,1)S(1)} %get-tuple-element.58), channel_id=1, source_target_pairs={{0,6},{1,25},{4,2},{5,29},{2,4},{3,27},{6,0},{7,31},{8,14},{9,17},... | collective-permute-start | bytes 1572872 | tf_op jit(solution)/shard_map/ppermute | solution.py:34
  131.9 2.0 %collective-permute-done.36.refs_2_ = bf16[4,2,32,1024]{3,2,1,0:T(8,128)(2,1)S(1)} collective-permute-done((bf16[4,2,32,1024]{3,2,1,0:T(8,128)(2,1)S(1)}, bf16[4,2,32,1024]{3,2,1,0:T(8,128)(2,1)S(1)}, u32[]{:S(2)}, u32[]{:S(2)}) %collective-permute-start.36) | collective-permute-done | bytes 524320 | tf_op jit(solution)/shard_map/ppermute | solution.py:34
  133.9 3.1 %collective-permute-done.37.refs_3_ = bf16[4,2,32,1024]{3,2,1,0:T(8,128)(2,1)S(1)} collective-permute-done((bf16[4,2,32,1024]{3,2,1,0:T(8,128)(2,1)S(1)}, bf16[4,2,32,1024]{3,2,1,0:T(8,128)(2,1)S(1)}, u32[]{:S(2)}, u32[]{:S(2)}) %collective-permute-start.37) | collective-permute-done | bytes 524320 | tf_op jit(solution)/shard_map/ppermute | solution.py:34
  137.6 1.7 collective-permute-start.39
  139.3 1.1 collective-permute-done.25.refs_1_
  140.4 1.9 %collective-permute-start.40 = (bf16[128,1024]{1,0:T(8,128)(2,1)S(1)}, bf16[128,1024]{1,0:T(8,128)(2,1)S(1)}, u32[]{:S(2)}, u32[]{:S(2)}) collective-permute-start(bf16[128,1024]{1,0:T(8,128)(2,1)S(1)} %get-tuple-element.74), channel_id=1, source_target_pairs={{0,24},{1,7},{4,28},{5,3},{2,26},{3,5},{6,30},{7,1},{8,16},{9,15},... | collective-permute-start | bytes 786440 | tf_op jit(solution)/shard_map/ppermute | solution.py:34
  142.3 8.5 %collective-permute-done.26.refs_2_ = bf16[4,2,32,1024]{3,2,1,0:T(8,128)(2,1)S(1)} collective-permute-done((bf16[4,2,32,1024]{3,2,1,0:T(8,128)(2,1)S(1)}, bf16[4,2,32,1024]{3,2,1,0:T(8,128)(2,1)S(1)}, u32[]{:S(2)}, u32[]{:S(2)}) %collective-permute-start.26) | collective-permute-done | bytes 524320 | tf_op jit(solution)/shard_map/ppermute | solution.py:34
  150.8 1.5 collective-permute-done.27.refs_3_
  152.8 2.3 %collective-permute-start.29 = (bf16[128,1024]{1,0:T(8,128)(2,1)S(1)}, bf16[128,1024]{1,0:T(8,128)(2,1)S(1)}, u32[]{:S(2)}, u32[]{:S(2)}) collective-permute-start(bf16[128,1024]{1,0:T(8,128)(2,1)S(1)} %get-tuple-element.61), channel_id=1, source_target_pairs={{0,16},{1,3},{4,20},{5,7},{2,18},{3,1},{6,22},{7,5},{8,24},{9,11},... | collective-permute-start | bytes 786440 | tf_op jit(solution)/shard_map/ppermute | solution.py:34
  155.1 2.4 %collective-permute-start.30 = (bf16[128,1024]{1,0:T(8,128)(2,1)S(1)}, bf16[128,1024]{1,0:T(8,128)(2,1)S(1)}, u32[]{:S(2)}, u32[]{:S(2)}) collective-permute-start(bf16[128,1024]{1,0:T(8,128)(2,1)S(1)} %get-tuple-element.62), channel_id=1, source_target_pairs={{0,24},{1,7},{4,28},{5,3},{2,26},{3,5},{6,30},{7,1},{8,16},{9,15},... | collective-permute-start | bytes 786440 | tf_op jit(solution)/shard_map/ppermute | solution.py:34
  157.6 1.5 collective-permute-done.28
  159.2 3.2 %collective-permute-done.29 = bf16[128,1024]{1,0:T(8,128)(2,1)S(1)} collective-permute-done((bf16[128,1024]{1,0:T(8,128)(2,1)S(1)}, bf16[128,1024]{1,0:T(8,128)(2,1)S(1)}, u32[]{:S(2)}, u32[]{:S(2)}) %collective-permute-start.29) | collective-permute-done | bytes 262176 | tf_op jit(solution)/shard_map/ppermute | solution.py:34
  162.4 2.7 %collective-permute-done.30 = bf16[128,1024]{1,0:T(8,128)(2,1)S(1)} collective-permute-done((bf16[128,1024]{1,0:T(8,128)(2,1)S(1)}, bf16[128,1024]{1,0:T(8,128)(2,1)S(1)}, u32[]{:S(2)}, u32[]{:S(2)}) %collective-permute-start.30) | collective-permute-done | bytes 262176 | tf_op jit(solution)/shard_map/ppermute | solution.py:34
  165.4 1.4 collective-permute-start.42
  166.8 3.3 %collective-permute-start.43 = (bf16[32,2048]{1,0:T(8,128)(2,1)S(1)}, bf16[32,2048]{1,0:T(8,128)(2,1)S(1)}, u32[]{:S(2)}, u32[]{:S(2)}) collective-permute-start(bf16[32,2048]{1,0:T(8,128)(2,1)S(1)} %get-tuple-element.76), channel_id=1, source_target_pairs={{0,96},{1,97},{4,100},{5,101},{2,98},{3,99},{6,102},{7,103},{8,104... | collective-permute-start | bytes 393224 | tf_op jit(solution)/shard_map/ppermute | solution.py:34
  170.4 1.6 collective-permute-done.42
  172.0 1.4 collective-permute-done.43
  173.5 1.2 collective-permute-done.44
  (106 shorter events, 23.0 us)
Async XLA Ops:
  5.1 1.3 collective-permute-start
  6.5 6.2 %collective-permute-start.1 = (bf16[32,2176]{1,0:T(8,128)(2,1)S(1)}, bf16[32,2176]{1,0:T(8,128)(2,1)S(1)}, u32[]{:S(2)}, u32[]{:S(2)}) collective-permute-start(bf16[32,2176]{1,0:T(8,128)(2,1)S(1)} %get-tuple-element.81), channel_id=1, source_target_pairs={{0,32},{1,33},{4,36},{5,37},{2,34},{3,35},{6,38},{7,39},{8,40},{9,... | collective-permute-start | bytes 417800 | tf_op jit(solution)/shard_map/ppermute | solution.py:34
  8.5 10.4 %collective-permute-start.2 = (bf16[32,2176]{1,0:T(8,128)(2,1)S(1)}, bf16[32,2176]{1,0:T(8,128)(2,1)S(1)}, u32[]{:S(2)}, u32[]{:S(2)}) collective-permute-start(bf16[32,2176]{1,0:T(8,128)(2,1)S(1)} %get-tuple-element.81), channel_id=1, source_target_pairs={{0,64},{1,65},{4,68},{5,69},{2,66},{3,67},{6,70},{7,71},{8,72},{9,... | collective-permute-start | bytes 417800 | tf_op jit(solution)/shard_map/ppermute | solution.py:34
  12.1 9.1 %collective-permute-start.3 = (bf16[32,2176]{1,0:T(8,128)(2,1)S(1)}, bf16[32,2176]{1,0:T(8,128)(2,1)S(1)}, u32[]{:S(2)}, u32[]{:S(2)}) collective-permute-start(bf16[32,2176]{1,0:T(8,128)(2,1)S(1)} %get-tuple-element.81), channel_id=1, source_target_pairs={{0,96},{1,97},{4,100},{5,101},{2,98},{3,99},{6,102},{7,103},{8,104... | collective-permute-start | bytes 417800 | tf_op jit(solution)/shard_map/ppermute | solution.py:34
  21.3 9.6 %collective-permute-start.4 = (bf16[128,2176]{1,0:T(8,128)(2,1)S(1)}, bf16[128,2176]{1,0:T(8,128)(2,1)S(1)}, u32[]{:S(2)}, u32[]{:S(2)}) collective-permute-start(bf16[128,2176]{1,0:T(8,128)(2,1)S(1)} %bitcast.9), channel_id=1, source_target_pairs={{0,8},{1,5},{4,12},{5,1},{2,10},{3,7},{6,14},{7,3},{8,0},{9,13},{1... | collective-permute-start | bytes 1671176 | tf_op jit(solution)/shard_map/ppermute | solution.py:34
  23.0 16.5 %collective-permute-start.5 = (bf16[128,2176]{1,0:T(8,128)(2,1)S(1)}, bf16[128,2176]{1,0:T(8,128)(2,1)S(1)}, u32[]{:S(2)}, u32[]{:S(2)}) collective-permute-start(bf16[128,2176]{1,0:T(8,128)(2,1)S(1)} %bitcast.10), channel_id=1, source_target_pairs={{0,16},{1,3},{4,20},{5,7},{2,18},{3,1},{6,22},{7,5},{8,24},{9,11},... | collective-permute-start | bytes 1671176 | tf_op jit(solution)/shard_map/ppermute | solution.py:34
  25.9 16.7 %collective-permute-start.6 = (bf16[128,2176]{1,0:T(8,128)(2,1)S(1)}, bf16[128,2176]{1,0:T(8,128)(2,1)S(1)}, u32[]{:S(2)}, u32[]{:S(2)}) collective-permute-start(bf16[128,2176]{1,0:T(8,128)(2,1)S(1)} %bitcast.11), channel_id=1, source_target_pairs={{0,24},{1,7},{4,28},{5,3},{2,26},{3,5},{6,30},{7,1},{8,16},{9,15},... | collective-permute-start | bytes 1671176 | tf_op jit(solution)/shard_map/ppermute | solution.py:34
  45.3 9.2 %collective-permute-start.14 = (bf16[4,2,32,1024]{3,2,1,0:T(8,128)(2,1)S(1)}, bf16[4,2,32,1024]{3,2,1,0:T(8,128)(2,1)S(1)}, u32[]{:S(2)}, u32[]{:S(2)}) collective-permute-start(bf16[4,2,32,1024]{3,2,1,0:T(8,128)(2,1)S(1)} %get-tuple-element.46), channel_id=1, source_target_pairs={{0,4},{1,9},{4,0},{5,13},{2,6},{3,11},{6,2},{7,15},{8,12},{9,1},{1... | collective-permute-start | bytes 1572872 | tf_op jit(solution)/shard_map/ppermute | solution.py:34
  46.8 15.6 %collective-permute-start.15 = (bf16[4,2,32,1024]{3,2,1,0:T(8,128)(2,1)S(1)}, bf16[4,2,32,1024]{3,2,1,0:T(8,128)(2,1)S(1)}, u32[]{:S(2)}, u32[]{:S(2)}) collective-permute-start(bf16[4,2,32,1024]{3,2,1,0:T(8,128)(2,1)S(1)} %get-tuple-element.47), channel_id=1, source_target_pairs={{0,2},{1,17},{4,6},{5,21},{2,0},{3,19},{6,4},{7,23},{8,10},{9,25},... | collective-permute-start | bytes 1572872 | tf_op jit(solution)/shard_map/ppermute | solution.py:34
  49.5 22.4 %collective-permute-start.16 = (bf16[4,2,32,1024]{3,2,1,0:T(8,128)(2,1)S(1)}, bf16[4,2,32,1024]{3,2,1,0:T(8,128)(2,1)}, u32[]{:S(2)}, u32[]{:S(2)}) collective-permute-start(bf16[4,2,32,1024]{3,2,1,0:T(8,128)(2,1)S(1)} %get-tuple-element.48), channel_id=1, source_target_pairs={{0,6},{1,25},{4,2},{5,29},{2,4},{3,27},{6,0},{7,31},{8,14},{9,17},... | collective-permute-start | bytes 1572872 | tf_op jit(solution)/shard_map/ppermute | solution.py:34
  50.0 22.0 %collective-permute-start.17 = (bf16[4,2,32,1024]{3,2,1,0:T(8,128)(2,1)S(1)}, bf16[4,2,32,1024]{3,2,1,0:T(8,128)(2,1)S(1)}, u32[]{:S(2)}, u32[]{:S(2)}) collective-permute-start(bf16[4,2,32,1024]{3,2,1,0:T(8,128)(2,1)S(1)} %get-tuple-element.45.refs_0_), channel_id=1, source_target_pairs={{0,1},{1,0},{2,3},{3,2},{4,5},{5,4},{6,7},{7,6},{8,9},{9,8},{10,11... | collective-permute-start | bytes 1572872 | tf_op jit(solution)/shard_map/ppermute | solution.py:49
  50.8 23.3 %collective-permute-start.10 = (bf16[4,2,32,1152]{3,2,1,0:T(8,128)(2,1)}, bf16[4,2,32,1152]{3,2,1,0:T(8,128)(2,1)S(1)}, u32[]{:S(2)}, u32[]{:S(2)}) collective-permute-start(bf16[4,2,32,1152]{3,2,1,0:T(8,128)(2,1)} %get-tuple-element.43), channel_id=1, source_target_pairs={{0,2},{1,17},{4,6},{5,21},{2,0},{3,19},{6,4},{7,23},{8,10},{9,25},... | collective-permute-start | bytes 1769480 | tf_op jit(solution)/shard_map/ppermute | solution.py:34
  54.5 23.7 %collective-permute-start.12 = (bf16[4,2,32,1152]{3,2,1,0:T(8,128)(2,1)}, bf16[4,2,32,1152]{3,2,1,0:T(8,128)(2,1)S(1)}, u32[]{:S(2)}, u32[]{:S(2)}) collective-permute-start(bf16[4,2,32,1152]{3,2,1,0:T(8,128)(2,1)} %get-tuple-element.44), channel_id=1, source_target_pairs={{0,6},{1,25},{4,2},{5,29},{2,4},{3,27},{6,0},{7,31},{8,14},{9,17},... | collective-permute-start | bytes 1769480 | tf_op jit(solution)/shard_map/ppermute | solution.py:34
  62.4 15.8 %collective-permute-start.8 = (bf16[4,2,32,1152]{3,2,1,0:T(8,128)(2,1)S(1)}, bf16[4,2,32,1152]{3,2,1,0:T(8,128)(2,1)S(1)}, u32[]{:S(2)}, u32[]{:S(2)}) collective-permute-start(bf16[4,2,32,1152]{3,2,1,0:T(8,128)(2,1)S(1)} %get-tuple-element.42), channel_id=1, source_target_pairs={{0,4},{1,9},{4,0},{5,13},{2,6},{3,11},{6,2},{7,15},{8,12},{9,1},{1... | collective-permute-start | bytes 1769480 | tf_op jit(solution)/shard_map/ppermute | solution.py:34
  72.0 6.7 %collective-permute-start.18 = (bf16[4,2,32,1024]{3,2,1,0:T(8,128)(2,1)S(1)}, bf16[4,2,32,1024]{3,2,1,0:T(8,128)(2,1)S(1)}, u32[]{:S(2)}, u32[]{:S(2)}) collective-permute-start(bf16[4,2,32,1024]{3,2,1,0:T(8,128)(2,1)S(1)} %collective-permute-done.14.refs_1_), channel_id=1, source_target_pairs={{0,1},{1,0},{2,3},{3,2},{4,5},{5,4},{6,7},{7,6},{8,9},{9,8},{10,11... | collective-permute-start | bytes 1572872 | tf_op jit(solution)/shard_map/ppermute | solution.py:49
  72.8 6.8 %collective-permute-start.19 = (bf16[4,2,32,1024]{3,2,1,0:T(8,128)(2,1)S(1)}, bf16[4,2,32,1024]{3,2,1,0:T(8,128)(2,1)S(1)}, u32[]{:S(2)}, u32[]{:S(2)}) collective-permute-start(bf16[4,2,32,1024]{3,2,1,0:T(8,128)(2,1)S(1)} %collective-permute-done.15.refs_2_), channel_id=1, source_target_pairs={{0,1},{1,0},{2,3},{3,2},{4,5},{5,4},{6,7},{7,6},{8,9},{9,8},{10,11... | collective-permute-start | bytes 1572872 | tf_op jit(solution)/shard_map/ppermute | solution.py:49
  74.1 6.8 %collective-permute-start.20 = (bf16[4,2,32,1024]{3,2,1,0:T(8,128)(2,1)}, bf16[4,2,32,1024]{3,2,1,0:T(8,128)(2,1)}, u32[]{:S(2)}, u32[]{:S(2)}) collective-permute-start(bf16[4,2,32,1024]{3,2,1,0:T(8,128)(2,1)} %collective-permute-done.16.refs_3_), channel_id=1, source_target_pairs={{0,1},{1,0},{2,3},{3,2},{4,5},{5,4},{6,7},{7,6},{8,9},{9,8},{10,11... | collective-permute-start | bytes 1572872 | tf_op jit(solution)/shard_map/ppermute | solution.py:49
  78.2 23.2 %collective-permute-start.7 = (bf16[4,2,32,1152]{3,2,1,0:T(8,128)(2,1)S(1)}, bf16[4,2,32,1152]{3,2,1,0:T(8,128)(2,1)}, u32[]{:S(2)}, u32[]{:S(2)}) collective-permute-start(bf16[4,2,32,1152]{3,2,1,0:T(8,128)(2,1)S(1)} %get-tuple-element.41.refs_1_), channel_id=1, source_target_pairs={{0,1},{1,0},{2,3},{3,2},{4,5},{5,4},{6,7},{7,6},{8,9},{9,8},{10,11... | collective-permute-start | bytes 1769480 | tf_op jit(solution)/shard_map/ppermute | solution.py:49
  78.2 23.2 %collective-permute-start.11 = (bf16[4,2,32,1152]{3,2,1,0:T(8,128)(2,1)S(1)}, bf16[4,2,32,1152]{3,2,1,0:T(8,128)(2,1)}, u32[]{:S(2)}, u32[]{:S(2)}) collective-permute-start(bf16[4,2,32,1152]{3,2,1,0:T(8,128)(2,1)S(1)} %collective-permute-done.10.refs_3_), channel_id=1, source_target_pairs={{0,1},{1,0},{2,3},{3,2},{4,5},{5,4},{6,7},{7,6},{8,9},{9,8},{10,11... | collective-permute-start | bytes 1769480 | tf_op jit(solution)/shard_map/ppermute | solution.py:49
  79.5 21.9 %collective-permute-start.13 = (bf16[4,2,32,1152]{3,2,1,0:T(8,128)(2,1)S(1)}, bf16[4,2,32,1152]{3,2,1,0:T(8,128)(2,1)}, u32[]{:S(2)}, u32[]{:S(2)}) collective-permute-start(bf16[4,2,32,1152]{3,2,1,0:T(8,128)(2,1)S(1)} %collective-permute-done.12.refs_4_), channel_id=1, source_target_pairs={{0,1},{1,0},{2,3},{3,2},{4,5},{5,4},{6,7},{7,6},{8,9},{9,8},{10,11... | collective-permute-start | bytes 1769480 | tf_op jit(solution)/shard_map/ppermute | solution.py:49
  80.3 21.1 %collective-permute-start.9 = (bf16[4,2,32,1152]{3,2,1,0:T(8,128)(2,1)S(1)}, bf16[4,2,32,1152]{3,2,1,0:T(8,128)(2,1)}, u32[]{:S(2)}, u32[]{:S(2)}) collective-permute-start(bf16[4,2,32,1152]{3,2,1,0:T(8,128)(2,1)S(1)} %collective-permute-done.8.refs_2_), channel_id=1, source_target_pairs={{0,1},{1,0},{2,3},{3,2},{4,5},{5,4},{6,7},{7,6},{8,9},{9,8},{10,11... | collective-permute-start | bytes 1769480 | tf_op jit(solution)/shard_map/ppermute | solution.py:49
  80.9 1.0 copy-start.2
  83.0 1.0 copy-start.6
  99.8 1.6 copy-start
  110.1 4.6 %collective-permute-start.31 = (bf16[4,2,32,1024]{3,2,1,0:T(8,128)(2,1)S(1)}, bf16[4,2,32,1024]{3,2,1,0:T(8,128)(2,1)S(1)}, u32[]{:S(2)}, u32[]{:S(2)}) collective-permute-start(bf16[4,2,32,1024]{3,2,1,0:T(8,128)(2,1)S(1)} %get-tuple-element.63), channel_id=1, source_target_pairs={{0,1},{1,0},{2,3},{3,2},{4,5},{5,4},{6,7},{7,6},{8,9},{9,8},{10,11... | collective-permute-start | bytes 1572872 | tf_op jit(solution)/shard_map/ppermute | solution.py:49
  110.2 4.9 %collective-permute-start.32 = (bf16[4,2,32,1024]{3,2,1,0:T(8,128)(2,1)S(1)}, bf16[4,2,32,1024]{3,2,1,0:T(8,128)(2,1)S(1)}, u32[]{:S(2)}, u32[]{:S(2)}) collective-permute-start(bf16[4,2,32,1024]{3,2,1,0:T(8,128)(2,1)S(1)} %get-tuple-element.64), channel_id=1, source_target_pairs={{0,1},{1,0},{2,3},{3,2},{4,5},{5,4},{6,7},{7,6},{8,9},{9,8},{10,11... | collective-permute-start | bytes 1572872 | tf_op jit(solution)/shard_map/ppermute | solution.py:49
  110.7 4.5 %collective-permute-start.33 = (bf16[4,2,32,1024]{3,2,1,0:T(8,128)(2,1)S(1)}, bf16[4,2,32,1024]{3,2,1,0:T(8,128)(2,1)S(1)}, u32[]{:S(2)}, u32[]{:S(2)}) collective-permute-start(bf16[4,2,32,1024]{3,2,1,0:T(8,128)(2,1)S(1)} %get-tuple-element.65), channel_id=1, source_target_pairs={{0,1},{1,0},{2,3},{3,2},{4,5},{5,4},{6,7},{7,6},{8,9},{9,8},{10,11... | collective-permute-start | bytes 1572872 | tf_op jit(solution)/shard_map/ppermute | solution.py:49
  110.8 4.8 %collective-permute-start.34 = (bf16[4,2,32,1024]{3,2,1,0:T(8,128)(2,1)S(1)}, bf16[4,2,32,1024]{3,2,1,0:T(8,128)(2,1)S(1)}, u32[]{:S(2)}, u32[]{:S(2)}) collective-permute-start(bf16[4,2,32,1024]{3,2,1,0:T(8,128)(2,1)S(1)} %get-tuple-element.66), channel_id=1, source_target_pairs={{0,1},{1,0},{2,3},{3,2},{4,5},{5,4},{6,7},{7,6},{8,9},{9,8},{10,11... | collective-permute-start | bytes 1572872 | tf_op jit(solution)/shard_map/ppermute | solution.py:49
  114.5 4.6 %collective-permute-start.21 = (bf16[4,2,32,1024]{3,2,1,0:T(8,128)(2,1)S(1)}, bf16[4,2,32,1024]{3,2,1,0:T(8,128)(2,1)S(1)}, u32[]{:S(2)}, u32[]{:S(2)}) collective-permute-start(bf16[4,2,32,1024]{3,2,1,0:T(8,128)(2,1)S(1)} %get-tuple-element.51), channel_id=1, source_target_pairs={{0,1},{1,0},{2,3},{3,2},{4,5},{5,4},{6,7},{7,6},{8,9},{9,8},{10,11... | collective-permute-start | bytes 1572872 | tf_op jit(solution)/shard_map/ppermute | solution.py:49
  114.7 6.3 %collective-permute-start.22 = (bf16[4,2,32,1024]{3,2,1,0:T(8,128)(2,1)S(1)}, bf16[4,2,32,1024]{3,2,1,0:T(8,128)(2,1)S(1)}, u32[]{:S(2)}, u32[]{:S(2)}) collective-permute-start(bf16[4,2,32,1024]{3,2,1,0:T(8,128)(2,1)S(1)} %get-tuple-element.52), channel_id=1, source_target_pairs={{0,1},{1,0},{2,3},{3,2},{4,5},{5,4},{6,7},{7,6},{8,9},{9,8},{10,11... | collective-permute-start | bytes 1572872 | tf_op jit(solution)/shard_map/ppermute | solution.py:49
  115.1 8.7 %collective-permute-start.23 = (bf16[4,2,32,1024]{3,2,1,0:T(8,128)(2,1)S(1)}, bf16[4,2,32,1024]{3,2,1,0:T(8,128)(2,1)S(1)}, u32[]{:S(2)}, u32[]{:S(2)}) collective-permute-start(bf16[4,2,32,1024]{3,2,1,0:T(8,128)(2,1)S(1)} %get-tuple-element.53), channel_id=1, source_target_pairs={{0,1},{1,0},{2,3},{3,2},{4,5},{5,4},{6,7},{7,6},{8,9},{9,8},{10,11... | collective-permute-start | bytes 1572872 | tf_op jit(solution)/shard_map/ppermute | solution.py:49
  115.2 8.6 %collective-permute-start.24 = (bf16[4,2,32,1024]{3,2,1,0:T(8,128)(2,1)S(1)}, bf16[4,2,32,1024]{3,2,1,0:T(8,128)(2,1)S(1)}, u32[]{:S(2)}, u32[]{:S(2)}) collective-permute-start(bf16[4,2,32,1024]{3,2,1,0:T(8,128)(2,1)S(1)} %get-tuple-element.54), channel_id=1, source_target_pairs={{0,1},{1,0},{2,3},{3,2},{4,5},{5,4},{6,7},{7,6},{8,9},{9,8},{10,11... | collective-permute-start | bytes 1572872 | tf_op jit(solution)/shard_map/ppermute | solution.py:49
  119.0 10.2 %collective-permute-start.35 = (bf16[4,2,32,1024]{3,2,1,0:T(8,128)(2,1)S(1)}, bf16[4,2,32,1024]{3,2,1,0:T(8,128)(2,1)S(1)}, u32[]{:S(2)}, u32[]{:S(2)}) collective-permute-start(bf16[4,2,32,1024]{3,2,1,0:T(8,128)(2,1)S(1)} %get-tuple-element.68), channel_id=1, source_target_pairs={{0,4},{1,9},{4,0},{5,13},{2,6},{3,11},{6,2},{7,15},{8,12},{9,1},{1... | collective-permute-start | bytes 1572872 | tf_op jit(solution)/shard_map/ppermute | solution.py:34
  119.1 14.8 %collective-permute-start.36 = (bf16[4,2,32,1024]{3,2,1,0:T(8,128)(2,1)S(1)}, bf16[4,2,32,1024]{3,2,1,0:T(8,128)(2,1)S(1)}, u32[]{:S(2)}, u32[]{:S(2)}) collective-permute-start(bf16[4,2,32,1024]{3,2,1,0:T(8,128)(2,1)S(1)} %get-tuple-element.69), channel_id=1, source_target_pairs={{0,2},{1,17},{4,6},{5,21},{2,0},{3,19},{6,4},{7,23},{8,10},{9,25},... | collective-permute-start | bytes 1572872 | tf_op jit(solution)/shard_map/ppermute | solution.py:34
  121.0 16.0 %collective-permute-start.37 = (bf16[4,2,32,1024]{3,2,1,0:T(8,128)(2,1)S(1)}, bf16[4,2,32,1024]{3,2,1,0:T(8,128)(2,1)S(1)}, u32[]{:S(2)}, u32[]{:S(2)}) collective-permute-start(bf16[4,2,32,1024]{3,2,1,0:T(8,128)(2,1)S(1)} %get-tuple-element.70), channel_id=1, source_target_pairs={{0,6},{1,25},{4,2},{5,29},{2,4},{3,27},{6,0},{7,31},{8,14},{9,17},... | collective-permute-start | bytes 1572872 | tf_op jit(solution)/shard_map/ppermute | solution.py:34
  127.2 13.2 %collective-permute-start.25 = (bf16[4,2,32,1024]{3,2,1,0:T(8,128)(2,1)S(1)}, bf16[4,2,32,1024]{3,2,1,0:T(8,128)(2,1)S(1)}, u32[]{:S(2)}, u32[]{:S(2)}) collective-permute-start(bf16[4,2,32,1024]{3,2,1,0:T(8,128)(2,1)S(1)} %get-tuple-element.56), channel_id=1, source_target_pairs={{0,4},{1,9},{4,0},{5,13},{2,6},{3,11},{6,2},{7,15},{8,12},{9,1},{1... | collective-permute-start | bytes 1572872 | tf_op jit(solution)/shard_map/ppermute | solution.py:34
  127.2 23.6 %collective-permute-start.26 = (bf16[4,2,32,1024]{3,2,1,0:T(8,128)(2,1)S(1)}, bf16[4,2,32,1024]{3,2,1,0:T(8,128)(2,1)S(1)}, u32[]{:S(2)}, u32[]{:S(2)}) collective-permute-start(bf16[4,2,32,1024]{3,2,1,0:T(8,128)(2,1)S(1)} %get-tuple-element.57), channel_id=1, source_target_pairs={{0,2},{1,17},{4,6},{5,21},{2,0},{3,19},{6,4},{7,23},{8,10},{9,25},... | collective-permute-start | bytes 1572872 | tf_op jit(solution)/shard_map/ppermute | solution.py:34
  129.2 23.1 %collective-permute-start.27 = (bf16[4,2,32,1024]{3,2,1,0:T(8,128)(2,1)S(1)}, bf16[4,2,32,1024]{3,2,1,0:T(8,128)(2,1)S(1)}, u32[]{:S(2)}, u32[]{:S(2)}) collective-permute-start(bf16[4,2,32,1024]{3,2,1,0:T(8,128)(2,1)S(1)} %get-tuple-element.58), channel_id=1, source_target_pairs={{0,6},{1,25},{4,2},{5,29},{2,4},{3,27},{6,0},{7,31},{8,14},{9,17},... | collective-permute-start | bytes 1572872 | tf_op jit(solution)/shard_map/ppermute | solution.py:34
  137.5 17.6 %collective-permute-start.38 = (bf16[128,1024]{1,0:T(8,128)(2,1)S(1)}, bf16[128,1024]{1,0:T(8,128)(2,1)S(1)}, u32[]{:S(2)}, u32[]{:S(2)}) collective-permute-start(bf16[128,1024]{1,0:T(8,128)(2,1)S(1)} %get-tuple-element.72), channel_id=1, source_target_pairs={{0,8},{1,5},{4,12},{5,1},{2,10},{3,7},{6,14},{7,3},{8,0},{9,13},{1... | collective-permute-start | bytes 786440 | tf_op jit(solution)/shard_map/ppermute | solution.py:34
  137.6 19.9 %collective-permute-start.39 = (bf16[128,1024]{1,0:T(8,128)(2,1)S(1)}, bf16[128,1024]{1,0:T(8,128)(2,1)S(1)}, u32[]{:S(2)}, u32[]{:S(2)}) collective-permute-start(bf16[128,1024]{1,0:T(8,128)(2,1)S(1)} %get-tuple-element.73), channel_id=1, source_target_pairs={{0,16},{1,3},{4,20},{5,7},{2,18},{3,1},{6,22},{7,5},{8,24},{9,11},... | collective-permute-start | bytes 786440 | tf_op jit(solution)/shard_map/ppermute | solution.py:34
  140.4 17.1 %collective-permute-start.40 = (bf16[128,1024]{1,0:T(8,128)(2,1)S(1)}, bf16[128,1024]{1,0:T(8,128)(2,1)S(1)}, u32[]{:S(2)}, u32[]{:S(2)}) collective-permute-start(bf16[128,1024]{1,0:T(8,128)(2,1)S(1)} %get-tuple-element.74), channel_id=1, source_target_pairs={{0,24},{1,7},{4,28},{5,3},{2,26},{3,5},{6,30},{7,1},{8,16},{9,15},... | collective-permute-start | bytes 786440 | tf_op jit(solution)/shard_map/ppermute | solution.py:34
  152.7 6.5 %collective-permute-start.28 = (bf16[128,1024]{1,0:T(8,128)(2,1)S(1)}, bf16[128,1024]{1,0:T(8,128)(2,1)S(1)}, u32[]{:S(2)}, u32[]{:S(2)}) collective-permute-start(bf16[128,1024]{1,0:T(8,128)(2,1)S(1)} %get-tuple-element.60), channel_id=1, source_target_pairs={{0,8},{1,5},{4,12},{5,1},{2,10},{3,7},{6,14},{7,3},{8,0},{9,13},{1... | collective-permute-start | bytes 786440 | tf_op jit(solution)/shard_map/ppermute | solution.py:34
  152.8 9.6 %collective-permute-start.29 = (bf16[128,1024]{1,0:T(8,128)(2,1)S(1)}, bf16[128,1024]{1,0:T(8,128)(2,1)S(1)}, u32[]{:S(2)}, u32[]{:S(2)}) collective-permute-start(bf16[128,1024]{1,0:T(8,128)(2,1)S(1)} %get-tuple-element.61), channel_id=1, source_target_pairs={{0,16},{1,3},{4,20},{5,7},{2,18},{3,1},{6,22},{7,5},{8,24},{9,11},... | collective-permute-start | bytes 786440 | tf_op jit(solution)/shard_map/ppermute | solution.py:34
  155.1 10.0 %collective-permute-start.30 = (bf16[128,1024]{1,0:T(8,128)(2,1)S(1)}, bf16[128,1024]{1,0:T(8,128)(2,1)S(1)}, u32[]{:S(2)}, u32[]{:S(2)}) collective-permute-start(bf16[128,1024]{1,0:T(8,128)(2,1)S(1)} %get-tuple-element.62), channel_id=1, source_target_pairs={{0,24},{1,7},{4,28},{5,3},{2,26},{3,5},{6,30},{7,1},{8,16},{9,15},... | collective-permute-start | bytes 786440 | tf_op jit(solution)/shard_map/ppermute | solution.py:34
  165.3 5.0 %collective-permute-start.41 = (bf16[32,2048]{1,0:T(8,128)(2,1)S(1)}, bf16[32,2048]{1,0:T(8,128)(2,1)S(1)}, u32[]{:S(2)}, u32[]{:S(2)}) collective-permute-start(bf16[32,2048]{1,0:T(8,128)(2,1)S(1)} %get-tuple-element.75), channel_id=1, source_target_pairs={{0,32},{1,33},{4,36},{5,37},{2,34},{3,35},{6,38},{7,39},{8,40},{9,... | collective-permute-start | bytes 393224 | tf_op jit(solution)/shard_map/ppermute | solution.py:34
  165.4 6.6 %collective-permute-start.42 = (bf16[32,2048]{1,0:T(8,128)(2,1)S(1)}, bf16[32,2048]{1,0:T(8,128)(2,1)S(1)}, u32[]{:S(2)}, u32[]{:S(2)}) collective-permute-start(bf16[32,2048]{1,0:T(8,128)(2,1)S(1)} %get-tuple-element.77), channel_id=1, source_target_pairs={{0,64},{1,65},{4,68},{5,69},{2,66},{3,67},{6,70},{7,71},{8,72},{9,... | collective-permute-start | bytes 393224 | tf_op jit(solution)/shard_map/ppermute | solution.py:34
  166.8 6.6 %collective-permute-start.43 = (bf16[32,2048]{1,0:T(8,128)(2,1)S(1)}, bf16[32,2048]{1,0:T(8,128)(2,1)S(1)}, u32[]{:S(2)}, u32[]{:S(2)}) collective-permute-start(bf16[32,2048]{1,0:T(8,128)(2,1)S(1)} %get-tuple-element.76), channel_id=1, source_target_pairs={{0,96},{1,97},{4,100},{5,101},{2,98},{3,99},{6,102},{7,103},{8,104... | collective-permute-start | bytes 393224 | tf_op jit(solution)/shard_map/ppermute | solution.py:34
  173.4 1.3 collective-permute-start.44
  (8 other events, 7.1 us)

commit v3 on v0

v3 whole, which is shorter than its diff:
```python
import functools

import jax
import jax.numpy as jnp
from jax import lax
from jax.experimental import pallas as pl
from jax.experimental.pallas import tpu as pltpu
from jax.sharding import PartitionSpec as P

AXES = ("expert", "dp")
SIDE = 4
META = 128
CAP = 4
PARTS = 1
BACK = 2


def place(z, y, x, core):
    return ((z * SIDE + y) * 2 + x % 2) * 4 + (x // 2) * 2 + core


def partners(axes, masks):
    masks = (masks, masks) if isinstance(masks, int) else masks
    pairs = []
    for z in range(SIDE):
        for y in range(SIDE):
            for x in range(SIDE):
                for core in range(2):
                    other = [z, y, x]
                    other["zyx".index(axes[core])] ^= masks[core]
                    pairs.append((place(z, y, x, core), place(*other, core)))
    return pairs


def exchange(value, axes):
    over = lax.ppermute(value[2], AXES, partners(axes, 2))
    one, three = (lax.ppermute(value[j], AXES, partners(axes, j)) for j in (1, 3))
    return [value[0], one, over, three]


def exchange_z(value, first_core):
    over = lax.ppermute(value[2], AXES, partners("zz", 2))
    near = lax.ppermute(jnp.where(first_core, value[1], value[3]), AXES, partners("zz", (1, 3)))
    far = lax.ppermute(jnp.where(first_core, value[3], value[1]), AXES, partners("zz", (3, 1)))
    return [value[0], jnp.where(first_core, near, far), over, jnp.where(first_core, far, near)]


def sibling(value):
    pairs = [(i, i ^ 1) for i in range(SIDE**3 * 2)]
    return lax.ppermute(value, AXES, pairs)


def prepare_kernel(core_ref, tokens_ref, ids_ref, weights_ref, placement_ref, kept_ref, sent_ref):
    top, count = ids_ref.shape
    width = tokens_ref.shape[1]
    half, step = width // 2, width // 2 // PARTS
    slot_count = placement_ref.shape[1]
    lanes = lax.broadcasted_iota(jnp.int32, (count, slot_count), 1)
    placement = placement_ref[...].astype(jnp.float32)
    line = lax.broadcasted_iota(jnp.int32, (count, count), 0)
    column = lax.broadcasted_iota(jnp.int32, (count, count), 1)
    diagonal = line == column
    slots = []
    named = jnp.zeros((count, slot_count), jnp.float32)
    for k in range(top):
        ids = jnp.sum(jnp.where(diagonal, ids_ref[k : k + 1], 0), axis=1, keepdims=True)
        slot = jnp.sum(jnp.where(ids == lanes, placement, 0.0), axis=1, keepdims=True)
        slots.append(slot)
        named = jnp.where(lanes.astype(jnp.float32) == slot, 1.0, named)
    before = jnp.where(line > column, 1.0, 0.0)
    ranks = jnp.dot(before.astype(jnp.bfloat16), named.astype(jnp.bfloat16), preferred_element_type=jnp.float32)
    lane = lax.broadcasted_iota(jnp.int32, (count, META), 1)
    meta = jnp.full((count, META), -1.0, jnp.float32)
    for k in range(top):
        rank = jnp.sum(jnp.where(lanes.astype(jnp.float32) == slots[k], ranks, 0.0), axis=1, keepdims=True)
        weight = jnp.sum(jnp.where(diagonal, weights_ref[k : k + 1], 0.0), axis=1, keepdims=True)
        high = weight.astype(jnp.bfloat16).astype(jnp.float32)
        middle = (weight - high).astype(jnp.bfloat16).astype(jnp.float32)
        for turn, term in enumerate((high, middle, weight - high - middle)):
            at = turn * top + k
            meta = jnp.where(lane == at, slots[k] * CAP + rank, meta)
            meta = jnp.where(lane == META // 2 + at, term, meta)
    meta = meta.astype(jnp.bfloat16)
    for ref, own in ((kept_ref, True), (sent_ref, False)):
        begin = core_ref[0] * half if own else half - core_ref[0] * half
        begin = pl.multiple_of(begin, 128)
        ref[:, :step] = tokens_ref[:, pl.ds(begin, step)]
        ref[:, step : step + META] = meta
        if step < half:
            ref[:, step + META :] = tokens_ref[:, pl.ds(pl.multiple_of(begin + step, 128), half - step)]


def fetch_kernel(gate_ref, up_ref, both_ref, sems):
    columns = gate_ref.shape[2]
    copies = [
        pltpu.make_async_copy(ref, both_ref.at[:, :, pl.ds(i * columns, columns)], sems.at[i])
        for i, ref in enumerate((gate_ref, up_ref))
    ]
    for copy in copies:
        copy.start()
    for copy in copies:
        copy.wait()


def pack_kernel(*refs, top, tok_count, step, first):
    wanted_ref, planes, outs = refs[0], refs[1 : 1 + SIDE], refs[1 + SIDE : 1 + 2 * SIDE]
    if first:
        choice_ref = refs[-1]
        wanted = wanted_ref[...]
        tokens, lines = planes[0].shape[0], wanted.shape[1]
        blocks = tokens // tok_count
        token_block = lax.broadcasted_iota(jnp.int32, (tokens, lines), 0) // tok_count
        line_block = lax.broadcasted_iota(jnp.int32, (tokens, lines), 1) // CAP % blocks
        inside = token_block == line_block
    for p in range(SIDE):
        if first:
            codes = planes[p][:, step : step + META].astype(jnp.float32)
            found = codes[:, :1] == wanted
            for k in range(1, top):
                found = found | (codes[:, k : k + 1] == wanted)
            choice = jnp.where(found & inside, 1.0, 0.0)
            choice_ref[p] = choice.astype(jnp.bfloat16)
        else:
            choice = wanted_ref[p].astype(jnp.float32)
        take = choice.T.astype(jnp.bfloat16)
        rows = jnp.dot(take, planes[p][...], preferred_element_type=jnp.float32).astype(jnp.bfloat16)
        share = rows.shape[0] // SIDE
        for j in range(SIDE):
            outs[j][p] = rows[j * share : (j + 1) * share].reshape(outs[j].shape[1:])


def gate_kernel(base_ref, *refs, source, part, weigh, has_total, finish):
    refs = list(refs)
    pieces = [refs.pop(0) for _ in range(SIDE)]
    w_ref = refs.pop(0)
    total_in = refs.pop(0) if has_total else None
    total_ref = refs.pop(0)
    weight_ref = refs.pop(0) if weigh else None
    [rows_ref] = refs
    granule, columns = pieces[0].shape[2], w_ref.shape[2] // 2
    step = rows_ref.shape[1]
    which = 0 if source == "own" else 1
    begin = pl.multiple_of((base_ref[which] * PARTS + part) * step, step)
    for slot in range(w_ref.shape[0]):
        for last in range(SIDE):
            for plane in range(SIDE):
                piece = pieces[last][plane, slot] if source == "own" else pieces[plane][last, slot]
                line = (last * SIDE + plane) * granule
                rows_ref[line : line + granule] = piece[:, :step]
                if weigh:
                    info = piece[:, step:].astype(jnp.float32)
                    code = (CAP * (base_ref[2] + slot)).astype(jnp.float32)
                    lane = lax.broadcasted_iota(jnp.int32, info.shape, 1)
                    named = (info >= code) & (info < code + CAP) & (lane < META // 2)
                    value = pltpu.roll(info, META // 2, 1)
                    weight_ref[slot, line : line + granule] = jnp.sum(jnp.where(named, value, 0.0), axis=1, keepdims=True)
        total = jnp.dot(rows_ref[...], w_ref[slot, pl.ds(begin, step)], preferred_element_type=jnp.float32)
        if has_total:
            total = total + total_in[slot]
        if finish:
            total_ref[slot] = (jax.nn.silu(total[:, :columns]) * total[:, columns:]).astype(jnp.bfloat16)
        else:
            total_ref[slot] = total


def down_kernel(base_ref, hidden_ref, weight_ref, w_ref, *refs, part, turned):
    outs, added = refs[-SIDE:], refs[:-SIDE]
    granule, step = outs[0].shape[2:]
    which = 1 if turned else 0
    begin = pl.multiple_of((base_ref[which] * BACK + part) * step, step)
    for slot in range(hidden_ref.shape[0]):
        value = jnp.dot(hidden_ref[slot], w_ref[slot, :, pl.ds(begin, step)], preferred_element_type=jnp.float32)
        value = weight_ref[slot] * value
        for last in range(SIDE):
            for plane in range(SIDE):
                line = (last * SIDE + plane) * granule
                rows = value[line : line + granule]
                if turned:
                    outs[plane][last, slot] = rows.astype(jnp.bfloat16)
                else:
                    outs[last][plane, slot] = (rows + added[last][plane, slot].astype(jnp.float32)).astype(jnp.bfloat16)


def unpack_kernel(choice_ref, *refs):
    pieces, outs = refs[:SIDE], refs[SIDE:]
    for p in range(SIDE):
        values = jnp.concatenate([piece[p].reshape(-1, piece.shape[3]) for piece in pieces])
        dense = jnp.dot(choice_ref[p], values, preferred_element_type=jnp.float32)
        outs[p][...] = dense.astype(outs[p].dtype)


def whole(count):
    return [pl.BlockSpec(memory_space=pltpu.VMEM)] * count


def params(mebibytes=12):
    return pltpu.CompilerParams(vmem_limit_bytes=mebibytes * 2**20)


def cost(flops, read):
    return pl.CostEstimate(flops=int(flops), bytes_accessed=int(read), transcendentals=0)


def shards(tokens, expert_ids, gate_weights, placement, w_gate, w_up, w_down):
    tok_count, width = tokens.shape
    top = expert_ids.shape[1]
    per_device = w_gate.shape[0]
    half = width // 2
    step = half // PARTS
    core = lax.axis_index("dp") % 2
    first_core = core == 0
    own_slot = lax.axis_index("expert") * per_device
    local = jnp.arange(per_device, dtype=jnp.int32)
    scalar = [pl.BlockSpec(memory_space=pltpu.SMEM)]
    base = jnp.stack([core, 1 - core, own_slot]).astype(jnp.int32)

    carried = jax.ShapeDtypeStruct((tok_count, half + META), jnp.bfloat16)
    kept, sent = pl.pallas_call(
        prepare_kernel,
        grid=(1,),
        out_shape=[carried, carried],
        in_specs=scalar
        + [
            pl.BlockSpec(shape, lambda i: (0, 0))
            for shape in (tokens.shape, (top, tok_count), (top, tok_count), (1, placement.shape[0]))
        ],
        out_specs=whole(2),
        compiler_params=params(),
    )(base, tokens, expert_ids.T, gate_weights.T, placement.reshape(1, -1))
    got = sibling(sent)
    both = jnp.concatenate([jnp.where(first_core, kept, got), jnp.where(first_core, got, kept)])

    near_pieces = exchange_z([both] * SIDE, first_core)
    widths = [step + META] + [step] * (PARTS - 1)
    begins = [0] + [META + part * step for part in range(1, PARTS)]
    nears = [
        jnp.concatenate([piece[:, begin : begin + columns] for piece in near_pieces])
        for begin, columns in zip(begins, widths)
    ]
    near_count = nears[0].shape[0]

    lines = near_count // tok_count * CAP * per_device * SIDE
    masks = jnp.arange(SIDE, dtype=jnp.int32)
    moved = jnp.where(first_core, (masks & 1) * 2, masks * 4)
    slots = ((own_slot ^ moved)[:, None] + local[None, :]).reshape(-1)
    wanted = slots[:, None, None] * CAP + jnp.zeros((1, near_count // tok_count, 1), jnp.int32) + jnp.arange(CAP, dtype=jnp.int32)
    wanted = wanted.astype(jnp.float32).reshape(1, lines)
    granule = near_count // tok_count * CAP
    rows_of = lambda columns: jax.ShapeDtypeStruct((SIDE, per_device, granule, columns), jnp.bfloat16)
    rows_count, hidden_count = SIDE * SIDE * granule, w_gate.shape[2]

    def pack(part, chooser, planes):
        first = part == 0
        out_shape = [rows_of(widths[part])] * SIDE
        if first:
            out_shape.append(jax.ShapeDtypeStruct((SIDE, near_count, lines), jnp.bfloat16))
        return pl.pallas_call(
            functools.partial(pack_kernel, top=top, tok_count=tok_count, step=step, first=first),
            out_shape=out_shape,
            in_specs=whole(1 + SIDE),
            out_specs=whole(len(out_shape)),
            compiler_params=params(),
            cost_estimate=cost(2 * SIDE * lines * near_count * widths[part], 1e6),
        )(chooser, *planes)

    def project(source, part, pieces, total):
        weigh, finish = source == "own" and part == 0, source != "own" and part == PARTS - 1
        if finish:
            out_shape = [jax.ShapeDtypeStruct((per_device, rows_count, hidden_count), jnp.bfloat16)]
        else:
            out_shape = [jax.ShapeDtypeStruct((per_device, rows_count, 2 * hidden_count), jnp.float32)]
        if weigh:
            out_shape.append(jax.ShapeDtypeStruct((per_device, rows_count, 1), jnp.float32))
        operands = [*pieces, gate_up] + ([] if total is None else [total])
        return pl.pallas_call(
            functools.partial(
                gate_kernel, source=source, part=part, weigh=weigh, has_total=total is not None, finish=finish
            ),
            out_shape=out_shape,
            in_specs=scalar + whole(len(operands)),
            out_specs=whole(len(out_shape)),
            scratch_shapes=[pltpu.VMEM((rows_count, step), jnp.bfloat16)],
            compiler_params=params(),
            cost_estimate=cost(4 * per_device * rows_count * step * hidden_count, 4e6),
        )(base, *operands)

    total = choice = None
    for part in range(PARTS):
        planes = exchange([nears[part]] * SIDE, "yx")
        if part == 0:
            *packed, choice = pack(part, wanted, planes)
        else:
            packed = pack(part, choice, planes)
        if part == 0:
            gate_w, up_w, _ = lax.optimization_barrier((w_gate, w_up, packed[0]))
            gate_up = pl.pallas_call(
                fetch_kernel,
                out_shape=jax.ShapeDtypeStruct((*w_gate.shape[:2], 2 * w_gate.shape[2]), w_gate.dtype),
                in_specs=[pl.BlockSpec(memory_space=pltpu.HBM)] * 2,
                out_specs=pl.BlockSpec(memory_space=pltpu.VMEM),
                scratch_shapes=[pltpu.SemaphoreType.DMA((2,))],
                compiler_params=params(),
                cost_estimate=cost(0, 12e6),
            )(gate_w, up_w)
        own = exchange(packed, "xy")
        own[1], gate_up = lax.optimization_barrier((own[1], gate_up))
        found = project("own", part, own, total)
        if part == 0:
            total, weight = found
        else:
            [total] = found
        [total] = project("sibling", part, [sibling(piece) for piece in own], total)
    hidden = total

    back_step = half // BACK

    def down(hidden, part, turned, added):
        return pl.pallas_call(
            functools.partial(down_kernel, part=part, turned=turned),
            out_shape=[rows_of(back_step)] * SIDE,
            in_specs=scalar + whole(3 + len(added)),
            out_specs=whole(SIDE),
            compiler_params=params(),
            cost_estimate=cost(2 * per_device * rows_count * back_step * hidden_count, 5e6),
        )(base, hidden, weight, w_down, *added)

    sums = []
    for part in range(BACK):
        added = [sibling(piece) for piece in down(hidden, part, True, [])]
        mine = down(hidden, part, False, added)
        hidden, _ = lax.optimization_barrier((hidden, mine[0]))
        values = exchange(mine, "xy")
        kinds = [jnp.float32] + [jnp.bfloat16] * (SIDE - 1)
        dense = pl.pallas_call(
            unpack_kernel,
            out_shape=[jax.ShapeDtypeStruct((near_count, back_step), kind) for kind in kinds],
            in_specs=whole(1 + SIDE),
            out_specs=whole(SIDE),
            compiler_params=params(),
        )(choice, *values)
        sums.append(sum(piece.astype(jnp.float32) for piece in exchange(dense, "yx")))
    total = jnp.concatenate(sums, axis=1).reshape(SIDE, -1, half)
    sent = [total[0]] + [total[j].astype(jnp.bfloat16) for j in (1, 2, 3)]
    sent = exchange_z(sent, first_core)
    total = sum(piece.astype(jnp.float32) for piece in sent).astype(jnp.bfloat16).reshape(2, tok_count, half)
    kept = jnp.where(first_core, total[0], total[1])
    got = sibling(jnp.where(first_core, total[1], total[0]))
    return jnp.concatenate([jnp.where(first_core, kept, got), jnp.where(first_core, got, kept)], axis=1)


def solution(mesh):
    in_specs = (
        P(AXES, None),
        P(AXES, None),
        P(AXES, None),
        P(),
        P("expert", None, "dp"),
        P("expert", None, "dp"),
        P("expert", "dp", None),
    )
    return jax.shard_map(shards, mesh=mesh, in_specs=in_specs, out_specs=P(AXES, None), check_vma=False)
```

time: 290 us -> 151 us (0.52)
  waiting for transfers between devices: 157 us -> 80.2 us
  blocking collectives: 38.6 us -> 0 us
  starting transfers between devices: 8.67 us -> 39 us
  local copies, waits for them, and re-layouts: 34.1 us -> 8.73 us
  matrix products: 24.6 us -> 0 us
  Pallas kernels: 0 us -> 20 us
  between operations: 13.5 us -> 0.3 us
  other arithmetic: 11.5 us -> 1.52 us
    all_to_all x1 -> x0, waiting for transfers between devices: 97.9 us -> none  [shards(): lax.all_to_all(sending, ('expert', 'dp'), split_axis=0, concat_axis=0, ti...]
    ppermute x0 -> x38, waiting for transfers between devices: none -> 80.2 us  [the longest x6 37.8 us: exchange(): over = lax.ppermute(value[2], AXES, partners(axes, 2))]
    all_gather x1 -> x0, waiting for transfers between devices: 59.6 us -> none  [shards(): rows_in = lax.all_gather(arrived[:, None], 'dp', axis=1, tiled=True)]
    ppermute x0 -> x38, starting transfers between devices: none -> 39 us  [the longest x12 14.3 us: exchange(): lax.ppermute(value[j], AXES, partners(axes, j))]
    all_to_all x1 -> x0, blocking collectives: 38.6 us -> none  [shards(): lax.all_to_all(outgoing, 'expert', split_axis=0, concat_axis=0, tiled=True)]
    dot_general x3 -> x0, matrix products: 24.6 us -> none  [the longest x1 15.1 us: shards(): jnp.einsum('sqlcf,lfd->sqlcd', hidden, w_down, preferred_element_type=jnp...]
    pallas_call x0 -> x11, Pallas kernels: none -> 20 us  [the longest x2 8.04 us: project(): pl.pallas_call(functools.partial(gate_kernel, source=source, part=part, w...]
    convert_element_type x1, local copies, waits for them, and re-layouts: 12.2 us -> 0.11 us  [shards(): wanted = wanted.astype(jnp.float32).reshape(1, lines)]
  transfers between devices with their start and end apart: 2 -> 38, of which waited for: 2 -> 26; matrix products, arithmetic and copies ran while one was open for 0% -> 0% of each run, Pallas kernels for 0% -> 5%
where the time goes in v3:
time: 151 us; the launch traced here: 150 us
  waiting for transfers between devices  80.2 us (53%)
  starting transfers between devices  39 us (26%)
  Pallas kernels  20 us (13%)
  local copies, waits for them, and re-layouts  8.73 us (6%)
  other arithmetic  1.52 us (1%)
    ppermute x6, waiting for transfers between devices, exchange(): over = lax.ppermute(value[2], AXES, partners(axes, 2))  37.8 us
    ppermute x12, waiting for transfers between devices, exchange(): lax.ppermute(value[j], AXES, partners(axes, j))  24.7 us
    ppermute x12, starting transfers between devices, exchange(): lax.ppermute(value[j], AXES, partners(axes, j))  14.3 us
    ppermute x6, starting transfers between devices, exchange(): over = lax.ppermute(value[2], AXES, partners(axes, 2))  12.4 us
    unnamed x17, local copies, waits for them, and re-layouts  8.53 us
    pallas_call x2, Pallas kernels, project(): pl.pallas_call(functools.partial(gate_kernel, source=source, part=part, w...  8.04 us
    ppermute x2, waiting for transfers between devices, exchange_z(): lax.ppermute(jnp.where(first_core, value[3], value[1]), AXES, partners('z...  7.35 us
    pallas_call x4, Pallas kernels, down(): pl.pallas_call(functools.partial(down_kernel, part=part, turned=turned),...  7.22 us
  transfers between devices with their start and end apart: 38, of which 26 were waited for; matrix products, arithmetic and copies ran while one was open for 0% of the time, Pallas kernels for 5%

profile of v3, /device:TPU:0, one launch (start us, length us, event | category | flops | bytes accessed | tf_op | source)
XLA Modules:
  0.0 149.8 jit_solution(7792522152245820404)
XLA Ops:
  3.0 0.9 shard_map.73
  4.1 1.2 collective-permute-done
  5.4 2.1 %collective-permute-start.1 = (bf16[32,2176]{1,0:T(8,128)(2,1)S(1)}, bf16[32,2176]{1,0:T(8,128)(2,1)S(1)}, u32[]{:S(2)}, u32[]{:S(2)}) collective-permute-start(bf16[32,2176]{1,0:T(8,128)(2,1)S(1)} %pad_maximum_fusion.1), channel_id=1, source_target_pairs={{0,32},{1,97},{4,36},{5,101},{2,34},{3,99},{6,38},{7,103},{8,40},{... | collective-permute-start | bytes 417800 | tf_op jit(solution)/shard_map/ppermute | solution.py:43
  7.5 2.5 %collective-permute-start.2 = (bf16[32,2176]{1,0:T(8,128)(2,1)S(1)}, bf16[32,2176]{1,0:T(8,128)(2,1)S(1)}, u32[]{:S(2)}, u32[]{:S(2)}) collective-permute-start(bf16[32,2176]{1,0:T(8,128)(2,1)S(1)} %pad_maximum_fusion.1), channel_id=1, source_target_pairs={{0,96},{1,33},{4,100},{5,37},{2,98},{3,35},{6,102},{7,39},{8,104},... | collective-permute-start | bytes 417800 | tf_op jit(solution)/shard_map/ppermute | solution.py:44
  10.0 1.1 collective-permute-start.3
  11.1 4.8 %collective-permute-done.2 = bf16[32,2176]{1,0:T(8,128)(2,1)S(1)} collective-permute-done((bf16[32,2176]{1,0:T(8,128)(2,1)S(1)}, bf16[32,2176]{1,0:T(8,128)(2,1)S(1)}, u32[]{:S(2)}, u32[]{:S(2)}) %collective-permute-start.2) | collective-permute-done | bytes 139296 | tf_op jit(solution)/shard_map/ppermute | solution.py:44
  15.9 1.9 %collective-permute-done.3 = bf16[32,2176]{1,0:T(8,128)(2,1)S(1)} collective-permute-done((bf16[32,2176]{1,0:T(8,128)(2,1)S(1)}, bf16[32,2176]{1,0:T(8,128)(2,1)S(1)}, u32[]{:S(2)}, u32[]{:S(2)}) %collective-permute-start.3) | collective-permute-done | bytes 139296 | tf_op jit(solution)/shard_map/ppermute | solution.py:42
  17.9 1.7 %collective-permute-start.4 = (bf16[128,2176]{1,0:T(8,128)(2,1)S(1)}, bf16[128,2176]{1,0:T(8,128)(2,1)S(1)}, u32[]{:S(2)}, u32[]{:S(2)}) collective-permute-start(bf16[128,2176]{1,0:T(8,128)(2,1)S(1)} %select_dynamic-update-slice_fusion.refs_1_), channel_id=1, source_target_pairs={{0,8},{1,5},{4,12},{5,1},{2,10},{3,7},{6,14},{7,3},{8,0},{9,13},{1... | collective-permute-start | bytes 1671176 | tf_op jit(solution)/shard_map/ppermute | solution.py:37
  19.6 2.9 %collective-permute-start.5 = (bf16[128,2176]{1,0:T(8,128)(2,1)S(1)}, bf16[128,2176]{1,0:T(8,128)(2,1)S(1)}, u32[]{:S(2)}, u32[]{:S(2)}) collective-permute-start(bf16[128,2176]{1,0:T(8,128)(2,1)S(1)} %select_dynamic-update-slice_fusion.refs_1_), channel_id=1, source_target_pairs={{0,16},{1,3},{4,20},{5,7},{2,18},{3,1},{6,22},{7,5},{8,24},{9,11},... | collective-permute-start | bytes 1671176 | tf_op jit(solution)/shard_map/ppermute | solution.py:36
  23.0 4.5 %collective-permute-done.4.refs_2_ = bf16[128,2176]{1,0:T(8,128)(2,1)S(1)} collective-permute-done((bf16[128,2176]{1,0:T(8,128)(2,1)S(1)}, bf16[128,2176]{1,0:T(8,128)(2,1)S(1)}, u32[]{:S(2)}, u32[]{:S(2)}) %collective-permute-start.4) | collective-permute-done | bytes 557088 | tf_op jit(solution)/shard_map/ppermute | solution.py:37
  27.5 8.5 %collective-permute-done.5.refs_3_ = bf16[128,2176]{1,0:T(8,128)(2,1)S(1)} collective-permute-done((bf16[128,2176]{1,0:T(8,128)(2,1)S(1)}, bf16[128,2176]{1,0:T(8,128)(2,1)S(1)}, u32[]{:S(2)}, u32[]{:S(2)}) %collective-permute-start.5) | collective-permute-done | bytes 557088 | tf_op jit(solution)/shard_map/ppermute | solution.py:36
  36.0 3.1 %collective-permute-done.6.refs_4_ = bf16[128,2176]{1,0:T(8,128)(2,1)S(1)} collective-permute-done((bf16[128,2176]{1,0:T(8,128)(2,1)S(1)}, bf16[128,2176]{1,0:T(8,128)(2,1)S(1)}, u32[]{:S(2)}, u32[]{:S(2)}) %collective-permute-start.6) | collective-permute-done | bytes 557088 | tf_op jit(solution)/shard_map/ppermute | solution.py:37
  39.2 1.6 %shard_map.74 = (bf16[4,2,32,2176]{3,2,1,0:T(8,128)(2,1)S(1)}, bf16[4,2,32,2176]{3,2,1,0:T(8,128)(2,1)S(1)}, bf16[4,2,32,2176]{3,2,1,0:T(8,128)(2,1)S(1)}, bf16[...) custom-call(f32[1,256]{1,0:T(1,128)S(1)} %convert_element_type.47.refs_0_, ...), custom_call_target="tpu_custom_call" | custom-call | flops 570425344 | bytes 1000000 | tf_op jit(solution)/shard_map/pallas_call | solution.py:257
  40.8 1.6 %collective-permute-start.8 = (bf16[4,2,32,2176]{3,2,1,0:T(8,128)(2,1)S(1)}, bf16[4,2,32,2176]{3,2,1,0:T(8,128)(2,1)S(1)}, u32[]{:S(2)}, u32[]{:S(2)}) collective-permute-start(bf16[4,2,32,2176]{3,2,1,0:T(8,128)(2,1)S(1)} %get-tuple-element.47), channel_id=1, source_target_pairs={{0,4},{1,9},{4,0},{5,13},{2,6},{3,11},{6,2},{7,15},{8,12},{9,1},{1... | collective-permute-start | bytes 3342344 | tf_op jit(solution)/shard_map/ppermute | solution.py:37
  42.4 2.7 %collective-permute-start.10 = (bf16[4,2,32,2176]{3,2,1,0:T(8,128)(2,1)S(1)}, bf16[4,2,32,2176]{3,2,1,0:T(8,128)(2,1)S(1)}, u32[]{:S(2)}, u32[]{:S(2)}) collective-permute-start(bf16[4,2,32,2176]{3,2,1,0:T(8,128)(2,1)S(1)} %get-tuple-element.51), channel_id=1, source_target_pairs={{0,2},{1,17},{4,6},{5,21},{2,0},{3,19},{6,4},{7,23},{8,10},{9,25},... | collective-permute-start | bytes 3342344 | tf_op jit(solution)/shard_map/ppermute | solution.py:36
  45.6 2.8 %copy-done = bf16[2,4096,384]{2,1,0:T(8,128)(2,1)S(1)} copy-done((bf16[2,4096,384]{2,1,0:T(8,128)(2,1)S(1)}, bf16[2,4096,384]{2,1,0:T(8,128)(2,1)}, u32[]{:S(2)}) %copy-start) | copy-done | bytes 6291480
  48.4 2.8 %copy-done.1 = bf16[2,4096,384]{2,1,0:T(8,128)(2,1)S(1)} copy-done((bf16[2,4096,384]{2,1,0:T(8,128)(2,1)S(1)}, bf16[2,4096,384]{2,1,0:T(8,128)(2,1)}, u32[]{:S(2)}) %copy-start.1) | copy-done | bytes 6291480
  51.2 1.3 shard_map.75.refs_4_
  52.5 3.9 %collective-permute-done.8.refs_1_ = bf16[4,2,32,2176]{3,2,1,0:T(8,128)(2,1)S(1)} collective-permute-done((bf16[4,2,32,2176]{3,2,1,0:T(8,128)(2,1)S(1)}, bf16[4,2,32,2176]{3,2,1,0:T(8,128)(2,1)S(1)}, u32[]{:S(2)}, u32[]{:S(2)}) %collective-permute-start.8) | collective-permute-done | bytes 1114144 | tf_op jit(solution)/shard_map/ppermute | solution.py:37
  56.4 14.2 %collective-permute-done.10.refs_2_ = bf16[4,2,32,2176]{3,2,1,0:T(8,128)(2,1)S(1)} collective-permute-done((bf16[4,2,32,2176]{3,2,1,0:T(8,128)(2,1)S(1)}, bf16[4,2,32,2176]{3,2,1,0:T(8,128)(2,1)S(1)}, u32[]{:S(2)}, u32[]{:S(2)}) %collective-permute-start.10) | collective-permute-done | bytes 1114144 | tf_op jit(solution)/shard_map/ppermute | solution.py:36
  70.6 3.1 %collective-permute-done.12.refs_3_ = bf16[4,2,32,2176]{3,2,1,0:T(8,128)(2,1)S(1)} collective-permute-done((bf16[4,2,32,2176]{3,2,1,0:T(8,128)(2,1)S(1)}, bf16[4,2,32,2176]{3,2,1,0:T(8,128)(2,1)S(1)}, u32[]{:S(2)}, u32[]{:S(2)}) %collective-permute-start.12) | collective-permute-done | bytes 1114144 | tf_op jit(solution)/shard_map/ppermute | solution.py:37
  73.8 4.0 %shard_map.76 = (f32[2,512,768]{2,1,0:T(8,128)S(1)}, f32[2,512,1]{2,1,0:T(8,128)S(1)}) custom-call(s32[3]{0:T(128)S(1)} %pad_add_fusion.core_ref.base_ref, bf16[4,2,32,2176]{3,2,1,0:T(8,128)(2,1)S(1)} %get-tuple-element.46.refs_0_, bf16[4,2,32,2176]{3,2,1,0:T(8,128)(2,1)S(1)} %collective-permute-done.8.refs_1_, ...), custom_call_target="tpu_custom_call" | custom-call | flops 3221225472 | bytes 4000000 | tf_op jit(solution)/shard_map/pallas_call | solution.py:275
  77.8 4.0 %shard_map.77.hidden_ref = bf16[2,512,384]{2,1,0:T(8,128)(2,1)S(1)} custom-call(s32[3]{0:T(128)S(1)} %pad_add_fusion.core_ref.base_ref, bf16[4,2,32,2176]{3,2,1,0:T(8,128)(2,1)S(1)} %collective-permute-done.7.refs_0_, bf16[4,2,32,2176]{3,2,1,0:T(8,128)(2,1)S(1)} %collective-permute-done.9.refs_1_, ...), custom_call_target="tpu_custom_call" | custom-call | flops 3221225472 | bytes 4000000 | tf_op jit(solution)/shard_map/pallas_call | solution.py:275
  81.9 1.8 %shard_map.78 = (bf16[4,2,32,1024]{3,2,1,0:T(8,128)(2,1)S(1)}, bf16[4,2,32,1024]{3,2,1,0:T(8,128)(2,1)S(1)}, bf16[4,2,32,1024]{3,2,1,0:T(8,128)(2,1)S(1)}, bf16[4,2,32,1024]{3,2,1,0:T(8,128)(2,1)S(1)}) custom-call(s32[3]{0:T(128)S(1)} %pad_add_fusion.core_ref.base_ref, bf16[2,512,384]{2,1,0:T(8,128)(2,1)S(1)} %shard_map.77.hidden_ref, ...), custom_call_target="tpu_custom_call" | custom-call | flops 805306368 | bytes 5000000 | tf_op jit(solution)/shard_map/pallas_call | solution.py:318
  84.9 0.9 collective-permute-done.14.refs_0_
  88.1 1.8 %shard_map.79 = (bf16[4,2,32,1024]{3,2,1,0:T(8,128)(2,1)S(1)}, bf16[4,2,32,1024]{3,2,1,0:T(8,128)(2,1)S(1)}, bf16[4,2,32,1024]{3,2,1,0:T(8,128)(2,1)S(1)}, bf16[4,2,32,1024]{3,2,1,0:T(8,128)(2,1)S(1)}) custom-call(s32[3]{0:T(128)S(1)} %pad_add_fusion.core_ref.base_ref, bf16[2,512,384]{2,1,0:T(8,128)(2,1)S(1)} %shard_map.77.hidden_ref, ...), custom_call_target="tpu_custom_call" | custom-call | flops 805306368 | bytes 5000000 | tf_op jit(solution)/shard_map/pallas_call | solution.py:318
  89.9 1.8 %shard_map.81 = (bf16[4,2,32,1024]{3,2,1,0:T(8,128)(2,1)S(1)}, bf16[4,2,32,1024]{3,2,1,0:T(8,128)(2,1)S(1)}, bf16[4,2,32,1024]{3,2,1,0:T(8,128)(2,1)S(1)}, bf16[4,2,32,1024]{3,2,1,0:T(8,128)(2,1)S(1)}) custom-call(s32[3]{0:T(128)S(1)} %pad_add_fusion.core_ref.base_ref, bf16[2,512,384]{2,1,0:T(8,128)(2,1)S(1)} %shard_map.77.hidden_ref, ...), custom_call_target="tpu_custom_call" | custom-call | flops 805306368 | bytes 5000000 | tf_op jit(solution)/shard_map/pallas_call | solution.py:318
  93.7 1.1 collective-permute-start.19
  94.8 2.8 %collective-permute-start.20 = (bf16[4,2,32,1024]{3,2,1,0:T(8,128)(2,1)S(1)}, bf16[4,2,32,1024]{3,2,1,0:T(8,128)(2,1)S(1)}, u32[]{:S(2)}, u32[]{:S(2)}) collective-permute-start(bf16[4,2,32,1024]{3,2,1,0:T(8,128)(2,1)S(1)} %get-tuple-element.63), channel_id=1, source_target_pairs={{0,6},{1,25},{4,2},{5,29},{2,4},{3,27},{6,0},{7,31},{8,14},{9,17},... | collective-permute-start | bytes 1572872 | tf_op jit(solution)/shard_map/ppermute | solution.py:37
  97.5 1.8 %shard_map.82 = (bf16[4,2,32,1024]{3,2,1,0:T(8,128)(2,1)S(1)}, bf16[4,2,32,1024]{3,2,1,0:T(8,128)(2,1)S(1)}, bf16[4,2,32,1024]{3,2,1,0:T(8,128)(2,1)S(1)}, bf16[4,2,32,1024]{3,2,1,0:T(8,128)(2,1)S(1)}) custom-call(s32[3]{0:T(128)S(1)} %pad_add_fusion.core_ref.base_ref, bf16[2,512,384]{2,1,0:T(8,128)(2,1)S(1)} %shard_map.77.hidden_ref, ...), custom_call_target="tpu_custom_call" | custom-call | flops 805306368 | bytes 5000000 | tf_op jit(solution)/shard_map/pallas_call | solution.py:318
  99.4 1.9 %collective-permute-start.29 = (bf16[4,2,32,1024]{3,2,1,0:T(8,128)(2,1)S(1)}, bf16[4,2,32,1024]{3,2,1,0:T(8,128)(2,1)S(1)}, u32[]{:S(2)}, u32[]{:S(2)}) collective-permute-start(bf16[4,2,32,1024]{3,2,1,0:T(8,128)(2,1)S(1)} %get-tuple-element.75), channel_id=1, source_target_pairs={{0,2},{1,17},{4,6},{5,21},{2,0},{3,19},{6,4},{7,23},{8,10},{9,25},... | collective-permute-start | bytes 1572872 | tf_op jit(solution)/shard_map/ppermute | solution.py:36
  102.0 2.1 %collective-permute-start.30 = (bf16[4,2,32,1024]{3,2,1,0:T(8,128)(2,1)S(1)}, bf16[4,2,32,1024]{3,2,1,0:T(8,128)(2,1)S(1)}, u32[]{:S(2)}, u32[]{:S(2)}) collective-permute-start(bf16[4,2,32,1024]{3,2,1,0:T(8,128)(2,1)S(1)} %get-tuple-element.76), channel_id=1, source_target_pairs={{0,6},{1,25},{4,2},{5,29},{2,4},{3,27},{6,0},{7,31},{8,14},{9,17},... | collective-permute-start | bytes 1572872 | tf_op jit(solution)/shard_map/ppermute | solution.py:37
  104.1 3.5 %collective-permute-done.19.refs_2_ = bf16[4,2,32,1024]{3,2,1,0:T(8,128)(2,1)S(1)} collective-permute-done((bf16[4,2,32,1024]{3,2,1,0:T(8,128)(2,1)S(1)}, bf16[4,2,32,1024]{3,2,1,0:T(8,128)(2,1)S(1)}, u32[]{:S(2)}, u32[]{:S(2)}) %collective-permute-start.19) | collective-permute-done | bytes 524320 | tf_op jit(solution)/shard_map/ppermute | solution.py:36
  107.6 3.1 %collective-permute-done.20.refs_3_ = bf16[4,2,32,1024]{3,2,1,0:T(8,128)(2,1)S(1)} collective-permute-done((bf16[4,2,32,1024]{3,2,1,0:T(8,128)(2,1)S(1)}, bf16[4,2,32,1024]{3,2,1,0:T(8,128)(2,1)S(1)}, u32[]{:S(2)}, u32[]{:S(2)}) %collective-permute-start.20) | collective-permute-done | bytes 524320 | tf_op jit(solution)/shard_map/ppermute | solution.py:37
  111.3 1.7 %collective-permute-start.22 = (bf16[128,1024]{1,0:T(8,128)(2,1)S(1)}, bf16[128,1024]{1,0:T(8,128)(2,1)S(1)}, u32[]{:S(2)}, u32[]{:S(2)}) collective-permute-start(bf16[128,1024]{1,0:T(8,128)(2,1)S(1)} %get-tuple-element.66), channel_id=1, source_target_pairs={{0,16},{1,3},{4,20},{5,7},{2,18},{3,1},{6,22},{7,5},{8,24},{9,11},... | collective-permute-start | bytes 786440 | tf_op jit(solution)/shard_map/ppermute | solution.py:36
  113.4 2.7 %collective-permute-start.23 = (bf16[128,1024]{1,0:T(8,128)(2,1)S(1)}, bf16[128,1024]{1,0:T(8,128)(2,1)S(1)}, u32[]{:S(2)}, u32[]{:S(2)}) collective-permute-start(bf16[128,1024]{1,0:T(8,128)(2,1)S(1)} %get-tuple-element.67), channel_id=1, source_target_pairs={{0,24},{1,7},{4,28},{5,3},{2,26},{3,5},{6,30},{7,1},{8,16},{9,15},... | collective-permute-start | bytes 786440 | tf_op jit(solution)/shard_map/ppermute | solution.py:37
  116.0 8.5 %collective-permute-done.29.refs_2_ = bf16[4,2,32,1024]{3,2,1,0:T(8,128)(2,1)S(1)} collective-permute-done((bf16[4,2,32,1024]{3,2,1,0:T(8,128)(2,1)S(1)}, bf16[4,2,32,1024]{3,2,1,0:T(8,128)(2,1)S(1)}, u32[]{:S(2)}, u32[]{:S(2)}) %collective-permute-start.29) | collective-permute-done | bytes 524320 | tf_op jit(solution)/shard_map/ppermute | solution.py:36
  124.5 1.7 %collective-permute-done.30.refs_3_ = bf16[4,2,32,1024]{3,2,1,0:T(8,128)(2,1)S(1)} collective-permute-done((bf16[4,2,32,1024]{3,2,1,0:T(8,128)(2,1)S(1)}, bf16[4,2,32,1024]{3,2,1,0:T(8,128)(2,1)S(1)}, u32[]{:S(2)}, u32[]{:S(2)}) %collective-permute-start.30) | collective-permute-done | bytes 524320 | tf_op jit(solution)/shard_map/ppermute | solution.py:37
  126.7 2.1 %collective-permute-start.32 = (bf16[128,1024]{1,0:T(8,128)(2,1)S(1)}, bf16[128,1024]{1,0:T(8,128)(2,1)S(1)}, u32[]{:S(2)}, u32[]{:S(2)}) collective-permute-start(bf16[128,1024]{1,0:T(8,128)(2,1)S(1)} %get-tuple-element.79), channel_id=1, source_target_pairs={{0,16},{1,3},{4,20},{5,7},{2,18},{3,1},{6,22},{7,5},{8,24},{9,11},... | collective-permute-start | bytes 786440 | tf_op jit(solution)/shard_map/ppermute | solution.py:36
  128.8 2.6 %collective-permute-start.33 = (bf16[128,1024]{1,0:T(8,128)(2,1)S(1)}, bf16[128,1024]{1,0:T(8,128)(2,1)S(1)}, u32[]{:S(2)}, u32[]{:S(2)}) collective-permute-start(bf16[128,1024]{1,0:T(8,128)(2,1)S(1)} %get-tuple-element.80), channel_id=1, source_target_pairs={{0,24},{1,7},{4,28},{5,3},{2,26},{3,5},{6,30},{7,1},{8,16},{9,15},... | collective-permute-start | bytes 786440 | tf_op jit(solution)/shard_map/ppermute | solution.py:37
  131.6 1.5 %collective-permute-done.31 = bf16[128,1024]{1,0:T(8,128)(2,1)S(1)} collective-permute-done((bf16[128,1024]{1,0:T(8,128)(2,1)S(1)}, bf16[128,1024]{1,0:T(8,128)(2,1)S(1)}, u32[]{:S(2)}, u32[]{:S(2)}) %collective-permute-start.31) | collective-permute-done | bytes 262176 | tf_op jit(solution)/shard_map/ppermute | solution.py:37
  133.1 3.0 %collective-permute-done.32 = bf16[128,1024]{1,0:T(8,128)(2,1)S(1)} collective-permute-done((bf16[128,1024]{1,0:T(8,128)(2,1)S(1)}, bf16[128,1024]{1,0:T(8,128)(2,1)S(1)}, u32[]{:S(2)}, u32[]{:S(2)}) %collective-permute-start.32) | collective-permute-done | bytes 262176 | tf_op jit(solution)/shard_map/ppermute | solution.py:36
  136.1 2.7 %collective-permute-done.33 = bf16[128,1024]{1,0:T(8,128)(2,1)S(1)} collective-permute-done((bf16[128,1024]{1,0:T(8,128)(2,1)S(1)}, bf16[128,1024]{1,0:T(8,128)(2,1)S(1)}, u32[]{:S(2)}, u32[]{:S(2)}) %collective-permute-start.33) | collective-permute-done | bytes 262176 | tf_op jit(solution)/shard_map/ppermute | solution.py:37
  139.6 1.4 collective-permute-start.35
  141.0 2.2 %collective-permute-start.36 = (bf16[32,2048]{1,0:T(8,128)(2,1)S(1)}, bf16[32,2048]{1,0:T(8,128)(2,1)S(1)}, u32[]{:S(2)}, u32[]{:S(2)}) collective-permute-start(bf16[32,2048]{1,0:T(8,128)(2,1)S(1)} %get-tuple-element.86), channel_id=1, source_target_pairs={{0,64},{1,65},{4,68},{5,69},{2,66},{3,67},{6,70},{7,71},{8,72},{9,... | collective-permute-start | bytes 393224 | tf_op jit(solution)/shard_map/ppermute | solution.py:42
  143.2 1.9 %collective-permute-done.34 = bf16[32,2048]{1,0:T(8,128)(2,1)S(1)} collective-permute-done((bf16[32,2048]{1,0:T(8,128)(2,1)S(1)}, bf16[32,2048]{1,0:T(8,128)(2,1)S(1)}, u32[]{:S(2)}, u32[]{:S(2)}) %collective-permute-start.34) | collective-permute-done | bytes 131104 | tf_op jit(solution)/shard_map/ppermute | solution.py:43
  145.1 2.5 %collective-permute-done.35 = bf16[32,2048]{1,0:T(8,128)(2,1)S(1)} collective-permute-done((bf16[32,2048]{1,0:T(8,128)(2,1)S(1)}, bf16[32,2048]{1,0:T(8,128)(2,1)S(1)}, u32[]{:S(2)}, u32[]{:S(2)}) %collective-permute-start.35) | collective-permute-done | bytes 131104 | tf_op jit(solution)/shard_map/ppermute | solution.py:44
  147.9 1.2 collective-permute-done.37
  (76 shorter events, 13.7 us)
Async XLA Ops:
  0.1 0.9 copy-start.2
  1.0 0.7 copy-start.3
  1.7 0.7 copy-start.4
  2.4 0.7 copy-start.5
  4.0 1.3 collective-permute-start
  5.4 5.7 %collective-permute-start.1 = (bf16[32,2176]{1,0:T(8,128)(2,1)S(1)}, bf16[32,2176]{1,0:T(8,128)(2,1)S(1)}, u32[]{:S(2)}, u32[]{:S(2)}) collective-permute-start(bf16[32,2176]{1,0:T(8,128)(2,1)S(1)} %pad_maximum_fusion.1), channel_id=1, source_target_pairs={{0,32},{1,97},{4,36},{5,101},{2,34},{3,99},{6,38},{7,103},{8,40},{... | collective-permute-start | bytes 417800 | tf_op jit(solution)/shard_map/ppermute | solution.py:43
  7.5 8.4 %collective-permute-start.2 = (bf16[32,2176]{1,0:T(8,128)(2,1)S(1)}, bf16[32,2176]{1,0:T(8,128)(2,1)S(1)}, u32[]{:S(2)}, u32[]{:S(2)}) collective-permute-start(bf16[32,2176]{1,0:T(8,128)(2,1)S(1)} %pad_maximum_fusion.1), channel_id=1, source_target_pairs={{0,96},{1,33},{4,100},{5,37},{2,98},{3,35},{6,102},{7,39},{8,104},... | collective-permute-start | bytes 417800 | tf_op jit(solution)/shard_map/ppermute | solution.py:44
  10.0 7.8 %collective-permute-start.3 = (bf16[32,2176]{1,0:T(8,128)(2,1)S(1)}, bf16[32,2176]{1,0:T(8,128)(2,1)S(1)}, u32[]{:S(2)}, u32[]{:S(2)}) collective-permute-start(bf16[32,2176]{1,0:T(8,128)(2,1)S(1)} %pad_maximum_fusion.1), channel_id=1, source_target_pairs={{0,64},{1,65},{4,68},{5,69},{2,66},{3,67},{6,70},{7,71},{8,72},{9,... | collective-permute-start | bytes 417800 | tf_op jit(solution)/shard_map/ppermute | solution.py:42
  17.9 9.6 %collective-permute-start.4 = (bf16[128,2176]{1,0:T(8,128)(2,1)S(1)}, bf16[128,2176]{1,0:T(8,128)(2,1)S(1)}, u32[]{:S(2)}, u32[]{:S(2)}) collective-permute-start(bf16[128,2176]{1,0:T(8,128)(2,1)S(1)} %select_dynamic-update-slice_fusion.refs_1_), channel_id=1, source_target_pairs={{0,8},{1,5},{4,12},{5,1},{2,10},{3,7},{6,14},{7,3},{8,0},{9,13},{1... | collective-permute-start | bytes 1671176 | tf_op jit(solution)/shard_map/ppermute | solution.py:37
  19.6 16.5 %collective-permute-start.5 = (bf16[128,2176]{1,0:T(8,128)(2,1)S(1)}, bf16[128,2176]{1,0:T(8,128)(2,1)S(1)}, u32[]{:S(2)}, u32[]{:S(2)}) collective-permute-start(bf16[128,2176]{1,0:T(8,128)(2,1)S(1)} %select_dynamic-update-slice_fusion.refs_1_), channel_id=1, source_target_pairs={{0,16},{1,3},{4,20},{5,7},{2,18},{3,1},{6,22},{7,5},{8,24},{9,11},... | collective-permute-start | bytes 1671176 | tf_op jit(solution)/shard_map/ppermute | solution.py:36
  22.5 16.7 %collective-permute-start.6 = (bf16[128,2176]{1,0:T(8,128)(2,1)S(1)}, bf16[128,2176]{1,0:T(8,128)(2,1)S(1)}, u32[]{:S(2)}, u32[]{:S(2)}) collective-permute-start(bf16[128,2176]{1,0:T(8,128)(2,1)S(1)} %select_dynamic-update-slice_fusion.refs_1_), channel_id=1, source_target_pairs={{0,24},{1,7},{4,28},{5,3},{2,26},{3,5},{6,30},{7,1},{8,16},{9,15},... | collective-permute-start | bytes 1671176 | tf_op jit(solution)/shard_map/ppermute | solution.py:37
  40.8 15.6 %collective-permute-start.8 = (bf16[4,2,32,2176]{3,2,1,0:T(8,128)(2,1)S(1)}, bf16[4,2,32,2176]{3,2,1,0:T(8,128)(2,1)S(1)}, u32[]{:S(2)}, u32[]{:S(2)}) collective-permute-start(bf16[4,2,32,2176]{3,2,1,0:T(8,128)(2,1)S(1)} %get-tuple-element.47), channel_id=1, source_target_pairs={{0,4},{1,9},{4,0},{5,13},{2,6},{3,11},{6,2},{7,15},{8,12},{9,1},{1... | collective-permute-start | bytes 3342344 | tf_op jit(solution)/shard_map/ppermute | solution.py:37
  42.4 28.2 %collective-permute-start.10 = (bf16[4,2,32,2176]{3,2,1,0:T(8,128)(2,1)S(1)}, bf16[4,2,32,2176]{3,2,1,0:T(8,128)(2,1)S(1)}, u32[]{:S(2)}, u32[]{:S(2)}) collective-permute-start(bf16[4,2,32,2176]{3,2,1,0:T(8,128)(2,1)S(1)} %get-tuple-element.51), channel_id=1, source_target_pairs={{0,2},{1,17},{4,6},{5,21},{2,0},{3,19},{6,4},{7,23},{8,10},{9,25},... | collective-permute-start | bytes 3342344 | tf_op jit(solution)/shard_map/ppermute | solution.py:36
  45.1 28.6 %collective-permute-start.12 = (bf16[4,2,32,2176]{3,2,1,0:T(8,128)(2,1)S(1)}, bf16[4,2,32,2176]{3,2,1,0:T(8,128)(2,1)S(1)}, u32[]{:S(2)}, u32[]{:S(2)}) collective-permute-start(bf16[4,2,32,2176]{3,2,1,0:T(8,128)(2,1)S(1)} %get-tuple-element.52), channel_id=1, source_target_pairs={{0,6},{1,25},{4,2},{5,29},{2,4},{3,27},{6,0},{7,31},{8,14},{9,17},... | collective-permute-start | bytes 3342344 | tf_op jit(solution)/shard_map/ppermute | solution.py:37
  45.6 32.2 %collective-permute-start.7 = (bf16[4,2,32,2176]{3,2,1,0:T(8,128)(2,1)S(1)}, bf16[4,2,32,2176]{3,2,1,0:T(8,128)(2,1)S(1)}, u32[]{:S(2)}, u32[]{:S(2)}) collective-permute-start(bf16[4,2,32,2176]{3,2,1,0:T(8,128)(2,1)S(1)} %get-tuple-element.46.refs_0_), channel_id=1, source_target_pairs={{0,1},{1,0},{2,3},{3,2},{4,5},{5,4},{6,7},{7,6},{8,9},{9,8},{10,11... | collective-permute-start | bytes 3342344 | tf_op jit(solution)/shard_map/ppermute | solution.py:50
  45.6 2.8 %copy-start = (bf16[2,4096,384]{2,1,0:T(8,128)(2,1)S(1)}, bf16[2,4096,384]{2,1,0:T(8,128)(2,1)}, u32[]{:S(2)}) copy-start(bf16[2,4096,384]{2,1,0:T(8,128)(2,1)} %gate_ref) | copy-start | bytes 18874372
  48.4 2.8 %copy-start.1 = (bf16[2,4096,384]{2,1,0:T(8,128)(2,1)S(1)}, bf16[2,4096,384]{2,1,0:T(8,128)(2,1)}, u32[]{:S(2)}) copy-start(bf16[2,4096,384]{2,1,0:T(8,128)(2,1)} %up_ref) | copy-start | bytes 18874372
  56.4 21.4 %collective-permute-start.9 = (bf16[4,2,32,2176]{3,2,1,0:T(8,128)(2,1)S(1)}, bf16[4,2,32,2176]{3,2,1,0:T(8,128)(2,1)S(1)}, u32[]{:S(2)}, u32[]{:S(2)}) collective-permute-start(bf16[4,2,32,2176]{3,2,1,0:T(8,128)(2,1)S(1)} %collective-permute-done.8.refs_1_), channel_id=1, source_target_pairs={{0,1},{1,0},{2,3},{3,2},{4,5},{5,4},{6,7},{7,6},{8,9},{9,8},{10,11... | collective-permute-start | bytes 3342344 | tf_op jit(solution)/shard_map/ppermute | solution.py:50
  70.6 7.2 %collective-permute-start.11 = (bf16[4,2,32,2176]{3,2,1,0:T(8,128)(2,1)S(1)}, bf16[4,2,32,2176]{3,2,1,0:T(8,128)(2,1)S(1)}, u32[]{:S(2)}, u32[]{:S(2)}) collective-permute-start(bf16[4,2,32,2176]{3,2,1,0:T(8,128)(2,1)S(1)} %collective-permute-done.10.refs_2_), channel_id=1, source_target_pairs={{0,1},{1,0},{2,3},{3,2},{4,5},{5,4},{6,7},{7,6},{8,9},{9,8},{10,11... | collective-permute-start | bytes 3342344 | tf_op jit(solution)/shard_map/ppermute | solution.py:50
  73.8 4.0 %collective-permute-start.13 = (bf16[4,2,32,2176]{3,2,1,0:T(8,128)(2,1)S(1)}, bf16[4,2,32,2176]{3,2,1,0:T(8,128)(2,1)S(1)}, u32[]{:S(2)}, u32[]{:S(2)}) collective-permute-start(bf16[4,2,32,2176]{3,2,1,0:T(8,128)(2,1)S(1)} %collective-permute-done.12.refs_3_), channel_id=1, source_target_pairs={{0,1},{1,0},{2,3},{3,2},{4,5},{5,4},{6,7},{7,6},{8,9},{9,8},{10,11... | collective-permute-start | bytes 3342344 | tf_op jit(solution)/shard_map/ppermute | solution.py:50
  73.8 8.1 %slice-start = ((s8[6291456]{0:T(1024)(128)(4,1)}), s8[4194304]{0:T(1024)(128)(4,1)S(1)}, s32[]{:S(2)}) async-start(s8[6291456]{0:T(1024)(128)(4,1)} %bitcast.6), calls=%async_computation | async-start | bytes 8388608
  77.8 4.1 %slice-start.1 = ((s8[6291456]{0:T(1024)(128)(4,1)}), s8[2097152]{0:T(1024)(128)(4,1)S(1)}, s32[]{:S(2)}) async-start(s8[6291456]{0:T(1024)(128)(4,1)} %bitcast.6), calls=%async_computation.1 | async-start | bytes 4194304
  83.7 2.1 %collective-permute-start.14 = (bf16[4,2,32,1024]{3,2,1,0:T(8,128)(2,1)S(1)}, bf16[4,2,32,1024]{3,2,1,0:T(8,128)(2,1)S(1)}, u32[]{:S(2)}, u32[]{:S(2)}) collective-permute-start(bf16[4,2,32,1024]{3,2,1,0:T(8,128)(2,1)S(1)} %get-tuple-element.56), channel_id=1, source_target_pairs={{0,1},{1,0},{2,3},{3,2},{4,5},{5,4},{6,7},{7,6},{8,9},{9,8},{10,11... | collective-permute-start | bytes 1572872 | tf_op jit(solution)/shard_map/ppermute | solution.py:50
  84.3 2.3 %collective-permute-start.15 = (bf16[4,2,32,1024]{3,2,1,0:T(8,128)(2,1)S(1)}, bf16[4,2,32,1024]{3,2,1,0:T(8,128)(2,1)S(1)}, u32[]{:S(2)}, u32[]{:S(2)}) collective-permute-start(bf16[4,2,32,1024]{3,2,1,0:T(8,128)(2,1)S(1)} %get-tuple-element.57), channel_id=1, source_target_pairs={{0,1},{1,0},{2,3},{3,2},{4,5},{5,4},{6,7},{7,6},{8,9},{9,8},{10,11... | collective-permute-start | bytes 1572872 | tf_op jit(solution)/shard_map/ppermute | solution.py:50
  84.4 2.9 %collective-permute-start.16 = (bf16[4,2,32,1024]{3,2,1,0:T(8,128)(2,1)S(1)}, bf16[4,2,32,1024]{3,2,1,0:T(8,128)(2,1)S(1)}, u32[]{:S(2)}, u32[]{:S(2)}) collective-permute-start(bf16[4,2,32,1024]{3,2,1,0:T(8,128)(2,1)S(1)} %get-tuple-element.58), channel_id=1, source_target_pairs={{0,1},{1,0},{2,3},{3,2},{4,5},{5,4},{6,7},{7,6},{8,9},{9,8},{10,11... | collective-permute-start | bytes 1572872 | tf_op jit(solution)/shard_map/ppermute | solution.py:50
  84.8 3.3 %collective-permute-start.17 = (bf16[4,2,32,1024]{3,2,1,0:T(8,128)(2,1)S(1)}, bf16[4,2,32,1024]{3,2,1,0:T(8,128)(2,1)S(1)}, u32[]{:S(2)}, u32[]{:S(2)}) collective-permute-start(bf16[4,2,32,1024]{3,2,1,0:T(8,128)(2,1)S(1)} %get-tuple-element.59), channel_id=1, source_target_pairs={{0,1},{1,0},{2,3},{3,2},{4,5},{5,4},{6,7},{7,6},{8,9},{9,8},{10,11... | collective-permute-start | bytes 1572872 | tf_op jit(solution)/shard_map/ppermute | solution.py:50
  91.7 2.0 %collective-permute-start.24 = (bf16[4,2,32,1024]{3,2,1,0:T(8,128)(2,1)S(1)}, bf16[4,2,32,1024]{3,2,1,0:T(8,128)(2,1)S(1)}, u32[]{:S(2)}, u32[]{:S(2)}) collective-permute-start(bf16[4,2,32,1024]{3,2,1,0:T(8,128)(2,1)S(1)} %get-tuple-element.69), channel_id=1, source_target_pairs={{0,1},{1,0},{2,3},{3,2},{4,5},{5,4},{6,7},{7,6},{8,9},{9,8},{10,11... | collective-permute-start | bytes 1572872 | tf_op jit(solution)/shard_map/ppermute | solution.py:50
  92.2 2.6 %collective-permute-start.25 = (bf16[4,2,32,1024]{3,2,1,0:T(8,128)(2,1)S(1)}, bf16[4,2,32,1024]{3,2,1,0:T(8,128)(2,1)S(1)}, u32[]{:S(2)}, u32[]{:S(2)}) collective-permute-start(bf16[4,2,32,1024]{3,2,1,0:T(8,128)(2,1)S(1)} %get-tuple-element.70), channel_id=1, source_target_pairs={{0,1},{1,0},{2,3},{3,2},{4,5},{5,4},{6,7},{7,6},{8,9},{9,8},{10,11... | collective-permute-start | bytes 1572872 | tf_op jit(solution)/shard_map/ppermute | solution.py:50
  92.3 5.2 %collective-permute-start.26 = (bf16[4,2,32,1024]{3,2,1,0:T(8,128)(2,1)S(1)}, bf16[4,2,32,1024]{3,2,1,0:T(8,128)(2,1)S(1)}, u32[]{:S(2)}, u32[]{:S(2)}) collective-permute-start(bf16[4,2,32,1024]{3,2,1,0:T(8,128)(2,1)S(1)} %get-tuple-element.71), channel_id=1, source_target_pairs={{0,1},{1,0},{2,3},{3,2},{4,5},{5,4},{6,7},{7,6},{8,9},{9,8},{10,11... | collective-permute-start | bytes 1572872 | tf_op jit(solution)/shard_map/ppermute | solution.py:50
  92.7 4.8 %collective-permute-start.27 = (bf16[4,2,32,1024]{3,2,1,0:T(8,128)(2,1)S(1)}, bf16[4,2,32,1024]{3,2,1,0:T(8,128)(2,1)S(1)}, u32[]{:S(2)}, u32[]{:S(2)}) collective-permute-start(bf16[4,2,32,1024]{3,2,1,0:T(8,128)(2,1)S(1)} %get-tuple-element.72), channel_id=1, source_target_pairs={{0,1},{1,0},{2,3},{3,2},{4,5},{5,4},{6,7},{7,6},{8,9},{9,8},{10,11... | collective-permute-start | bytes 1572872 | tf_op jit(solution)/shard_map/ppermute | solution.py:50
  92.8 9.2 %collective-permute-start.18 = (bf16[4,2,32,1024]{3,2,1,0:T(8,128)(2,1)S(1)}, bf16[4,2,32,1024]{3,2,1,0:T(8,128)(2,1)S(1)}, u32[]{:S(2)}, u32[]{:S(2)}) collective-permute-start(bf16[4,2,32,1024]{3,2,1,0:T(8,128)(2,1)S(1)} %get-tuple-element.61), channel_id=1, source_target_pairs={{0,4},{1,9},{4,0},{5,13},{2,6},{3,11},{6,2},{7,15},{8,12},{9,1},{1... | collective-permute-start | bytes 1572872 | tf_op jit(solution)/shard_map/ppermute | solution.py:37
  93.7 13.9 %collective-permute-start.19 = (bf16[4,2,32,1024]{3,2,1,0:T(8,128)(2,1)S(1)}, bf16[4,2,32,1024]{3,2,1,0:T(8,128)(2,1)S(1)}, u32[]{:S(2)}, u32[]{:S(2)}) collective-permute-start(bf16[4,2,32,1024]{3,2,1,0:T(8,128)(2,1)S(1)} %get-tuple-element.62), channel_id=1, source_target_pairs={{0,2},{1,17},{4,6},{5,21},{2,0},{3,19},{6,4},{7,23},{8,10},{9,25},... | collective-permute-start | bytes 1572872 | tf_op jit(solution)/shard_map/ppermute | solution.py:36
  94.8 16.0 %collective-permute-start.20 = (bf16[4,2,32,1024]{3,2,1,0:T(8,128)(2,1)S(1)}, bf16[4,2,32,1024]{3,2,1,0:T(8,128)(2,1)S(1)}, u32[]{:S(2)}, u32[]{:S(2)}) collective-permute-start(bf16[4,2,32,1024]{3,2,1,0:T(8,128)(2,1)S(1)} %get-tuple-element.63), channel_id=1, source_target_pairs={{0,6},{1,25},{4,2},{5,29},{2,4},{3,27},{6,0},{7,31},{8,14},{9,17},... | collective-permute-start | bytes 1572872 | tf_op jit(solution)/shard_map/ppermute | solution.py:37
  99.3 14.0 %collective-permute-start.28 = (bf16[4,2,32,1024]{3,2,1,0:T(8,128)(2,1)S(1)}, bf16[4,2,32,1024]{3,2,1,0:T(8,128)(2,1)S(1)}, u32[]{:S(2)}, u32[]{:S(2)}) collective-permute-start(bf16[4,2,32,1024]{3,2,1,0:T(8,128)(2,1)S(1)} %get-tuple-element.74), channel_id=1, source_target_pairs={{0,4},{1,9},{4,0},{5,13},{2,6},{3,11},{6,2},{7,15},{8,12},{9,1},{1... | collective-permute-start | bytes 1572872 | tf_op jit(solution)/shard_map/ppermute | solution.py:37
  99.4 25.1 %collective-permute-start.29 = (bf16[4,2,32,1024]{3,2,1,0:T(8,128)(2,1)S(1)}, bf16[4,2,32,1024]{3,2,1,0:T(8,128)(2,1)S(1)}, u32[]{:S(2)}, u32[]{:S(2)}) collective-permute-start(bf16[4,2,32,1024]{3,2,1,0:T(8,128)(2,1)S(1)} %get-tuple-element.75), channel_id=1, source_target_pairs={{0,2},{1,17},{4,6},{5,21},{2,0},{3,19},{6,4},{7,23},{8,10},{9,25},... | collective-permute-start | bytes 1572872 | tf_op jit(solution)/shard_map/ppermute | solution.py:36
  102.0 24.2 %collective-permute-start.30 = (bf16[4,2,32,1024]{3,2,1,0:T(8,128)(2,1)S(1)}, bf16[4,2,32,1024]{3,2,1,0:T(8,128)(2,1)S(1)}, u32[]{:S(2)}, u32[]{:S(2)}) collective-permute-start(bf16[4,2,32,1024]{3,2,1,0:T(8,128)(2,1)S(1)} %get-tuple-element.76), channel_id=1, source_target_pairs={{0,6},{1,25},{4,2},{5,29},{2,4},{3,27},{6,0},{7,31},{8,14},{9,17},... | collective-permute-start | bytes 1572872 | tf_op jit(solution)/shard_map/ppermute | solution.py:37
  111.2 17.6 %collective-permute-start.21 = (bf16[128,1024]{1,0:T(8,128)(2,1)S(1)}, bf16[128,1024]{1,0:T(8,128)(2,1)S(1)}, u32[]{:S(2)}, u32[]{:S(2)}) collective-permute-start(bf16[128,1024]{1,0:T(8,128)(2,1)S(1)} %get-tuple-element.65), channel_id=1, source_target_pairs={{0,8},{1,5},{4,12},{5,1},{2,10},{3,7},{6,14},{7,3},{8,0},{9,13},{1... | collective-permute-start | bytes 786440 | tf_op jit(solution)/shard_map/ppermute | solution.py:37
  111.3 20.1 %collective-permute-start.22 = (bf16[128,1024]{1,0:T(8,128)(2,1)S(1)}, bf16[128,1024]{1,0:T(8,128)(2,1)S(1)}, u32[]{:S(2)}, u32[]{:S(2)}) collective-permute-start(bf16[128,1024]{1,0:T(8,128)(2,1)S(1)} %get-tuple-element.66), channel_id=1, source_target_pairs={{0,16},{1,3},{4,20},{5,7},{2,18},{3,1},{6,22},{7,5},{8,24},{9,11},... | collective-permute-start | bytes 786440 | tf_op jit(solution)/shard_map/ppermute | solution.py:36
  113.4 18.1 %collective-permute-start.23 = (bf16[128,1024]{1,0:T(8,128)(2,1)S(1)}, bf16[128,1024]{1,0:T(8,128)(2,1)S(1)}, u32[]{:S(2)}, u32[]{:S(2)}) collective-permute-start(bf16[128,1024]{1,0:T(8,128)(2,1)S(1)} %get-tuple-element.67), channel_id=1, source_target_pairs={{0,24},{1,7},{4,28},{5,3},{2,26},{3,5},{6,30},{7,1},{8,16},{9,15},... | collective-permute-start | bytes 786440 | tf_op jit(solution)/shard_map/ppermute | solution.py:37
  126.7 6.5 %collective-permute-start.31 = (bf16[128,1024]{1,0:T(8,128)(2,1)S(1)}, bf16[128,1024]{1,0:T(8,128)(2,1)S(1)}, u32[]{:S(2)}, u32[]{:S(2)}) collective-permute-start(bf16[128,1024]{1,0:T(8,128)(2,1)S(1)} %get-tuple-element.78), channel_id=1, source_target_pairs={{0,8},{1,5},{4,12},{5,1},{2,10},{3,7},{6,14},{7,3},{8,0},{9,13},{1... | collective-permute-start | bytes 786440 | tf_op jit(solution)/shard_map/ppermute | solution.py:37
  126.7 9.3 %collective-permute-start.32 = (bf16[128,1024]{1,0:T(8,128)(2,1)S(1)}, bf16[128,1024]{1,0:T(8,128)(2,1)S(1)}, u32[]{:S(2)}, u32[]{:S(2)}) collective-permute-start(bf16[128,1024]{1,0:T(8,128)(2,1)S(1)} %get-tuple-element.79), channel_id=1, source_target_pairs={{0,16},{1,3},{4,20},{5,7},{2,18},{3,1},{6,22},{7,5},{8,24},{9,11},... | collective-permute-start | bytes 786440 | tf_op jit(solution)/shard_map/ppermute | solution.py:36
  128.8 10.0 %collective-permute-start.33 = (bf16[128,1024]{1,0:T(8,128)(2,1)S(1)}, bf16[128,1024]{1,0:T(8,128)(2,1)S(1)}, u32[]{:S(2)}, u32[]{:S(2)}) collective-permute-start(bf16[128,1024]{1,0:T(8,128)(2,1)S(1)} %get-tuple-element.80), channel_id=1, source_target_pairs={{0,24},{1,7},{4,28},{5,3},{2,26},{3,5},{6,30},{7,1},{8,16},{9,15},... | collective-permute-start | bytes 786440 | tf_op jit(solution)/shard_map/ppermute | solution.py:37
  139.0 6.1 %collective-permute-start.34 = (bf16[32,2048]{1,0:T(8,128)(2,1)S(1)}, bf16[32,2048]{1,0:T(8,128)(2,1)S(1)}, u32[]{:S(2)}, u32[]{:S(2)}) collective-permute-start(bf16[32,2048]{1,0:T(8,128)(2,1)S(1)} %get-tuple-element.85), channel_id=1, source_target_pairs={{0,32},{1,97},{4,36},{5,101},{2,34},{3,99},{6,38},{7,103},{8,40},{... | collective-permute-start | bytes 393224 | tf_op jit(solution)/shard_map/ppermute | solution.py:43
  139.6 8.1 %collective-permute-start.35 = (bf16[32,2048]{1,0:T(8,128)(2,1)S(1)}, bf16[32,2048]{1,0:T(8,128)(2,1)S(1)}, u32[]{:S(2)}, u32[]{:S(2)}) collective-permute-start(bf16[32,2048]{1,0:T(8,128)(2,1)S(1)} %get-tuple-element.87), channel_id=1, source_target_pairs={{0,96},{1,33},{4,100},{5,37},{2,98},{3,35},{6,102},{7,39},{8,104},... | collective-permute-start | bytes 393224 | tf_op jit(solution)/shard_map/ppermute | solution.py:44
  141.0 6.7 %collective-permute-start.36 = (bf16[32,2048]{1,0:T(8,128)(2,1)S(1)}, bf16[32,2048]{1,0:T(8,128)(2,1)S(1)}, u32[]{:S(2)}, u32[]{:S(2)}) collective-permute-start(bf16[32,2048]{1,0:T(8,128)(2,1)S(1)} %get-tuple-element.86), channel_id=1, source_target_pairs={{0,64},{1,65},{4,68},{5,69},{2,66},{3,67},{6,70},{7,71},{8,72},{9,... | collective-permute-start | bytes 393224 | tf_op jit(solution)/shard_map/ppermute | solution.py:42
  147.8 1.3 collective-permute-start.37

commit v4 on v3

v4 whole, which is shorter than its diff:
```python
import functools

import jax
import jax.numpy as jnp
from jax import lax
from jax.experimental import pallas as pl
from jax.experimental.pallas import tpu as pltpu
from jax.sharding import PartitionSpec as P

AXES = ("expert", "dp")
SIDE = 4
META = 128
CAP = 4
BACK = 2


def place(z, y, x, core):
    return ((z * SIDE + y) * 2 + x % 2) * 4 + (x // 2) * 2 + core


def partners(axes, masks):
    masks = (masks, masks) if isinstance(masks, int) else masks
    pairs = []
    for z in range(SIDE):
        for y in range(SIDE):
            for x in range(SIDE):
                for core in range(2):
                    other = [z, y, x]
                    other["zyx".index(axes[core])] ^= masks[core]
                    pairs.append((place(z, y, x, core), place(*other, core)))
    return pairs


def exchange(value, axes):
    over = lax.ppermute(value[2], AXES, partners(axes, 2))
    one, three = (lax.ppermute(value[j], AXES, partners(axes, j)) for j in (1, 3))
    return [value[0], one, over, three]


def exchange_z(value, first_core):
    over = lax.ppermute(value[2], AXES, partners("zz", 2))
    near = lax.ppermute(jnp.where(first_core, value[1], value[3]), AXES, partners("zz", (1, 3)))
    far = lax.ppermute(jnp.where(first_core, value[3], value[1]), AXES, partners("zz", (3, 1)))
    return [value[0], jnp.where(first_core, near, far), over, jnp.where(first_core, far, near)]


def sibling(value):
    pairs = [(i, i ^ 1) for i in range(SIDE**3 * 2)]
    return lax.ppermute(value, AXES, pairs)


def prepare_kernel(core_ref, tokens_ref, ids_ref, weights_ref, placement_ref, kept_ref, sent_ref):
    top, count = ids_ref.shape
    width = tokens_ref.shape[1]
    half = width // 2
    slot_count = placement_ref.shape[1]
    lanes = lax.broadcasted_iota(jnp.int32, (count, slot_count), 1)
    placement = placement_ref[...].astype(jnp.float32)
    line = lax.broadcasted_iota(jnp.int32, (count, count), 0)
    column = lax.broadcasted_iota(jnp.int32, (count, count), 1)
    diagonal = line == column
    slots = []
    named = jnp.zeros((count, slot_count), jnp.float32)
    for k in range(top):
        ids = jnp.sum(jnp.where(diagonal, ids_ref[k : k + 1], 0), axis=1, keepdims=True)
        slot = jnp.sum(jnp.where(ids == lanes, placement, 0.0), axis=1, keepdims=True)
        slots.append(slot)
        named = jnp.where(lanes.astype(jnp.float32) == slot, 1.0, named)
    before = jnp.where(line > column, 1.0, 0.0)
    ranks = jnp.dot(before.astype(jnp.bfloat16), named.astype(jnp.bfloat16), preferred_element_type=jnp.float32)
    lane = lax.broadcasted_iota(jnp.int32, (count, META), 1)
    meta = jnp.full((count, META), -1.0, jnp.float32)
    for k in range(top):
        rank = jnp.sum(jnp.where(lanes.astype(jnp.float32) == slots[k], ranks, 0.0), axis=1, keepdims=True)
        weight = jnp.sum(jnp.where(diagonal, weights_ref[k : k + 1], 0.0), axis=1, keepdims=True)
        high = weight.astype(jnp.bfloat16).astype(jnp.float32)
        middle = (weight - high).astype(jnp.bfloat16).astype(jnp.float32)
        for turn, term in enumerate((high, middle, weight - high - middle)):
            at = turn * top + k
            meta = jnp.where(lane == at, slots[k] * CAP + rank, meta)
            meta = jnp.where(lane == META // 2 + at, term, meta)
    meta = meta.astype(jnp.bfloat16)
    for ref, own in ((kept_ref, True), (sent_ref, False)):
        begin = core_ref[0] * half if own else half - core_ref[0] * half
        begin = pl.multiple_of(begin, 128)
        ref[:, :half] = tokens_ref[:, pl.ds(begin, half)]
        ref[:, half:] = meta


def fetch_kernel(wanted_ref, gate_ref, up_ref, *refs, top, tok_count):
    planes, (both_ref, high_ref, middle_ref, sems) = refs[:SIDE], refs[SIDE:]
    columns = gate_ref.shape[2]
    copies = [
        pltpu.make_async_copy(ref, both_ref.at[:, :, pl.ds(i * columns, columns)], sems.at[i])
        for i, ref in enumerate((gate_ref, up_ref))
    ]
    for copy in copies:
        copy.start()
    wanted = wanted_ref[...]
    inside = same_block(planes[0].shape[0], wanted.shape[1], tok_count)
    for p in range(SIDE):
        info = planes[p][:, planes[p].shape[1] - META :].astype(jnp.float32)
        weighted = jnp.zeros(inside.shape, jnp.float32)
        for k in range(top):
            at = [META // 2 + turn * top + k for turn in range(3)]
            weight = info[:, at[0] : at[0] + 1] + info[:, at[1] : at[1] + 1] + info[:, at[2] : at[2] + 1]
            weighted = jnp.where(info[:, k : k + 1] == wanted, weight, weighted)
        weighted = jnp.where(inside, weighted, 0.0)
        high = weighted.astype(jnp.bfloat16)
        high_ref[p] = high
        middle_ref[p] = (weighted - high.astype(jnp.float32)).astype(jnp.bfloat16)
    for copy in copies:
        copy.wait()


def same_block(tokens, lines, tok_count):
    blocks = tokens // tok_count
    token_block = lax.broadcasted_iota(jnp.int32, (tokens, lines), 0) // tok_count
    return token_block == lax.broadcasted_iota(jnp.int32, (tokens, lines), 1) // CAP % blocks


def pack_kernel(wanted_ref, *refs, top, tok_count):
    planes, outs = refs[:SIDE], refs[SIDE:]
    wanted = wanted_ref[...]
    inside = same_block(planes[0].shape[0], wanted.shape[1], tok_count)
    share = wanted.shape[1] // SIDE
    half = outs[0].shape[3]
    for p in range(SIDE):
        codes = planes[p][:, half:].astype(jnp.float32)
        found = codes[:, :1] == wanted
        for k in range(1, top):
            found = found | (codes[:, k : k + 1] == wanted)
        take = jnp.where(found & inside, 1.0, 0.0).T.astype(jnp.bfloat16)
        rows = jnp.dot(take, planes[p][:, :half], preferred_element_type=jnp.float32).astype(jnp.bfloat16)
        for j in range(SIDE):
            outs[j][p] = rows[j * share : (j + 1) * share].reshape(outs[j].shape[1:])


def gate_kernel(base_ref, *refs, source):
    pieces, (w_ref, total_ref, rows_ref) = refs[:2], refs[2:]
    step = rows_ref.shape[1]
    begin = pl.multiple_of(base_ref[0 if source == "own" else 1] * step, step)
    count = rows_ref.shape[0] // 2
    for slot in range(w_ref.shape[0]):
        for i, piece in enumerate(pieces):
            for other in range(SIDE):
                line = i * count + other * piece.shape[2]
                rows_ref[line : line + piece.shape[2]] = piece[other, slot]
        total_ref[slot] = jnp.dot(rows_ref[...], w_ref[slot, pl.ds(begin, step)], preferred_element_type=jnp.float32)


def hidden_kernel(base_ref, *refs):
    pieces, (w_ref, own_0, own_1, sib_0, hidden_ref, rows_ref) = refs[:2], refs[2:]
    step = rows_ref.shape[1]
    begin = pl.multiple_of(base_ref[1] * step, step)
    granule, count, columns = pieces[0].shape[2], rows_ref.shape[0] // 2, w_ref.shape[2] // 2
    for slot in range(w_ref.shape[0]):
        for i, piece in enumerate(pieces):
            for last in range(SIDE):
                line = i * count + last * granule
                rows_ref[line : line + granule] = piece[last, slot]
        sib_1 = jnp.dot(rows_ref[...], w_ref[slot, pl.ds(begin, step)], preferred_element_type=jnp.float32)
        for last in range(SIDE):
            own = own_0 if last < 2 else own_1
            for plane in range(SIDE):
                line = last % 2 * count + plane * granule
                across = plane % 2 * count + last * granule
                sib = sib_0[slot, across : across + granule] if plane < 2 else sib_1[across : across + granule]
                total = own[slot, line : line + granule] + sib
                line = (last * SIDE + plane) * granule
                hidden = jax.nn.silu(total[:, :columns]) * total[:, columns:]
                hidden_ref[slot, line : line + granule] = hidden.astype(jnp.bfloat16)


def down_kernel(base_ref, hidden_ref, w_ref, *refs, part, turned):
    outs, added = refs[-SIDE:], refs[:-SIDE]
    granule, step = outs[0].shape[2:]
    which = 1 if turned else 0
    begin = pl.multiple_of((base_ref[which] * BACK + part) * step, step)
    for slot in range(hidden_ref.shape[0]):
        value = jnp.dot(hidden_ref[slot], w_ref[slot, :, pl.ds(begin, step)], preferred_element_type=jnp.float32)
        for last in range(SIDE):
            for plane in range(SIDE):
                line = (last * SIDE + plane) * granule
                rows = value[line : line + granule]
                if turned:
                    outs[plane][last, slot] = rows.astype(jnp.bfloat16)
                else:
                    outs[last][plane, slot] = (rows + added[last][plane, slot].astype(jnp.float32)).astype(jnp.bfloat16)


def unpack_kernel(high_ref, middle_ref, *refs):
    pieces, outs = refs[:SIDE], refs[SIDE:]
    for p in range(SIDE):
        values = jnp.concatenate([piece[p].reshape(-1, piece.shape[3]) for piece in pieces])
        dense = jnp.dot(high_ref[p], values, preferred_element_type=jnp.float32)
        dense += jnp.dot(middle_ref[p], values, preferred_element_type=jnp.float32)
        outs[p][...] = dense.astype(outs[p].dtype)


def whole(count):
    return [pl.BlockSpec(memory_space=pltpu.VMEM)] * count


def params(mebibytes=12):
    return pltpu.CompilerParams(vmem_limit_bytes=mebibytes * 2**20)


def cost(flops, read):
    return pl.CostEstimate(flops=int(flops), bytes_accessed=int(read), transcendentals=0)


def shards(tokens, expert_ids, gate_weights, placement, w_gate, w_up, w_down):
    tok_count, width = tokens.shape
    top = expert_ids.shape[1]
    per_device = w_gate.shape[0]
    half = width // 2
    core = lax.axis_index("dp") % 2
    first_core = core == 0
    own_slot = lax.axis_index("expert") * per_device
    local = jnp.arange(per_device, dtype=jnp.int32)
    scalar = [pl.BlockSpec(memory_space=pltpu.SMEM)]
    base = jnp.stack([core, 1 - core, own_slot]).astype(jnp.int32)

    carried = jax.ShapeDtypeStruct((tok_count, half + META), jnp.bfloat16)
    kept, sent = pl.pallas_call(
        prepare_kernel,
        grid=(1,),
        out_shape=[carried, carried],
        in_specs=scalar
        + [
            pl.BlockSpec(shape, lambda i: (0, 0))
            for shape in (tokens.shape, (top, tok_count), (top, tok_count), (1, placement.shape[0]))
        ],
        out_specs=whole(2),
        compiler_params=params(56),
    )(base, tokens, expert_ids.T, gate_weights.T, placement.reshape(1, -1))
    got = sibling(sent)
    both = jnp.concatenate([jnp.where(first_core, kept, got), jnp.where(first_core, got, kept)])

    near_pieces = exchange_z([both] * SIDE, first_core)
    near = jnp.concatenate(near_pieces)
    near_count = near.shape[0]

    lines = near_count // tok_count * CAP * per_device * SIDE
    masks = jnp.arange(SIDE, dtype=jnp.int32)
    moved = jnp.where(first_core, (masks & 1) * 2, masks * 4)
    slots = ((own_slot ^ moved)[:, None] + local[None, :]).reshape(-1)
    wanted = slots[:, None, None] * CAP + jnp.zeros((1, near_count // tok_count, 1), jnp.int32) + jnp.arange(CAP, dtype=jnp.int32)
    wanted = wanted.astype(jnp.float32).reshape(1, lines)
    granule = near_count // tok_count * CAP
    rows_of = lambda columns: jax.ShapeDtypeStruct((SIDE, per_device, granule, columns), jnp.bfloat16)
    rows_count, hidden_count = SIDE * SIDE * granule, w_gate.shape[2]

    planes = exchange([near] * SIDE, "yx")
    packed = pl.pallas_call(
        functools.partial(pack_kernel, top=top, tok_count=tok_count),
        out_shape=[rows_of(half)] * SIDE,
        in_specs=whole(1 + SIDE),
        out_specs=whole(SIDE),
        compiler_params=params(),
        cost_estimate=cost(2 * SIDE * lines * near_count * half, 1e6),
    )(wanted, *planes)
    own = exchange(packed, "xy")

    gate_w, up_w, _ = lax.optimization_barrier((w_gate, w_up, packed[0]))
    back_matrix = jax.ShapeDtypeStruct((SIDE, near_count, lines), jnp.bfloat16)
    gate_up, high, middle = pl.pallas_call(
        functools.partial(fetch_kernel, top=top, tok_count=tok_count),
        out_shape=[
            jax.ShapeDtypeStruct((*w_gate.shape[:2], 2 * w_gate.shape[2]), w_gate.dtype),
            back_matrix,
            back_matrix,
        ],
        in_specs=whole(1) + [pl.BlockSpec(memory_space=pltpu.HBM)] * 2 + whole(SIDE),
        out_specs=whole(3),
        scratch_shapes=[pltpu.SemaphoreType.DMA((2,))],
        compiler_params=params(),
        cost_estimate=cost(1, 1),
    )(wanted, gate_w, up_w, *planes)

    own[1], gate_up = lax.optimization_barrier((own[1], gate_up))

    def project(source, pieces):
        return pl.pallas_call(
            functools.partial(gate_kernel, source=source),
            out_shape=jax.ShapeDtypeStruct((per_device, rows_count // 2, 2 * hidden_count), jnp.float32),
            in_specs=scalar + whole(3),
            out_specs=pl.BlockSpec(memory_space=pltpu.VMEM),
            scratch_shapes=[pltpu.VMEM((rows_count // 2, half), jnp.bfloat16)],
            compiler_params=params(),
            cost_estimate=cost(1, 1),
        )(base, *pieces, gate_up)

    own_0 = project("own", own[:2])
    sib_0 = project("sibling", [sibling(piece) for piece in own[:2]])
    own[2], own_0 = lax.optimization_barrier((own[2], own_0))
    own_1 = project("own", own[2:])
    hidden = pl.pallas_call(
        hidden_kernel,
        out_shape=jax.ShapeDtypeStruct((per_device, rows_count, hidden_count), jnp.bfloat16),
        in_specs=scalar + whole(6),
        out_specs=pl.BlockSpec(memory_space=pltpu.VMEM),
        scratch_shapes=[pltpu.VMEM((rows_count // 2, half), jnp.bfloat16)],
        compiler_params=params(),
        cost_estimate=cost(2 * per_device * rows_count * half * hidden_count, 4e6),
    )(base, *[sibling(piece) for piece in own[2:]], gate_up, own_0, own_1, sib_0)

    back_step = half // BACK

    def down(hidden, part, turned, added):
        return pl.pallas_call(
            functools.partial(down_kernel, part=part, turned=turned),
            out_shape=[rows_of(back_step)] * SIDE,
            in_specs=scalar + whole(2 + len(added)),
            out_specs=whole(SIDE),
            compiler_params=params(),
            cost_estimate=cost(2 * per_device * rows_count * back_step * hidden_count, 5e6),
        )(base, hidden, w_down, *added)

    sent = [down(hidden, part, True, []) for part in range(BACK)]
    hidden, _ = lax.optimization_barrier((hidden, [piece for pieces in sent for piece in pieces[:1]]))
    sums = []
    for part in range(BACK):
        mine = down(hidden, part, False, [sibling(piece) for piece in sent[part]])
        values = exchange(mine, "xy")
        kinds = [jnp.float32] + [jnp.bfloat16] * (SIDE - 1)
        dense = pl.pallas_call(
            unpack_kernel,
            out_shape=[jax.ShapeDtypeStruct((near_count, back_step), kind) for kind in kinds],
            in_specs=whole(2 + SIDE),
            out_specs=whole(SIDE),
            compiler_params=params(),
        )(high, middle, *values)
        sums.append(sum(piece.astype(jnp.float32) for piece in exchange(dense, "yx")))
    total = jnp.concatenate(sums, axis=1).reshape(SIDE, -1, half)
    sent = [total[0]] + [total[j].astype(jnp.bfloat16) for j in (1, 2, 3)]
    sent = exchange_z(sent, first_core)
    total = sum(piece.astype(jnp.float32) for piece in sent).astype(jnp.bfloat16).reshape(2, tok_count, half)
    kept = jnp.where(first_core, total[0], total[1])
    got = sibling(jnp.where(first_core, total[1], total[0]))
    return jnp.concatenate([jnp.where(first_core, kept, got), jnp.where(first_core, got, kept)], axis=1)


def solution(mesh):
    in_specs = (
        P(AXES, None),
        P(AXES, None),
        P(AXES, None),
        P(),
        P("expert", None, "dp"),
        P("expert", None, "dp"),
        P("expert", "dp", None),
    )
    return jax.shard_map(shards, mesh=mesh, in_specs=in_specs, out_specs=P(AXES, None), check_vma=False)
```

time: 151 us -> 146 us (0.967)
  waiting for transfers between devices: 80.2 us -> 70.4 us
  Pallas kernels: 20 us -> 25 us
  local copies, waits for them, and re-layouts: 8.73 us -> 5.8 us
    ppermute x14, waiting for transfers between devices: 6.57 us -> 3 us  [sibling(): return lax.ppermute(value, AXES, pairs)]
    pallas_call x4 -> x6, Pallas kernels: 11 us -> 14.4 us  [the longest x3 7.02 us: project(): pl.pallas_call(functools.partial(gate_kernel, source=source), out_shape=j...]
    ppermute x6, waiting for transfers between devices: 37.8 us -> 34.5 us  [exchange(): over = lax.ppermute(value[2], AXES, partners(axes, 2))]
    unnamed x17 -> x11, local copies, waits for them, and re-layouts: 8.53 us -> 5.6 us
    ppermute x12, waiting for transfers between devices: 24.7 us -> 21.9 us  [exchange(): lax.ppermute(value[j], AXES, partners(axes, j))]
    ppermute x2, waiting for transfers between devices: 1.94 us -> 3.66 us  [exchange_z(): over = lax.ppermute(value[2], AXES, partners('zz', 2))]
  transfers between devices with their start and end apart: 38 -> 38, of which waited for: 26 -> 23; matrix products, arithmetic and copies ran while one was open for 0% -> 0% of each run, Pallas kernels for 5% -> 12%
where the time goes in v4:
time: 146 us; the launch traced here: 144 us
  waiting for transfers between devices  70.4 us (48%)
  starting transfers between devices  39.9 us (27%)
  Pallas kernels  25 us (17%)
  local copies, waits for them, and re-layouts  5.8 us (4%)
  other arithmetic  2.99 us (2%)
    ppermute x6, waiting for transfers between devices, exchange(): over = lax.ppermute(value[2], AXES, partners(axes, 2))  34.5 us
    ppermute x12, waiting for transfers between devices, exchange(): lax.ppermute(value[j], AXES, partners(axes, j))  21.9 us
    ppermute x12, starting transfers between devices, exchange(): lax.ppermute(value[j], AXES, partners(axes, j))  14.4 us
    ppermute x6, starting transfers between devices, exchange(): over = lax.ppermute(value[2], AXES, partners(axes, 2))  13.3 us
    pallas_call x4, Pallas kernels, down(): pl.pallas_call(functools.partial(down_kernel, part=part, turned=turned),...  7.19 us
    pallas_call x3, Pallas kernels, project(): pl.pallas_call(functools.partial(gate_kernel, source=source), out_shape=j...  7.02 us
    ppermute x2, waiting for transfers between devices, exchange_z(): lax.ppermute(jnp.where(first_core, value[3], value[1]), AXES, partners('z...  6.47 us
    unnamed x11, local copies, waits for them, and re-layouts  5.6 us
  transfers between devices with their start and end apart: 38, of which 23 were waited for; matrix products, arithmetic and copies ran while one was open for 0% of the time, Pallas kernels for 12%

profile of v4, /device:TPU:0, one launch (start us, length us, event | category | flops | bytes accessed | tf_op | source)
XLA Modules:
  0.0 144.4 jit_solution(8744614120258774252)
XLA Ops:
  0.7 2.0 %shard_map.73 = (bf16[16,2176]{1,0:T(8,128)(2,1)}, bf16[16,2176]{1,0:T(8,128)(2,1)}) custom-call(s32[3]{0:T(128)} %pad_add_fusion.core_ref.base_ref, bf16[16,4096]{1,0:T(8,128)(2,1)} %tokens_ref.1, s32[8,16]{1,0:T(8,128)} %bitcast.8, f32[8,16]{1,0:T(8,128)} %bitcast.9, s32[1,64]{1,0:T(1,128)} %bitcast.10), custom_call_target="tpu_custom_call" | custom-call | tf_op jit(solution)/shard_map/pallas_call | solution.py:226
  2.7 1.5 %collective-permute-done = bf16[16,2176]{1,0:T(8,128)(2,1)S(1)} collective-permute-done((bf16[16,2176]{1,0:T(8,128)(2,1)}, bf16[16,2176]{1,0:T(8,128)(2,1)S(1)}, u32[]{:S(2)}, u32[]{:S(2)}) %collective-permute-start) | collective-permute-done | bytes 69664 | tf_op jit(solution)/shard_map/ppermute | solution.py:49
  5.1 2.1 %collective-permute-start.1 = (bf16[32,2176]{1,0:T(8,128)(2,1)S(1)}, bf16[32,2176]{1,0:T(8,128)(2,1)S(1)}, u32[]{:S(2)}, u32[]{:S(2)}) collective-permute-start(bf16[32,2176]{1,0:T(8,128)(2,1)S(1)} %pad_maximum_fusion.1), channel_id=1, source_target_pairs={{0,32},{1,97},{4,36},{5,101},{2,34},{3,99},{6,38},{7,103},{8,40},{... | collective-permute-start | bytes 417800 | tf_op jit(solution)/shard_map/ppermute | solution.py:42
  7.2 2.5 %collective-permute-start.2 = (bf16[32,2176]{1,0:T(8,128)(2,1)S(1)}, bf16[32,2176]{1,0:T(8,128)(2,1)S(1)}, u32[]{:S(2)}, u32[]{:S(2)}) collective-permute-start(bf16[32,2176]{1,0:T(8,128)(2,1)S(1)} %pad_maximum_fusion.1), channel_id=1, source_target_pairs={{0,96},{1,33},{4,100},{5,37},{2,98},{3,35},{6,102},{7,39},{8,104},... | collective-permute-start | bytes 417800 | tf_op jit(solution)/shard_map/ppermute | solution.py:43
  10.8 4.8 %collective-permute-done.2 = bf16[32,2176]{1,0:T(8,128)(2,1)S(1)} collective-permute-done((bf16[32,2176]{1,0:T(8,128)(2,1)S(1)}, bf16[32,2176]{1,0:T(8,128)(2,1)S(1)}, u32[]{:S(2)}, u32[]{:S(2)}) %collective-permute-start.2) | collective-permute-done | bytes 139296 | tf_op jit(solution)/shard_map/ppermute | solution.py:43
  15.6 1.9 %collective-permute-done.3 = bf16[32,2176]{1,0:T(8,128)(2,1)S(1)} collective-permute-done((bf16[32,2176]{1,0:T(8,128)(2,1)S(1)}, bf16[32,2176]{1,0:T(8,128)(2,1)S(1)}, u32[]{:S(2)}, u32[]{:S(2)}) %collective-permute-start.3) | collective-permute-done | bytes 139296 | tf_op jit(solution)/shard_map/ppermute | solution.py:41
  17.6 1.7 %collective-permute-start.4 = (bf16[128,2176]{1,0:T(8,128)(2,1)S(1)}, bf16[128,2176]{1,0:T(8,128)(2,1)S(1)}, u32[]{:S(2)}, u32[]{:S(2)}) collective-permute-start(bf16[128,2176]{1,0:T(8,128)(2,1)S(1)} %select_dynamic-update-slice_fusion.refs_0_), channel_id=1, source_target_pairs={{0,8},{1,5},{4,12},{5,1},{2,10},{3,7},{6,14},{7,3},{8,0},{9,13},{1... | collective-permute-start | bytes 1671176 | tf_op jit(solution)/shard_map/ppermute | solution.py:36
  19.3 2.9 %collective-permute-start.5 = (bf16[128,2176]{1,0:T(8,128)(2,1)S(1)}, bf16[128,2176]{1,0:T(8,128)(2,1)S(1)}, u32[]{:S(2)}, u32[]{:S(2)}) collective-permute-start(bf16[128,2176]{1,0:T(8,128)(2,1)S(1)} %select_dynamic-update-slice_fusion.refs_0_), channel_id=1, source_target_pairs={{0,16},{1,3},{4,20},{5,7},{2,18},{3,1},{6,22},{7,5},{8,24},{9,11},... | collective-permute-start | bytes 1671176 | tf_op jit(solution)/shard_map/ppermute | solution.py:35
  22.8 4.5 %collective-permute-done.4.refs_1_ = bf16[128,2176]{1,0:T(8,128)(2,1)S(1)} collective-permute-done((bf16[128,2176]{1,0:T(8,128)(2,1)S(1)}, bf16[128,2176]{1,0:T(8,128)(2,1)S(1)}, u32[]{:S(2)}, u32[]{:S(2)}) %collective-permute-start.4) | collective-permute-done | bytes 557088 | tf_op jit(solution)/shard_map/ppermute | solution.py:36
  27.2 8.5 %collective-permute-done.5.refs_2_ = bf16[128,2176]{1,0:T(8,128)(2,1)S(1)} collective-permute-done((bf16[128,2176]{1,0:T(8,128)(2,1)S(1)}, bf16[128,2176]{1,0:T(8,128)(2,1)S(1)}, u32[]{:S(2)}, u32[]{:S(2)}) %collective-permute-start.5) | collective-permute-done | bytes 557088 | tf_op jit(solution)/shard_map/ppermute | solution.py:35
  35.8 3.1 %collective-permute-done.6.refs_3_ = bf16[128,2176]{1,0:T(8,128)(2,1)S(1)} collective-permute-done((bf16[128,2176]{1,0:T(8,128)(2,1)S(1)}, bf16[128,2176]{1,0:T(8,128)(2,1)S(1)}, u32[]{:S(2)}, u32[]{:S(2)}) %collective-permute-start.6) | collective-permute-done | bytes 557088 | tf_op jit(solution)/shard_map/ppermute | solution.py:36
  38.9 1.6 %shard_map.74 = (bf16[4,2,32,2048]{3,2,1,0:T(8,128)(2,1)S(1)}, bf16[4,2,32,2048]{3,2,1,0:T(8,128)(2,1)S(1)}, bf16[4,2,32,2048]{3,2,1,0:T(8,128)(2,1)S(1)}, bf16[4,2,32,2048]{3,2,1,0:T(8,128)(2,1)S(1)}) custom-call(f32[1,256]{1,0:T(1,128)S(1)} %convert_element_type.47.wanted_ref, bf16[128,2176]{1,0:T(8,128)(2,1)S(1)} %select_dynamic-update-slice_fusion.refs_0_, ...), custom_call_target="tpu_custom_call" | custom-call | flops 536870912 | bytes 1000000 | tf_op jit(solution)/shard_map/pallas_call | solution.py:256
  40.5 1.6 %collective-permute-start.8 = (bf16[4,2,32,2048]{3,2,1,0:T(8,128)(2,1)S(1)}, bf16[4,2,32,2048]{3,2,1,0:T(8,128)(2,1)S(1)}, u32[]{:S(2)}, u32[]{:S(2)}) collective-permute-start(bf16[4,2,32,2048]{3,2,1,0:T(8,128)(2,1)S(1)} %get-tuple-element.53), channel_id=1, source_target_pairs={{0,4},{1,9},{4,0},{5,13},{2,6},{3,11},{6,2},{7,15},{8,12},{9,1},{1... | collective-permute-start | bytes 3145736 | tf_op jit(solution)/shard_map/ppermute | solution.py:36
  42.1 2.7 %collective-permute-start.7 = (bf16[4,2,32,2048]{3,2,1,0:T(8,128)(2,1)S(1)}, bf16[4,2,32,2048]{3,2,1,0:T(8,128)(2,1)S(1)}, u32[]{:S(2)}, u32[]{:S(2)}) collective-permute-start(bf16[4,2,32,2048]{3,2,1,0:T(8,128)(2,1)S(1)} %get-tuple-element.52), channel_id=1, source_target_pairs={{0,2},{1,17},{4,6},{5,21},{2,0},{3,19},{6,4},{7,23},{8,10},{9,25},... | collective-permute-start | bytes 3145736 | tf_op jit(solution)/shard_map/ppermute | solution.py:35
  45.3 2.8 %copy-done = bf16[2,4096,384]{2,1,0:T(8,128)(2,1)S(1)} copy-done((bf16[2,4096,384]{2,1,0:T(8,128)(2,1)S(1)}, bf16[2,4096,384]{2,1,0:T(8,128)(2,1)}, u32[]{:S(2)}) %copy-start) | copy-done | bytes 6291480
  48.0 2.8 %copy-done.1 = bf16[2,4096,384]{2,1,0:T(8,128)(2,1)S(1)} copy-done((bf16[2,4096,384]{2,1,0:T(8,128)(2,1)S(1)}, bf16[2,4096,384]{2,1,0:T(8,128)(2,1)}, u32[]{:S(2)}) %copy-start.1) | copy-done | bytes 6291480
  50.8 3.3 %shard_map.75 = (bf16[2,4096,768]{2,1,0:T(8,128)(2,1)S(1)}, bf16[4,128,256]{2,1,0:T(8,128)(2,1)S(1)}, bf16[4,128,256]{2,1,0:T(8,128)(2,1)S(1)}) custom-call(f32[1,256]{1,0:T(1,128)S(1)} %convert_element_type.47.wanted_ref, bf16[2,4096,384]{2,1,0:T(8,128)(2,1)S(1)} %copy-done, bf16[2,4096,384]{2,1,0:T(8,128)(2,1)S(1)} %copy-done.1, ...), custom_call_target="tpu_custom_call" | custom-call | flops 1 | bytes 1 | tf_op jit(solution)/shard_map/pallas_call | solution.py:268
  54.1 1.3 collective-permute-done.8.refs_1_
  55.4 2.3 %shard_map.76.refs_3_ = f32[2,256,768]{2,1,0:T(8,128)S(1)} custom-call(s32[3]{0:T(128)S(1)} %copy-done.2, bf16[4,2,32,2048]{3,2,1,0:T(8,128)(2,1)S(1)} %get-tuple-element.47.refs_0_, bf16[4,2,32,2048]{3,2,1,0:T(8,128)(2,1)S(1)} %collective-permute-done.8.refs_1_, bf16[2,4096,768]{2,1,0:T(8,128)(2,1)S(1)} %get-tuple-element.56.refs_2_), custom_call_target="tpu_custom_call" | custom-call | flops 1 | bytes 1 | tf_op jit(solution)/shard_map/pallas_call | solution.py:285
  57.7 11.2 %collective-permute-done.7.refs_0_ = bf16[4,2,32,2048]{3,2,1,0:T(8,128)(2,1)S(1)} collective-permute-done((bf16[4,2,32,2048]{3,2,1,0:T(8,128)(2,1)S(1)}, bf16[4,2,32,2048]{3,2,1,0:T(8,128)(2,1)S(1)}, u32[]{:S(2)}, u32[]{:S(2)}) %collective-permute-start.7) | collective-permute-done | bytes 1048608 | tf_op jit(solution)/shard_map/ppermute | solution.py:35
  68.9 3.1 %collective-permute-done.10.refs_1_ = bf16[4,2,32,2048]{3,2,1,0:T(8,128)(2,1)S(1)} collective-permute-done((bf16[4,2,32,2048]{3,2,1,0:T(8,128)(2,1)S(1)}, bf16[4,2,32,2048]{3,2,1,0:T(8,128)(2,1)S(1)}, u32[]{:S(2)}, u32[]{:S(2)}) %collective-permute-start.10) | collective-permute-done | bytes 1048608 | tf_op jit(solution)/shard_map/ppermute | solution.py:36
  72.0 2.3 %shard_map.77.refs_4_ = f32[2,256,768]{2,1,0:T(8,128)S(1)} custom-call(s32[3]{0:T(128)S(1)} %copy-done.2, bf16[4,2,32,2048]{3,2,1,0:T(8,128)(2,1)S(1)} %collective-permute-done.7.refs_0_, bf16[4,2,32,2048]{3,2,1,0:T(8,128)(2,1)S(1)} %collective-permute-done.10.refs_1_, bf16[2,4096,768]{2,1,0:T(8,128)(2,1)S(1)} %get-tuple-element.56.refs_2_), custom_call_target="tpu_custom_call" | custom-call | flops 1 | bytes 1 | tf_op jit(solution)/shard_map/pallas_call | solution.py:285
  74.4 2.3 %shard_map.78.refs_5_ = f32[2,256,768]{2,1,0:T(8,128)S(1)} custom-call(s32[3]{0:T(128)S(1)} %copy-done.2, bf16[4,2,32,2048]{3,2,1,0:T(8,128)(2,1)S(1)} %collective-permute-done.12.refs_0_, bf16[4,2,32,2048]{3,2,1,0:T(8,128)(2,1)S(1)} %collective-permute-done.13.refs_1_, bf16[2,4096,768]{2,1,0:T(8,128)(2,1)S(1)} %get-tuple-element.56.refs_2_), custom_call_target="tpu_custom_call" | custom-call | flops 1 | bytes 1 | tf_op jit(solution)/shard_map/pallas_call | solution.py:285
  76.8 2.5 %shard_map.79.hidden_ref = bf16[2,512,384]{2,1,0:T(8,128)(2,1)S(1)} custom-call(s32[3]{0:T(128)S(1)} %copy-done.2, bf16[4,2,32,2048]{3,2,1,0:T(8,128)(2,1)S(1)} %collective-permute-done.9.refs_0_, bf16[4,2,32,2048]{3,2,1,0:T(8,128)(2,1)S(1)} %collective-permute-done.11.refs_1_, bf16[2,4096,768]{2,1,0:T(8,128)(2,1)S(1)} %get-tuple-element.56.refs_2_, ...), custom_call_target="tpu_custom_call" | custom-call | flops 1610612736 | bytes 4000000 | tf_op jit(solution)/shard_map/pallas_call | solution.py:299
  79.3 1.8 %shard_map.81 = (bf16[4,2,32,1024]{3,2,1,0:T(8,128)(2,1)S(1)}, bf16[4,2,32,1024]{3,2,1,0:T(8,128)(2,1)S(1)}, bf16[4,2,32,1024]{3,2,1,0:T(8,128)(2,1)S(1)}, bf16[4,2,32,1024]{3,2,1,0:T(8,128)(2,1)S(1)}) custom-call(s32[3]{0:T(128)S(1)} %copy-done.2, bf16[2,512,384]{2,1,0:T(8,128)(2,1)S(1)} %shard_map.79.hidden_ref, bf16[2,384,4096]{2,1,0:T(8,128)(2,1)S(1)} %bitcast.7), custom_call_target="tpu_custom_call" | custom-call | flops 805306368 | bytes 5000000 | tf_op jit(solution)/shard_map/pallas_call | solution.py:312
  82.3 1.8 %shard_map.80 = (bf16[4,2,32,1024]{3,2,1,0:T(8,128)(2,1)S(1)}, bf16[4,2,32,1024]{3,2,1,0:T(8,128)(2,1)S(1)}, bf16[4,2,32,1024]{3,2,1,0:T(8,128)(2,1)S(1)}, bf16[4,2,32,1024]{3,2,1,0:T(8,128)(2,1)S(1)}) custom-call(s32[3]{0:T(128)S(1)} %copy-done.2, bf16[2,512,384]{2,1,0:T(8,128)(2,1)S(1)} %shard_map.79.hidden_ref, bf16[2,384,4096]{2,1,0:T(8,128)(2,1)S(1)} %bitcast.7), custom_call_target="tpu_custom_call" | custom-call | flops 805306368 | bytes 5000000 | tf_op jit(solution)/shard_map/pallas_call | solution.py:312
  85.5 1.8 %shard_map.84 = (bf16[4,2,32,1024]{3,2,1,0:T(8,128)(2,1)S(1)}, bf16[4,2,32,1024]{3,2,1,0:T(8,128)(2,1)S(1)}, bf16[4,2,32,1024]{3,2,1,0:T(8,128)(2,1)S(1)}, bf16[4,2,32,1024]{3,2,1,0:T(8,128)(2,1)S(1)}) custom-call(s32[3]{0:T(128)S(1)} %copy-done.2, bf16[2,512,384]{2,1,0:T(8,128)(2,1)S(1)} %shard_map.79.hidden_ref, bf16[2,384,4096]{2,1,0:T(8,128)(2,1)S(1)} %bitcast.7, ...), custom_call_target="tpu_custom_call" | custom-call | flops 805306368 | bytes 5000000 | tf_op jit(solution)/shard_map/pallas_call | solution.py:312
  87.4 1.9 %collective-permute-start.29 = (bf16[4,2,32,1024]{3,2,1,0:T(8,128)(2,1)S(1)}, bf16[4,2,32,1024]{3,2,1,0:T(8,128)(2,1)S(1)}, u32[]{:S(2)}, u32[]{:S(2)}) collective-permute-start(bf16[4,2,32,1024]{3,2,1,0:T(8,128)(2,1)S(1)} %get-tuple-element.79), channel_id=1, source_target_pairs={{0,2},{1,17},{4,6},{5,21},{2,0},{3,19},{6,4},{7,23},{8,10},{9,25},... | collective-permute-start | bytes 1572872 | tf_op jit(solution)/shard_map/ppermute | solution.py:35
  89.4 2.8 %collective-permute-start.30 = (bf16[4,2,32,1024]{3,2,1,0:T(8,128)(2,1)S(1)}, bf16[4,2,32,1024]{3,2,1,0:T(8,128)(2,1)S(1)}, u32[]{:S(2)}, u32[]{:S(2)}) collective-permute-start(bf16[4,2,32,1024]{3,2,1,0:T(8,128)(2,1)S(1)} %get-tuple-element.80), channel_id=1, source_target_pairs={{0,6},{1,25},{4,2},{5,29},{2,4},{3,27},{6,0},{7,31},{8,14},{9,17},... | collective-permute-start | bytes 1572872 | tf_op jit(solution)/shard_map/ppermute | solution.py:36
  92.1 1.8 %shard_map.82 = (bf16[4,2,32,1024]{3,2,1,0:T(8,128)(2,1)S(1)}, bf16[4,2,32,1024]{3,2,1,0:T(8,128)(2,1)S(1)}, bf16[4,2,32,1024]{3,2,1,0:T(8,128)(2,1)S(1)}, bf16[4,2,32,1024]{3,2,1,0:T(8,128)(2,1)S(1)}) custom-call(s32[3]{0:T(128)S(1)} %copy-done.2, bf16[2,512,384]{2,1,0:T(8,128)(2,1)S(1)} %shard_map.79.hidden_ref, bf16[2,384,4096]{2,1,0:T(8,128)(2,1)S(1)} %bitcast.7, ...), custom_call_target="tpu_custom_call" | custom-call | flops 805306368 | bytes 5000000 | tf_op jit(solution)/shard_map/pallas_call | solution.py:312
  94.0 1.9 %collective-permute-start.19 = (bf16[4,2,32,1024]{3,2,1,0:T(8,128)(2,1)S(1)}, bf16[4,2,32,1024]{3,2,1,0:T(8,128)(2,1)S(1)}, u32[]{:S(2)}, u32[]{:S(2)}) collective-permute-start(bf16[4,2,32,1024]{3,2,1,0:T(8,128)(2,1)S(1)} %get-tuple-element.68), channel_id=1, source_target_pairs={{0,2},{1,17},{4,6},{5,21},{2,0},{3,19},{6,4},{7,23},{8,10},{9,25},... | collective-permute-start | bytes 1572872 | tf_op jit(solution)/shard_map/ppermute | solution.py:35
  96.6 2.1 %collective-permute-start.20 = (bf16[4,2,32,1024]{3,2,1,0:T(8,128)(2,1)S(1)}, bf16[4,2,32,1024]{3,2,1,0:T(8,128)(2,1)S(1)}, u32[]{:S(2)}, u32[]{:S(2)}) collective-permute-start(bf16[4,2,32,1024]{3,2,1,0:T(8,128)(2,1)S(1)} %get-tuple-element.69), channel_id=1, source_target_pairs={{0,6},{1,25},{4,2},{5,29},{2,4},{3,27},{6,0},{7,31},{8,14},{9,17},... | collective-permute-start | bytes 1572872 | tf_op jit(solution)/shard_map/ppermute | solution.py:36
  98.7 3.5 %collective-permute-done.29.refs_2_ = bf16[4,2,32,1024]{3,2,1,0:T(8,128)(2,1)S(1)} collective-permute-done((bf16[4,2,32,1024]{3,2,1,0:T(8,128)(2,1)S(1)}, bf16[4,2,32,1024]{3,2,1,0:T(8,128)(2,1)S(1)}, u32[]{:S(2)}, u32[]{:S(2)}) %collective-permute-start.29) | collective-permute-done | bytes 524320 | tf_op jit(solution)/shard_map/ppermute | solution.py:35
  102.2 3.1 %collective-permute-done.30.refs_3_ = bf16[4,2,32,1024]{3,2,1,0:T(8,128)(2,1)S(1)} collective-permute-done((bf16[4,2,32,1024]{3,2,1,0:T(8,128)(2,1)S(1)}, bf16[4,2,32,1024]{3,2,1,0:T(8,128)(2,1)S(1)}, u32[]{:S(2)}, u32[]{:S(2)}) %collective-permute-start.30) | collective-permute-done | bytes 524320 | tf_op jit(solution)/shard_map/ppermute | solution.py:36
  106.2 1.7 %collective-permute-start.32 = (bf16[128,1024]{1,0:T(8,128)(2,1)S(1)}, bf16[128,1024]{1,0:T(8,128)(2,1)S(1)}, u32[]{:S(2)}, u32[]{:S(2)}) collective-permute-start(bf16[128,1024]{1,0:T(8,128)(2,1)S(1)} %get-tuple-element.83), channel_id=1, source_target_pairs={{0,16},{1,3},{4,20},{5,7},{2,18},{3,1},{6,22},{7,5},{8,24},{9,11},... | collective-permute-start | bytes 786440 | tf_op jit(solution)/shard_map/ppermute | solution.py:35
  108.1 2.7 %collective-permute-start.33 = (bf16[128,1024]{1,0:T(8,128)(2,1)S(1)}, bf16[128,1024]{1,0:T(8,128)(2,1)S(1)}, u32[]{:S(2)}, u32[]{:S(2)}) collective-permute-start(bf16[128,1024]{1,0:T(8,128)(2,1)S(1)} %get-tuple-element.84), channel_id=1, source_target_pairs={{0,24},{1,7},{4,28},{5,3},{2,26},{3,5},{6,30},{7,1},{8,16},{9,15},... | collective-permute-start | bytes 786440 | tf_op jit(solution)/shard_map/ppermute | solution.py:36
  110.9 8.2 %collective-permute-done.19.refs_2_ = bf16[4,2,32,1024]{3,2,1,0:T(8,128)(2,1)S(1)} collective-permute-done((bf16[4,2,32,1024]{3,2,1,0:T(8,128)(2,1)S(1)}, bf16[4,2,32,1024]{3,2,1,0:T(8,128)(2,1)S(1)}, u32[]{:S(2)}, u32[]{:S(2)}) %collective-permute-start.19) | collective-permute-done | bytes 524320 | tf_op jit(solution)/shard_map/ppermute | solution.py:35
  119.1 1.6 %collective-permute-done.20.refs_3_ = bf16[4,2,32,1024]{3,2,1,0:T(8,128)(2,1)S(1)} collective-permute-done((bf16[4,2,32,1024]{3,2,1,0:T(8,128)(2,1)S(1)}, bf16[4,2,32,1024]{3,2,1,0:T(8,128)(2,1)S(1)}, u32[]{:S(2)}, u32[]{:S(2)}) %collective-permute-start.20) | collective-permute-done | bytes 524320 | tf_op jit(solution)/shard_map/ppermute | solution.py:36
  121.5 2.1 %collective-permute-start.22 = (bf16[128,1024]{1,0:T(8,128)(2,1)S(1)}, bf16[128,1024]{1,0:T(8,128)(2,1)S(1)}, u32[]{:S(2)}, u32[]{:S(2)}) collective-permute-start(bf16[128,1024]{1,0:T(8,128)(2,1)S(1)} %get-tuple-element.72), channel_id=1, source_target_pairs={{0,16},{1,3},{4,20},{5,7},{2,18},{3,1},{6,22},{7,5},{8,24},{9,11},... | collective-permute-start | bytes 786440 | tf_op jit(solution)/shard_map/ppermute | solution.py:35
  123.7 2.5 %collective-permute-start.23 = (bf16[128,1024]{1,0:T(8,128)(2,1)S(1)}, bf16[128,1024]{1,0:T(8,128)(2,1)S(1)}, u32[]{:S(2)}, u32[]{:S(2)}) collective-permute-start(bf16[128,1024]{1,0:T(8,128)(2,1)S(1)} %get-tuple-element.73), channel_id=1, source_target_pairs={{0,24},{1,7},{4,28},{5,3},{2,26},{3,5},{6,30},{7,1},{8,16},{9,15},... | collective-permute-start | bytes 786440 | tf_op jit(solution)/shard_map/ppermute | solution.py:36
  126.4 1.5 %collective-permute-done.21 = bf16[128,1024]{1,0:T(8,128)(2,1)S(1)} collective-permute-done((bf16[128,1024]{1,0:T(8,128)(2,1)S(1)}, bf16[128,1024]{1,0:T(8,128)(2,1)S(1)}, u32[]{:S(2)}, u32[]{:S(2)}) %collective-permute-start.21) | collective-permute-done | bytes 262176 | tf_op jit(solution)/shard_map/ppermute | solution.py:36
  127.9 3.0 %collective-permute-done.22 = bf16[128,1024]{1,0:T(8,128)(2,1)S(1)} collective-permute-done((bf16[128,1024]{1,0:T(8,128)(2,1)S(1)}, bf16[128,1024]{1,0:T(8,128)(2,1)S(1)}, u32[]{:S(2)}, u32[]{:S(2)}) %collective-permute-start.22) | collective-permute-done | bytes 262176 | tf_op jit(solution)/shard_map/ppermute | solution.py:35
  130.9 2.7 %collective-permute-done.23 = bf16[128,1024]{1,0:T(8,128)(2,1)S(1)} collective-permute-done((bf16[128,1024]{1,0:T(8,128)(2,1)S(1)}, bf16[128,1024]{1,0:T(8,128)(2,1)S(1)}, u32[]{:S(2)}, u32[]{:S(2)}) %collective-permute-start.23) | collective-permute-done | bytes 262176 | tf_op jit(solution)/shard_map/ppermute | solution.py:36
  134.4 1.4 collective-permute-start.35
  135.9 2.2 %collective-permute-start.36 = (bf16[32,2048]{1,0:T(8,128)(2,1)S(1)}, bf16[32,2048]{1,0:T(8,128)(2,1)S(1)}, u32[]{:S(2)}, u32[]{:S(2)}) collective-permute-start(bf16[32,2048]{1,0:T(8,128)(2,1)S(1)} %get-tuple-element.90), channel_id=1, source_target_pairs={{0,64},{1,65},{4,68},{5,69},{2,66},{3,67},{6,70},{7,71},{8,72},{9,... | collective-permute-start | bytes 393224 | tf_op jit(solution)/shard_map/ppermute | solution.py:41
  138.9 1.7 %collective-permute-done.35 = bf16[32,2048]{1,0:T(8,128)(2,1)S(1)} collective-permute-done((bf16[32,2048]{1,0:T(8,128)(2,1)S(1)}, bf16[32,2048]{1,0:T(8,128)(2,1)S(1)}, u32[]{:S(2)}, u32[]{:S(2)}) %collective-permute-start.35) | collective-permute-done | bytes 131104 | tf_op jit(solution)/shard_map/ppermute | solution.py:43
  140.6 1.7 %collective-permute-done.36 = bf16[32,2048]{1,0:T(8,128)(2,1)S(1)} collective-permute-done((bf16[32,2048]{1,0:T(8,128)(2,1)S(1)}, bf16[32,2048]{1,0:T(8,128)(2,1)S(1)}, u32[]{:S(2)}, u32[]{:S(2)}) %collective-permute-start.36) | collective-permute-done | bytes 131104 | tf_op jit(solution)/shard_map/ppermute | solution.py:41
  142.5 1.2 collective-permute-done.37
  (72 shorter events, 11.8 us)
Async XLA Ops:
  2.7 1.5 %collective-permute-start = (bf16[16,2176]{1,0:T(8,128)(2,1)}, bf16[16,2176]{1,0:T(8,128)(2,1)S(1)}, u32[]{:S(2)}, u32[]{:S(2)}) collective-permute-start(bf16[16,2176]{1,0:T(8,128)(2,1)} %get-tuple-element.46), channel_id=1, source_target_pairs={{0,1},{1,0},{2,3},{3,2},{4,5},{5,4},{6,7},{7,6},{8,9},{9,8},{10,11... | collective-permute-start | bytes 208904 | tf_op jit(solution)/shard_map/ppermute | solution.py:49
  5.1 5.7 %collective-permute-start.1 = (bf16[32,2176]{1,0:T(8,128)(2,1)S(1)}, bf16[32,2176]{1,0:T(8,128)(2,1)S(1)}, u32[]{:S(2)}, u32[]{:S(2)}) collective-permute-start(bf16[32,2176]{1,0:T(8,128)(2,1)S(1)} %pad_maximum_fusion.1), channel_id=1, source_target_pairs={{0,32},{1,97},{4,36},{5,101},{2,34},{3,99},{6,38},{7,103},{8,40},{... | collective-permute-start | bytes 417800 | tf_op jit(solution)/shard_map/ppermute | solution.py:42
  7.2 8.4 %collective-permute-start.2 = (bf16[32,2176]{1,0:T(8,128)(2,1)S(1)}, bf16[32,2176]{1,0:T(8,128)(2,1)S(1)}, u32[]{:S(2)}, u32[]{:S(2)}) collective-permute-start(bf16[32,2176]{1,0:T(8,128)(2,1)S(1)} %pad_maximum_fusion.1), channel_id=1, source_target_pairs={{0,96},{1,33},{4,100},{5,37},{2,98},{3,35},{6,102},{7,39},{8,104},... | collective-permute-start | bytes 417800 | tf_op jit(solution)/shard_map/ppermute | solution.py:43
  9.7 7.8 %collective-permute-start.3 = (bf16[32,2176]{1,0:T(8,128)(2,1)S(1)}, bf16[32,2176]{1,0:T(8,128)(2,1)S(1)}, u32[]{:S(2)}, u32[]{:S(2)}) collective-permute-start(bf16[32,2176]{1,0:T(8,128)(2,1)S(1)} %pad_maximum_fusion.1), channel_id=1, source_target_pairs={{0,64},{1,65},{4,68},{5,69},{2,66},{3,67},{6,70},{7,71},{8,72},{9,... | collective-permute-start | bytes 417800 | tf_op jit(solution)/shard_map/ppermute | solution.py:41
  17.6 9.6 %collective-permute-start.4 = (bf16[128,2176]{1,0:T(8,128)(2,1)S(1)}, bf16[128,2176]{1,0:T(8,128)(2,1)S(1)}, u32[]{:S(2)}, u32[]{:S(2)}) collective-permute-start(bf16[128,2176]{1,0:T(8,128)(2,1)S(1)} %select_dynamic-update-slice_fusion.refs_0_), channel_id=1, source_target_pairs={{0,8},{1,5},{4,12},{5,1},{2,10},{3,7},{6,14},{7,3},{8,0},{9,13},{1... | collective-permute-start | bytes 1671176 | tf_op jit(solution)/shard_map/ppermute | solution.py:36
  19.3 16.5 %collective-permute-start.5 = (bf16[128,2176]{1,0:T(8,128)(2,1)S(1)}, bf16[128,2176]{1,0:T(8,128)(2,1)S(1)}, u32[]{:S(2)}, u32[]{:S(2)}) collective-permute-start(bf16[128,2176]{1,0:T(8,128)(2,1)S(1)} %select_dynamic-update-slice_fusion.refs_0_), channel_id=1, source_target_pairs={{0,16},{1,3},{4,20},{5,7},{2,18},{3,1},{6,22},{7,5},{8,24},{9,11},... | collective-permute-start | bytes 1671176 | tf_op jit(solution)/shard_map/ppermute | solution.py:35
  22.2 16.7 %collective-permute-start.6 = (bf16[128,2176]{1,0:T(8,128)(2,1)S(1)}, bf16[128,2176]{1,0:T(8,128)(2,1)S(1)}, u32[]{:S(2)}, u32[]{:S(2)}) collective-permute-start(bf16[128,2176]{1,0:T(8,128)(2,1)S(1)} %select_dynamic-update-slice_fusion.refs_0_), channel_id=1, source_target_pairs={{0,24},{1,7},{4,28},{5,3},{2,26},{3,5},{6,30},{7,1},{8,16},{9,15},... | collective-permute-start | bytes 1671176 | tf_op jit(solution)/shard_map/ppermute | solution.py:36
  40.5 14.9 %collective-permute-start.8 = (bf16[4,2,32,2048]{3,2,1,0:T(8,128)(2,1)S(1)}, bf16[4,2,32,2048]{3,2,1,0:T(8,128)(2,1)S(1)}, u32[]{:S(2)}, u32[]{:S(2)}) collective-permute-start(bf16[4,2,32,2048]{3,2,1,0:T(8,128)(2,1)S(1)} %get-tuple-element.53), channel_id=1, source_target_pairs={{0,4},{1,9},{4,0},{5,13},{2,6},{3,11},{6,2},{7,15},{8,12},{9,1},{1... | collective-permute-start | bytes 3145736 | tf_op jit(solution)/shard_map/ppermute | solution.py:36
  42.1 26.8 %collective-permute-start.7 = (bf16[4,2,32,2048]{3,2,1,0:T(8,128)(2,1)S(1)}, bf16[4,2,32,2048]{3,2,1,0:T(8,128)(2,1)S(1)}, u32[]{:S(2)}, u32[]{:S(2)}) collective-permute-start(bf16[4,2,32,2048]{3,2,1,0:T(8,128)(2,1)S(1)} %get-tuple-element.52), channel_id=1, source_target_pairs={{0,2},{1,17},{4,6},{5,21},{2,0},{3,19},{6,4},{7,23},{8,10},{9,25},... | collective-permute-start | bytes 3145736 | tf_op jit(solution)/shard_map/ppermute | solution.py:35
  44.8 27.2 %collective-permute-start.10 = (bf16[4,2,32,2048]{3,2,1,0:T(8,128)(2,1)S(1)}, bf16[4,2,32,2048]{3,2,1,0:T(8,128)(2,1)S(1)}, u32[]{:S(2)}, u32[]{:S(2)}) collective-permute-start(bf16[4,2,32,2048]{3,2,1,0:T(8,128)(2,1)S(1)} %get-tuple-element.58), channel_id=1, source_target_pairs={{0,6},{1,25},{4,2},{5,29},{2,4},{3,27},{6,0},{7,31},{8,14},{9,17},... | collective-permute-start | bytes 3145736 | tf_op jit(solution)/shard_map/ppermute | solution.py:36
  45.3 29.1 %collective-permute-start.12 = (bf16[4,2,32,2048]{3,2,1,0:T(8,128)(2,1)S(1)}, bf16[4,2,32,2048]{3,2,1,0:T(8,128)(2,1)S(1)}, u32[]{:S(2)}, u32[]{:S(2)}) collective-permute-start(bf16[4,2,32,2048]{3,2,1,0:T(8,128)(2,1)S(1)} %get-tuple-element.47.refs_0_), channel_id=1, source_target_pairs={{0,1},{1,0},{2,3},{3,2},{4,5},{5,4},{6,7},{7,6},{8,9},{9,8},{10,11... | collective-permute-start | bytes 3145736 | tf_op jit(solution)/shard_map/ppermute | solution.py:49
  45.3 2.8 %copy-start = (bf16[2,4096,384]{2,1,0:T(8,128)(2,1)S(1)}, bf16[2,4096,384]{2,1,0:T(8,128)(2,1)}, u32[]{:S(2)}) copy-start(bf16[2,4096,384]{2,1,0:T(8,128)(2,1)} %gate_ref) | copy-start | bytes 18874372
  48.0 2.8 %copy-start.1 = (bf16[2,4096,384]{2,1,0:T(8,128)(2,1)S(1)}, bf16[2,4096,384]{2,1,0:T(8,128)(2,1)}, u32[]{:S(2)}) copy-start(bf16[2,4096,384]{2,1,0:T(8,128)(2,1)} %up_ref) | copy-start | bytes 18874372
  50.8 4.5 %copy-start.2 = (s32[3]{0:T(128)S(1)}, s32[3]{0:T(128)}, u32[]{:S(2)}) copy-start(s32[3]{0:T(128)} %pad_add_fusion.core_ref.base_ref) | copy-start | bytes 40
  55.4 19.0 %collective-permute-start.13 = (bf16[4,2,32,2048]{3,2,1,0:T(8,128)(2,1)S(1)}, bf16[4,2,32,2048]{3,2,1,0:T(8,128)(2,1)S(1)}, u32[]{:S(2)}, u32[]{:S(2)}) collective-permute-start(bf16[4,2,32,2048]{3,2,1,0:T(8,128)(2,1)S(1)} %collective-permute-done.8.refs_1_), channel_id=1, source_target_pairs={{0,1},{1,0},{2,3},{3,2},{4,5},{5,4},{6,7},{7,6},{8,9},{9,8},{10,11... | collective-permute-start | bytes 3145736 | tf_op jit(solution)/shard_map/ppermute | solution.py:49
  68.9 7.9 %collective-permute-start.9 = (bf16[4,2,32,2048]{3,2,1,0:T(8,128)(2,1)S(1)}, bf16[4,2,32,2048]{3,2,1,0:T(8,128)(2,1)S(1)}, u32[]{:S(2)}, u32[]{:S(2)}) collective-permute-start(bf16[4,2,32,2048]{3,2,1,0:T(8,128)(2,1)S(1)} %collective-permute-done.7.refs_0_), channel_id=1, source_target_pairs={{0,1},{1,0},{2,3},{3,2},{4,5},{5,4},{6,7},{7,6},{8,9},{9,8},{10,11... | collective-permute-start | bytes 3145736 | tf_op jit(solution)/shard_map/ppermute | solution.py:49
  72.0 4.8 %collective-permute-start.11 = (bf16[4,2,32,2048]{3,2,1,0:T(8,128)(2,1)S(1)}, bf16[4,2,32,2048]{3,2,1,0:T(8,128)(2,1)S(1)}, u32[]{:S(2)}, u32[]{:S(2)}) collective-permute-start(bf16[4,2,32,2048]{3,2,1,0:T(8,128)(2,1)S(1)} %collective-permute-done.10.refs_1_), channel_id=1, source_target_pairs={{0,1},{1,0},{2,3},{3,2},{4,5},{5,4},{6,7},{7,6},{8,9},{9,8},{10,11... | collective-permute-start | bytes 3145736 | tf_op jit(solution)/shard_map/ppermute | solution.py:49
  74.4 4.9 %slice-start = ((s8[6291456]{0:T(1024)(128)(4,1)}), s8[4194304]{0:T(1024)(128)(4,1)S(1)}, s32[]{:S(2)}) async-start(s8[6291456]{0:T(1024)(128)(4,1)} %bitcast.6), calls=%async_computation | async-start | bytes 8388608
  76.8 2.6 %slice-start.1 = ((s8[6291456]{0:T(1024)(128)(4,1)}), s8[2097152]{0:T(1024)(128)(4,1)S(1)}, s32[]{:S(2)}) async-start(s8[6291456]{0:T(1024)(128)(4,1)} %bitcast.6), calls=%async_computation.1 | async-start | bytes 4194304
  81.1 3.5 %collective-permute-start.24 = (bf16[4,2,32,1024]{3,2,1,0:T(8,128)(2,1)S(1)}, bf16[4,2,32,1024]{3,2,1,0:T(8,128)(2,1)S(1)}, u32[]{:S(2)}, u32[]{:S(2)}) collective-permute-start(bf16[4,2,32,1024]{3,2,1,0:T(8,128)(2,1)S(1)} %get-tuple-element.61), channel_id=1, source_target_pairs={{0,1},{1,0},{2,3},{3,2},{4,5},{5,4},{6,7},{7,6},{8,9},{9,8},{10,11... | collective-permute-start | bytes 1572872 | tf_op jit(solution)/shard_map/ppermute | solution.py:49
  81.7 3.0 %collective-permute-start.25 = (bf16[4,2,32,1024]{3,2,1,0:T(8,128)(2,1)S(1)}, bf16[4,2,32,1024]{3,2,1,0:T(8,128)(2,1)S(1)}, u32[]{:S(2)}, u32[]{:S(2)}) collective-permute-start(bf16[4,2,32,1024]{3,2,1,0:T(8,128)(2,1)S(1)} %get-tuple-element.74), channel_id=1, source_target_pairs={{0,1},{1,0},{2,3},{3,2},{4,5},{5,4},{6,7},{7,6},{8,9},{9,8},{10,11... | collective-permute-start | bytes 1572872 | tf_op jit(solution)/shard_map/ppermute | solution.py:49
  81.8 3.3 %collective-permute-start.26 = (bf16[4,2,32,1024]{3,2,1,0:T(8,128)(2,1)S(1)}, bf16[4,2,32,1024]{3,2,1,0:T(8,128)(2,1)S(1)}, u32[]{:S(2)}, u32[]{:S(2)}) collective-permute-start(bf16[4,2,32,1024]{3,2,1,0:T(8,128)(2,1)S(1)} %get-tuple-element.75), channel_id=1, source_target_pairs={{0,1},{1,0},{2,3},{3,2},{4,5},{5,4},{6,7},{7,6},{8,9},{9,8},{10,11... | collective-permute-start | bytes 1572872 | tf_op jit(solution)/shard_map/ppermute | solution.py:49
  82.2 3.3 %collective-permute-start.27 = (bf16[4,2,32,1024]{3,2,1,0:T(8,128)(2,1)S(1)}, bf16[4,2,32,1024]{3,2,1,0:T(8,128)(2,1)S(1)}, u32[]{:S(2)}, u32[]{:S(2)}) collective-permute-start(bf16[4,2,32,1024]{3,2,1,0:T(8,128)(2,1)S(1)} %get-tuple-element.76), channel_id=1, source_target_pairs={{0,1},{1,0},{2,3},{3,2},{4,5},{5,4},{6,7},{7,6},{8,9},{9,8},{10,11... | collective-permute-start | bytes 1572872 | tf_op jit(solution)/shard_map/ppermute | solution.py:49
  84.1 3.3 %collective-permute-start.14 = (bf16[4,2,32,1024]{3,2,1,0:T(8,128)(2,1)S(1)}, bf16[4,2,32,1024]{3,2,1,0:T(8,128)(2,1)S(1)}, u32[]{:S(2)}, u32[]{:S(2)}) collective-permute-start(bf16[4,2,32,1024]{3,2,1,0:T(8,128)(2,1)S(1)} %get-tuple-element.60), channel_id=1, source_target_pairs={{0,1},{1,0},{2,3},{3,2},{4,5},{5,4},{6,7},{7,6},{8,9},{9,8},{10,11... | collective-permute-start | bytes 1572872 | tf_op jit(solution)/shard_map/ppermute | solution.py:49
  84.6 4.7 %collective-permute-start.15 = (bf16[4,2,32,1024]{3,2,1,0:T(8,128)(2,1)S(1)}, bf16[4,2,32,1024]{3,2,1,0:T(8,128)(2,1)S(1)}, u32[]{:S(2)}, u32[]{:S(2)}) collective-permute-start(bf16[4,2,32,1024]{3,2,1,0:T(8,128)(2,1)S(1)} %get-tuple-element.63), channel_id=1, source_target_pairs={{0,1},{1,0},{2,3},{3,2},{4,5},{5,4},{6,7},{7,6},{8,9},{9,8},{10,11... | collective-permute-start | bytes 1572872 | tf_op jit(solution)/shard_map/ppermute | solution.py:49
  84.7 7.4 %collective-permute-start.16 = (bf16[4,2,32,1024]{3,2,1,0:T(8,128)(2,1)S(1)}, bf16[4,2,32,1024]{3,2,1,0:T(8,128)(2,1)S(1)}, u32[]{:S(2)}, u32[]{:S(2)}) collective-permute-start(bf16[4,2,32,1024]{3,2,1,0:T(8,128)(2,1)S(1)} %get-tuple-element.64), channel_id=1, source_target_pairs={{0,1},{1,0},{2,3},{3,2},{4,5},{5,4},{6,7},{7,6},{8,9},{9,8},{10,11... | collective-permute-start | bytes 1572872 | tf_op jit(solution)/shard_map/ppermute | solution.py:49
  85.2 7.0 %collective-permute-start.17 = (bf16[4,2,32,1024]{3,2,1,0:T(8,128)(2,1)S(1)}, bf16[4,2,32,1024]{3,2,1,0:T(8,128)(2,1)S(1)}, u32[]{:S(2)}, u32[]{:S(2)}) collective-permute-start(bf16[4,2,32,1024]{3,2,1,0:T(8,128)(2,1)S(1)} %get-tuple-element.65), channel_id=1, source_target_pairs={{0,1},{1,0},{2,3},{3,2},{4,5},{5,4},{6,7},{7,6},{8,9},{9,8},{10,11... | collective-permute-start | bytes 1572872 | tf_op jit(solution)/shard_map/ppermute | solution.py:49
  87.3 9.3 %collective-permute-start.28 = (bf16[4,2,32,1024]{3,2,1,0:T(8,128)(2,1)S(1)}, bf16[4,2,32,1024]{3,2,1,0:T(8,128)(2,1)S(1)}, u32[]{:S(2)}, u32[]{:S(2)}) collective-permute-start(bf16[4,2,32,1024]{3,2,1,0:T(8,128)(2,1)S(1)} %get-tuple-element.78), channel_id=1, source_target_pairs={{0,4},{1,9},{4,0},{5,13},{2,6},{3,11},{6,2},{7,15},{8,12},{9,1},{1... | collective-permute-start | bytes 1572872 | tf_op jit(solution)/shard_map/ppermute | solution.py:36
  87.4 14.8 %collective-permute-start.29 = (bf16[4,2,32,1024]{3,2,1,0:T(8,128)(2,1)S(1)}, bf16[4,2,32,1024]{3,2,1,0:T(8,128)(2,1)S(1)}, u32[]{:S(2)}, u32[]{:S(2)}) collective-permute-start(bf16[4,2,32,1024]{3,2,1,0:T(8,128)(2,1)S(1)} %get-tuple-element.79), channel_id=1, source_target_pairs={{0,2},{1,17},{4,6},{5,21},{2,0},{3,19},{6,4},{7,23},{8,10},{9,25},... | collective-permute-start | bytes 1572872 | tf_op jit(solution)/shard_map/ppermute | solution.py:35
  89.4 16.0 %collective-permute-start.30 = (bf16[4,2,32,1024]{3,2,1,0:T(8,128)(2,1)S(1)}, bf16[4,2,32,1024]{3,2,1,0:T(8,128)(2,1)S(1)}, u32[]{:S(2)}, u32[]{:S(2)}) collective-permute-start(bf16[4,2,32,1024]{3,2,1,0:T(8,128)(2,1)S(1)} %get-tuple-element.80), channel_id=1, source_target_pairs={{0,6},{1,25},{4,2},{5,29},{2,4},{3,27},{6,0},{7,31},{8,14},{9,17},... | collective-permute-start | bytes 1572872 | tf_op jit(solution)/shard_map/ppermute | solution.py:36
  93.9 14.2 %collective-permute-start.18 = (bf16[4,2,32,1024]{3,2,1,0:T(8,128)(2,1)S(1)}, bf16[4,2,32,1024]{3,2,1,0:T(8,128)(2,1)S(1)}, u32[]{:S(2)}, u32[]{:S(2)}) collective-permute-start(bf16[4,2,32,1024]{3,2,1,0:T(8,128)(2,1)S(1)} %get-tuple-element.67), channel_id=1, source_target_pairs={{0,4},{1,9},{4,0},{5,13},{2,6},{3,11},{6,2},{7,15},{8,12},{9,1},{1... | collective-permute-start | bytes 1572872 | tf_op jit(solution)/shard_map/ppermute | solution.py:36
  94.0 25.1 %collective-permute-start.19 = (bf16[4,2,32,1024]{3,2,1,0:T(8,128)(2,1)S(1)}, bf16[4,2,32,1024]{3,2,1,0:T(8,128)(2,1)S(1)}, u32[]{:S(2)}, u32[]{:S(2)}) collective-permute-start(bf16[4,2,32,1024]{3,2,1,0:T(8,128)(2,1)S(1)} %get-tuple-element.68), channel_id=1, source_target_pairs={{0,2},{1,17},{4,6},{5,21},{2,0},{3,19},{6,4},{7,23},{8,10},{9,25},... | collective-permute-start | bytes 1572872 | tf_op jit(solution)/shard_map/ppermute | solution.py:35
  96.6 24.1 %collective-permute-start.20 = (bf16[4,2,32,1024]{3,2,1,0:T(8,128)(2,1)S(1)}, bf16[4,2,32,1024]{3,2,1,0:T(8,128)(2,1)S(1)}, u32[]{:S(2)}, u32[]{:S(2)}) collective-permute-start(bf16[4,2,32,1024]{3,2,1,0:T(8,128)(2,1)S(1)} %get-tuple-element.69), channel_id=1, source_target_pairs={{0,6},{1,25},{4,2},{5,29},{2,4},{3,27},{6,0},{7,31},{8,14},{9,17},... | collective-permute-start | bytes 1572872 | tf_op jit(solution)/shard_map/ppermute | solution.py:36
  106.1 17.6 %collective-permute-start.31 = (bf16[128,1024]{1,0:T(8,128)(2,1)S(1)}, bf16[128,1024]{1,0:T(8,128)(2,1)S(1)}, u32[]{:S(2)}, u32[]{:S(2)}) collective-permute-start(bf16[128,1024]{1,0:T(8,128)(2,1)S(1)} %get-tuple-element.82), channel_id=1, source_target_pairs={{0,8},{1,5},{4,12},{5,1},{2,10},{3,7},{6,14},{7,3},{8,0},{9,13},{1... | collective-permute-start | bytes 786440 | tf_op jit(solution)/shard_map/ppermute | solution.py:36
  106.2 20.0 %collective-permute-start.32 = (bf16[128,1024]{1,0:T(8,128)(2,1)S(1)}, bf16[128,1024]{1,0:T(8,128)(2,1)S(1)}, u32[]{:S(2)}, u32[]{:S(2)}) collective-permute-start(bf16[128,1024]{1,0:T(8,128)(2,1)S(1)} %get-tuple-element.83), channel_id=1, source_target_pairs={{0,16},{1,3},{4,20},{5,7},{2,18},{3,1},{6,22},{7,5},{8,24},{9,11},... | collective-permute-start | bytes 786440 | tf_op jit(solution)/shard_map/ppermute | solution.py:35
  108.1 18.1 %collective-permute-start.33 = (bf16[128,1024]{1,0:T(8,128)(2,1)S(1)}, bf16[128,1024]{1,0:T(8,128)(2,1)S(1)}, u32[]{:S(2)}, u32[]{:S(2)}) collective-permute-start(bf16[128,1024]{1,0:T(8,128)(2,1)S(1)} %get-tuple-element.84), channel_id=1, source_target_pairs={{0,24},{1,7},{4,28},{5,3},{2,26},{3,5},{6,30},{7,1},{8,16},{9,15},... | collective-permute-start | bytes 786440 | tf_op jit(solution)/shard_map/ppermute | solution.py:36
  121.4 6.5 %collective-permute-start.21 = (bf16[128,1024]{1,0:T(8,128)(2,1)S(1)}, bf16[128,1024]{1,0:T(8,128)(2,1)S(1)}, u32[]{:S(2)}, u32[]{:S(2)}) collective-permute-start(bf16[128,1024]{1,0:T(8,128)(2,1)S(1)} %get-tuple-element.71), channel_id=1, source_target_pairs={{0,8},{1,5},{4,12},{5,1},{2,10},{3,7},{6,14},{7,3},{8,0},{9,13},{1... | collective-permute-start | bytes 786440 | tf_op jit(solution)/shard_map/ppermute | solution.py:36
  121.5 9.4 %collective-permute-start.22 = (bf16[128,1024]{1,0:T(8,128)(2,1)S(1)}, bf16[128,1024]{1,0:T(8,128)(2,1)S(1)}, u32[]{:S(2)}, u32[]{:S(2)}) collective-permute-start(bf16[128,1024]{1,0:T(8,128)(2,1)S(1)} %get-tuple-element.72), channel_id=1, source_target_pairs={{0,16},{1,3},{4,20},{5,7},{2,18},{3,1},{6,22},{7,5},{8,24},{9,11},... | collective-permute-start | bytes 786440 | tf_op jit(solution)/shard_map/ppermute | solution.py:35
  123.7 10.0 %collective-permute-start.23 = (bf16[128,1024]{1,0:T(8,128)(2,1)S(1)}, bf16[128,1024]{1,0:T(8,128)(2,1)S(1)}, u32[]{:S(2)}, u32[]{:S(2)}) collective-permute-start(bf16[128,1024]{1,0:T(8,128)(2,1)S(1)} %get-tuple-element.73), channel_id=1, source_target_pairs={{0,24},{1,7},{4,28},{5,3},{2,26},{3,5},{6,30},{7,1},{8,16},{9,15},... | collective-permute-start | bytes 786440 | tf_op jit(solution)/shard_map/ppermute | solution.py:36
  133.9 5.0 %collective-permute-start.34 = (bf16[32,2048]{1,0:T(8,128)(2,1)S(1)}, bf16[32,2048]{1,0:T(8,128)(2,1)S(1)}, u32[]{:S(2)}, u32[]{:S(2)}) collective-permute-start(bf16[32,2048]{1,0:T(8,128)(2,1)S(1)} %get-tuple-element.89), channel_id=1, source_target_pairs={{0,32},{1,97},{4,36},{5,101},{2,34},{3,99},{6,38},{7,103},{8,40},{... | collective-permute-start | bytes 393224 | tf_op jit(solution)/shard_map/ppermute | solution.py:42
  134.4 6.2 %collective-permute-start.35 = (bf16[32,2048]{1,0:T(8,128)(2,1)S(1)}, bf16[32,2048]{1,0:T(8,128)(2,1)S(1)}, u32[]{:S(2)}, u32[]{:S(2)}) collective-permute-start(bf16[32,2048]{1,0:T(8,128)(2,1)S(1)} %get-tuple-element.91), channel_id=1, source_target_pairs={{0,96},{1,33},{4,100},{5,37},{2,98},{3,35},{6,102},{7,39},{8,104},... | collective-permute-start | bytes 393224 | tf_op jit(solution)/shard_map/ppermute | solution.py:43
  135.9 6.5 %collective-permute-start.36 = (bf16[32,2048]{1,0:T(8,128)(2,1)S(1)}, bf16[32,2048]{1,0:T(8,128)(2,1)S(1)}, u32[]{:S(2)}, u32[]{:S(2)}) collective-permute-start(bf16[32,2048]{1,0:T(8,128)(2,1)S(1)} %get-tuple-element.90), channel_id=1, source_target_pairs={{0,64},{1,65},{4,68},{5,69},{2,66},{3,67},{6,70},{7,71},{8,72},{9,... | collective-permute-start | bytes 393224 | tf_op jit(solution)/shard_map/ppermute | solution.py:41
  142.4 1.3 collective-permute-start.37

commit v5 on v4

--- a/solution.py
+++ b/solution.py
@@ -12,6 +12,8 @@
 META = 128
 CAP = 4
 BACK = 2
+ORDER = (2, 1, 3, 0)
+EARLY, LATE = (0, 1, 3), (2,)
 
 
 def place(z, y, x, core):
@@ -47,6 +49,14 @@
 def sibling(value):
     pairs = [(i, i ^ 1) for i in range(SIDE**3 * 2)]
     return lax.ppermute(value, AXES, pairs)
+
+
+def taken(pieces, order=ORDER):
+    return [pieces[j] for j in order]
+
+
+def placed(pieces, order=ORDER):
+    return [pieces[order.index(j)] for j in range(SIDE)]
 
 
 def prepare_kernel(core_ref, tokens_ref, ids_ref, weights_ref, placement_ref, kept_ref, sent_ref):
@@ -88,7 +98,7 @@
 
 
 def fetch_kernel(wanted_ref, gate_ref, up_ref, *refs, top, tok_count):
-    planes, (both_ref, high_ref, middle_ref, sems) = refs[:SIDE], refs[SIDE:]
+    planes, (both_ref, high_ref, middle_ref, sems) = placed(refs[:SIDE], ORDER[::-1]), refs[SIDE:]
     columns = gate_ref.shape[2]
     copies = [
         pltpu.make_async_copy(ref, both_ref.at[:, :, pl.ds(i * columns, columns)], sems.at[i])
@@ -120,7 +130,7 @@
 
 
 def pack_kernel(wanted_ref, *refs, top, tok_count):
-    planes, outs = refs[:SIDE], refs[SIDE:]
+    planes, outs = placed(refs[:SIDE], ORDER[::-1]), refs[SIDE:]
     wanted = wanted_ref[...]
     inside = same_block(planes[0].shape[0], wanted.shape[1], tok_count)
     share = wanted.shape[1] // SIDE
@@ -137,36 +147,34 @@
 
 
 def gate_kernel(base_ref, *refs, source):
-    pieces, (w_ref, total_ref, rows_ref) = refs[:2], refs[2:]
+    pieces, (w_ref, total_ref, rows_ref) = refs[:-3], refs[-3:]
+    for slot in range(w_ref.shape[0]):
+        total_ref[slot] = products(base_ref, slot, pieces, w_ref, rows_ref, source)
+
+
+def products(base_ref, slot, pieces, w_ref, rows_ref, source):
     step = rows_ref.shape[1]
     begin = pl.multiple_of(base_ref[0 if source == "own" else 1] * step, step)
-    count = rows_ref.shape[0] // 2
+    granule = pieces[0].shape[2]
+    for i, piece in enumerate(pieces):
+        for other in range(SIDE):
+            line = (i * SIDE + other) * granule
+            rows_ref[line : line + granule] = piece[other, slot]
+    return jnp.dot(rows_ref[...], w_ref[slot, pl.ds(begin, step)], preferred_element_type=jnp.float32)
+
+
+def hidden_kernel(base_ref, *refs):
+    pieces, (w_ref, own_early, own_late, sib_early, hidden_ref, rows_ref) = refs[: len(LATE)], refs[len(LATE) :]
+    granule, columns = pieces[0].shape[2], w_ref.shape[2] // 2
     for slot in range(w_ref.shape[0]):
-        for i, piece in enumerate(pieces):
-            for other in range(SIDE):
-                line = i * count + other * piece.shape[2]
-                rows_ref[line : line + piece.shape[2]] = piece[other, slot]
-        total_ref[slot] = jnp.dot(rows_ref[...], w_ref[slot, pl.ds(begin, step)], preferred_element_type=jnp.float32)
-
-
-def hidden_kernel(base_ref, *refs):
-    pieces, (w_ref, own_0, own_1, sib_0, hidden_ref, rows_ref) = refs[:2], refs[2:]
-    step = rows_ref.shape[1]
-    begin = pl.multiple_of(base_ref[1] * step, step)
-    granule, count, columns = pieces[0].shape[2], rows_ref.shape[0] // 2, w_ref.shape[2] // 2
-    for slot in range(w_ref.shape[0]):
-        for i, piece in enumerate(pieces):
-            for last in range(SIDE):
-                line = i * count + last * granule
-                rows_ref[line : line + granule] = piece[last, slot]
-        sib_1 = jnp.dot(rows_ref[...], w_ref[slot, pl.ds(begin, step)], preferred_element_type=jnp.float32)
+        sib_late = products(base_ref, slot, pieces, w_ref, rows_ref, "sibling")
         for last in range(SIDE):
-            own = own_0 if last < 2 else own_1
             for plane in range(SIDE):
-                line = last % 2 * count + plane * granule
-                across = plane % 2 * count + last * granule
-                sib = sib_0[slot, across : across + granule] if plane < 2 else sib_1[across : across + granule]
-                total = own[slot, line : line + granule] + sib
+                own = own_early if last in EARLY else own_late
+                line = ((EARLY if last in EARLY else LATE).index(last) * SIDE + plane) * granule
+                total = own[slot, line : line + granule]
+                line = ((EARLY if plane in EARLY else LATE).index(plane) * SIDE + last) * granule
+                total += sib_early[slot, line : line + granule] if plane in EARLY else sib_late[line : line + granule]
                 line = (last * SIDE + plane) * granule
                 hidden = jax.nn.silu(total[:, :columns]) * total[:, columns:]
                 hidden_ref[slot, line : line + granule] = hidden.astype(jnp.bfloat16)
@@ -190,7 +198,7 @@
 
 
 def unpack_kernel(high_ref, middle_ref, *refs):
-    pieces, outs = refs[:SIDE], refs[SIDE:]
+    pieces, outs = placed(refs[:SIDE]), refs[SIDE:]
     for p in range(SIDE):
         values = jnp.concatenate([piece[p].reshape(-1, piece.shape[3]) for piece in pieces])
         dense = jnp.dot(high_ref[p], values, preferred_element_type=jnp.float32)
@@ -260,7 +268,7 @@
         out_specs=whole(SIDE),
         compiler_params=params(),
         cost_estimate=cost(2 * SIDE * lines * near_count * half, 1e6),
-    )(wanted, *planes)
+    )(wanted, *taken(planes, ORDER[::-1]))
     own = exchange(packed, "xy")
 
     gate_w, up_w, _ = lax.optimization_barrier((w_gate, w_up, packed[0]))
@@ -277,34 +285,35 @@
         scratch_shapes=[pltpu.SemaphoreType.DMA((2,))],
         compiler_params=params(),
         cost_estimate=cost(1, 1),
-    )(wanted, gate_w, up_w, *planes)
+    )(wanted, gate_w, up_w, *taken(planes, ORDER[::-1]))
 
     own[1], gate_up = lax.optimization_barrier((own[1], gate_up))
 
     def project(source, pieces):
+        count = len(pieces) * SIDE * granule
         return pl.pallas_call(
             functools.partial(gate_kernel, source=source),
-            out_shape=jax.ShapeDtypeStruct((per_device, rows_count // 2, 2 * hidden_count), jnp.float32),
-            in_specs=scalar + whole(3),
+            out_shape=jax.ShapeDtypeStruct((per_device, count, 2 * hidden_count), jnp.float32),
+            in_specs=scalar + whole(len(pieces) + 1),
             out_specs=pl.BlockSpec(memory_space=pltpu.VMEM),
-            scratch_shapes=[pltpu.VMEM((rows_count // 2, half), jnp.bfloat16)],
+            scratch_shapes=[pltpu.VMEM((count, half), jnp.bfloat16)],
             compiler_params=params(),
             cost_estimate=cost(1, 1),
         )(base, *pieces, gate_up)
 
-    own_0 = project("own", own[:2])
-    sib_0 = project("sibling", [sibling(piece) for piece in own[:2]])
-    own[2], own_0 = lax.optimization_barrier((own[2], own_0))
-    own_1 = project("own", own[2:])
+    own_early = project("own", [own[j] for j in EARLY])
+    sib_early = project("sibling", [sibling(own[j]) for j in EARLY])
+    own[2], own_early, sib_early = lax.optimization_barrier((own[2], own_early, sib_early))
+    own_late = project("own", [own[j] for j in LATE])
     hidden = pl.pallas_call(
         hidden_kernel,
         out_shape=jax.ShapeDtypeStruct((per_device, rows_count, hidden_count), jnp.bfloat16),
-        in_specs=scalar + whole(6),
+        in_specs=scalar + whole(4 + len(LATE)),
         out_specs=pl.BlockSpec(memory_space=pltpu.VMEM),
-        scratch_shapes=[pltpu.VMEM((rows_count // 2, half), jnp.bfloat16)],
+        scratch_shapes=[pltpu.VMEM((len(LATE) * SIDE * granule, half), jnp.bfloat16)],
         compiler_params=params(),
         cost_estimate=cost(2 * per_device * rows_count * half * hidden_count, 4e6),
-    )(base, *[sibling(piece) for piece in own[2:]], gate_up, own_0, own_1, sib_0)
+    )(base, *[sibling(own[j]) for j in LATE], gate_up, own_early, own_late, sib_early)
 
     back_step = half // BACK
 
@@ -331,12 +340,12 @@
             in_specs=whole(2 + SIDE),
             out_specs=whole(SIDE),
             compiler_params=params(),
-        )(high, middle, *values)
-        sums.append(sum(piece.astype(jnp.float32) for piece in exchange(dense, "yx")))
+        )(high, middle, *taken(values))
+        sums.append(sum(piece.astype(jnp.float32) for piece in taken(exchange(dense, "yx"))))
     total = jnp.concatenate(sums, axis=1).reshape(SIDE, -1, half)
     sent = [total[0]] + [total[j].astype(jnp.bfloat16) for j in (1, 2, 3)]
     sent = exchange_z(sent, first_core)
-    total = sum(piece.astype(jnp.float32) for piece in sent).astype(jnp.bfloat16).reshape(2, tok_count, half)
+    total = sum(piece.astype(jnp.float32) for piece in taken(sent)).astype(jnp.bfloat16).reshape(2, tok_count, half)
     kept = jnp.where(first_core, total[0], total[1])
     got = sibling(jnp.where(first_core, total[1], total[0]))
     return jnp.concatenate([jnp.where(first_core, kept, got), jnp.where(first_core, got, kept)], axis=1)

time: 146 us -> 142 us (0.973)
  waiting for transfers between devices: 70.4 us -> 63.9 us
  starting transfers between devices: 39.9 us -> 42.5 us
    ppermute x6, waiting for transfers between devices: 34.5 us -> 23.3 us  [exchange(): over = lax.ppermute(value[2], AXES, partners(axes, 2))]
    ppermute x12, waiting for transfers between devices: 21.9 us -> 25 us  [exchange(): lax.ppermute(value[j], AXES, partners(axes, j))]
    ppermute x2, starting transfers between devices: 2.62 us -> 0.51 us  [exchange_z(): lax.ppermute(jnp.where(first_core, value[1], value[3]), AXES, partners('z...]
    ppermute x2, starting transfers between devices: 3.95 us -> 5.48 us  [exchange_z(): lax.ppermute(jnp.where(first_core, value[3], value[1]), AXES, partners('z...]
  transfers between devices with their start and end apart: 38 -> 38, of which waited for: 23 -> 23; matrix products, arithmetic and copies ran while one was open for 0% -> 0% of each run, Pallas kernels for 12% -> 13%
where the time goes in v5:
time: 142 us; the launch traced here: 141 us
  waiting for transfers between devices  63.9 us (45%)
  starting transfers between devices  42.5 us (30%)
  Pallas kernels  25.1 us (18%)
  local copies, waits for them, and re-layouts  5.8 us (4%)
  other arithmetic  3 us (2%)
    ppermute x12, waiting for transfers between devices, exchange(): lax.ppermute(value[j], AXES, partners(axes, j))  25 us
    ppermute x6, waiting for transfers between devices, exchange(): over = lax.ppermute(value[2], AXES, partners(axes, 2))  23.3 us
    ppermute x12, starting transfers between devices, exchange(): lax.ppermute(value[j], AXES, partners(axes, j))  15.4 us
    ppermute x6, starting transfers between devices, exchange(): over = lax.ppermute(value[2], AXES, partners(axes, 2))  13.8 us
    pallas_call x3, Pallas kernels, project(): pl.pallas_call(functools.partial(gate_kernel, source=source), out_shape=j...  7.87 us
    pallas_call x4, Pallas kernels, down(): pl.pallas_call(functools.partial(down_kernel, part=part, turned=turned),...  7.18 us
    ppermute x2, waiting for transfers between devices, exchange_z(): lax.ppermute(jnp.where(first_core, value[3], value[1]), AXES, partners('z...  6.23 us
    unnamed x11, local copies, waits for them, and re-layouts  5.6 us
  transfers between devices with their start and end apart: 38, of which 23 were waited for; matrix products, arithmetic and copies ran while one was open for 0% of the time, Pallas kernels for 13%

profile of v5, /device:TPU:0, one launch (start us, length us, event | category | flops | bytes accessed | tf_op | source)
XLA Modules:
  0.0 140.6 jit_solution(2797504961949024578)
XLA Ops:
  0.7 2.0 %shard_map.73 = (bf16[16,2176]{1,0:T(8,128)(2,1)}, bf16[16,2176]{1,0:T(8,128)(2,1)}) custom-call(s32[3]{0:T(128)} %pad_add_fusion.core_ref.base_ref, bf16[16,4096]{1,0:T(8,128)(2,1)} %tokens_ref.1, s32[8,16]{1,0:T(8,128)} %bitcast.8, f32[8,16]{1,0:T(8,128)} %bitcast.9, s32[1,64]{1,0:T(1,128)} %bitcast.10), custom_call_target="tpu_custom_call" | custom-call | tf_op jit(solution)/shard_map/pallas_call | solution.py:234
  2.7 1.5 %collective-permute-done = bf16[16,2176]{1,0:T(8,128)(2,1)S(1)} collective-permute-done((bf16[16,2176]{1,0:T(8,128)(2,1)}, bf16[16,2176]{1,0:T(8,128)(2,1)S(1)}, u32[]{:S(2)}, u32[]{:S(2)}) %collective-permute-start) | collective-permute-done | bytes 69664 | tf_op jit(solution)/shard_map/ppermute | solution.py:51
  5.1 4.2 %collective-permute-start.2 = (bf16[32,2176]{1,0:T(8,128)(2,1)S(1)}, bf16[32,2176]{1,0:T(8,128)(2,1)S(1)}, u32[]{:S(2)}, u32[]{:S(2)}) collective-permute-start(bf16[32,2176]{1,0:T(8,128)(2,1)S(1)} %pad_maximum_fusion.1), channel_id=1, source_target_pairs={{0,96},{1,33},{4,100},{5,37},{2,98},{3,35},{6,102},{7,39},{8,104},... | collective-permute-start | bytes 417800 | tf_op jit(solution)/shard_map/ppermute | solution.py:45
  9.3 1.6 %collective-permute-start.3 = (bf16[32,2176]{1,0:T(8,128)(2,1)S(1)}, bf16[32,2176]{1,0:T(8,128)(2,1)S(1)}, u32[]{:S(2)}, u32[]{:S(2)}) collective-permute-start(bf16[32,2176]{1,0:T(8,128)(2,1)S(1)} %pad_maximum_fusion.1), channel_id=1, source_target_pairs={{0,64},{1,65},{4,68},{5,69},{2,66},{3,67},{6,70},{7,71},{8,72},{9,... | collective-permute-start | bytes 417800 | tf_op jit(solution)/shard_map/ppermute | solution.py:43
  10.9 4.8 %collective-permute-done.2 = bf16[32,2176]{1,0:T(8,128)(2,1)S(1)} collective-permute-done((bf16[32,2176]{1,0:T(8,128)(2,1)S(1)}, bf16[32,2176]{1,0:T(8,128)(2,1)S(1)}, u32[]{:S(2)}, u32[]{:S(2)}) %collective-permute-start.2) | collective-permute-done | bytes 139296 | tf_op jit(solution)/shard_map/ppermute | solution.py:45
  15.7 1.7 %collective-permute-done.3 = bf16[32,2176]{1,0:T(8,128)(2,1)S(1)} collective-permute-done((bf16[32,2176]{1,0:T(8,128)(2,1)S(1)}, bf16[32,2176]{1,0:T(8,128)(2,1)S(1)}, u32[]{:S(2)}, u32[]{:S(2)}) %collective-permute-start.3) | collective-permute-done | bytes 139296 | tf_op jit(solution)/shard_map/ppermute | solution.py:43
  17.5 3.3 %collective-permute-start.6 = (bf16[128,2176]{1,0:T(8,128)(2,1)S(1)}, bf16[128,2176]{1,0:T(8,128)(2,1)S(1)}, u32[]{:S(2)}, u32[]{:S(2)}) collective-permute-start(bf16[128,2176]{1,0:T(8,128)(2,1)S(1)} %select_dynamic-update-slice_fusion.refs_0_), channel_id=1, source_target_pairs={{0,16},{1,3},{4,20},{5,7},{2,18},{3,1},{6,22},{7,5},{8,24},{9,11},... | collective-permute-start | bytes 1671176 | tf_op jit(solution)/shard_map/ppermute | solution.py:37
  22.2 6.5 %collective-permute-done.6.refs_3_ = bf16[128,2176]{1,0:T(8,128)(2,1)S(1)} collective-permute-done((bf16[128,2176]{1,0:T(8,128)(2,1)S(1)}, bf16[128,2176]{1,0:T(8,128)(2,1)S(1)}, u32[]{:S(2)}, u32[]{:S(2)}) %collective-permute-start.6) | collective-permute-done | bytes 557088 | tf_op jit(solution)/shard_map/ppermute | solution.py:37
  28.7 6.2 %collective-permute-done.5.refs_2_ = bf16[128,2176]{1,0:T(8,128)(2,1)S(1)} collective-permute-done((bf16[128,2176]{1,0:T(8,128)(2,1)S(1)}, bf16[128,2176]{1,0:T(8,128)(2,1)S(1)}, u32[]{:S(2)}, u32[]{:S(2)}) %collective-permute-start.5) | collective-permute-done | bytes 557088 | tf_op jit(solution)/shard_map/ppermute | solution.py:38
  35.0 1.6 %shard_map.74 = (bf16[4,2,32,2048]{3,2,1,0:T(8,128)(2,1)S(1)}, bf16[4,2,32,2048]{3,2,1,0:T(8,128)(2,1)S(1)}, bf16[4,2,32,2048]{3,2,1,0:T(8,128)(2,1)S(1)}, bf16[4,2,32,2048]{3,2,1,0:T(8,128)(2,1)S(1)}) custom-call(f32[1,256]{1,0:T(1,128)S(1)} %convert_element_type.47.wanted_ref, bf16[128,2176]{1,0:T(8,128)(2,1)S(1)} %select_dynamic-update-slice_fusion.refs_0_, ...), custom_call_target="tpu_custom_call" | custom-call | flops 536870912 | bytes 1000000 | tf_op jit(solution)/shard_map/pallas_call | solution.py:264
  36.6 1.6 %collective-permute-start.8 = (bf16[4,2,32,2048]{3,2,1,0:T(8,128)(2,1)S(1)}, bf16[4,2,32,2048]{3,2,1,0:T(8,128)(2,1)S(1)}, u32[]{:S(2)}, u32[]{:S(2)}) collective-permute-start(bf16[4,2,32,2048]{3,2,1,0:T(8,128)(2,1)S(1)} %get-tuple-element.54), channel_id=1, source_target_pairs={{0,4},{1,9},{4,0},{5,13},{2,6},{3,11},{6,2},{7,15},{8,12},{9,1},{1... | collective-permute-start | bytes 3145736 | tf_op jit(solution)/shard_map/ppermute | solution.py:38
  38.2 2.1 %collective-permute-start.9 = (bf16[4,2,32,2048]{3,2,1,0:T(8,128)(2,1)S(1)}, bf16[4,2,32,2048]{3,2,1,0:T(8,128)(2,1)S(1)}, u32[]{:S(2)}, u32[]{:S(2)}) collective-permute-start(bf16[4,2,32,2048]{3,2,1,0:T(8,128)(2,1)S(1)} %get-tuple-element.57), channel_id=1, source_target_pairs={{0,6},{1,25},{4,2},{5,29},{2,4},{3,27},{6,0},{7,31},{8,14},{9,17},... | collective-permute-start | bytes 3145736 | tf_op jit(solution)/shard_map/ppermute | solution.py:38
  40.3 2.8 %copy-done = bf16[2,4096,384]{2,1,0:T(8,128)(2,1)S(1)} copy-done((bf16[2,4096,384]{2,1,0:T(8,128)(2,1)S(1)}, bf16[2,4096,384]{2,1,0:T(8,128)(2,1)}, u32[]{:S(2)}) %copy-start) | copy-done | bytes 6291480
  43.1 2.8 %copy-done.1 = bf16[2,4096,384]{2,1,0:T(8,128)(2,1)S(1)} copy-done((bf16[2,4096,384]{2,1,0:T(8,128)(2,1)S(1)}, bf16[2,4096,384]{2,1,0:T(8,128)(2,1)}, u32[]{:S(2)}) %copy-start.1) | copy-done | bytes 6291480
  45.8 3.3 %shard_map.75 = (bf16[2,4096,768]{2,1,0:T(8,128)(2,1)S(1)}, bf16[4,128,256]{2,1,0:T(8,128)(2,1)S(1)}, bf16[4,128,256]{2,1,0:T(8,128)(2,1)S(1)}) custom-call(f32[1,256]{1,0:T(1,128)S(1)} %convert_element_type.47.wanted_ref, bf16[2,4096,384]{2,1,0:T(8,128)(2,1)S(1)} %copy-done, bf16[2,4096,384]{2,1,0:T(8,128)(2,1)S(1)} %copy-done.1, ...), custom_call_target="tpu_custom_call" | custom-call | flops 1 | bytes 1 | tf_op jit(solution)/shard_map/pallas_call | solution.py:276
  49.1 2.4 %collective-permute-done.8.refs_1_ = bf16[4,2,32,2048]{3,2,1,0:T(8,128)(2,1)S(1)} collective-permute-done((bf16[4,2,32,2048]{3,2,1,0:T(8,128)(2,1)S(1)}, bf16[4,2,32,2048]{3,2,1,0:T(8,128)(2,1)S(1)}, u32[]{:S(2)}, u32[]{:S(2)}) %collective-permute-start.8) | collective-permute-done | bytes 1048608 | tf_op jit(solution)/shard_map/ppermute | solution.py:38
  51.5 2.7 %collective-permute-done.9.refs_2_ = bf16[4,2,32,2048]{3,2,1,0:T(8,128)(2,1)S(1)} collective-permute-done((bf16[4,2,32,2048]{3,2,1,0:T(8,128)(2,1)S(1)}, bf16[4,2,32,2048]{3,2,1,0:T(8,128)(2,1)S(1)}, u32[]{:S(2)}, u32[]{:S(2)}) %collective-permute-start.9) | collective-permute-done | bytes 1048608 | tf_op jit(solution)/shard_map/ppermute | solution.py:38
  54.7 1.5 %collective-permute-start.7 = (bf16[4,2,32,2048]{3,2,1,0:T(8,128)(2,1)S(1)}, bf16[4,2,32,2048]{3,2,1,0:T(8,128)(2,1)S(1)}, u32[]{:S(2)}, u32[]{:S(2)}) collective-permute-start(bf16[4,2,32,2048]{3,2,1,0:T(8,128)(2,1)S(1)} %get-tuple-element.53), channel_id=1, source_target_pairs={{0,2},{1,17},{4,6},{5,21},{2,0},{3,19},{6,4},{7,23},{8,10},{9,25},... | collective-permute-start | bytes 3145736 | tf_op jit(solution)/shard_map/ppermute | solution.py:37
  56.2 3.2 %shard_map.76.refs_2_ = f32[2,384,768]{2,1,0:T(8,128)S(1)} custom-call(s32[3]{0:T(128)S(1)} %copy-done.2, bf16[4,2,32,2048]{3,2,1,0:T(8,128)(2,1)S(1)} %get-tuple-element.48.refs_0_, bf16[4,2,32,2048]{3,2,1,0:T(8,128)(2,1)S(1)} %collective-permute-done.8.refs_1_, bf16[4,2,32,2048]{3,2,1,0:T(8,128)(2,1)S(1)} %collective-permute-done.9.refs_2_, ...), custom_call_target="tpu_custom_call" | custom-call | flops 1 | bytes 1 | tf_op jit(solution)/shard_map/pallas_call | solution.py:294
  59.4 3.2 %shard_map.77.refs_4_ = f32[2,384,768]{2,1,0:T(8,128)S(1)} custom-call(s32[3]{0:T(128)S(1)} %copy-done.2, bf16[4,2,32,2048]{3,2,1,0:T(8,128)(2,1)S(1)} %collective-permute-done.10.refs_0_, bf16[4,2,32,2048]{3,2,1,0:T(8,128)(2,1)S(1)} %collective-permute-done.11.refs_1_, bf16[4,2,32,2048]{3,2,1,0:T(8,128)(2,1)S(1)} %collective-permute-done.12.refs_2_, ...), custom_call_target="tpu_custom_call" | custom-call | flops 1 | bytes 1 | tf_op jit(solution)/shard_map/pallas_call | solution.py:294
  62.6 8.4 %collective-permute-done.7.refs_0_ = bf16[4,2,32,2048]{3,2,1,0:T(8,128)(2,1)S(1)} collective-permute-done((bf16[4,2,32,2048]{3,2,1,0:T(8,128)(2,1)S(1)}, bf16[4,2,32,2048]{3,2,1,0:T(8,128)(2,1)S(1)}, u32[]{:S(2)}, u32[]{:S(2)}) %collective-permute-start.7) | collective-permute-done | bytes 1048608 | tf_op jit(solution)/shard_map/ppermute | solution.py:37
  71.0 1.6 %shard_map.78.refs_3_ = f32[2,128,768]{2,1,0:T(8,128)S(1)} custom-call(s32[3]{0:T(128)S(1)} %copy-done.2, bf16[4,2,32,2048]{3,2,1,0:T(8,128)(2,1)S(1)} %collective-permute-done.7.refs_0_, bf16[2,4096,768]{2,1,0:T(8,128)(2,1)S(1)} %get-tuple-element.58.refs_3_.refs_1_), custom_call_target="tpu_custom_call" | custom-call | flops 1 | bytes 1 | tf_op jit(solution)/shard_map/pallas_call | solution.py:294
  72.6 1.1 collective-permute-done.13.refs_0_
  73.6 1.8 %shard_map.79.hidden_ref = bf16[2,512,384]{2,1,0:T(8,128)(2,1)S(1)} custom-call(s32[3]{0:T(128)S(1)} %copy-done.2, bf16[4,2,32,2048]{3,2,1,0:T(8,128)(2,1)S(1)} %collective-permute-done.13.refs_0_, bf16[2,4096,768]{2,1,0:T(8,128)(2,1)S(1)} %get-tuple-element.58.refs_3_.refs_1_, f32[2,384,768]{2,1,0:T(8,128)S(1)} %shard_map.76.refs_2_, ...), custom_call_target="tpu_custom_call" | custom-call | flops 1610612736 | bytes 4000000 | tf_op jit(solution)/shard_map/pallas_call | solution.py:308
  75.5 1.8 %shard_map.81 = (bf16[4,2,32,1024]{3,2,1,0:T(8,128)(2,1)S(1)}, bf16[4,2,32,1024]{3,2,1,0:T(8,128)(2,1)S(1)}, bf16[4,2,32,1024]{3,2,1,0:T(8,128)(2,1)S(1)}, bf16[4,2,32,1024]{3,2,1,0:T(8,128)(2,1)S(1)}) custom-call(s32[3]{0:T(128)S(1)} %copy-done.2, bf16[2,512,384]{2,1,0:T(8,128)(2,1)S(1)} %shard_map.79.hidden_ref, bf16[2,384,4096]{2,1,0:T(8,128)(2,1)S(1)} %bitcast.7), custom_call_target="tpu_custom_call" | custom-call | flops 805306368 | bytes 5000000 | tf_op jit(solution)/shard_map/pallas_call | solution.py:321
  78.4 1.8 %shard_map.80 = (bf16[4,2,32,1024]{3,2,1,0:T(8,128)(2,1)S(1)}, bf16[4,2,32,1024]{3,2,1,0:T(8,128)(2,1)S(1)}, bf16[4,2,32,1024]{3,2,1,0:T(8,128)(2,1)S(1)}, bf16[4,2,32,1024]{3,2,1,0:T(8,128)(2,1)S(1)}) custom-call(s32[3]{0:T(128)S(1)} %copy-done.2, bf16[2,512,384]{2,1,0:T(8,128)(2,1)S(1)} %shard_map.79.hidden_ref, bf16[2,384,4096]{2,1,0:T(8,128)(2,1)S(1)} %bitcast.7), custom_call_target="tpu_custom_call" | custom-call | flops 805306368 | bytes 5000000 | tf_op jit(solution)/shard_map/pallas_call | solution.py:321
  81.5 1.8 %shard_map.84 = (bf16[4,2,32,1024]{3,2,1,0:T(8,128)(2,1)S(1)}, bf16[4,2,32,1024]{3,2,1,0:T(8,128)(2,1)S(1)}, bf16[4,2,32,1024]{3,2,1,0:T(8,128)(2,1)S(1)}, bf16[4,2,32,1024]{3,2,1,0:T(8,128)(2,1)S(1)}) custom-call(s32[3]{0:T(128)S(1)} %copy-done.2, bf16[2,512,384]{2,1,0:T(8,128)(2,1)S(1)} %shard_map.79.hidden_ref, bf16[2,384,4096]{2,1,0:T(8,128)(2,1)S(1)} %bitcast.7, ...), custom_call_target="tpu_custom_call" | custom-call | flops 805306368 | bytes 5000000 | tf_op jit(solution)/shard_map/pallas_call | solution.py:321
  83.3 1.6 %collective-permute-start.28 = (bf16[4,2,32,1024]{3,2,1,0:T(8,128)(2,1)S(1)}, bf16[4,2,32,1024]{3,2,1,0:T(8,128)(2,1)S(1)}, u32[]{:S(2)}, u32[]{:S(2)}) collective-permute-start(bf16[4,2,32,1024]{3,2,1,0:T(8,128)(2,1)S(1)} %get-tuple-element.79), channel_id=1, source_target_pairs={{0,2},{1,17},{4,6},{5,21},{2,0},{3,19},{6,4},{7,23},{8,10},{9,25},... | collective-permute-start | bytes 1572872 | tf_op jit(solution)/shard_map/ppermute | solution.py:37
  84.9 1.4 %collective-permute-start.29 = (bf16[4,2,32,1024]{3,2,1,0:T(8,128)(2,1)S(1)}, bf16[4,2,32,1024]{3,2,1,0:T(8,128)(2,1)S(1)}, u32[]{:S(2)}, u32[]{:S(2)}) collective-permute-start(bf16[4,2,32,1024]{3,2,1,0:T(8,128)(2,1)S(1)} %get-tuple-element.80), channel_id=1, source_target_pairs={{0,4},{1,9},{4,0},{5,13},{2,6},{3,11},{6,2},{7,15},{8,12},{9,1},{1... | collective-permute-start | bytes 1572872 | tf_op jit(solution)/shard_map/ppermute | solution.py:38
  86.3 1.1 collective-permute-start.30
  87.5 1.8 %shard_map.82 = (bf16[4,2,32,1024]{3,2,1,0:T(8,128)(2,1)S(1)}, bf16[4,2,32,1024]{3,2,1,0:T(8,128)(2,1)S(1)}, bf16[4,2,32,1024]{3,2,1,0:T(8,128)(2,1)S(1)}, bf16[4,2,32,1024]{3,2,1,0:T(8,128)(2,1)S(1)}) custom-call(s32[3]{0:T(128)S(1)} %copy-done.2, bf16[2,512,384]{2,1,0:T(8,128)(2,1)S(1)} %shard_map.79.hidden_ref, bf16[2,384,4096]{2,1,0:T(8,128)(2,1)S(1)} %bitcast.7, ...), custom_call_target="tpu_custom_call" | custom-call | flops 805306368 | bytes 5000000 | tf_op jit(solution)/shard_map/pallas_call | solution.py:321
  89.3 1.6 %collective-permute-start.18 = (bf16[4,2,32,1024]{3,2,1,0:T(8,128)(2,1)S(1)}, bf16[4,2,32,1024]{3,2,1,0:T(8,128)(2,1)S(1)}, u32[]{:S(2)}, u32[]{:S(2)}) collective-permute-start(bf16[4,2,32,1024]{3,2,1,0:T(8,128)(2,1)S(1)} %get-tuple-element.68), channel_id=1, source_target_pairs={{0,2},{1,17},{4,6},{5,21},{2,0},{3,19},{6,4},{7,23},{8,10},{9,25},... | collective-permute-start | bytes 1572872 | tf_op jit(solution)/shard_map/ppermute | solution.py:37
  90.9 1.4 %collective-permute-start.19 = (bf16[4,2,32,1024]{3,2,1,0:T(8,128)(2,1)S(1)}, bf16[4,2,32,1024]{3,2,1,0:T(8,128)(2,1)S(1)}, u32[]{:S(2)}, u32[]{:S(2)}) collective-permute-start(bf16[4,2,32,1024]{3,2,1,0:T(8,128)(2,1)S(1)} %get-tuple-element.69), channel_id=1, source_target_pairs={{0,4},{1,9},{4,0},{5,13},{2,6},{3,11},{6,2},{7,15},{8,12},{9,1},{1... | collective-permute-start | bytes 1572872 | tf_op jit(solution)/shard_map/ppermute | solution.py:38
  92.3 1.8 %collective-permute-done.28.refs_0_ = bf16[4,2,32,1024]{3,2,1,0:T(8,128)(2,1)S(1)} collective-permute-done((bf16[4,2,32,1024]{3,2,1,0:T(8,128)(2,1)S(1)}, bf16[4,2,32,1024]{3,2,1,0:T(8,128)(2,1)S(1)}, u32[]{:S(2)}, u32[]{:S(2)}) %collective-permute-start.28) | collective-permute-done | bytes 524320 | tf_op jit(solution)/shard_map/ppermute | solution.py:37
  94.2 2.1 %collective-permute-start.20 = (bf16[4,2,32,1024]{3,2,1,0:T(8,128)(2,1)S(1)}, bf16[4,2,32,1024]{3,2,1,0:T(8,128)(2,1)S(1)}, u32[]{:S(2)}, u32[]{:S(2)}) collective-permute-start(bf16[4,2,32,1024]{3,2,1,0:T(8,128)(2,1)S(1)} %get-tuple-element.70), channel_id=1, source_target_pairs={{0,6},{1,25},{4,2},{5,29},{2,4},{3,27},{6,0},{7,31},{8,14},{9,17},... | collective-permute-start | bytes 1572872 | tf_op jit(solution)/shard_map/ppermute | solution.py:38
  96.3 2.9 %collective-permute-done.29.refs_1_ = bf16[4,2,32,1024]{3,2,1,0:T(8,128)(2,1)S(1)} collective-permute-done((bf16[4,2,32,1024]{3,2,1,0:T(8,128)(2,1)S(1)}, bf16[4,2,32,1024]{3,2,1,0:T(8,128)(2,1)S(1)}, u32[]{:S(2)}, u32[]{:S(2)}) %collective-permute-start.29) | collective-permute-done | bytes 524320 | tf_op jit(solution)/shard_map/ppermute | solution.py:38
  100.4 2.9 %collective-permute-start.31 = (bf16[128,1024]{1,0:T(8,128)(2,1)S(1)}, bf16[128,1024]{1,0:T(8,128)(2,1)S(1)}, u32[]{:S(2)}, u32[]{:S(2)}) collective-permute-start(bf16[128,1024]{1,0:T(8,128)(2,1)S(1)} %get-tuple-element.83), channel_id=1, source_target_pairs={{0,16},{1,3},{4,20},{5,7},{2,18},{3,1},{6,22},{7,5},{8,24},{9,11},... | collective-permute-start | bytes 786440 | tf_op jit(solution)/shard_map/ppermute | solution.py:37
  104.0 2.9 %collective-permute-done.18.refs_0_ = bf16[4,2,32,1024]{3,2,1,0:T(8,128)(2,1)S(1)} collective-permute-done((bf16[4,2,32,1024]{3,2,1,0:T(8,128)(2,1)S(1)}, bf16[4,2,32,1024]{3,2,1,0:T(8,128)(2,1)S(1)}, u32[]{:S(2)}, u32[]{:S(2)}) %collective-permute-start.18) | collective-permute-done | bytes 524320 | tf_op jit(solution)/shard_map/ppermute | solution.py:37
  106.9 2.6 %collective-permute-start.33 = (bf16[128,1024]{1,0:T(8,128)(2,1)S(1)}, bf16[128,1024]{1,0:T(8,128)(2,1)S(1)}, u32[]{:S(2)}, u32[]{:S(2)}) collective-permute-start(bf16[128,1024]{1,0:T(8,128)(2,1)S(1)} %get-tuple-element.85), channel_id=1, source_target_pairs={{0,24},{1,7},{4,28},{5,3},{2,26},{3,5},{6,30},{7,1},{8,16},{9,15},... | collective-permute-start | bytes 786440 | tf_op jit(solution)/shard_map/ppermute | solution.py:38
  109.5 6.5 %collective-permute-done.19.refs_1_ = bf16[4,2,32,1024]{3,2,1,0:T(8,128)(2,1)S(1)} collective-permute-done((bf16[4,2,32,1024]{3,2,1,0:T(8,128)(2,1)S(1)}, bf16[4,2,32,1024]{3,2,1,0:T(8,128)(2,1)S(1)}, u32[]{:S(2)}, u32[]{:S(2)}) %collective-permute-start.19) | collective-permute-done | bytes 524320 | tf_op jit(solution)/shard_map/ppermute | solution.py:38
  117.3 2.9 %collective-permute-start.21 = (bf16[128,1024]{1,0:T(8,128)(2,1)S(1)}, bf16[128,1024]{1,0:T(8,128)(2,1)S(1)}, u32[]{:S(2)}, u32[]{:S(2)}) collective-permute-start(bf16[128,1024]{1,0:T(8,128)(2,1)S(1)} %get-tuple-element.72), channel_id=1, source_target_pairs={{0,16},{1,3},{4,20},{5,7},{2,18},{3,1},{6,22},{7,5},{8,24},{9,11},... | collective-permute-start | bytes 786440 | tf_op jit(solution)/shard_map/ppermute | solution.py:37
  121.6 3.6 %collective-permute-done.21 = bf16[128,1024]{1,0:T(8,128)(2,1)S(1)} collective-permute-done((bf16[128,1024]{1,0:T(8,128)(2,1)S(1)}, bf16[128,1024]{1,0:T(8,128)(2,1)S(1)}, u32[]{:S(2)}, u32[]{:S(2)}) %collective-permute-start.21) | collective-permute-done | bytes 262176 | tf_op jit(solution)/shard_map/ppermute | solution.py:37
  125.2 2.8 %collective-permute-done.22 = bf16[128,1024]{1,0:T(8,128)(2,1)S(1)} collective-permute-done((bf16[128,1024]{1,0:T(8,128)(2,1)S(1)}, bf16[128,1024]{1,0:T(8,128)(2,1)S(1)}, u32[]{:S(2)}, u32[]{:S(2)}) %collective-permute-start.22) | collective-permute-done | bytes 262176 | tf_op jit(solution)/shard_map/ppermute | solution.py:38
  129.2 3.0 %collective-permute-start.34 = (bf16[32,2048]{1,0:T(8,128)(2,1)S(1)}, bf16[32,2048]{1,0:T(8,128)(2,1)S(1)}, u32[]{:S(2)}, u32[]{:S(2)}) collective-permute-start(bf16[32,2048]{1,0:T(8,128)(2,1)S(1)} %get-tuple-element.92), channel_id=1, source_target_pairs={{0,64},{1,65},{4,68},{5,69},{2,66},{3,67},{6,70},{7,71},{8,72},{9,... | collective-permute-start | bytes 393224 | tf_op jit(solution)/shard_map/ppermute | solution.py:43
  132.2 1.3 collective-permute-start.36
  134.3 2.8 %collective-permute-done.34 = bf16[32,2048]{1,0:T(8,128)(2,1)S(1)} collective-permute-done((bf16[32,2048]{1,0:T(8,128)(2,1)S(1)}, bf16[32,2048]{1,0:T(8,128)(2,1)S(1)}, u32[]{:S(2)}, u32[]{:S(2)}) %collective-permute-start.34) | collective-permute-done | bytes 131104 | tf_op jit(solution)/shard_map/ppermute | solution.py:43
  137.1 1.4 collective-permute-done.36
  138.7 1.2 collective-permute-done.37
  (72 shorter events, 13.6 us)
Async XLA Ops:
  2.7 1.5 %collective-permute-start = (bf16[16,2176]{1,0:T(8,128)(2,1)}, bf16[16,2176]{1,0:T(8,128)(2,1)S(1)}, u32[]{:S(2)}, u32[]{:S(2)}) collective-permute-start(bf16[16,2176]{1,0:T(8,128)(2,1)} %get-tuple-element.47), channel_id=1, source_target_pairs={{0,1},{1,0},{2,3},{3,2},{4,5},{5,4},{6,7},{7,6},{8,9},{9,8},{10,11... | collective-permute-start | bytes 208904 | tf_op jit(solution)/shard_map/ppermute | solution.py:51
  5.1 10.6 %collective-permute-start.2 = (bf16[32,2176]{1,0:T(8,128)(2,1)S(1)}, bf16[32,2176]{1,0:T(8,128)(2,1)S(1)}, u32[]{:S(2)}, u32[]{:S(2)}) collective-permute-start(bf16[32,2176]{1,0:T(8,128)(2,1)S(1)} %pad_maximum_fusion.1), channel_id=1, source_target_pairs={{0,96},{1,33},{4,100},{5,37},{2,98},{3,35},{6,102},{7,39},{8,104},... | collective-permute-start | bytes 417800 | tf_op jit(solution)/shard_map/ppermute | solution.py:45
  9.3 6.4 %collective-permute-start.1 = (bf16[32,2176]{1,0:T(8,128)(2,1)S(1)}, bf16[32,2176]{1,0:T(8,128)(2,1)S(1)}, u32[]{:S(2)}, u32[]{:S(2)}) collective-permute-start(bf16[32,2176]{1,0:T(8,128)(2,1)S(1)} %pad_maximum_fusion.1), channel_id=1, source_target_pairs={{0,32},{1,97},{4,36},{5,101},{2,34},{3,99},{6,38},{7,103},{8,40},{... | collective-permute-start | bytes 417800 | tf_op jit(solution)/shard_map/ppermute | solution.py:44
  9.3 8.1 %collective-permute-start.3 = (bf16[32,2176]{1,0:T(8,128)(2,1)S(1)}, bf16[32,2176]{1,0:T(8,128)(2,1)S(1)}, u32[]{:S(2)}, u32[]{:S(2)}) collective-permute-start(bf16[32,2176]{1,0:T(8,128)(2,1)S(1)} %pad_maximum_fusion.1), channel_id=1, source_target_pairs={{0,64},{1,65},{4,68},{5,69},{2,66},{3,67},{6,70},{7,71},{8,72},{9,... | collective-permute-start | bytes 417800 | tf_op jit(solution)/shard_map/ppermute | solution.py:43
  17.5 11.2 %collective-permute-start.6 = (bf16[128,2176]{1,0:T(8,128)(2,1)S(1)}, bf16[128,2176]{1,0:T(8,128)(2,1)S(1)}, u32[]{:S(2)}, u32[]{:S(2)}) collective-permute-start(bf16[128,2176]{1,0:T(8,128)(2,1)S(1)} %select_dynamic-update-slice_fusion.refs_0_), channel_id=1, source_target_pairs={{0,16},{1,3},{4,20},{5,7},{2,18},{3,1},{6,22},{7,5},{8,24},{9,11},... | collective-permute-start | bytes 1671176 | tf_op jit(solution)/shard_map/ppermute | solution.py:37
  20.8 14.2 %collective-permute-start.5 = (bf16[128,2176]{1,0:T(8,128)(2,1)S(1)}, bf16[128,2176]{1,0:T(8,128)(2,1)S(1)}, u32[]{:S(2)}, u32[]{:S(2)}) collective-permute-start(bf16[128,2176]{1,0:T(8,128)(2,1)S(1)} %select_dynamic-update-slice_fusion.refs_0_), channel_id=1, source_target_pairs={{0,8},{1,5},{4,12},{5,1},{2,10},{3,7},{6,14},{7,3},{8,0},{9,13},{1... | collective-permute-start | bytes 1671176 | tf_op jit(solution)/shard_map/ppermute | solution.py:38
  21.5 13.5 %collective-permute-start.4 = (bf16[128,2176]{1,0:T(8,128)(2,1)S(1)}, bf16[128,2176]{1,0:T(8,128)(2,1)S(1)}, u32[]{:S(2)}, u32[]{:S(2)}) collective-permute-start(bf16[128,2176]{1,0:T(8,128)(2,1)S(1)} %select_dynamic-update-slice_fusion.refs_0_), channel_id=1, source_target_pairs={{0,24},{1,7},{4,28},{5,3},{2,26},{3,5},{6,30},{7,1},{8,16},{9,15},... | collective-permute-start | bytes 1671176 | tf_op jit(solution)/shard_map/ppermute | solution.py:38
  36.6 14.9 %collective-permute-start.8 = (bf16[4,2,32,2048]{3,2,1,0:T(8,128)(2,1)S(1)}, bf16[4,2,32,2048]{3,2,1,0:T(8,128)(2,1)S(1)}, u32[]{:S(2)}, u32[]{:S(2)}) collective-permute-start(bf16[4,2,32,2048]{3,2,1,0:T(8,128)(2,1)S(1)} %get-tuple-element.54), channel_id=1, source_target_pairs={{0,4},{1,9},{4,0},{5,13},{2,6},{3,11},{6,2},{7,15},{8,12},{9,1},{1... | collective-permute-start | bytes 3145736 | tf_op jit(solution)/shard_map/ppermute | solution.py:38
  38.2 16.0 %collective-permute-start.9 = (bf16[4,2,32,2048]{3,2,1,0:T(8,128)(2,1)S(1)}, bf16[4,2,32,2048]{3,2,1,0:T(8,128)(2,1)S(1)}, u32[]{:S(2)}, u32[]{:S(2)}) collective-permute-start(bf16[4,2,32,2048]{3,2,1,0:T(8,128)(2,1)S(1)} %get-tuple-element.57), channel_id=1, source_target_pairs={{0,6},{1,25},{4,2},{5,29},{2,4},{3,27},{6,0},{7,31},{8,14},{9,17},... | collective-permute-start | bytes 3145736 | tf_op jit(solution)/shard_map/ppermute | solution.py:38
  40.3 19.1 %collective-permute-start.10 = (bf16[4,2,32,2048]{3,2,1,0:T(8,128)(2,1)S(1)}, bf16[4,2,32,2048]{3,2,1,0:T(8,128)(2,1)S(1)}, u32[]{:S(2)}, u32[]{:S(2)}) collective-permute-start(bf16[4,2,32,2048]{3,2,1,0:T(8,128)(2,1)S(1)} %get-tuple-element.48.refs_0_), channel_id=1, source_target_pairs={{0,1},{1,0},{2,3},{3,2},{4,5},{5,4},{6,7},{7,6},{8,9},{9,8},{10,11... | collective-permute-start | bytes 3145736 | tf_op jit(solution)/shard_map/ppermute | solution.py:51
  40.3 2.8 %copy-start = (bf16[2,4096,384]{2,1,0:T(8,128)(2,1)S(1)}, bf16[2,4096,384]{2,1,0:T(8,128)(2,1)}, u32[]{:S(2)}) copy-start(bf16[2,4096,384]{2,1,0:T(8,128)(2,1)} %gate_ref) | copy-start | bytes 18874372
  43.0 2.8 %copy-start.1 = (bf16[2,4096,384]{2,1,0:T(8,128)(2,1)S(1)}, bf16[2,4096,384]{2,1,0:T(8,128)(2,1)}, u32[]{:S(2)}) copy-start(bf16[2,4096,384]{2,1,0:T(8,128)(2,1)} %up_ref) | copy-start | bytes 18874372
  45.8 10.4 %copy-start.2 = (s32[3]{0:T(128)S(1)}, s32[3]{0:T(128)}, u32[]{:S(2)}) copy-start(s32[3]{0:T(128)} %pad_add_fusion.core_ref.base_ref) | copy-start | bytes 40
  54.2 5.2 %collective-permute-start.12 = (bf16[4,2,32,2048]{3,2,1,0:T(8,128)(2,1)S(1)}, bf16[4,2,32,2048]{3,2,1,0:T(8,128)(2,1)S(1)}, u32[]{:S(2)}, u32[]{:S(2)}) collective-permute-start(bf16[4,2,32,2048]{3,2,1,0:T(8,128)(2,1)S(1)} %collective-permute-done.9.refs_2_), channel_id=1, source_target_pairs={{0,1},{1,0},{2,3},{3,2},{4,5},{5,4},{6,7},{7,6},{8,9},{9,8},{10,11... | collective-permute-start | bytes 3145736 | tf_op jit(solution)/shard_map/ppermute | solution.py:51
  54.2 5.2 %collective-permute-start.11 = (bf16[4,2,32,2048]{3,2,1,0:T(8,128)(2,1)S(1)}, bf16[4,2,32,2048]{3,2,1,0:T(8,128)(2,1)S(1)}, u32[]{:S(2)}, u32[]{:S(2)}) collective-permute-start(bf16[4,2,32,2048]{3,2,1,0:T(8,128)(2,1)S(1)} %collective-permute-done.8.refs_1_), channel_id=1, source_target_pairs={{0,1},{1,0},{2,3},{3,2},{4,5},{5,4},{6,7},{7,6},{8,9},{9,8},{10,11... | collective-permute-start | bytes 3145736 | tf_op jit(solution)/shard_map/ppermute | solution.py:51
  54.7 16.3 %collective-permute-start.7 = (bf16[4,2,32,2048]{3,2,1,0:T(8,128)(2,1)S(1)}, bf16[4,2,32,2048]{3,2,1,0:T(8,128)(2,1)S(1)}, u32[]{:S(2)}, u32[]{:S(2)}) collective-permute-start(bf16[4,2,32,2048]{3,2,1,0:T(8,128)(2,1)S(1)} %get-tuple-element.53), channel_id=1, source_target_pairs={{0,2},{1,17},{4,6},{5,21},{2,0},{3,19},{6,4},{7,23},{8,10},{9,25},... | collective-permute-start | bytes 3145736 | tf_op jit(solution)/shard_map/ppermute | solution.py:37
  71.0 2.7 %collective-permute-start.13 = (bf16[4,2,32,2048]{3,2,1,0:T(8,128)(2,1)S(1)}, bf16[4,2,32,2048]{3,2,1,0:T(8,128)(2,1)S(1)}, u32[]{:S(2)}, u32[]{:S(2)}) collective-permute-start(bf16[4,2,32,2048]{3,2,1,0:T(8,128)(2,1)S(1)} %collective-permute-done.7.refs_0_), channel_id=1, source_target_pairs={{0,1},{1,0},{2,3},{3,2},{4,5},{5,4},{6,7},{7,6},{8,9},{9,8},{10,11... | collective-permute-start | bytes 3145736 | tf_op jit(solution)/shard_map/ppermute | solution.py:51
  71.0 4.4 %slice-start = ((s8[6291456]{0:T(1024)(128)(4,1)}), s8[4194304]{0:T(1024)(128)(4,1)S(1)}, s32[]{:S(2)}) async-start(s8[6291456]{0:T(1024)(128)(4,1)} %bitcast.6), calls=%async_computation | async-start | bytes 8388608
  72.6 2.9 %slice-start.1 = ((s8[6291456]{0:T(1024)(128)(4,1)}), s8[2097152]{0:T(1024)(128)(4,1)S(1)}, s32[]{:S(2)}) async-start(s8[6291456]{0:T(1024)(128)(4,1)} %bitcast.6), calls=%async_computation.1 | async-start | bytes 4194304
  77.3 3.1 %collective-permute-start.25 = (bf16[4,2,32,1024]{3,2,1,0:T(8,128)(2,1)S(1)}, bf16[4,2,32,1024]{3,2,1,0:T(8,128)(2,1)S(1)}, u32[]{:S(2)}, u32[]{:S(2)}) collective-permute-start(bf16[4,2,32,1024]{3,2,1,0:T(8,128)(2,1)S(1)} %get-tuple-element.76), channel_id=1, source_target_pairs={{0,1},{1,0},{2,3},{3,2},{4,5},{5,4},{6,7},{7,6},{8,9},{9,8},{10,11... | collective-permute-start | bytes 1572872 | tf_op jit(solution)/shard_map/ppermute | solution.py:51
  77.5 3.3 %collective-permute-start.26 = (bf16[4,2,32,1024]{3,2,1,0:T(8,128)(2,1)S(1)}, bf16[4,2,32,1024]{3,2,1,0:T(8,128)(2,1)S(1)}, u32[]{:S(2)}, u32[]{:S(2)}) collective-permute-start(bf16[4,2,32,1024]{3,2,1,0:T(8,128)(2,1)S(1)} %get-tuple-element.77), channel_id=1, source_target_pairs={{0,1},{1,0},{2,3},{3,2},{4,5},{5,4},{6,7},{7,6},{8,9},{9,8},{10,11... | collective-permute-start | bytes 1572872 | tf_op jit(solution)/shard_map/ppermute | solution.py:51
  77.8 3.0 %collective-permute-start.27 = (bf16[4,2,32,1024]{3,2,1,0:T(8,128)(2,1)S(1)}, bf16[4,2,32,1024]{3,2,1,0:T(8,128)(2,1)S(1)}, u32[]{:S(2)}, u32[]{:S(2)}) collective-permute-start(bf16[4,2,32,1024]{3,2,1,0:T(8,128)(2,1)S(1)} %get-tuple-element.78), channel_id=1, source_target_pairs={{0,1},{1,0},{2,3},{3,2},{4,5},{5,4},{6,7},{7,6},{8,9},{9,8},{10,11... | collective-permute-start | bytes 1572872 | tf_op jit(solution)/shard_map/ppermute | solution.py:51
  78.0 3.5 %collective-permute-start.24 = (bf16[4,2,32,1024]{3,2,1,0:T(8,128)(2,1)S(1)}, bf16[4,2,32,1024]{3,2,1,0:T(8,128)(2,1)S(1)}, u32[]{:S(2)}, u32[]{:S(2)}) collective-permute-start(bf16[4,2,32,1024]{3,2,1,0:T(8,128)(2,1)S(1)} %get-tuple-element.63), channel_id=1, source_target_pairs={{0,1},{1,0},{2,3},{3,2},{4,5},{5,4},{6,7},{7,6},{8,9},{9,8},{10,11... | collective-permute-start | bytes 1572872 | tf_op jit(solution)/shard_map/ppermute | solution.py:51
  80.2 4.7 %collective-permute-start.15 = (bf16[4,2,32,1024]{3,2,1,0:T(8,128)(2,1)S(1)}, bf16[4,2,32,1024]{3,2,1,0:T(8,128)(2,1)S(1)}, u32[]{:S(2)}, u32[]{:S(2)}) collective-permute-start(bf16[4,2,32,1024]{3,2,1,0:T(8,128)(2,1)S(1)} %get-tuple-element.65), channel_id=1, source_target_pairs={{0,1},{1,0},{2,3},{3,2},{4,5},{5,4},{6,7},{7,6},{8,9},{9,8},{10,11... | collective-permute-start | bytes 1572872 | tf_op jit(solution)/shard_map/ppermute | solution.py:51
  80.4 6.0 %collective-permute-start.16 = (bf16[4,2,32,1024]{3,2,1,0:T(8,128)(2,1)S(1)}, bf16[4,2,32,1024]{3,2,1,0:T(8,128)(2,1)S(1)}, u32[]{:S(2)}, u32[]{:S(2)}) collective-permute-start(bf16[4,2,32,1024]{3,2,1,0:T(8,128)(2,1)S(1)} %get-tuple-element.66), channel_id=1, source_target_pairs={{0,1},{1,0},{2,3},{3,2},{4,5},{5,4},{6,7},{7,6},{8,9},{9,8},{10,11... | collective-permute-start | bytes 1572872 | tf_op jit(solution)/shard_map/ppermute | solution.py:51
  80.7 6.7 %collective-permute-start.17 = (bf16[4,2,32,1024]{3,2,1,0:T(8,128)(2,1)S(1)}, bf16[4,2,32,1024]{3,2,1,0:T(8,128)(2,1)S(1)}, u32[]{:S(2)}, u32[]{:S(2)}) collective-permute-start(bf16[4,2,32,1024]{3,2,1,0:T(8,128)(2,1)S(1)} %get-tuple-element.67), channel_id=1, source_target_pairs={{0,1},{1,0},{2,3},{3,2},{4,5},{5,4},{6,7},{7,6},{8,9},{9,8},{10,11... | collective-permute-start | bytes 1572872 | tf_op jit(solution)/shard_map/ppermute | solution.py:51
  80.9 6.6 %collective-permute-start.14 = (bf16[4,2,32,1024]{3,2,1,0:T(8,128)(2,1)S(1)}, bf16[4,2,32,1024]{3,2,1,0:T(8,128)(2,1)S(1)}, u32[]{:S(2)}, u32[]{:S(2)}) collective-permute-start(bf16[4,2,32,1024]{3,2,1,0:T(8,128)(2,1)S(1)} %get-tuple-element.62), channel_id=1, source_target_pairs={{0,1},{1,0},{2,3},{3,2},{4,5},{5,4},{6,7},{7,6},{8,9},{9,8},{10,11... | collective-permute-start | bytes 1572872 | tf_op jit(solution)/shard_map/ppermute | solution.py:51
  83.3 10.9 %collective-permute-start.28 = (bf16[4,2,32,1024]{3,2,1,0:T(8,128)(2,1)S(1)}, bf16[4,2,32,1024]{3,2,1,0:T(8,128)(2,1)S(1)}, u32[]{:S(2)}, u32[]{:S(2)}) collective-permute-start(bf16[4,2,32,1024]{3,2,1,0:T(8,128)(2,1)S(1)} %get-tuple-element.79), channel_id=1, source_target_pairs={{0,2},{1,17},{4,6},{5,21},{2,0},{3,19},{6,4},{7,23},{8,10},{9,25},... | collective-permute-start | bytes 1572872 | tf_op jit(solution)/shard_map/ppermute | solution.py:37
  84.9 14.2 %collective-permute-start.29 = (bf16[4,2,32,1024]{3,2,1,0:T(8,128)(2,1)S(1)}, bf16[4,2,32,1024]{3,2,1,0:T(8,128)(2,1)S(1)}, u32[]{:S(2)}, u32[]{:S(2)}) collective-permute-start(bf16[4,2,32,1024]{3,2,1,0:T(8,128)(2,1)S(1)} %get-tuple-element.80), channel_id=1, source_target_pairs={{0,4},{1,9},{4,0},{5,13},{2,6},{3,11},{6,2},{7,15},{8,12},{9,1},{1... | collective-permute-start | bytes 1572872 | tf_op jit(solution)/shard_map/ppermute | solution.py:38
  86.3 13.3 %collective-permute-start.30 = (bf16[4,2,32,1024]{3,2,1,0:T(8,128)(2,1)S(1)}, bf16[4,2,32,1024]{3,2,1,0:T(8,128)(2,1)S(1)}, u32[]{:S(2)}, u32[]{:S(2)}) collective-permute-start(bf16[4,2,32,1024]{3,2,1,0:T(8,128)(2,1)S(1)} %get-tuple-element.81), channel_id=1, source_target_pairs={{0,6},{1,25},{4,2},{5,29},{2,4},{3,27},{6,0},{7,31},{8,14},{9,17},... | collective-permute-start | bytes 1572872 | tf_op jit(solution)/shard_map/ppermute | solution.py:38
  89.3 17.6 %collective-permute-start.18 = (bf16[4,2,32,1024]{3,2,1,0:T(8,128)(2,1)S(1)}, bf16[4,2,32,1024]{3,2,1,0:T(8,128)(2,1)S(1)}, u32[]{:S(2)}, u32[]{:S(2)}) collective-permute-start(bf16[4,2,32,1024]{3,2,1,0:T(8,128)(2,1)S(1)} %get-tuple-element.68), channel_id=1, source_target_pairs={{0,2},{1,17},{4,6},{5,21},{2,0},{3,19},{6,4},{7,23},{8,10},{9,25},... | collective-permute-start | bytes 1572872 | tf_op jit(solution)/shard_map/ppermute | solution.py:37
  90.9 25.1 %collective-permute-start.19 = (bf16[4,2,32,1024]{3,2,1,0:T(8,128)(2,1)S(1)}, bf16[4,2,32,1024]{3,2,1,0:T(8,128)(2,1)S(1)}, u32[]{:S(2)}, u32[]{:S(2)}) collective-permute-start(bf16[4,2,32,1024]{3,2,1,0:T(8,128)(2,1)S(1)} %get-tuple-element.69), channel_id=1, source_target_pairs={{0,4},{1,9},{4,0},{5,13},{2,6},{3,11},{6,2},{7,15},{8,12},{9,1},{1... | collective-permute-start | bytes 1572872 | tf_op jit(solution)/shard_map/ppermute | solution.py:38
  94.2 22.4 %collective-permute-start.20 = (bf16[4,2,32,1024]{3,2,1,0:T(8,128)(2,1)S(1)}, bf16[4,2,32,1024]{3,2,1,0:T(8,128)(2,1)S(1)}, u32[]{:S(2)}, u32[]{:S(2)}) collective-permute-start(bf16[4,2,32,1024]{3,2,1,0:T(8,128)(2,1)S(1)} %get-tuple-element.70), channel_id=1, source_target_pairs={{0,6},{1,25},{4,2},{5,29},{2,4},{3,27},{6,0},{7,31},{8,14},{9,17},... | collective-permute-start | bytes 1572872 | tf_op jit(solution)/shard_map/ppermute | solution.py:38
  100.4 20.4 %collective-permute-start.31 = (bf16[128,1024]{1,0:T(8,128)(2,1)S(1)}, bf16[128,1024]{1,0:T(8,128)(2,1)S(1)}, u32[]{:S(2)}, u32[]{:S(2)}) collective-permute-start(bf16[128,1024]{1,0:T(8,128)(2,1)S(1)} %get-tuple-element.83), channel_id=1, source_target_pairs={{0,16},{1,3},{4,20},{5,7},{2,18},{3,1},{6,22},{7,5},{8,24},{9,11},... | collective-permute-start | bytes 786440 | tf_op jit(solution)/shard_map/ppermute | solution.py:37
  103.3 18.1 %collective-permute-start.32 = (bf16[128,1024]{1,0:T(8,128)(2,1)S(1)}, bf16[128,1024]{1,0:T(8,128)(2,1)S(1)}, u32[]{:S(2)}, u32[]{:S(2)}) collective-permute-start(bf16[128,1024]{1,0:T(8,128)(2,1)S(1)} %get-tuple-element.84), channel_id=1, source_target_pairs={{0,8},{1,5},{4,12},{5,1},{2,10},{3,7},{6,14},{7,3},{8,0},{9,13},{1... | collective-permute-start | bytes 786440 | tf_op jit(solution)/shard_map/ppermute | solution.py:38
  106.9 14.6 %collective-permute-start.33 = (bf16[128,1024]{1,0:T(8,128)(2,1)S(1)}, bf16[128,1024]{1,0:T(8,128)(2,1)S(1)}, u32[]{:S(2)}, u32[]{:S(2)}) collective-permute-start(bf16[128,1024]{1,0:T(8,128)(2,1)S(1)} %get-tuple-element.85), channel_id=1, source_target_pairs={{0,24},{1,7},{4,28},{5,3},{2,26},{3,5},{6,30},{7,1},{8,16},{9,15},... | collective-permute-start | bytes 786440 | tf_op jit(solution)/shard_map/ppermute | solution.py:38
  117.3 8.0 %collective-permute-start.21 = (bf16[128,1024]{1,0:T(8,128)(2,1)S(1)}, bf16[128,1024]{1,0:T(8,128)(2,1)S(1)}, u32[]{:S(2)}, u32[]{:S(2)}) collective-permute-start(bf16[128,1024]{1,0:T(8,128)(2,1)S(1)} %get-tuple-element.72), channel_id=1, source_target_pairs={{0,16},{1,3},{4,20},{5,7},{2,18},{3,1},{6,22},{7,5},{8,24},{9,11},... | collective-permute-start | bytes 786440 | tf_op jit(solution)/shard_map/ppermute | solution.py:37
  120.1 7.8 %collective-permute-start.22 = (bf16[128,1024]{1,0:T(8,128)(2,1)S(1)}, bf16[128,1024]{1,0:T(8,128)(2,1)S(1)}, u32[]{:S(2)}, u32[]{:S(2)}) collective-permute-start(bf16[128,1024]{1,0:T(8,128)(2,1)S(1)} %get-tuple-element.73), channel_id=1, source_target_pairs={{0,8},{1,5},{4,12},{5,1},{2,10},{3,7},{6,14},{7,3},{8,0},{9,13},{1... | collective-permute-start | bytes 786440 | tf_op jit(solution)/shard_map/ppermute | solution.py:38
  120.8 7.6 %collective-permute-start.23 = (bf16[128,1024]{1,0:T(8,128)(2,1)S(1)}, bf16[128,1024]{1,0:T(8,128)(2,1)S(1)}, u32[]{:S(2)}, u32[]{:S(2)}) collective-permute-start(bf16[128,1024]{1,0:T(8,128)(2,1)S(1)} %get-tuple-element.74), channel_id=1, source_target_pairs={{0,24},{1,7},{4,28},{5,3},{2,26},{3,5},{6,30},{7,1},{8,16},{9,15},... | collective-permute-start | bytes 786440 | tf_op jit(solution)/shard_map/ppermute | solution.py:38
  128.7 5.6 %collective-permute-start.35 = (bf16[32,2048]{1,0:T(8,128)(2,1)S(1)}, bf16[32,2048]{1,0:T(8,128)(2,1)S(1)}, u32[]{:S(2)}, u32[]{:S(2)}) collective-permute-start(bf16[32,2048]{1,0:T(8,128)(2,1)S(1)} %get-tuple-element.91), channel_id=1, source_target_pairs={{0,32},{1,97},{4,36},{5,101},{2,34},{3,99},{6,38},{7,103},{8,40},{... | collective-permute-start | bytes 393224 | tf_op jit(solution)/shard_map/ppermute | solution.py:44
  129.2 7.9 %collective-permute-start.34 = (bf16[32,2048]{1,0:T(8,128)(2,1)S(1)}, bf16[32,2048]{1,0:T(8,128)(2,1)S(1)}, u32[]{:S(2)}, u32[]{:S(2)}) collective-permute-start(bf16[32,2048]{1,0:T(8,128)(2,1)S(1)} %get-tuple-element.92), channel_id=1, source_target_pairs={{0,64},{1,65},{4,68},{5,69},{2,66},{3,67},{6,70},{7,71},{8,72},{9,... | collective-permute-start | bytes 393224 | tf_op jit(solution)/shard_map/ppermute | solution.py:43
  132.2 6.3 %collective-permute-start.36 = (bf16[32,2048]{1,0:T(8,128)(2,1)S(1)}, bf16[32,2048]{1,0:T(8,128)(2,1)S(1)}, u32[]{:S(2)}, u32[]{:S(2)}) collective-permute-start(bf16[32,2048]{1,0:T(8,128)(2,1)S(1)} %get-tuple-element.93), channel_id=1, source_target_pairs={{0,96},{1,33},{4,100},{5,37},{2,98},{3,35},{6,102},{7,39},{8,104},... | collective-permute-start | bytes 393224 | tf_op jit(solution)/shard_map/ppermute | solution.py:45
  138.6 1.3 collective-permute-start.37

commit v6 on v5

--- a/solution.py
+++ b/solution.py
@@ -341,11 +341,10 @@
             out_specs=whole(SIDE),
             compiler_params=params(),
         )(high, middle, *taken(values))
-        sums.append(sum(piece.astype(jnp.float32) for piece in taken(exchange(dense, "yx"))))
-    total = jnp.concatenate(sums, axis=1).reshape(SIDE, -1, half)
-    sent = [total[0]] + [total[j].astype(jnp.bfloat16) for j in (1, 2, 3)]
-    sent = exchange_z(sent, first_core)
-    total = sum(piece.astype(jnp.float32) for piece in taken(sent)).astype(jnp.bfloat16).reshape(2, tok_count, half)
+        total = sum(piece.astype(jnp.float32) for piece in taken(exchange(dense, "yx"))).reshape(SIDE, -1, back_step)
+        pieces = exchange_z([total[0]] + [total[j].astype(jnp.bfloat16) for j in (1, 2, 3)], first_core)
+        sums.append(sum(piece.astype(jnp.float32) for piece in taken(pieces)))
+    total = jnp.concatenate(sums, axis=1).astype(jnp.bfloat16).reshape(2, tok_count, half)
     kept = jnp.where(first_core, total[0], total[1])
     got = sibling(jnp.where(first_core, total[1], total[0]))
     return jnp.concatenate([jnp.where(first_core, kept, got), jnp.where(first_core, got, kept)], axis=1)

time: 142 us -> 141 us (level)
  waiting for transfers between devices: 63.9 us -> 57.6 us
  starting transfers between devices: 42.5 us -> 48 us
    ppermute x6, waiting for transfers between devices: 23.3 us -> 19.8 us  [exchange(): over = lax.ppermute(value[2], AXES, partners(axes, 2))]
    ppermute x2 -> x3, starting transfers between devices: 4.54 us -> 7.51 us  [exchange_z(): over = lax.ppermute(value[2], AXES, partners('zz', 2))]
    ppermute x12, waiting for transfers between devices: 25 us -> 23 us  [exchange(): lax.ppermute(value[j], AXES, partners(axes, j))]
    ppermute x2 -> x3, starting transfers between devices: 5.48 us -> 7.44 us  [exchange_z(): lax.ppermute(jnp.where(first_core, value[3], value[1]), AXES, partners('z...]
    ppermute x2 -> x3, waiting for transfers between devices: 4.48 us -> 3.31 us  [exchange_z(): over = lax.ppermute(value[2], AXES, partners('zz', 2))]
    ppermute x2 -> x3, waiting for transfers between devices: 6.23 us -> 7.37 us  [exchange_z(): lax.ppermute(jnp.where(first_core, value[3], value[1]), AXES, partners('z...]
  transfers between devices with their start and end apart: 38 -> 41, of which waited for: 23 -> 22; matrix products, arithmetic and copies ran while one was open for 0% -> 1% of each run, Pallas kernels for 13% -> 13%
where the time goes in v6:
time: 141 us; the launch traced here: 140 us
  waiting for transfers between devices  57.6 us (41%)
  starting transfers between devices  48 us (34%)
  Pallas kernels  25.1 us (18%)
  local copies, waits for them, and re-layouts  5.8 us (4%)
  other arithmetic  2.99 us (2%)
    ppermute x12, waiting for transfers between devices, exchange(): lax.ppermute(value[j], AXES, partners(axes, j))  23 us
    ppermute x6, waiting for transfers between devices, exchange(): over = lax.ppermute(value[2], AXES, partners(axes, 2))  19.8 us
    ppermute x12, starting transfers between devices, exchange(): lax.ppermute(value[j], AXES, partners(axes, j))  15.4 us
    ppermute x6, starting transfers between devices, exchange(): over = lax.ppermute(value[2], AXES, partners(axes, 2))  13.7 us
    pallas_call x3, Pallas kernels, project(): pl.pallas_call(functools.partial(gate_kernel, source=source), out_shape=j...  7.86 us
    ppermute x3, starting transfers between devices, exchange_z(): over = lax.ppermute(value[2], AXES, partners('zz', 2))  7.51 us
    ppermute x3, starting transfers between devices, exchange_z(): lax.ppermute(jnp.where(first_core, value[3], value[1]), AXES, partners('z...  7.44 us
    ppermute x3, waiting for transfers between devices, exchange_z(): lax.ppermute(jnp.where(first_core, value[3], value[1]), AXES, partners('z...  7.37 us
  transfers between devices with their start and end apart: 41, of which 22 were waited for; matrix products, arithmetic and copies ran while one was open for 1% of the time, Pallas kernels for 13%

profile of v6, /device:TPU:0, one launch (start us, length us, event | category | flops | bytes accessed | tf_op | source)
XLA Modules:
  0.0 139.7 jit_solution(2717499500144063369)
XLA Ops:
  0.6 2.0 %shard_map.73 = (bf16[16,2176]{1,0:T(8,128)(2,1)}, bf16[16,2176]{1,0:T(8,128)(2,1)}) custom-call(s32[3]{0:T(128)} %pad_add_fusion.core_ref.base_ref, bf16[16,4096]{1,0:T(8,128)(2,1)} %tokens_ref.1, s32[8,16]{1,0:T(8,128)} %bitcast.8, f32[8,16]{1,0:T(8,128)} %bitcast.9, s32[1,64]{1,0:T(1,128)} %bitcast.10), custom_call_target="tpu_custom_call" | custom-call | tf_op jit(solution)/shard_map/pallas_call | solution.py:234
  2.6 1.5 %collective-permute-done = bf16[16,2176]{1,0:T(8,128)(2,1)S(1)} collective-permute-done((bf16[16,2176]{1,0:T(8,128)(2,1)}, bf16[16,2176]{1,0:T(8,128)(2,1)S(1)}, u32[]{:S(2)}, u32[]{:S(2)}) %collective-permute-start) | collective-permute-done | bytes 69664 | tf_op jit(solution)/shard_map/ppermute | solution.py:51
  5.1 4.2 %collective-permute-start.2 = (bf16[32,2176]{1,0:T(8,128)(2,1)S(1)}, bf16[32,2176]{1,0:T(8,128)(2,1)S(1)}, u32[]{:S(2)}, u32[]{:S(2)}) collective-permute-start(bf16[32,2176]{1,0:T(8,128)(2,1)S(1)} %pad_maximum_fusion), channel_id=1, source_target_pairs={{0,96},{1,33},{4,100},{5,37},{2,98},{3,35},{6,102},{7,39},{8,104},... | collective-permute-start | bytes 417800 | tf_op jit(solution)/shard_map/ppermute | solution.py:45
  9.3 1.6 %collective-permute-start.3 = (bf16[32,2176]{1,0:T(8,128)(2,1)S(1)}, bf16[32,2176]{1,0:T(8,128)(2,1)S(1)}, u32[]{:S(2)}, u32[]{:S(2)}) collective-permute-start(bf16[32,2176]{1,0:T(8,128)(2,1)S(1)} %pad_maximum_fusion), channel_id=1, source_target_pairs={{0,64},{1,65},{4,68},{5,69},{2,66},{3,67},{6,70},{7,71},{8,72},{9,... | collective-permute-start | bytes 417800 | tf_op jit(solution)/shard_map/ppermute | solution.py:43
  10.8 4.8 %collective-permute-done.2 = bf16[32,2176]{1,0:T(8,128)(2,1)S(1)} collective-permute-done((bf16[32,2176]{1,0:T(8,128)(2,1)S(1)}, bf16[32,2176]{1,0:T(8,128)(2,1)S(1)}, u32[]{:S(2)}, u32[]{:S(2)}) %collective-permute-start.2) | collective-permute-done | bytes 139296 | tf_op jit(solution)/shard_map/ppermute | solution.py:45
  15.7 1.7 %collective-permute-done.3 = bf16[32,2176]{1,0:T(8,128)(2,1)S(1)} collective-permute-done((bf16[32,2176]{1,0:T(8,128)(2,1)S(1)}, bf16[32,2176]{1,0:T(8,128)(2,1)S(1)}, u32[]{:S(2)}, u32[]{:S(2)}) %collective-permute-start.3) | collective-permute-done | bytes 139296 | tf_op jit(solution)/shard_map/ppermute | solution.py:43
  17.5 3.3 %collective-permute-start.6 = (bf16[128,2176]{1,0:T(8,128)(2,1)S(1)}, bf16[128,2176]{1,0:T(8,128)(2,1)S(1)}, u32[]{:S(2)}, u32[]{:S(2)}) collective-permute-start(bf16[128,2176]{1,0:T(8,128)(2,1)S(1)} %select_dynamic-update-slice_fusion.refs_0_), channel_id=1, source_target_pairs={{0,16},{1,3},{4,20},{5,7},{2,18},{3,1},{6,22},{7,5},{8,24},{9,11},... | collective-permute-start | bytes 1671176 | tf_op jit(solution)/shard_map/ppermute | solution.py:37
  22.2 6.5 %collective-permute-done.6.refs_3_ = bf16[128,2176]{1,0:T(8,128)(2,1)S(1)} collective-permute-done((bf16[128,2176]{1,0:T(8,128)(2,1)S(1)}, bf16[128,2176]{1,0:T(8,128)(2,1)S(1)}, u32[]{:S(2)}, u32[]{:S(2)}) %collective-permute-start.6) | collective-permute-done | bytes 557088 | tf_op jit(solution)/shard_map/ppermute | solution.py:37
  28.7 6.2 %collective-permute-done.5.refs_2_ = bf16[128,2176]{1,0:T(8,128)(2,1)S(1)} collective-permute-done((bf16[128,2176]{1,0:T(8,128)(2,1)S(1)}, bf16[128,2176]{1,0:T(8,128)(2,1)S(1)}, u32[]{:S(2)}, u32[]{:S(2)}) %collective-permute-start.5) | collective-permute-done | bytes 557088 | tf_op jit(solution)/shard_map/ppermute | solution.py:38
  35.0 1.6 %shard_map.74 = (bf16[4,2,32,2048]{3,2,1,0:T(8,128)(2,1)S(1)}, bf16[4,2,32,2048]{3,2,1,0:T(8,128)(2,1)S(1)}, bf16[4,2,32,2048]{3,2,1,0:T(8,128)(2,1)S(1)}, bf16[4,2,32,2048]{3,2,1,0:T(8,128)(2,1)S(1)}) custom-call(f32[1,256]{1,0:T(1,128)S(1)} %convert_element_type.57.wanted_ref, bf16[128,2176]{1,0:T(8,128)(2,1)S(1)} %select_dynamic-update-slice_fusion.refs_0_, ...), custom_call_target="tpu_custom_call" | custom-call | flops 536870912 | bytes 1000000 | tf_op jit(solution)/shard_map/pallas_call | solution.py:264
  36.6 1.6 %collective-permute-start.8 = (bf16[4,2,32,2048]{3,2,1,0:T(8,128)(2,1)S(1)}, bf16[4,2,32,2048]{3,2,1,0:T(8,128)(2,1)S(1)}, u32[]{:S(2)}, u32[]{:S(2)}) collective-permute-start(bf16[4,2,32,2048]{3,2,1,0:T(8,128)(2,1)S(1)} %get-tuple-element.54), channel_id=1, source_target_pairs={{0,4},{1,9},{4,0},{5,13},{2,6},{3,11},{6,2},{7,15},{8,12},{9,1},{1... | collective-permute-start | bytes 3145736 | tf_op jit(solution)/shard_map/ppermute | solution.py:38
  38.1 2.1 %collective-permute-start.9 = (bf16[4,2,32,2048]{3,2,1,0:T(8,128)(2,1)S(1)}, bf16[4,2,32,2048]{3,2,1,0:T(8,128)(2,1)S(1)}, u32[]{:S(2)}, u32[]{:S(2)}) collective-permute-start(bf16[4,2,32,2048]{3,2,1,0:T(8,128)(2,1)S(1)} %get-tuple-element.57), channel_id=1, source_target_pairs={{0,6},{1,25},{4,2},{5,29},{2,4},{3,27},{6,0},{7,31},{8,14},{9,17},... | collective-permute-start | bytes 3145736 | tf_op jit(solution)/shard_map/ppermute | solution.py:38
  40.2 2.8 %copy-done = bf16[2,4096,384]{2,1,0:T(8,128)(2,1)S(1)} copy-done((bf16[2,4096,384]{2,1,0:T(8,128)(2,1)S(1)}, bf16[2,4096,384]{2,1,0:T(8,128)(2,1)}, u32[]{:S(2)}) %copy-start) | copy-done | bytes 6291480
  43.0 2.8 %copy-done.1 = bf16[2,4096,384]{2,1,0:T(8,128)(2,1)S(1)} copy-done((bf16[2,4096,384]{2,1,0:T(8,128)(2,1)S(1)}, bf16[2,4096,384]{2,1,0:T(8,128)(2,1)}, u32[]{:S(2)}) %copy-start.1) | copy-done | bytes 6291480
  45.8 3.3 %shard_map.75 = (bf16[2,4096,768]{2,1,0:T(8,128)(2,1)S(1)}, bf16[4,128,256]{2,1,0:T(8,128)(2,1)S(1)}, bf16[4,128,256]{2,1,0:T(8,128)(2,1)S(1)}) custom-call(f32[1,256]{1,0:T(1,128)S(1)} %convert_element_type.57.wanted_ref, bf16[2,4096,384]{2,1,0:T(8,128)(2,1)S(1)} %copy-done, bf16[2,4096,384]{2,1,0:T(8,128)(2,1)S(1)} %copy-done.1, ...), custom_call_target="tpu_custom_call" | custom-call | flops 1 | bytes 1 | tf_op jit(solution)/shard_map/pallas_call | solution.py:276
  49.1 2.4 %collective-permute-done.8.refs_1_ = bf16[4,2,32,2048]{3,2,1,0:T(8,128)(2,1)S(1)} collective-permute-done((bf16[4,2,32,2048]{3,2,1,0:T(8,128)(2,1)S(1)}, bf16[4,2,32,2048]{3,2,1,0:T(8,128)(2,1)S(1)}, u32[]{:S(2)}, u32[]{:S(2)}) %collective-permute-start.8) | collective-permute-done | bytes 1048608 | tf_op jit(solution)/shard_map/ppermute | solution.py:38
  51.4 2.7 %collective-permute-done.9.refs_2_ = bf16[4,2,32,2048]{3,2,1,0:T(8,128)(2,1)S(1)} collective-permute-done((bf16[4,2,32,2048]{3,2,1,0:T(8,128)(2,1)S(1)}, bf16[4,2,32,2048]{3,2,1,0:T(8,128)(2,1)S(1)}, u32[]{:S(2)}, u32[]{:S(2)}) %collective-permute-start.9) | collective-permute-done | bytes 1048608 | tf_op jit(solution)/shard_map/ppermute | solution.py:38
  54.7 1.5 %collective-permute-start.7 = (bf16[4,2,32,2048]{3,2,1,0:T(8,128)(2,1)S(1)}, bf16[4,2,32,2048]{3,2,1,0:T(8,128)(2,1)S(1)}, u32[]{:S(2)}, u32[]{:S(2)}) collective-permute-start(bf16[4,2,32,2048]{3,2,1,0:T(8,128)(2,1)S(1)} %get-tuple-element.53), channel_id=1, source_target_pairs={{0,2},{1,17},{4,6},{5,21},{2,0},{3,19},{6,4},{7,23},{8,10},{9,25},... | collective-permute-start | bytes 3145736 | tf_op jit(solution)/shard_map/ppermute | solution.py:37
  56.2 3.2 %shard_map.76.refs_2_ = f32[2,384,768]{2,1,0:T(8,128)S(1)} custom-call(s32[3]{0:T(128)S(1)} %copy-done.2, bf16[4,2,32,2048]{3,2,1,0:T(8,128)(2,1)S(1)} %get-tuple-element.48.refs_0_, bf16[4,2,32,2048]{3,2,1,0:T(8,128)(2,1)S(1)} %collective-permute-done.8.refs_1_, bf16[4,2,32,2048]{3,2,1,0:T(8,128)(2,1)S(1)} %collective-permute-done.9.refs_2_, ...), custom_call_target="tpu_custom_call" | custom-call | flops 1 | bytes 1 | tf_op jit(solution)/shard_map/pallas_call | solution.py:294
  59.4 3.2 %shard_map.77.refs_4_ = f32[2,384,768]{2,1,0:T(8,128)S(1)} custom-call(s32[3]{0:T(128)S(1)} %copy-done.2, bf16[4,2,32,2048]{3,2,1,0:T(8,128)(2,1)S(1)} %collective-permute-done.10.refs_0_, bf16[4,2,32,2048]{3,2,1,0:T(8,128)(2,1)S(1)} %collective-permute-done.11.refs_1_, bf16[4,2,32,2048]{3,2,1,0:T(8,128)(2,1)S(1)} %collective-permute-done.12.refs_2_, ...), custom_call_target="tpu_custom_call" | custom-call | flops 1 | bytes 1 | tf_op jit(solution)/shard_map/pallas_call | solution.py:294
  62.5 8.4 %collective-permute-done.7.refs_0_ = bf16[4,2,32,2048]{3,2,1,0:T(8,128)(2,1)S(1)} collective-permute-done((bf16[4,2,32,2048]{3,2,1,0:T(8,128)(2,1)S(1)}, bf16[4,2,32,2048]{3,2,1,0:T(8,128)(2,1)S(1)}, u32[]{:S(2)}, u32[]{:S(2)}) %collective-permute-start.7) | collective-permute-done | bytes 1048608 | tf_op jit(solution)/shard_map/ppermute | solution.py:37
  71.0 1.6 %shard_map.78.refs_3_ = f32[2,128,768]{2,1,0:T(8,128)S(1)} custom-call(s32[3]{0:T(128)S(1)} %copy-done.2, bf16[4,2,32,2048]{3,2,1,0:T(8,128)(2,1)S(1)} %collective-permute-done.7.refs_0_, bf16[2,4096,768]{2,1,0:T(8,128)(2,1)S(1)} %get-tuple-element.58.refs_3_.refs_1_), custom_call_target="tpu_custom_call" | custom-call | flops 1 | bytes 1 | tf_op jit(solution)/shard_map/pallas_call | solution.py:294
  72.5 1.1 collective-permute-done.13.refs_0_
  73.6 1.8 %shard_map.79.hidden_ref = bf16[2,512,384]{2,1,0:T(8,128)(2,1)S(1)} custom-call(s32[3]{0:T(128)S(1)} %copy-done.2, bf16[4,2,32,2048]{3,2,1,0:T(8,128)(2,1)S(1)} %collective-permute-done.13.refs_0_, bf16[2,4096,768]{2,1,0:T(8,128)(2,1)S(1)} %get-tuple-element.58.refs_3_.refs_1_, f32[2,384,768]{2,1,0:T(8,128)S(1)} %shard_map.76.refs_2_, ...), custom_call_target="tpu_custom_call" | custom-call | flops 1610612736 | bytes 4000000 | tf_op jit(solution)/shard_map/pallas_call | solution.py:308
  75.4 1.8 %shard_map.81 = (bf16[4,2,32,1024]{3,2,1,0:T(8,128)(2,1)S(1)}, bf16[4,2,32,1024]{3,2,1,0:T(8,128)(2,1)S(1)}, bf16[4,2,32,1024]{3,2,1,0:T(8,128)(2,1)S(1)}, bf16[4,2,32,1024]{3,2,1,0:T(8,128)(2,1)S(1)}) custom-call(s32[3]{0:T(128)S(1)} %copy-done.2, bf16[2,512,384]{2,1,0:T(8,128)(2,1)S(1)} %shard_map.79.hidden_ref, bf16[2,384,4096]{2,1,0:T(8,128)(2,1)S(1)} %bitcast.7), custom_call_target="tpu_custom_call" | custom-call | flops 805306368 | bytes 5000000 | tf_op jit(solution)/shard_map/pallas_call | solution.py:321
  78.3 1.8 %shard_map.80 = (bf16[4,2,32,1024]{3,2,1,0:T(8,128)(2,1)S(1)}, bf16[4,2,32,1024]{3,2,1,0:T(8,128)(2,1)S(1)}, bf16[4,2,32,1024]{3,2,1,0:T(8,128)(2,1)S(1)}, bf16[4,2,32,1024]{3,2,1,0:T(8,128)(2,1)S(1)}) custom-call(s32[3]{0:T(128)S(1)} %copy-done.2, bf16[2,512,384]{2,1,0:T(8,128)(2,1)S(1)} %shard_map.79.hidden_ref, bf16[2,384,4096]{2,1,0:T(8,128)(2,1)S(1)} %bitcast.7), custom_call_target="tpu_custom_call" | custom-call | flops 805306368 | bytes 5000000 | tf_op jit(solution)/shard_map/pallas_call | solution.py:321
  81.5 1.8 %shard_map.84 = (bf16[4,2,32,1024]{3,2,1,0:T(8,128)(2,1)S(1)}, bf16[4,2,32,1024]{3,2,1,0:T(8,128)(2,1)S(1)}, bf16[4,2,32,1024]{3,2,1,0:T(8,128)(2,1)S(1)}, bf16[4,2,32,1024]{3,2,1,0:T(8,128)(2,1)S(1)}) custom-call(s32[3]{0:T(128)S(1)} %copy-done.2, bf16[2,512,384]{2,1,0:T(8,128)(2,1)S(1)} %shard_map.79.hidden_ref, bf16[2,384,4096]{2,1,0:T(8,128)(2,1)S(1)} %bitcast.7, ...), custom_call_target="tpu_custom_call" | custom-call | flops 805306368 | bytes 5000000 | tf_op jit(solution)/shard_map/pallas_call | solution.py:321
  83.3 1.6 %collective-permute-start.31 = (bf16[4,2,32,1024]{3,2,1,0:T(8,128)(2,1)S(1)}, bf16[4,2,32,1024]{3,2,1,0:T(8,128)(2,1)S(1)}, u32[]{:S(2)}, u32[]{:S(2)}) collective-permute-start(bf16[4,2,32,1024]{3,2,1,0:T(8,128)(2,1)S(1)} %get-tuple-element.79), channel_id=1, source_target_pairs={{0,2},{1,17},{4,6},{5,21},{2,0},{3,19},{6,4},{7,23},{8,10},{9,25},... | collective-permute-start | bytes 1572872 | tf_op jit(solution)/shard_map/ppermute | solution.py:37
  84.9 1.4 %collective-permute-start.32 = (bf16[4,2,32,1024]{3,2,1,0:T(8,128)(2,1)S(1)}, bf16[4,2,32,1024]{3,2,1,0:T(8,128)(2,1)S(1)}, u32[]{:S(2)}, u32[]{:S(2)}) collective-permute-start(bf16[4,2,32,1024]{3,2,1,0:T(8,128)(2,1)S(1)} %get-tuple-element.80), channel_id=1, source_target_pairs={{0,4},{1,9},{4,0},{5,13},{2,6},{3,11},{6,2},{7,15},{8,12},{9,1},{1... | collective-permute-start | bytes 1572872 | tf_op jit(solution)/shard_map/ppermute | solution.py:38
  86.3 1.1 collective-permute-start.33
  87.5 1.8 %shard_map.82 = (bf16[4,2,32,1024]{3,2,1,0:T(8,128)(2,1)S(1)}, bf16[4,2,32,1024]{3,2,1,0:T(8,128)(2,1)S(1)}, bf16[4,2,32,1024]{3,2,1,0:T(8,128)(2,1)S(1)}, bf16[4,2,32,1024]{3,2,1,0:T(8,128)(2,1)S(1)}) custom-call(s32[3]{0:T(128)S(1)} %copy-done.2, bf16[2,512,384]{2,1,0:T(8,128)(2,1)S(1)} %shard_map.79.hidden_ref, bf16[2,384,4096]{2,1,0:T(8,128)(2,1)S(1)} %bitcast.7, ...), custom_call_target="tpu_custom_call" | custom-call | flops 805306368 | bytes 5000000 | tf_op jit(solution)/shard_map/pallas_call | solution.py:321
  89.3 1.6 %collective-permute-start.18 = (bf16[4,2,32,1024]{3,2,1,0:T(8,128)(2,1)S(1)}, bf16[4,2,32,1024]{3,2,1,0:T(8,128)(2,1)S(1)}, u32[]{:S(2)}, u32[]{:S(2)}) collective-permute-start(bf16[4,2,32,1024]{3,2,1,0:T(8,128)(2,1)S(1)} %get-tuple-element.68), channel_id=1, source_target_pairs={{0,2},{1,17},{4,6},{5,21},{2,0},{3,19},{6,4},{7,23},{8,10},{9,25},... | collective-permute-start | bytes 1572872 | tf_op jit(solution)/shard_map/ppermute | solution.py:37
  90.9 1.4 %collective-permute-start.19 = (bf16[4,2,32,1024]{3,2,1,0:T(8,128)(2,1)S(1)}, bf16[4,2,32,1024]{3,2,1,0:T(8,128)(2,1)S(1)}, u32[]{:S(2)}, u32[]{:S(2)}) collective-permute-start(bf16[4,2,32,1024]{3,2,1,0:T(8,128)(2,1)S(1)} %get-tuple-element.69), channel_id=1, source_target_pairs={{0,4},{1,9},{4,0},{5,13},{2,6},{3,11},{6,2},{7,15},{8,12},{9,1},{1... | collective-permute-start | bytes 1572872 | tf_op jit(solution)/shard_map/ppermute | solution.py:38
  92.3 1.8 %collective-permute-done.31.refs_0_ = bf16[4,2,32,1024]{3,2,1,0:T(8,128)(2,1)S(1)} collective-permute-done((bf16[4,2,32,1024]{3,2,1,0:T(8,128)(2,1)S(1)}, bf16[4,2,32,1024]{3,2,1,0:T(8,128)(2,1)S(1)}, u32[]{:S(2)}, u32[]{:S(2)}) %collective-permute-start.31) | collective-permute-done | bytes 524320 | tf_op jit(solution)/shard_map/ppermute | solution.py:37
  94.2 2.1 %collective-permute-start.20 = (bf16[4,2,32,1024]{3,2,1,0:T(8,128)(2,1)S(1)}, bf16[4,2,32,1024]{3,2,1,0:T(8,128)(2,1)S(1)}, u32[]{:S(2)}, u32[]{:S(2)}) collective-permute-start(bf16[4,2,32,1024]{3,2,1,0:T(8,128)(2,1)S(1)} %get-tuple-element.70), channel_id=1, source_target_pairs={{0,6},{1,25},{4,2},{5,29},{2,4},{3,27},{6,0},{7,31},{8,14},{9,17},... | collective-permute-start | bytes 1572872 | tf_op jit(solution)/shard_map/ppermute | solution.py:38
  96.2 2.9 %collective-permute-done.32.refs_1_ = bf16[4,2,32,1024]{3,2,1,0:T(8,128)(2,1)S(1)} collective-permute-done((bf16[4,2,32,1024]{3,2,1,0:T(8,128)(2,1)S(1)}, bf16[4,2,32,1024]{3,2,1,0:T(8,128)(2,1)S(1)}, u32[]{:S(2)}, u32[]{:S(2)}) %collective-permute-start.32) | collective-permute-done | bytes 524320 | tf_op jit(solution)/shard_map/ppermute | solution.py:38
  100.4 2.9 %collective-permute-start.34 = (bf16[128,1024]{1,0:T(8,128)(2,1)S(1)}, bf16[128,1024]{1,0:T(8,128)(2,1)S(1)}, u32[]{:S(2)}, u32[]{:S(2)}) collective-permute-start(bf16[128,1024]{1,0:T(8,128)(2,1)S(1)} %get-tuple-element.83), channel_id=1, source_target_pairs={{0,16},{1,3},{4,20},{5,7},{2,18},{3,1},{6,22},{7,5},{8,24},{9,11},... | collective-permute-start | bytes 786440 | tf_op jit(solution)/shard_map/ppermute | solution.py:37
  103.9 2.9 %collective-permute-done.18.refs_0_ = bf16[4,2,32,1024]{3,2,1,0:T(8,128)(2,1)S(1)} collective-permute-done((bf16[4,2,32,1024]{3,2,1,0:T(8,128)(2,1)S(1)}, bf16[4,2,32,1024]{3,2,1,0:T(8,128)(2,1)S(1)}, u32[]{:S(2)}, u32[]{:S(2)}) %collective-permute-start.18) | collective-permute-done | bytes 524320 | tf_op jit(solution)/shard_map/ppermute | solution.py:37
  106.9 2.6 %collective-permute-start.36 = (bf16[128,1024]{1,0:T(8,128)(2,1)S(1)}, bf16[128,1024]{1,0:T(8,128)(2,1)S(1)}, u32[]{:S(2)}, u32[]{:S(2)}) collective-permute-start(bf16[128,1024]{1,0:T(8,128)(2,1)S(1)} %get-tuple-element.85), channel_id=1, source_target_pairs={{0,24},{1,7},{4,28},{5,3},{2,26},{3,5},{6,30},{7,1},{8,16},{9,15},... | collective-permute-start | bytes 786440 | tf_op jit(solution)/shard_map/ppermute | solution.py:38
  109.5 6.5 %collective-permute-done.19.refs_1_ = bf16[4,2,32,1024]{3,2,1,0:T(8,128)(2,1)S(1)} collective-permute-done((bf16[4,2,32,1024]{3,2,1,0:T(8,128)(2,1)S(1)}, bf16[4,2,32,1024]{3,2,1,0:T(8,128)(2,1)S(1)}, u32[]{:S(2)}, u32[]{:S(2)}) %collective-permute-start.19) | collective-permute-done | bytes 524320 | tf_op jit(solution)/shard_map/ppermute | solution.py:38
  117.3 2.9 %collective-permute-start.21 = (bf16[128,1024]{1,0:T(8,128)(2,1)S(1)}, bf16[128,1024]{1,0:T(8,128)(2,1)S(1)}, u32[]{:S(2)}, u32[]{:S(2)}) collective-permute-start(bf16[128,1024]{1,0:T(8,128)(2,1)S(1)} %get-tuple-element.72), channel_id=1, source_target_pairs={{0,16},{1,3},{4,20},{5,7},{2,18},{3,1},{6,22},{7,5},{8,24},{9,11},... | collective-permute-start | bytes 786440 | tf_op jit(solution)/shard_map/ppermute | solution.py:37
  122.1 3.0 %collective-permute-start.37 = (bf16[32,1024]{1,0:T(8,128)(2,1)S(1)}, bf16[32,1024]{1,0:T(8,128)(2,1)S(1)}, u32[]{:S(2)}, u32[]{:S(2)}) collective-permute-start(bf16[32,1024]{1,0:T(8,128)(2,1)S(1)} %get-tuple-element.99), channel_id=1, source_target_pairs={{0,64},{1,65},{4,68},{5,69},{2,66},{3,67},{6,70},{7,71},{8,72},{9,... | collective-permute-start | bytes 196616 | tf_op jit(solution)/shard_map/ppermute | solution.py:43
  125.2 2.0 %collective-permute-start.39 = (bf16[32,1024]{1,0:T(8,128)(2,1)S(1)}, bf16[32,1024]{1,0:T(8,128)(2,1)S(1)}, u32[]{:S(2)}, u32[]{:S(2)}) collective-permute-start(bf16[32,1024]{1,0:T(8,128)(2,1)S(1)} %get-tuple-element.100), channel_id=1, source_target_pairs={{0,96},{1,33},{4,100},{5,37},{2,98},{3,35},{6,102},{7,39},{8,104},... | collective-permute-start | bytes 196616 | tf_op jit(solution)/shard_map/ppermute | solution.py:45
  129.1 3.0 %collective-permute-start.24 = (bf16[32,1024]{1,0:T(8,128)(2,1)S(1)}, bf16[32,1024]{1,0:T(8,128)(2,1)S(1)}, u32[]{:S(2)}, u32[]{:S(2)}) collective-permute-start(bf16[32,1024]{1,0:T(8,128)(2,1)S(1)} %get-tuple-element.96), channel_id=1, source_target_pairs={{0,64},{1,65},{4,68},{5,69},{2,66},{3,67},{6,70},{7,71},{8,72},{9,... | collective-permute-start | bytes 196616 | tf_op jit(solution)/shard_map/ppermute | solution.py:43
  132.1 1.3 collective-permute-start.26
  133.4 1.6 %collective-permute-done.24 = bf16[32,1024]{1,0:T(8,128)(2,1)S(1)} collective-permute-done((bf16[32,1024]{1,0:T(8,128)(2,1)S(1)}, bf16[32,1024]{1,0:T(8,128)(2,1)S(1)}, u32[]{:S(2)}, u32[]{:S(2)}) %collective-permute-start.24) | collective-permute-done | bytes 65568 | tf_op jit(solution)/shard_map/ppermute | solution.py:43
  135.0 2.5 %collective-permute-done.26 = bf16[32,1024]{1,0:T(8,128)(2,1)S(1)} collective-permute-done((bf16[32,1024]{1,0:T(8,128)(2,1)S(1)}, bf16[32,1024]{1,0:T(8,128)(2,1)S(1)}, u32[]{:S(2)}, u32[]{:S(2)}) %collective-permute-start.26) | collective-permute-done | bytes 65568 | tf_op jit(solution)/shard_map/ppermute | solution.py:45
  137.7 1.2 collective-permute-done.40
  (79 shorter events, 14.2 us)
Async XLA Ops:
  2.6 1.5 %collective-permute-start = (bf16[16,2176]{1,0:T(8,128)(2,1)}, bf16[16,2176]{1,0:T(8,128)(2,1)S(1)}, u32[]{:S(2)}, u32[]{:S(2)}) collective-permute-start(bf16[16,2176]{1,0:T(8,128)(2,1)} %get-tuple-element.47), channel_id=1, source_target_pairs={{0,1},{1,0},{2,3},{3,2},{4,5},{5,4},{6,7},{7,6},{8,9},{9,8},{10,11... | collective-permute-start | bytes 208904 | tf_op jit(solution)/shard_map/ppermute | solution.py:51
  5.1 10.6 %collective-permute-start.2 = (bf16[32,2176]{1,0:T(8,128)(2,1)S(1)}, bf16[32,2176]{1,0:T(8,128)(2,1)S(1)}, u32[]{:S(2)}, u32[]{:S(2)}) collective-permute-start(bf16[32,2176]{1,0:T(8,128)(2,1)S(1)} %pad_maximum_fusion), channel_id=1, source_target_pairs={{0,96},{1,33},{4,100},{5,37},{2,98},{3,35},{6,102},{7,39},{8,104},... | collective-permute-start | bytes 417800 | tf_op jit(solution)/shard_map/ppermute | solution.py:45
  9.3 6.4 %collective-permute-start.1 = (bf16[32,2176]{1,0:T(8,128)(2,1)S(1)}, bf16[32,2176]{1,0:T(8,128)(2,1)S(1)}, u32[]{:S(2)}, u32[]{:S(2)}) collective-permute-start(bf16[32,2176]{1,0:T(8,128)(2,1)S(1)} %pad_maximum_fusion), channel_id=1, source_target_pairs={{0,32},{1,97},{4,36},{5,101},{2,34},{3,99},{6,38},{7,103},{8,40},{... | collective-permute-start | bytes 417800 | tf_op jit(solution)/shard_map/ppermute | solution.py:44
  9.3 8.1 %collective-permute-start.3 = (bf16[32,2176]{1,0:T(8,128)(2,1)S(1)}, bf16[32,2176]{1,0:T(8,128)(2,1)S(1)}, u32[]{:S(2)}, u32[]{:S(2)}) collective-permute-start(bf16[32,2176]{1,0:T(8,128)(2,1)S(1)} %pad_maximum_fusion), channel_id=1, source_target_pairs={{0,64},{1,65},{4,68},{5,69},{2,66},{3,67},{6,70},{7,71},{8,72},{9,... | collective-permute-start | bytes 417800 | tf_op jit(solution)/shard_map/ppermute | solution.py:43
  17.5 11.2 %collective-permute-start.6 = (bf16[128,2176]{1,0:T(8,128)(2,1)S(1)}, bf16[128,2176]{1,0:T(8,128)(2,1)S(1)}, u32[]{:S(2)}, u32[]{:S(2)}) collective-permute-start(bf16[128,2176]{1,0:T(8,128)(2,1)S(1)} %select_dynamic-update-slice_fusion.refs_0_), channel_id=1, source_target_pairs={{0,16},{1,3},{4,20},{5,7},{2,18},{3,1},{6,22},{7,5},{8,24},{9,11},... | collective-permute-start | bytes 1671176 | tf_op jit(solution)/shard_map/ppermute | solution.py:37
  20.8 14.2 %collective-permute-start.5 = (bf16[128,2176]{1,0:T(8,128)(2,1)S(1)}, bf16[128,2176]{1,0:T(8,128)(2,1)S(1)}, u32[]{:S(2)}, u32[]{:S(2)}) collective-permute-start(bf16[128,2176]{1,0:T(8,128)(2,1)S(1)} %select_dynamic-update-slice_fusion.refs_0_), channel_id=1, source_target_pairs={{0,8},{1,5},{4,12},{5,1},{2,10},{3,7},{6,14},{7,3},{8,0},{9,13},{1... | collective-permute-start | bytes 1671176 | tf_op jit(solution)/shard_map/ppermute | solution.py:38
  21.5 13.5 %collective-permute-start.4 = (bf16[128,2176]{1,0:T(8,128)(2,1)S(1)}, bf16[128,2176]{1,0:T(8,128)(2,1)S(1)}, u32[]{:S(2)}, u32[]{:S(2)}) collective-permute-start(bf16[128,2176]{1,0:T(8,128)(2,1)S(1)} %select_dynamic-update-slice_fusion.refs_0_), channel_id=1, source_target_pairs={{0,24},{1,7},{4,28},{5,3},{2,26},{3,5},{6,30},{7,1},{8,16},{9,15},... | collective-permute-start | bytes 1671176 | tf_op jit(solution)/shard_map/ppermute | solution.py:38
  36.6 14.9 %collective-permute-start.8 = (bf16[4,2,32,2048]{3,2,1,0:T(8,128)(2,1)S(1)}, bf16[4,2,32,2048]{3,2,1,0:T(8,128)(2,1)S(1)}, u32[]{:S(2)}, u32[]{:S(2)}) collective-permute-start(bf16[4,2,32,2048]{3,2,1,0:T(8,128)(2,1)S(1)} %get-tuple-element.54), channel_id=1, source_target_pairs={{0,4},{1,9},{4,0},{5,13},{2,6},{3,11},{6,2},{7,15},{8,12},{9,1},{1... | collective-permute-start | bytes 3145736 | tf_op jit(solution)/shard_map/ppermute | solution.py:38
  38.1 16.0 %collective-permute-start.9 = (bf16[4,2,32,2048]{3,2,1,0:T(8,128)(2,1)S(1)}, bf16[4,2,32,2048]{3,2,1,0:T(8,128)(2,1)S(1)}, u32[]{:S(2)}, u32[]{:S(2)}) collective-permute-start(bf16[4,2,32,2048]{3,2,1,0:T(8,128)(2,1)S(1)} %get-tuple-element.57), channel_id=1, source_target_pairs={{0,6},{1,25},{4,2},{5,29},{2,4},{3,27},{6,0},{7,31},{8,14},{9,17},... | collective-permute-start | bytes 3145736 | tf_op jit(solution)/shard_map/ppermute | solution.py:38
  40.2 19.1 %collective-permute-start.10 = (bf16[4,2,32,2048]{3,2,1,0:T(8,128)(2,1)S(1)}, bf16[4,2,32,2048]{3,2,1,0:T(8,128)(2,1)S(1)}, u32[]{:S(2)}, u32[]{:S(2)}) collective-permute-start(bf16[4,2,32,2048]{3,2,1,0:T(8,128)(2,1)S(1)} %get-tuple-element.48.refs_0_), channel_id=1, source_target_pairs={{0,1},{1,0},{2,3},{3,2},{4,5},{5,4},{6,7},{7,6},{8,9},{9,8},{10,11... | collective-permute-start | bytes 3145736 | tf_op jit(solution)/shard_map/ppermute | solution.py:51
  40.2 2.8 %copy-start = (bf16[2,4096,384]{2,1,0:T(8,128)(2,1)S(1)}, bf16[2,4096,384]{2,1,0:T(8,128)(2,1)}, u32[]{:S(2)}) copy-start(bf16[2,4096,384]{2,1,0:T(8,128)(2,1)} %gate_ref) | copy-start | bytes 18874372
  43.0 2.8 %copy-start.1 = (bf16[2,4096,384]{2,1,0:T(8,128)(2,1)S(1)}, bf16[2,4096,384]{2,1,0:T(8,128)(2,1)}, u32[]{:S(2)}) copy-start(bf16[2,4096,384]{2,1,0:T(8,128)(2,1)} %up_ref) | copy-start | bytes 18874372
  45.8 10.4 %copy-start.2 = (s32[3]{0:T(128)S(1)}, s32[3]{0:T(128)}, u32[]{:S(2)}) copy-start(s32[3]{0:T(128)} %pad_add_fusion.core_ref.base_ref) | copy-start | bytes 40
  54.2 5.2 %collective-permute-start.12 = (bf16[4,2,32,2048]{3,2,1,0:T(8,128)(2,1)S(1)}, bf16[4,2,32,2048]{3,2,1,0:T(8,128)(2,1)S(1)}, u32[]{:S(2)}, u32[]{:S(2)}) collective-permute-start(bf16[4,2,32,2048]{3,2,1,0:T(8,128)(2,1)S(1)} %collective-permute-done.9.refs_2_), channel_id=1, source_target_pairs={{0,1},{1,0},{2,3},{3,2},{4,5},{5,4},{6,7},{7,6},{8,9},{9,8},{10,11... | collective-permute-start | bytes 3145736 | tf_op jit(solution)/shard_map/ppermute | solution.py:51
  54.2 5.2 %collective-permute-start.11 = (bf16[4,2,32,2048]{3,2,1,0:T(8,128)(2,1)S(1)}, bf16[4,2,32,2048]{3,2,1,0:T(8,128)(2,1)S(1)}, u32[]{:S(2)}, u32[]{:S(2)}) collective-permute-start(bf16[4,2,32,2048]{3,2,1,0:T(8,128)(2,1)S(1)} %collective-permute-done.8.refs_1_), channel_id=1, source_target_pairs={{0,1},{1,0},{2,3},{3,2},{4,5},{5,4},{6,7},{7,6},{8,9},{9,8},{10,11... | collective-permute-start | bytes 3145736 | tf_op jit(solution)/shard_map/ppermute | solution.py:51
  54.7 16.3 %collective-permute-start.7 = (bf16[4,2,32,2048]{3,2,1,0:T(8,128)(2,1)S(1)}, bf16[4,2,32,2048]{3,2,1,0:T(8,128)(2,1)S(1)}, u32[]{:S(2)}, u32[]{:S(2)}) collective-permute-start(bf16[4,2,32,2048]{3,2,1,0:T(8,128)(2,1)S(1)} %get-tuple-element.53), channel_id=1, source_target_pairs={{0,2},{1,17},{4,6},{5,21},{2,0},{3,19},{6,4},{7,23},{8,10},{9,25},... | collective-permute-start | bytes 3145736 | tf_op jit(solution)/shard_map/ppermute | solution.py:37
  71.0 2.7 %collective-permute-start.13 = (bf16[4,2,32,2048]{3,2,1,0:T(8,128)(2,1)S(1)}, bf16[4,2,32,2048]{3,2,1,0:T(8,128)(2,1)S(1)}, u32[]{:S(2)}, u32[]{:S(2)}) collective-permute-start(bf16[4,2,32,2048]{3,2,1,0:T(8,128)(2,1)S(1)} %collective-permute-done.7.refs_0_), channel_id=1, source_target_pairs={{0,1},{1,0},{2,3},{3,2},{4,5},{5,4},{6,7},{7,6},{8,9},{9,8},{10,11... | collective-permute-start | bytes 3145736 | tf_op jit(solution)/shard_map/ppermute | solution.py:51
  71.0 4.4 %slice-start = ((s8[6291456]{0:T(1024)(128)(4,1)}), s8[4194304]{0:T(1024)(128)(4,1)S(1)}, s32[]{:S(2)}) async-start(s8[6291456]{0:T(1024)(128)(4,1)} %bitcast.6), calls=%async_computation | async-start | bytes 8388608
  72.5 2.9 %slice-start.1 = ((s8[6291456]{0:T(1024)(128)(4,1)}), s8[2097152]{0:T(1024)(128)(4,1)S(1)}, s32[]{:S(2)}) async-start(s8[6291456]{0:T(1024)(128)(4,1)} %bitcast.6), calls=%async_computation.1 | async-start | bytes 4194304
  77.2 3.1 %collective-permute-start.28 = (bf16[4,2,32,1024]{3,2,1,0:T(8,128)(2,1)S(1)}, bf16[4,2,32,1024]{3,2,1,0:T(8,128)(2,1)S(1)}, u32[]{:S(2)}, u32[]{:S(2)}) collective-permute-start(bf16[4,2,32,1024]{3,2,1,0:T(8,128)(2,1)S(1)} %get-tuple-element.76), channel_id=1, source_target_pairs={{0,1},{1,0},{2,3},{3,2},{4,5},{5,4},{6,7},{7,6},{8,9},{9,8},{10,11... | collective-permute-start | bytes 1572872 | tf_op jit(solution)/shard_map/ppermute | solution.py:51
  77.4 3.3 %collective-permute-start.29 = (bf16[4,2,32,1024]{3,2,1,0:T(8,128)(2,1)S(1)}, bf16[4,2,32,1024]{3,2,1,0:T(8,128)(2,1)S(1)}, u32[]{:S(2)}, u32[]{:S(2)}) collective-permute-start(bf16[4,2,32,1024]{3,2,1,0:T(8,128)(2,1)S(1)} %get-tuple-element.77), channel_id=1, source_target_pairs={{0,1},{1,0},{2,3},{3,2},{4,5},{5,4},{6,7},{7,6},{8,9},{9,8},{10,11... | collective-permute-start | bytes 1572872 | tf_op jit(solution)/shard_map/ppermute | solution.py:51
  77.8 3.0 %collective-permute-start.30 = (bf16[4,2,32,1024]{3,2,1,0:T(8,128)(2,1)S(1)}, bf16[4,2,32,1024]{3,2,1,0:T(8,128)(2,1)S(1)}, u32[]{:S(2)}, u32[]{:S(2)}) collective-permute-start(bf16[4,2,32,1024]{3,2,1,0:T(8,128)(2,1)S(1)} %get-tuple-element.78), channel_id=1, source_target_pairs={{0,1},{1,0},{2,3},{3,2},{4,5},{5,4},{6,7},{7,6},{8,9},{9,8},{10,11... | collective-permute-start | bytes 1572872 | tf_op jit(solution)/shard_map/ppermute | solution.py:51
  78.0 3.5 %collective-permute-start.27 = (bf16[4,2,32,1024]{3,2,1,0:T(8,128)(2,1)S(1)}, bf16[4,2,32,1024]{3,2,1,0:T(8,128)(2,1)S(1)}, u32[]{:S(2)}, u32[]{:S(2)}) collective-permute-start(bf16[4,2,32,1024]{3,2,1,0:T(8,128)(2,1)S(1)} %get-tuple-element.63), channel_id=1, source_target_pairs={{0,1},{1,0},{2,3},{3,2},{4,5},{5,4},{6,7},{7,6},{8,9},{9,8},{10,11... | collective-permute-start | bytes 1572872 | tf_op jit(solution)/shard_map/ppermute | solution.py:51
  80.1 4.7 %collective-permute-start.15 = (bf16[4,2,32,1024]{3,2,1,0:T(8,128)(2,1)S(1)}, bf16[4,2,32,1024]{3,2,1,0:T(8,128)(2,1)S(1)}, u32[]{:S(2)}, u32[]{:S(2)}) collective-permute-start(bf16[4,2,32,1024]{3,2,1,0:T(8,128)(2,1)S(1)} %get-tuple-element.65), channel_id=1, source_target_pairs={{0,1},{1,0},{2,3},{3,2},{4,5},{5,4},{6,7},{7,6},{8,9},{9,8},{10,11... | collective-permute-start | bytes 1572872 | tf_op jit(solution)/shard_map/ppermute | solution.py:51
  80.3 6.0 %collective-permute-start.16 = (bf16[4,2,32,1024]{3,2,1,0:T(8,128)(2,1)S(1)}, bf16[4,2,32,1024]{3,2,1,0:T(8,128)(2,1)S(1)}, u32[]{:S(2)}, u32[]{:S(2)}) collective-permute-start(bf16[4,2,32,1024]{3,2,1,0:T(8,128)(2,1)S(1)} %get-tuple-element.66), channel_id=1, source_target_pairs={{0,1},{1,0},{2,3},{3,2},{4,5},{5,4},{6,7},{7,6},{8,9},{9,8},{10,11... | collective-permute-start | bytes 1572872 | tf_op jit(solution)/shard_map/ppermute | solution.py:51
  80.7 6.7 %collective-permute-start.17 = (bf16[4,2,32,1024]{3,2,1,0:T(8,128)(2,1)S(1)}, bf16[4,2,32,1024]{3,2,1,0:T(8,128)(2,1)S(1)}, u32[]{:S(2)}, u32[]{:S(2)}) collective-permute-start(bf16[4,2,32,1024]{3,2,1,0:T(8,128)(2,1)S(1)} %get-tuple-element.67), channel_id=1, source_target_pairs={{0,1},{1,0},{2,3},{3,2},{4,5},{5,4},{6,7},{7,6},{8,9},{9,8},{10,11... | collective-permute-start | bytes 1572872 | tf_op jit(solution)/shard_map/ppermute | solution.py:51
  80.9 6.6 %collective-permute-start.14 = (bf16[4,2,32,1024]{3,2,1,0:T(8,128)(2,1)S(1)}, bf16[4,2,32,1024]{3,2,1,0:T(8,128)(2,1)S(1)}, u32[]{:S(2)}, u32[]{:S(2)}) collective-permute-start(bf16[4,2,32,1024]{3,2,1,0:T(8,128)(2,1)S(1)} %get-tuple-element.62), channel_id=1, source_target_pairs={{0,1},{1,0},{2,3},{3,2},{4,5},{5,4},{6,7},{7,6},{8,9},{9,8},{10,11... | collective-permute-start | bytes 1572872 | tf_op jit(solution)/shard_map/ppermute | solution.py:51
  83.3 10.9 %collective-permute-start.31 = (bf16[4,2,32,1024]{3,2,1,0:T(8,128)(2,1)S(1)}, bf16[4,2,32,1024]{3,2,1,0:T(8,128)(2,1)S(1)}, u32[]{:S(2)}, u32[]{:S(2)}) collective-permute-start(bf16[4,2,32,1024]{3,2,1,0:T(8,128)(2,1)S(1)} %get-tuple-element.79), channel_id=1, source_target_pairs={{0,2},{1,17},{4,6},{5,21},{2,0},{3,19},{6,4},{7,23},{8,10},{9,25},... | collective-permute-start | bytes 1572872 | tf_op jit(solution)/shard_map/ppermute | solution.py:37
  84.9 14.3 %collective-permute-start.32 = (bf16[4,2,32,1024]{3,2,1,0:T(8,128)(2,1)S(1)}, bf16[4,2,32,1024]{3,2,1,0:T(8,128)(2,1)S(1)}, u32[]{:S(2)}, u32[]{:S(2)}) collective-permute-start(bf16[4,2,32,1024]{3,2,1,0:T(8,128)(2,1)S(1)} %get-tuple-element.80), channel_id=1, source_target_pairs={{0,4},{1,9},{4,0},{5,13},{2,6},{3,11},{6,2},{7,15},{8,12},{9,1},{1... | collective-permute-start | bytes 1572872 | tf_op jit(solution)/shard_map/ppermute | solution.py:38
  86.3 13.3 %collective-permute-start.33 = (bf16[4,2,32,1024]{3,2,1,0:T(8,128)(2,1)S(1)}, bf16[4,2,32,1024]{3,2,1,0:T(8,128)(2,1)S(1)}, u32[]{:S(2)}, u32[]{:S(2)}) collective-permute-start(bf16[4,2,32,1024]{3,2,1,0:T(8,128)(2,1)S(1)} %get-tuple-element.81), channel_id=1, source_target_pairs={{0,6},{1,25},{4,2},{5,29},{2,4},{3,27},{6,0},{7,31},{8,14},{9,17},... | collective-permute-start | bytes 1572872 | tf_op jit(solution)/shard_map/ppermute | solution.py:38
  89.3 17.6 %collective-permute-start.18 = (bf16[4,2,32,1024]{3,2,1,0:T(8,128)(2,1)S(1)}, bf16[4,2,32,1024]{3,2,1,0:T(8,128)(2,1)S(1)}, u32[]{:S(2)}, u32[]{:S(2)}) collective-permute-start(bf16[4,2,32,1024]{3,2,1,0:T(8,128)(2,1)S(1)} %get-tuple-element.68), channel_id=1, source_target_pairs={{0,2},{1,17},{4,6},{5,21},{2,0},{3,19},{6,4},{7,23},{8,10},{9,25},... | collective-permute-start | bytes 1572872 | tf_op jit(solution)/shard_map/ppermute | solution.py:37
  90.9 25.2 %collective-permute-start.19 = (bf16[4,2,32,1024]{3,2,1,0:T(8,128)(2,1)S(1)}, bf16[4,2,32,1024]{3,2,1,0:T(8,128)(2,1)S(1)}, u32[]{:S(2)}, u32[]{:S(2)}) collective-permute-start(bf16[4,2,32,1024]{3,2,1,0:T(8,128)(2,1)S(1)} %get-tuple-element.69), channel_id=1, source_target_pairs={{0,4},{1,9},{4,0},{5,13},{2,6},{3,11},{6,2},{7,15},{8,12},{9,1},{1... | collective-permute-start | bytes 1572872 | tf_op jit(solution)/shard_map/ppermute | solution.py:38
  94.2 22.4 %collective-permute-start.20 = (bf16[4,2,32,1024]{3,2,1,0:T(8,128)(2,1)S(1)}, bf16[4,2,32,1024]{3,2,1,0:T(8,128)(2,1)S(1)}, u32[]{:S(2)}, u32[]{:S(2)}) collective-permute-start(bf16[4,2,32,1024]{3,2,1,0:T(8,128)(2,1)S(1)} %get-tuple-element.70), channel_id=1, source_target_pairs={{0,6},{1,25},{4,2},{5,29},{2,4},{3,27},{6,0},{7,31},{8,14},{9,17},... | collective-permute-start | bytes 1572872 | tf_op jit(solution)/shard_map/ppermute | solution.py:38
  100.4 20.4 %collective-permute-start.34 = (bf16[128,1024]{1,0:T(8,128)(2,1)S(1)}, bf16[128,1024]{1,0:T(8,128)(2,1)S(1)}, u32[]{:S(2)}, u32[]{:S(2)}) collective-permute-start(bf16[128,1024]{1,0:T(8,128)(2,1)S(1)} %get-tuple-element.83), channel_id=1, source_target_pairs={{0,16},{1,3},{4,20},{5,7},{2,18},{3,1},{6,22},{7,5},{8,24},{9,11},... | collective-permute-start | bytes 786440 | tf_op jit(solution)/shard_map/ppermute | solution.py:37
  103.3 18.2 %collective-permute-start.35 = (bf16[128,1024]{1,0:T(8,128)(2,1)S(1)}, bf16[128,1024]{1,0:T(8,128)(2,1)S(1)}, u32[]{:S(2)}, u32[]{:S(2)}) collective-permute-start(bf16[128,1024]{1,0:T(8,128)(2,1)S(1)} %get-tuple-element.84), channel_id=1, source_target_pairs={{0,8},{1,5},{4,12},{5,1},{2,10},{3,7},{6,14},{7,3},{8,0},{9,13},{1... | collective-permute-start | bytes 786440 | tf_op jit(solution)/shard_map/ppermute | solution.py:38
  106.9 14.6 %collective-permute-start.36 = (bf16[128,1024]{1,0:T(8,128)(2,1)S(1)}, bf16[128,1024]{1,0:T(8,128)(2,1)S(1)}, u32[]{:S(2)}, u32[]{:S(2)}) collective-permute-start(bf16[128,1024]{1,0:T(8,128)(2,1)S(1)} %get-tuple-element.85), channel_id=1, source_target_pairs={{0,24},{1,7},{4,28},{5,3},{2,26},{3,5},{6,30},{7,1},{8,16},{9,15},... | collective-permute-start | bytes 786440 | tf_op jit(solution)/shard_map/ppermute | solution.py:38
  117.3 8.0 %collective-permute-start.21 = (bf16[128,1024]{1,0:T(8,128)(2,1)S(1)}, bf16[128,1024]{1,0:T(8,128)(2,1)S(1)}, u32[]{:S(2)}, u32[]{:S(2)}) collective-permute-start(bf16[128,1024]{1,0:T(8,128)(2,1)S(1)} %get-tuple-element.72), channel_id=1, source_target_pairs={{0,16},{1,3},{4,20},{5,7},{2,18},{3,1},{6,22},{7,5},{8,24},{9,11},... | collective-permute-start | bytes 786440 | tf_op jit(solution)/shard_map/ppermute | solution.py:37
  120.1 7.8 %collective-permute-start.22 = (bf16[128,1024]{1,0:T(8,128)(2,1)S(1)}, bf16[128,1024]{1,0:T(8,128)(2,1)S(1)}, u32[]{:S(2)}, u32[]{:S(2)}) collective-permute-start(bf16[128,1024]{1,0:T(8,128)(2,1)S(1)} %get-tuple-element.73), channel_id=1, source_target_pairs={{0,8},{1,5},{4,12},{5,1},{2,10},{3,7},{6,14},{7,3},{8,0},{9,13},{1... | collective-permute-start | bytes 786440 | tf_op jit(solution)/shard_map/ppermute | solution.py:38
  120.8 7.6 %collective-permute-start.23 = (bf16[128,1024]{1,0:T(8,128)(2,1)S(1)}, bf16[128,1024]{1,0:T(8,128)(2,1)S(1)}, u32[]{:S(2)}, u32[]{:S(2)}) collective-permute-start(bf16[128,1024]{1,0:T(8,128)(2,1)S(1)} %get-tuple-element.74), channel_id=1, source_target_pairs={{0,24},{1,7},{4,28},{5,3},{2,26},{3,5},{6,30},{7,1},{8,16},{9,15},... | collective-permute-start | bytes 786440 | tf_op jit(solution)/shard_map/ppermute | solution.py:38
  121.6 10.5 %collective-permute-start.38 = (bf16[32,1024]{1,0:T(8,128)(2,1)S(1)}, bf16[32,1024]{1,0:T(8,128)(2,1)S(1)}, u32[]{:S(2)}, u32[]{:S(2)}) collective-permute-start(bf16[32,1024]{1,0:T(8,128)(2,1)S(1)} %get-tuple-element.98), channel_id=1, source_target_pairs={{0,32},{1,97},{4,36},{5,101},{2,34},{3,99},{6,38},{7,103},{8,40},{... | collective-permute-start | bytes 196616 | tf_op jit(solution)/shard_map/ppermute | solution.py:44
  122.1 11.2 %collective-permute-start.37 = (bf16[32,1024]{1,0:T(8,128)(2,1)S(1)}, bf16[32,1024]{1,0:T(8,128)(2,1)S(1)}, u32[]{:S(2)}, u32[]{:S(2)}) collective-permute-start(bf16[32,1024]{1,0:T(8,128)(2,1)S(1)} %get-tuple-element.99), channel_id=1, source_target_pairs={{0,64},{1,65},{4,68},{5,69},{2,66},{3,67},{6,70},{7,71},{8,72},{9,... | collective-permute-start | bytes 196616 | tf_op jit(solution)/shard_map/ppermute | solution.py:43
  125.2 8.2 %collective-permute-start.39 = (bf16[32,1024]{1,0:T(8,128)(2,1)S(1)}, bf16[32,1024]{1,0:T(8,128)(2,1)S(1)}, u32[]{:S(2)}, u32[]{:S(2)}) collective-permute-start(bf16[32,1024]{1,0:T(8,128)(2,1)S(1)} %get-tuple-element.100), channel_id=1, source_target_pairs={{0,96},{1,33},{4,100},{5,37},{2,98},{3,35},{6,102},{7,39},{8,104},... | collective-permute-start | bytes 196616 | tf_op jit(solution)/shard_map/ppermute | solution.py:45
  128.6 4.8 %collective-permute-start.25 = (bf16[32,1024]{1,0:T(8,128)(2,1)S(1)}, bf16[32,1024]{1,0:T(8,128)(2,1)S(1)}, u32[]{:S(2)}, u32[]{:S(2)}) collective-permute-start(bf16[32,1024]{1,0:T(8,128)(2,1)S(1)} %get-tuple-element.95), channel_id=1, source_target_pairs={{0,32},{1,97},{4,36},{5,101},{2,34},{3,99},{6,38},{7,103},{8,40},{... | collective-permute-start | bytes 196616 | tf_op jit(solution)/shard_map/ppermute | solution.py:44
  129.1 5.9 %collective-permute-start.24 = (bf16[32,1024]{1,0:T(8,128)(2,1)S(1)}, bf16[32,1024]{1,0:T(8,128)(2,1)S(1)}, u32[]{:S(2)}, u32[]{:S(2)}) collective-permute-start(bf16[32,1024]{1,0:T(8,128)(2,1)S(1)} %get-tuple-element.96), channel_id=1, source_target_pairs={{0,64},{1,65},{4,68},{5,69},{2,66},{3,67},{6,70},{7,71},{8,72},{9,... | collective-permute-start | bytes 196616 | tf_op jit(solution)/shard_map/ppermute | solution.py:43
  132.1 5.5 %collective-permute-start.26 = (bf16[32,1024]{1,0:T(8,128)(2,1)S(1)}, bf16[32,1024]{1,0:T(8,128)(2,1)S(1)}, u32[]{:S(2)}, u32[]{:S(2)}) collective-permute-start(bf16[32,1024]{1,0:T(8,128)(2,1)S(1)} %get-tuple-element.97), channel_id=1, source_target_pairs={{0,96},{1,33},{4,100},{5,37},{2,98},{3,35},{6,102},{7,39},{8,104},... | collective-permute-start | bytes 196616 | tf_op jit(solution)/shard_map/ppermute | solution.py:45
  137.6 1.3 collective-permute-start.40
